TPU v7x, 32 devices: a whole 2x2x4 slice. The times are simulated.
32 devices in a mesh: clip: 2 (over y), height: 4 (over z), head: 4 (over x, core).
Axes of the slice: x: 2, y: 2, z: 4, core: 2. Of those that a mesh axis runs over, the one named last changes fastest.
Arguments:
- tokens: bfloat16 [8, 192, 5120], P(('clip', 'height'), None, 'head'), parts along dimension 0, may hold values from -6 to 6
- in_sign: int32 [5120], replicated, may hold values from 0 to 1
- qkv_codes: int32 [640, 3, 3072], P(None, None, 'head'), may hold values from 0 to 65535
- qkv_scale: float32 [3, 3072], P(None, 'head'), may hold values from 0.3 to 3
- qkv_sign: int32 [3, 3072], P(None, 'head'), may hold values from 0 to 1
- windows: int32 [8, 3, 27], P(('clip', 'height')), parts along dimension 0, may hold values from 0 to 11, as said below
- oin_sign: int32 [3072], P('head'), may hold values from 0 to 1
- out_codes: int32 [384, 5120], P('head'), may hold values from 0 to 65535
- out_scale: float32 [5120], replicated, may hold values from 2 to 20
- out_sign: int32 [5120], replicated, may hold values from 0 to 1
Outputs:
- attention_out: bfloat16 [8, 192, 5120], P(('clip', 'height'), 'head'), parts along dimension 0
There are 2 independent parts, one for each index of `clip`. A program takes and returns all parts, laid end to end along the dimension named above; an argument that names none is the same for every part. Nothing has to cross between parts.
Inputs may be any that keep to these rules, and one draw needn't show every extreme that they name: `windows`: each row lists the query tile itself and 26 further entries, each one of the 27 tiles of the 3 x 3 x 3 block of tiles centred on the query tile (each of the three coordinates clipped into the grid of 1 x 4 x 3 tiles); entries may repeat and appear in any order.
All inputs are finite; a program needn't handle non-finite values.
Results may differ from a plain program's by a relative error of at most 0.015.
Values may be sent and summed in bfloat16 or wider, within the bound.
No kernel may reach another device: no remote copies, remote signals or barrier semaphores. Data moves between devices by JAX's collectives and lax.ppermute only.
A program may use at most 128 MiB of HBM per device.

v0:
```python
import functools

import jax
import jax.numpy as jnp
import numpy as np
from jax import lax
from jax.experimental import pallas as pl
from jax.experimental.pallas import tpu as pltpu
from jax.sharding import PartitionSpec as P

D = 5120
HD = 128
HEADS = 24
HAD = 128
TILE = 64
HROWS = 4
WTILES = 3
PLANES = 8
WORDS = HAD // PLANES
EARLY = 2 * TILE

epsilon = 1e-06
f32 = jnp.float32
bf16 = jnp.bfloat16
VMEM = pl.BlockSpec(memory_space=pltpu.VMEM)
SMEM = pl.BlockSpec(memory_space=pltpu.SMEM)
ANY = pl.BlockSpec(memory_space=pl.ANY)


def shape_of(shape, dtype):
    return jax.ShapeDtypeStruct(tuple(shape), dtype)


def call(body, out_shape, in_specs, args, name, flops=0, out_specs=None, megabytes=16, **more):
    if out_specs is None:
        out_specs = jax.tree.map(lambda _: VMEM, out_shape)
    moved = sum(a.size * a.dtype.itemsize for a in args)
    return pl.pallas_call(
        body,
        out_shape=out_shape,
        in_specs=in_specs,
        out_specs=out_specs,
        compiler_params=pltpu.CompilerParams(vmem_limit_bytes=megabytes * 2**20),
        cost_estimate=pl.CostEstimate(
            flops=int(flops), bytes_accessed=int(moved), transcendentals=0
        ),
        name=name,
        **more,
    )(*args)


def lanes(shape=(HAD, HAD)):
    return lax.broadcasted_iota(jnp.int32, shape, len(shape) - 1)


def hadamard(plane_order):
    row = lax.broadcasted_iota(jnp.int32, (HAD, HAD), 0)
    column = lanes()
    if plane_order:
        column = PLANES * (column & (WORDS - 1)) + column // WORDS
    shared = row & column
    shared = shared ^ (shared >> 4)
    shared = shared ^ (shared >> 2)
    shared = shared ^ (shared >> 1)
    return (1 - 2 * (shared & 1)).astype(f32).astype(bf16)


def double_hadamard():
    plain = hadamard(False)
    return jnp.concatenate([plain, plain], 0)


def plane_power(base):
    plane = lanes((1, HAD)) // WORDS
    power = jnp.where(plane & 1 == 1, base, 1.0)
    power = power * jnp.where(plane & 2 == 2, base**2, 1.0)
    return power * jnp.where(plane & 4 == 4, base**4, 1.0)


def turn_factor():
    return plane_power(0.25) * np.float32(HAD ** (-0.5))


def signed(sign_bits):
    return (2 * sign_bits - 1).astype(f32)


def plane_piece(words, k):
    return (words & (3 << (2 * k))).astype(f32).astype(bf16)


def decode(words):
    blocks = []
    for first in range(0, words.shape[0], WORDS):
        part = words[first : first + WORDS]
        blocks += [plane_piece(part, k) for k in range(PLANES)]
    return jnp.concatenate(blocks, 0)


def row_correction(row_list):
    factor_row = plane_power(4.0) * 1.5
    total = None
    for rows in row_list:
        for first in range(0, rows.shape[1], HAD):
            term = rows[:, first : first + HAD].astype(f32)
            total = term if total is None else total + term
    return jnp.sum(total * factor_row, axis=1, keepdims=True)


def rotate_halves(values, doubled):
    high = values.astype(bf16)
    low = (values - high.astype(f32)).astype(bf16)
    return jnp.dot(jnp.concatenate([high, low], 1), doubled, preferred_element_type=f32)


def tile_width(columns):
    for width in (256, 128):
        if columns % width == 0:
            return width


def turn_kernel(place_ref, x_hbm, sign_hbm, own_ref, send_ref, x_ref, sign_ref, sems):
    copies = [
        pltpu.make_async_copy(x_hbm, x_ref, sems.at[0]),
        pltpu.make_async_copy(sign_hbm, sign_ref, sems.at[1]),
    ]
    for copy in copies:
        copy.start()
    matrix = hadamard(True)
    factor = turn_factor()
    for copy in copies:
        copy.wait()
    blocks = x_ref.shape[1] // HAD
    first = place_ref[0] * blocks
    end = place_ref[1]
    tiles = (end, 1, 2 - end)
    for b in range(blocks):
        cols = slice(b * HAD, (b + 1) * HAD)
        sign_row = signed(sign_ref[pl.ds(first + b, 1), :])
        own = [x_ref[pl.ds(pl.multiple_of(t * TILE, TILE), TILE), cols] for t in tiles]
        flipped = (jnp.concatenate(own, 0).astype(f32) * sign_row).astype(bf16)
        turned = jnp.dot(flipped, matrix, preferred_element_type=f32)
        turned = (turned * factor).astype(bf16)
        own_ref[:, cols] = turned
        send_ref[:TILE, cols] = turned[2 * TILE :]
        send_ref[TILE:, cols] = turned[TILE : 2 * TILE]


def turn(place, own_tokens, in_sign):
    sign_rows = in_sign.reshape(-1, HAD)
    rows, inner = own_tokens.shape
    return call(
        turn_kernel,
        (shape_of((rows, inner), bf16), shape_of((EARLY, inner), bf16)),
        [SMEM, ANY, ANY],
        (place, own_tokens, sign_rows),
        "turn",
        flops=2 * own_tokens.size * HAD,
        scratch_shapes=[
            pltpu.VMEM(own_tokens.shape, bf16),
            pltpu.VMEM(sign_rows.shape, jnp.int32),
            pltpu.SemaphoreType.DMA((2,)),
        ],
    )


def prepare_kernel(near, far, place_ref, *rest):
    shard_refs = rest[: len(near)]
    codes_hbm, sums_ref, weights_ref, late_ref, words_ref, sems = rest[len(near) :]
    words, columns = words_ref.shape[1:]
    flips = list(near) + list(far)

    def fetch(piece, kind, flip):
        first = pl.multiple_of((place_ref[0] ^ flip) * words, WORDS)
        return pltpu.make_async_copy(
            codes_hbm.at[kind, pl.ds(first, words), :], words_ref.at[piece], sems.at[piece]
        )

    def piece_of(position, kind):
        return position * 3 + kind

    for position, flip in enumerate(flips):
        for kind in range(3):
            fetch(piece_of(position, kind), kind, flip).start()
    fix = row_correction([ref[...] for ref in shard_refs])
    width = tile_width(columns)
    late_ref[...] = shard_refs[0][:TILE, :]

    def product(kind, carry):
        for position, flip in enumerate(near):
            fetch(piece_of(position, kind), kind, flip).wait()
        for first in range(0, columns, width):
            cols = slice(first, first + width)
            total = -fix
            for position, ref in enumerate(shard_refs):
                weights = decode(words_ref[piece_of(position, kind), :, cols])
                total = total + jnp.dot(ref[...], weights, preferred_element_type=f32)
            sums_ref[kind, :, cols] = total
        return carry

    lax.fori_loop(0, 3, product, 0)
    for position, flip in enumerate(far):

        def unpack(kind, carry):
            piece = piece_of(position + len(near), kind)
            fetch(piece, kind, flip).wait()
            for first in range(0, words, WORDS):
                part = words_ref[piece, first : first + WORDS, :]
                for k in range(PLANES):
                    at = first * PLANES + k * WORDS
                    weights_ref[position, kind, at : at + WORDS, :] = plane_piece(part, k)
            return carry

        lax.fori_loop(0, 3, unpack, 0)


def prepare(place, near, far, shards, codes):
    rows, inner = shards[0].shape
    columns = codes.shape[2]
    pieces = 3 * (len(near) + len(far))
    return call(
        functools.partial(prepare_kernel, near, far),
        (
            shape_of((3, rows, columns), f32),
            shape_of((len(far), 3, inner, columns), bf16),
            shape_of((TILE, inner), bf16),
        ),
        [SMEM] + [VMEM] * len(near) + [ANY],
        (place, *shards, codes),
        "prepare",
        flops=16 * rows * inner * 3 * columns,
        scratch_shapes=[
            pltpu.VMEM((pieces, inner // PLANES, columns), jnp.int32),
            pltpu.SemaphoreType.DMA((pieces,)),
        ],
    )


def project_kernel(kinds, first_row, groups, far, *rest):
    shard_refs = rest[: groups * far]
    sums_ref, weights_ref, scale_ref, sign_ref, out_ref = rest[groups * far :]
    columns = sums_ref.shape[2]
    width = tile_width(columns)
    doubled = double_hadamard()
    ones = jnp.ones((HD, HD), bf16)
    shards = []
    for position in range(far):
        parts = [shard_refs[g * far + position][...] for g in range(groups)]
        shards.append(parts[0] if groups == 1 else jnp.concatenate(parts, 0))
    fix = row_correction(shards)
    row_count = shards[0].shape[0]
    rows = slice(first_row, first_row + row_count)
    for place, kind in enumerate(kinds):
        for first in range(0, columns, width):
            cols = slice(first, first + width)
            part = sums_ref[kind, rows, cols] - fix
            for position in range(far):
                part = part + jnp.dot(
                    shards[position], weights_ref[position, kind, :, cols], preferred_element_type=f32
                )
            for lane in range(0, width, HD):
                at = slice(first + lane, first + lane + HD)
                scale_row = scale_ref[kind : kind + 1, at] * np.float32(D ** (-0.5))
                sign_row = signed(sign_ref[kind : kind + 1, at]) * np.float32(HAD ** (-0.5))
                mixed = rotate_halves(part[:, lane : lane + HD] * scale_row, doubled) * sign_row
                if kind != 2:
                    square = (mixed * mixed).astype(bf16)
                    mean = jnp.dot(square, ones, preferred_element_type=f32) * (1.0 / HD)
                    mixed = mixed * lax.rsqrt(mean + epsilon)
                out_ref[place, :, at] = mixed.astype(bf16)


def project(kinds, first_row, groups, sums, weights, scale, sign):
    far = len(groups[0])
    inner = groups[0][0].shape[1]
    columns = sums.shape[2]
    row_count = sum(group[0].shape[0] for group in groups)
    args = [shard for group in groups for shard in group] + [sums, weights, scale, sign]
    return call(
        functools.partial(project_kernel, kinds, first_row, len(groups), far),
        shape_of((len(kinds), row_count, columns), bf16),
        [VMEM] * len(args),
        args,
        "project",
        flops=2 * row_count * inner * far * len(kinds) * columns,
    )


def attend_kernel(blocks, has_sum, last, share_order, place_ref, q_ref, *rest):
    rest = list(rest)
    kv_refs = [rest.pop(0) for _ in range(blocks)]
    mask_ref = rest.pop(0)
    sum_ref = rest.pop(0) if has_sum else None
    if last:
        oin_ref, out_ref, rotated_ref = rest
    else:
        (out_ref,) = rest
    row_count, columns = q_ref.shape[1:]
    heads = [slice(head, head + HD) for head in range(0, columns, HD)]
    mask = jnp.concatenate(
        [
            jnp.broadcast_to(mask_ref[t : t + 1, :], (TILE, mask_ref.shape[1]))
            for t in range(row_count // TILE)
        ],
        0,
    )
    scores = []
    for at in heads:
        keys = jnp.concatenate([ref[0, :, at] for ref in kv_refs], 0)
        scores.append(
            lax.dot_general(
                q_ref[0, :, at], keys, (((1,), (1,)), ((), ())), preferred_element_type=f32
            )
        )
    weights = [
        (jnp.exp(score * np.float32(HD ** (-0.5))) * mask).astype(bf16) for score in scores
    ]
    totals = []
    for head, at in enumerate(heads):
        values = jnp.concatenate([ref[1, :, at] for ref in kv_refs], 0)
        values = jnp.concatenate([values, jnp.ones_like(values)], 1)
        total = jnp.dot(weights[head], values, preferred_element_type=f32)
        if has_sum:
            total = total + sum_ref[head]
        totals.append(total)
    if not last:
        for head, total in enumerate(totals):
            out_ref[head] = total
        return
    matrix = hadamard(True)
    factor = turn_factor()
    end = place_ref[1]
    for head, at in enumerate(heads):
        attended = (totals[head][:, :HD] / totals[head][:, HD:]).astype(bf16)
        sign_row = signed(oin_ref[head : head + 1, :])
        flipped = (attended.astype(f32) * sign_row).astype(bf16)
        rotated = jnp.dot(flipped, matrix, preferred_element_type=f32) * factor
        for position, tile in enumerate((end, 1, 2 - end)):
            rotated_ref[pl.ds(pl.multiple_of(tile * TILE, TILE), TILE), at] = rotated[
                position * TILE : (position + 1) * TILE
            ]
    share = row_count // len(share_order)
    pieces = []
    for flip in share_order:
        owner = place_ref[0] ^ flip
        pieces.append(rotated_ref[pl.ds(pl.multiple_of(owner * share, 8), share), :])
    out_ref[...] = jnp.concatenate(pieces, 0).astype(bf16)


def attend(place, queries, blocks, mask, running, ending):
    row_count, columns = queries.shape[1:]
    args = [place, queries, *blocks, mask]
    if running is not None:
        args.append(running)
    scratch, share_order = [], None
    if ending is None:
        out_shape = shape_of((columns // HD, row_count, 2 * HD), f32)
    else:
        oin_sign, share_order = ending
        args.append(oin_sign.reshape(-1, HAD))
        out_shape = shape_of((row_count, columns), bf16)
        scratch = [pltpu.VMEM((row_count, columns), f32)]
    return call(
        functools.partial(
            attend_kernel, len(blocks), running is not None, ending is not None, share_order
        ),
        out_shape,
        [SMEM] + [VMEM] * (len(args) - 1),
        args,
        "attend",
        flops=8 * row_count * columns * mask.shape[1],
        scratch_shapes=scratch,
    )


def unpack_out_kernel(codes_ref, after_ref, weights_ref):
    for first in range(0, codes_ref.shape[0], WORDS):

        def some(step, carry):
            cols = pl.ds(pl.multiple_of(step * 512, 512), 512)
            part = codes_ref[first : first + WORDS, cols]
            for k in range(PLANES):
                at = first * PLANES + k * WORDS
                weights_ref[at : at + WORDS, cols] = plane_piece(part, k)
            return carry

        lax.fori_loop(0, codes_ref.shape[1] // 512, some, 0)


def unpack_out(codes, after):
    words, columns = codes.shape
    return call(
        unpack_out_kernel,
        shape_of((words * PLANES, columns), bf16),
        [VMEM, ANY],
        (codes, after),
        "unpack_out",
        flops=2000 * words * columns,
    )


def out_kernel(first, rotated_ref, weights_ref, scale_ref, send_ref, keep_ref):
    rows = rotated_ref[...]
    fix = row_correction([rows])
    half, columns = send_ref.shape
    width = 256
    for at in range(0, columns, width):
        cols = slice(first + at, first + at + width)
        part = jnp.dot(rows, weights_ref[:, cols], preferred_element_type=f32) - fix
        for lane in range(0, width, HAD):
            place = (first + at + lane) // HAD
            scale_row = scale_ref[place : place + 1, :] * np.float32((HEADS * HD) ** (-0.5))
            done = (part[:, lane : lane + HAD] * scale_row).astype(bf16)
            send_ref[:, at + lane : at + lane + HAD] = done[:half]
            keep_ref[:, at + lane : at + lane + HAD] = done[half:]


def out_project(rotated, weights, scale_rows, first, columns):
    row_count, inner = rotated.shape
    result = shape_of((row_count // 2, columns), bf16)
    return call(
        functools.partial(out_kernel, first),
        (result, result),
        [VMEM] * 3,
        (rotated, weights, scale_rows),
        "out_project",
        flops=2 * row_count * inner * columns,
    )


def finish_kernel(first, has_base, sign_ref, keep_ref, more_ref, *rest):
    out_hbm, done_ref, sem = rest[1:] if has_base else rest
    columns = keep_ref.shape[1]
    doubled = double_hadamard()
    for at in range(0, columns, HAD):
        cols = slice(at, at + HAD)
        total = keep_ref[:, cols].astype(f32) + more_ref[:, cols].astype(f32)
        place = (first + at) // HAD
        sign_row = signed(sign_ref[place : place + 1, :]) * np.float32(HAD ** (-0.5))
        done_ref[:, cols] = (rotate_halves(total, doubled) * sign_row).astype(bf16)
    copy = pltpu.make_async_copy(done_ref, out_hbm.at[:, pl.ds(first, columns)], sem)
    copy.start()
    copy.wait()


def finish(base, sign_rows, keep, more, first):
    share, columns = keep.shape
    args = [sign_rows, keep, more]
    in_specs = [VMEM] * 3
    aliases = {}
    if base is not None:
        args.append(base)
        in_specs.append(ANY)
        aliases = {3: 0}
    return call(
        functools.partial(finish_kernel, first, base is not None),
        shape_of((share, D), bf16),
        in_specs,
        args,
        "finish",
        flops=4 * share * columns * HAD,
        out_specs=ANY,
        scratch_shapes=[pltpu.VMEM((share, columns), bf16), pltpu.SemaphoreType.DMA],
        input_output_aliases=aliases,
    )


def swap(shard, bit):
    peers = lax.axis_size("head")
    return lax.ppermute(shard, "head", [(i, i ^ bit) for i in range(peers)])


def row_swaps(row_tiles):
    swaps = []
    for by in (1, 3, 4, 5) if row_tiles > HROWS else (1,):
        for odd in (0, 1):
            low = [i for i in range(row_tiles - by) if (i // by) % 2 == odd]
            swaps.append((by, odd, [(i, i + by) for i in low] + [(i + by, i) for i in low]))
    return swaps


def halving_order(head_count):
    flips = [0]
    bit = head_count // 2
    while bit >= 1:
        flips = [f | bit for f in flips] + flips
        bit //= 2
    return tuple(flips)


CHUNKS = (2048, 3072)


def on_device(
    tokens,
    in_sign,
    qkv_codes,
    qkv_scale,
    qkv_sign,
    windows,
    oin_sign,
    out_codes,
    out_scale,
    out_sign,
):
    head_count = lax.axis_size("head")
    row_tiles = lax.axis_size("height")
    row_place = lax.axis_index("height")
    head_place = lax.axis_index("head").astype(jnp.int32)
    top = head_count // 2
    end = jnp.where(head_place >= top, 0, 2).astype(jnp.int32)
    place = jnp.stack([head_place, end])
    low_bits = [1 << b for b in range(top.bit_length() - 1)]

    own, early = turn(place, tokens[0], in_sign)
    early = {top: swap(early, top)}
    near = {0: own}
    for bit in low_bits:
        for flip in list(near):
            near[flip ^ bit] = swap(near[flip], bit)
    codes = jnp.transpose(qkv_codes, (1, 0, 2))
    near_flips = tuple(sorted(near))
    far_flips = tuple(flip ^ top for flip in near_flips)
    sums, weights, late = prepare(
        place, near_flips, far_flips, [near[flip] for flip in near_flips], codes
    )
    late = {top: swap(late, top)}
    for bit in low_bits:
        for flip in list(early):
            early[flip ^ bit] = swap(early[flip], bit)
    early = [early[flip] for flip in far_flips]
    swaps = row_swaps(row_tiles)
    key_values = [project((1, 2), 0, [early], sums, weights, qkv_scale, qkv_sign)]
    early_blocks = [lax.ppermute(key_values[0], "height", pairs) for _, _, pairs in swaps]
    for bit in low_bits:
        for flip in list(late):
            late[flip ^ bit] = swap(late[flip], bit)
    late = [late[flip] for flip in far_flips]
    key_values.append(project((1, 2), EARLY, [late], sums, weights, qkv_scale, qkv_sign))
    late_blocks = [lax.ppermute(key_values[1], "height", pairs) for _, _, pairs in swaps]
    queries = project((0,), 0, [early, late], sums, weights, qkv_scale, qkv_sign)
    out_weights = unpack_out(out_codes, key_values[1])

    listed = windows[0]
    qtile_count = listed.shape[0]
    listed = jnp.where(end == 0, listed, listed[::-1])
    near_rows = []
    for by, odd, _ in swaps:
        near_rows.append(jnp.where((row_place // by) % 2 == odd, row_place + by, row_place - by))
    near_rows = jnp.stack(near_rows)[:, None] * qtile_count
    tiles = jnp.stack([end, jnp.int32(1), 2 - end])

    def mask_of(ids):
        allowed = jnp.any(listed[:, :, None] == ids.reshape(1, 1, -1), axis=1)
        return jnp.repeat(allowed.astype(f32), TILE, axis=1)

    own_mask = mask_of(row_place * qtile_count + tiles)
    early_mask = mask_of(near_rows + tiles[None, :2])
    late_mask = mask_of(near_rows + tiles[None, 2:])
    running = attend(place, queries, key_values, own_mask, None, None)
    running = attend(place, queries, early_blocks, early_mask, running, None)
    rotated = attend(
        place, queries, late_blocks, late_mask, running, (oin_sign, halving_order(head_count))
    )

    bits = low_bits + [top]
    scale_rows = out_scale.reshape(-1, HAD)
    sign_rows = out_sign.reshape(-1, HAD)
    result = None
    first = 0
    for columns in CHUNKS:
        send, keep = out_project(rotated, out_weights, scale_rows, first, columns)
        for bit in bits:
            more = swap(send, bit)
            if bit == top:
                break
            total = keep.astype(f32) + more.astype(f32)
            half = total.shape[0] // 2
            send, keep = total[:half].astype(bf16), total[half:]
        result = finish(result, sign_rows, keep, more, first)
        first += columns
    return result[None]


def solution(mesh):
    return jax.shard_map(
        on_device,
        mesh=mesh,
        in_specs=(
            P(("clip", "height"), None, "head"),
            P(),
            P(None, None, "head"),
            P(None, "head"),
            P(None, "head"),
            P(("clip", "height"), None, None),
            P("head"),
            P("head", None),
            P(),
            P(),
        ),
        out_specs=P(("clip", "height"), "head", None),
        check_vma=False,
    )
```

profile of v0, /device:TPU:0, one launch (start us, length us, event | category | flops | bytes accessed | tf_op | source)
XLA Modules:
  0.0 88.9 jit_solution(8750508585177317402)
XLA Ops:
  1.8 1.2 %turn.1 = (bf16[192,1280]{1,0:T(8,128)(2,1)S(1)}, bf16[128,1280]{1,0:T(8,128)(2,1)S(1)}) custom-call(s32[2]{0:T(128)S(1)} %get-tuple-element.25.place_ref, bf16[192,1280]{1,0:T(8,128)(2,1)S(1)} %bitcast.17, s32[40,128]{1,0:T(8,128)S(1)} %bitcast.22), custom_call_target="tpu_custom_call" | custom-call | flops 62914560 | bytes 512008 | tf_op jit(solution)/shard_map/turn/pallas_call | solution.py:38
  3.1 3.0 %collective-permute-start = (bf16[128,1280]{1,0:T(8,128)(2,1)S(1)}, bf16[128,1280]{1,0:T(8,128)(2,1)S(1)}, u32[]{:S(2)}, u32[]{:S(2)}) collective-permute-start(bf16[128,1280]{1,0:T(8,128)(2,1)S(1)} %get-tuple-element.14), channel_id=1, source_target_pairs={{0,2},{1,3},{2,0},{3,1},{4,6},{5,7},{6,4},{7,5},{8,10},{9,11},{10,... | collective-permute-start | bytes 983048 | tf_op jit(solution)/shard_map/ppermute | solution.py:470
  8.5 5.3 %collective-permute-done.rest_0_ = bf16[128,1280]{1,0:T(8,128)(2,1)S(1)} collective-permute-done((bf16[128,1280]{1,0:T(8,128)(2,1)S(1)}, bf16[128,1280]{1,0:T(8,128)(2,1)S(1)}, u32[]{:S(2)}, u32[]{:S(2)}) %collective-permute-start) | collective-permute-done | bytes 327712 | tf_op jit(solution)/shard_map/ppermute | solution.py:470
  14.6 2.7 %copy-done.16 = s32[640,3,768]{2,0,1:T(8,128)S(1)} copy-done((s32[640,3,768]{2,0,1:T(8,128)S(1)}, s32[640,3,768]{2,0,1:T(8,128)}, u32[]{:S(2)}) %copy-start.16) | copy-done | bytes 5898264
  18.3 9.5 %prepare.1 = (f32[3,192,768]{2,1,0:T(8,128)S(1)}, bf16[2,3,1280,768]{3,2,1,0:T(8,128)(2,1)S(1)}, bf16[64,1280]{1,0:T(8,128)(2,1)S(1)}) custom-call(s32[2]{0:T(128)S(1)} %get-tuple-element.25.place_ref, bf16[192,1280]{1,0:T(8,128)(2,1)S(1)} %get-tuple-element.15.rest_0_, bf16[192,1280]{1,0:T(8,128)(2,1)S(1)} %copy-done.18, s32[3,640,768]{2,1,0:T(8,128)S(1)} %bitcast.24), custom_call_target="tpu_custom_call" | custom-call | flops 9059696640 | bytes 6881288 | tf_op jit(solution)/shard_map/prepare/pallas_call | solution.py:38
  27.8 1.8 %collective-permute-start.3 = (bf16[64,1280]{1,0:T(8,128)(2,1)S(1)}, bf16[64,1280]{1,0:T(8,128)(2,1)S(1)}, u32[]{:S(2)}, u32[]{:S(2)}) collective-permute-start(bf16[64,1280]{1,0:T(8,128)(2,1)S(1)} %get-tuple-element.16), channel_id=1, source_target_pairs={{0,2},{1,3},{2,0},{3,1},{4,6},{5,7},{6,4},{7,5},{8,10},{9,11},{10,... | collective-permute-start | bytes 491528 | tf_op jit(solution)/shard_map/ppermute | solution.py:470
  29.9 3.4 %project.5.rest_0_ = bf16[2,128,768]{2,1,0:T(8,128)(2,1)S(1)} custom-call(bf16[128,1280]{1,0:T(8,128)(2,1)S(1)} %collective-permute-done.rest_0_, bf16[128,1280]{1,0:T(8,128)(2,1)S(1)} %collective-permute-done.1.rest_1_, f32[3,192,768]{2,1,0:T(8,128)S(1)} %get-tuple-element.17.rest_4_.rest_2_, ...), custom_call_target="tpu_custom_call" | custom-call | flops 1006632960 | bytes 14239744 | tf_op jit(solution)/shard_map/project/pallas_call | solution.py:38
  33.9 4.4 %collective-permute-start.7 = (bf16[2,128,768]{2,1,0:T(8,128)(2,1)S(1)}, bf16[2,128,768]{2,1,0:T(8,128)(2,1)}, u32[]{:S(2)}, u32[]{:S(2)}) collective-permute-start(bf16[2,128,768]{2,1,0:T(8,128)(2,1)S(1)} %project.5.rest_0_), channel_id=1, source_target_pairs={{0,4},{8,12},{4,0},{12,8},{1,5},{9,13},{5,1},{13,9},{2,6},{10,14},... | collective-permute-start | bytes 1179656 | tf_op jit(solution)/shard_map/ppermute | solution.py:534
  39.6 1.3 %copy.12 = f32[3,2]{1,0:T(4,128)} copy(f32[3,2]{0,1:T(2,128)} %convert_element_type.23) | data formatting | bytes 48 | tf_op jit(solution)/shard_map/convert_element_type | solution.py:555
  40.9 1.3 %broadcast_in_dim.8 = f32[3,2,64]{2,1,0:T(2,128)} broadcast(f32[3,2]{1,0:T(4,128)} %copy.12), dimensions={0,1} | broadcast | bytes 1560 | tf_op jit(solution)/shard_map/broadcast_in_dim | solution.py:555
  42.2 1.3 %reshape.109.rest_2_ = f32[3,128]{1,0:T(4,128)} reshape(f32[3,2,64]{2,1,0:T(2,128)} %broadcast_in_dim.8) | data formatting | bytes 3072 | tf_op jit(solution)/shard_map/reshape | solution.py:555
  43.6 1.2 %convert_element_type.24 = f32[3,4]{1,0:T(4,128)} convert(pred[3,4]{1,0:T(4,128)(4,1)} %compare_reduce_fusion.1) | non-fusion elementwise | flops 12 | bytes 60 | tf_op jit(solution)/shard_map/convert_element_type | solution.py:555
  46.3 1.4 %reshape.111.rest_2_ = f32[3,192]{1,0:T(4,128)} reshape(f32[3,3,64]{2,1,0:T(4,128)} %broadcast_in_dim.19) | data formatting | bytes 4608 | tf_op jit(solution)/shard_map/reshape | solution.py:555
  47.6 1.3 %broadcast_in_dim.18 = f32[3,4,64]{2,1,0:T(4,128)} broadcast(f32[3,4]{1,0:T(4,128)} %convert_element_type.24), dimensions={0,1} | broadcast | bytes 3120 | tf_op jit(solution)/shard_map/broadcast_in_dim | solution.py:555
  49.8 4.4 %copy-done.1 = bf16[2,3,1280,768]{3,2,1,0:T(8,128)(2,1)S(1)} copy-done((bf16[2,3,1280,768]{3,2,1,0:T(8,128)(2,1)S(1)}, bf16[2,3,1280,768]{3,2,1,0:T(8,128)(2,1)}, u32[]{:S(2)}) %copy-start.1) | copy-done | bytes 11796504
  54.8 3.9 %project.4.rest_1_.after_ref = bf16[2,64,768]{2,1,0:T(8,128)(2,1)S(1)} custom-call(bf16[64,1280]{1,0:T(8,128)(2,1)S(1)} %collective-permute-done.3.rest_2_.rest_0_, bf16[64,1280]{1,0:T(8,128)(2,1)S(1)} %collective-permute-done.4.rest_3_.rest_1_, f32[3,192,768]{2,1,0:T(8,128)S(1)} %get-tuple-element.17.rest_4_.rest_2_, ...), custom_call_target="tpu_custom_call" | custom-call | flops 503316480 | bytes 13912064 | tf_op jit(solution)/shard_map/project/pallas_call | solution.py:38
  59.6 1.9 %collective-permute-start.5 = (bf16[2,64,768]{2,1,0:T(8,128)(2,1)S(1)}, bf16[2,64,768]{2,1,0:T(8,128)(2,1)S(1)}, u32[]{:S(2)}, u32[]{:S(2)}) collective-permute-start(bf16[2,64,768]{2,1,0:T(8,128)(2,1)S(1)} %project.4.rest_1_.after_ref), channel_id=1, source_target_pairs={{0,4},{8,12},{4,0},{12,8},{1,5},{9,13},{5,1},{13,9},{2,6},{10,14},... | collective-permute-start | bytes 589832 | tf_op jit(solution)/shard_map/ppermute | solution.py:540
  61.5 2.5 %project.3.q_ref = bf16[1,192,768]{2,1,0:T(8,128)(2,1)S(1)} custom-call(bf16[128,1280]{1,0:T(8,128)(2,1)S(1)} %collective-permute-done.rest_0_, bf16[128,1280]{1,0:T(8,128)(2,1)S(1)} %collective-permute-done.1.rest_1_, bf16[64,1280]{1,0:T(8,128)(2,1)S(1)} %collective-permute-done.3.rest_2_.rest_0_, ...), custom_call_target="tpu_custom_call" | custom-call | flops 754974720 | bytes 14567424 | tf_op jit(solution)/shard_map/project/pallas_call | solution.py:38
  65.5 1.6 %unpack_out.1.weights_ref = bf16[768,5120]{1,0:T(8,128)(2,1)S(1)} custom-call(s32[96,5120]{1,0:T(8,128)S(1)} %copy-done.2, bf16[2,64,768]{2,1,0:T(8,128)(2,1)S(1)} %project.4.rest_1_.after_ref), custom_call_target="tpu_custom_call" | custom-call | flops 983040000 | bytes 2162688 | tf_op jit(solution)/shard_map/unpack_out/pallas_call | solution.py:38
  67.1 1.5 %attend.4.rest_3_ = f32[6,192,256]{2,1,0:T(8,128)S(1)} custom-call(s32[2]{0:T(128)S(1)} %copy-done.13, bf16[1,192,768]{2,1,0:T(8,128)(2,1)S(1)} %project.3.q_ref, bf16[2,128,768]{2,1,0:T(8,128)(2,1)} %collective-permute-done.7.rest_0_, bf16[2,128,768]{2,1,0:T(8,128)(2,1)S(1)} %collective-permute-done.8.rest_1_, f32[3,256]{1,0:T(4,128)S(1)} %reshape.110.rest_2_, ...), custom_call_target="tpu_custom_call" | custom-call | flops 301989888 | bytes 2264072 | tf_op jit(solution)/shard_map/attend/pallas_call | solution.py:38
  68.7 1.2 %attend.5.rotated_ref = bf16[192,768]{1,0:T(8,128)(2,1)S(1)} custom-call(s32[2]{0:T(128)S(1)} %copy-done.13, bf16[1,192,768]{2,1,0:T(8,128)(2,1)S(1)} %project.3.q_ref, bf16[2,64,768]{2,1,0:T(8,128)(2,1)S(1)} %collective-permute-done.5.rest_0_, bf16[2,64,768]{2,1,0:T(8,128)(2,1)S(1)} %collective-permute-done.6.rest_1_, f32[3,128]{1,0:T(4,128)S(1)} %copy-done.14, ...), custom_call_target="tpu_custom_call" | custom-call | flops 150994944 | bytes 1872392 | tf_op jit(solution)/shard_map/attend/pallas_call | solution.py:38
  69.9 1.2 %out_project.2 = (bf16[96,3072]{1,0:T(8,128)(2,1)S(1)}, bf16[96,3072]{1,0:T(8,128)(2,1)S(1)}) custom-call(bf16[192,768]{1,0:T(8,128)(2,1)S(1)} %attend.5.rotated_ref, bf16[768,5120]{1,0:T(8,128)(2,1)S(1)} %unpack_out.1.weights_ref, f32[40,128]{1,0:T(8,128)S(1)} %bitcast.18), custom_call_target="tpu_custom_call" | custom-call | flops 905969664 | bytes 8179712 | tf_op jit(solution)/shard_map/out_project/pallas_call | solution.py:38
  74.3 1.3 %collective-permute-start.12 = (bf16[48,2048]{1,0:T(8,128)(2,1)S(1)}, bf16[48,2048]{1,0:T(8,128)(2,1)S(1)}, u32[]{:S(2)}, u32[]{:S(2)}) collective-permute-start(bf16[48,2048]{1,0:T(8,128)(2,1)S(1)} %slice.27), channel_id=1, source_target_pairs={{0,2},{1,3},{2,0},{3,1},{4,6},{5,7},{6,4},{7,5},{8,10},{9,11},{10,... | collective-permute-start | bytes 589832 | tf_op jit(solution)/shard_map/ppermute | solution.py:470
  75.7 10.9 %collective-permute-done.12.more_ref = bf16[48,2048]{1,0:T(8,128)(2,1)S(1)} collective-permute-done((bf16[48,2048]{1,0:T(8,128)(2,1)S(1)}, bf16[48,2048]{1,0:T(8,128)(2,1)S(1)}, u32[]{:S(2)}, u32[]{:S(2)}) %collective-permute-start.12) | collective-permute-done | bytes 196640 | tf_op jit(solution)/shard_map/ppermute | solution.py:470
  (80 shorter events, 18.9 us)
Async XLA Ops:
  0.1 27.7 %copy-start.12 = (s32[2]{0:T(128)}, s32[2]{0:T(128)S(1)}, u32[]{:S(2)}) copy-start(s32[2]{0:T(128)S(1)} %get-tuple-element.25.place_ref) | copy-start | bytes 28
  3.1 10.7 %collective-permute-start = (bf16[128,1280]{1,0:T(8,128)(2,1)S(1)}, bf16[128,1280]{1,0:T(8,128)(2,1)S(1)}, u32[]{:S(2)}, u32[]{:S(2)}) collective-permute-start(bf16[128,1280]{1,0:T(8,128)(2,1)S(1)} %get-tuple-element.14), channel_id=1, source_target_pairs={{0,2},{1,3},{2,0},{3,1},{4,6},{5,7},{6,4},{7,5},{8,10},{9,11},{10,... | collective-permute-start | bytes 983048 | tf_op jit(solution)/shard_map/ppermute | solution.py:470
  6.1 7.7 %collective-permute-start.2 = (bf16[192,1280]{1,0:T(8,128)(2,1)S(1)}, bf16[192,1280]{1,0:T(8,128)(2,1)S(1)}, u32[]{:S(2)}, u32[]{:S(2)}) collective-permute-start(bf16[192,1280]{1,0:T(8,128)(2,1)S(1)} %get-tuple-element.15.rest_0_), channel_id=1, source_target_pairs={{0,1},{1,0},{2,3},{3,2},{4,5},{5,4},{6,7},{7,6},{8,9},{9,8},{10,11... | collective-permute-start | bytes 1474568 | tf_op jit(solution)/shard_map/ppermute | solution.py:470
  13.8 16.0 %collective-permute-start.1 = (bf16[128,1280]{1,0:T(8,128)(2,1)S(1)}, bf16[128,1280]{1,0:T(8,128)(2,1)S(1)}, u32[]{:S(2)}, u32[]{:S(2)}) collective-permute-start(bf16[128,1280]{1,0:T(8,128)(2,1)S(1)} %collective-permute-done.rest_0_), channel_id=1, source_target_pairs={{0,1},{1,0},{2,3},{3,2},{4,5},{5,4},{6,7},{7,6},{8,9},{9,8},{10,11... | collective-permute-start | bytes 983048 | tf_op jit(solution)/shard_map/ppermute | solution.py:470
  14.6 2.7 %copy-start.16 = (s32[640,3,768]{2,0,1:T(8,128)S(1)}, s32[640,3,768]{2,0,1:T(8,128)}, u32[]{:S(2)}) copy-start(s32[640,3,768]{2,0,1:T(8,128)} %param.12) | copy-start | bytes 17694724
  18.3 11.6 %copy-start.4 = (f32[3,768]{1,0:T(4,128)S(1)}, f32[3,768]{1,0:T(4,128)}, u32[]{:S(2)}) copy-start(f32[3,768]{1,0:T(4,128)} %rest_4_.3) | copy-start | bytes 27652
  18.3 11.6 %copy-start.5 = (s32[3,768]{1,0:T(4,128)S(1)}, s32[3,768]{1,0:T(4,128)}, u32[]{:S(2)}) copy-start(s32[3,768]{1,0:T(4,128)} %rest_5_.3) | copy-start | bytes 27652
  27.8 5.4 %copy-start = (bf16[2,3,1280,768]{3,2,1,0:T(8,128)(2,1)}, bf16[2,3,1280,768]{3,2,1,0:T(8,128)(2,1)S(1)}, u32[]{:S(2)}) copy-start(bf16[2,3,1280,768]{3,2,1,0:T(8,128)(2,1)S(1)} %get-tuple-element.18.rest_5_.rest_3_) | copy-start | bytes 35389444
  27.8 10.6 %collective-permute-start.3 = (bf16[64,1280]{1,0:T(8,128)(2,1)S(1)}, bf16[64,1280]{1,0:T(8,128)(2,1)S(1)}, u32[]{:S(2)}, u32[]{:S(2)}) collective-permute-start(bf16[64,1280]{1,0:T(8,128)(2,1)S(1)} %get-tuple-element.16), channel_id=1, source_target_pairs={{0,2},{1,3},{2,0},{3,1},{4,6},{5,7},{6,4},{7,5},{8,10},{9,11},{10,... | collective-permute-start | bytes 491528 | tf_op jit(solution)/shard_map/ppermute | solution.py:470
  33.3 33.9 %collective-permute-start.8 = (bf16[2,128,768]{2,1,0:T(8,128)(2,1)S(1)}, bf16[2,128,768]{2,1,0:T(8,128)(2,1)S(1)}, u32[]{:S(2)}, u32[]{:S(2)}) collective-permute-start(bf16[2,128,768]{2,1,0:T(8,128)(2,1)S(1)} %project.5.rest_0_), channel_id=1, source_target_pairs={{4,8},{8,4},{5,9},{9,5},{6,10},{10,6},{7,11},{11,7},{20,24},{24,20... | collective-permute-start | bytes 1179656 | tf_op jit(solution)/shard_map/ppermute | solution.py:534
  33.9 33.2 %collective-permute-start.7 = (bf16[2,128,768]{2,1,0:T(8,128)(2,1)S(1)}, bf16[2,128,768]{2,1,0:T(8,128)(2,1)}, u32[]{:S(2)}, u32[]{:S(2)}) collective-permute-start(bf16[2,128,768]{2,1,0:T(8,128)(2,1)S(1)} %project.5.rest_0_), channel_id=1, source_target_pairs={{0,4},{8,12},{4,0},{12,8},{1,5},{9,13},{5,1},{13,9},{2,6},{10,14},... | collective-permute-start | bytes 1179656 | tf_op jit(solution)/shard_map/ppermute | solution.py:534
  38.4 11.4 %collective-permute-start.4 = (bf16[64,1280]{1,0:T(8,128)(2,1)S(1)}, bf16[64,1280]{1,0:T(8,128)(2,1)S(1)}, u32[]{:S(2)}, u32[]{:S(2)}) collective-permute-start(bf16[64,1280]{1,0:T(8,128)(2,1)S(1)} %collective-permute-done.3.rest_2_.rest_0_), channel_id=1, source_target_pairs={{0,1},{1,0},{2,3},{3,2},{4,5},{5,4},{6,7},{7,6},{8,9},{9,8},{10,11... | collective-permute-start | bytes 491528 | tf_op jit(solution)/shard_map/ppermute | solution.py:470
  49.8 4.4 %copy-start.1 = (bf16[2,3,1280,768]{3,2,1,0:T(8,128)(2,1)S(1)}, bf16[2,3,1280,768]{3,2,1,0:T(8,128)(2,1)}, u32[]{:S(2)}) copy-start(bf16[2,3,1280,768]{3,2,1,0:T(8,128)(2,1)} %copy-done) | copy-start | bytes 35389444
  54.8 6.7 %copy-start.7 = (s32[3,768]{1,0:T(4,128)S(1)}, s32[3,768]{1,0:T(4,128)}, u32[]{:S(2)}) copy-start(s32[3,768]{1,0:T(4,128)} %rest_5_.3) | copy-start | bytes 27652
  58.7 5.2 %copy-start.11 = (f32[3,192]{1,0:T(4,128)S(1)}, f32[3,192]{1,0:T(4,128)}, u32[]{:S(2)}) copy-start(f32[3,192]{1,0:T(4,128)} %reshape.111.rest_2_) | copy-start | bytes 6916
  58.8 5.2 %copy-start.13 = (s32[2]{0:T(128)S(1)}, s32[2]{0:T(128)}, u32[]{:S(2)}) copy-start(s32[2]{0:T(128)} %copy-done.12) | copy-start | bytes 28
  58.8 9.9 %collective-permute-start.6 = (bf16[2,64,768]{2,1,0:T(8,128)(2,1)S(1)}, bf16[2,64,768]{2,1,0:T(8,128)(2,1)S(1)}, u32[]{:S(2)}, u32[]{:S(2)}) collective-permute-start(bf16[2,64,768]{2,1,0:T(8,128)(2,1)S(1)} %project.4.rest_1_.after_ref), channel_id=1, source_target_pairs={{4,8},{8,4},{5,9},{9,5},{6,10},{10,6},{7,11},{11,7},{20,24},{24,20... | collective-permute-start | bytes 589832 | tf_op jit(solution)/shard_map/ppermute | solution.py:540
  59.6 9.1 %collective-permute-start.5 = (bf16[2,64,768]{2,1,0:T(8,128)(2,1)S(1)}, bf16[2,64,768]{2,1,0:T(8,128)(2,1)S(1)}, u32[]{:S(2)}, u32[]{:S(2)}) collective-permute-start(bf16[2,64,768]{2,1,0:T(8,128)(2,1)S(1)} %project.4.rest_1_.after_ref), channel_id=1, source_target_pairs={{0,4},{8,12},{4,0},{12,8},{1,5},{9,13},{5,1},{13,9},{2,6},{10,14},... | collective-permute-start | bytes 589832 | tf_op jit(solution)/shard_map/ppermute | solution.py:540
  67.1 1.6 %copy-start.14 = (f32[3,128]{1,0:T(4,128)S(1)}, f32[3,128]{1,0:T(4,128)}, u32[]{:S(2)}) copy-start(f32[3,128]{1,0:T(4,128)} %reshape.109.rest_2_) | copy-start | bytes 4612
  71.1 2.1 %collective-permute-start.9 = (bf16[96,3072]{1,0:T(8,128)(2,1)S(1)}, bf16[96,3072]{1,0:T(8,128)(2,1)S(1)}, u32[]{:S(2)}, u32[]{:S(2)}) collective-permute-start(bf16[96,3072]{1,0:T(8,128)(2,1)S(1)} %get-tuple-element.20), channel_id=1, source_target_pairs={{0,1},{1,0},{2,3},{3,2},{4,5},{5,4},{6,7},{7,6},{8,9},{9,8},{10,11... | collective-permute-start | bytes 1769480 | tf_op jit(solution)/shard_map/ppermute | solution.py:470
  72.0 2.2 %collective-permute-start.11 = (bf16[96,2048]{1,0:T(8,128)(2,1)S(1)}, bf16[96,2048]{1,0:T(8,128)(2,1)S(1)}, u32[]{:S(2)}, u32[]{:S(2)}) collective-permute-start(bf16[96,2048]{1,0:T(8,128)(2,1)S(1)} %get-tuple-element.22), channel_id=1, source_target_pairs={{0,1},{1,0},{2,3},{3,2},{4,5},{5,4},{6,7},{7,6},{8,9},{9,8},{10,11... | collective-permute-start | bytes 1179656 | tf_op jit(solution)/shard_map/ppermute | solution.py:470
  73.3 14.3 %collective-permute-start.10 = (bf16[48,3072]{1,0:T(8,128)(2,1)S(1)}, bf16[48,3072]{1,0:T(8,128)(2,1)S(1)}, u32[]{:S(2)}, u32[]{:S(2)}) collective-permute-start(bf16[48,3072]{1,0:T(8,128)(2,1)S(1)} %slice.26), channel_id=1, source_target_pairs={{0,2},{1,3},{2,0},{3,1},{4,6},{5,7},{6,4},{7,5},{8,10},{9,11},{10,... | collective-permute-start | bytes 884744 | tf_op jit(solution)/shard_map/ppermute | solution.py:470
  74.3 12.4 %copy-start.9 = (s32[5120]{0:T(1024)S(1)}, s32[5120]{0:T(1024)}, u32[]{:S(2)}) copy-start(s32[5120]{0:T(1024)} %param.19) | copy-start | bytes 61444
  74.3 12.3 %collective-permute-start.12 = (bf16[48,2048]{1,0:T(8,128)(2,1)S(1)}, bf16[48,2048]{1,0:T(8,128)(2,1)S(1)}, u32[]{:S(2)}, u32[]{:S(2)}) collective-permute-start(bf16[48,2048]{1,0:T(8,128)(2,1)S(1)} %slice.27), channel_id=1, source_target_pairs={{0,2},{1,3},{2,0},{3,1},{4,6},{5,7},{6,4},{7,5},{8,10},{9,11},{10,... | collective-permute-start | bytes 589832 | tf_op jit(solution)/shard_map/ppermute | solution.py:470
  (8 other events, 8.7 us)
where the time goes:
time: 89.6 us; the launch traced here: 88.9 us
  Pallas kernels  29.8 us (33%)
  local copies, waits for them, and re-layouts  20.9 us (23%)
  waiting for transfers between devices  16.9 us (19%)
  starting transfers between devices  15.4 us (17%)
  other arithmetic  5.33 us (6%)
    pallas_call x13, Pallas kernels, call(): pl.pallas_call(body, out_shape=out_shape, in_specs=in_specs, out_specs=ou...  29.8 us
    ppermute x9, waiting for transfers between devices, swap(): return lax.ppermute(shard, 'head', [(i, i ^ bit) for i in range(peers)])  16.9 us
    unnamed x39, local copies, waits for them, and re-layouts  12.5 us
    ppermute x9, starting transfers between devices, swap(): return lax.ppermute(shard, 'head', [(i, i ^ bit) for i in range(peers)])  7.61 us
    ppermute x2, starting transfers between devices, on_device(): lax.ppermute(key_values[0], 'height', pairs)  5.12 us
    reshape x3, local copies, waits for them, and re-layouts, mask_of(): return jnp.repeat(allowed.astype(f32), TILE, axis=1)  3.48 us
    broadcast_in_dim x3, local copies, waits for them, and re-layouts, mask_of(): return jnp.repeat(allowed.astype(f32), TILE, axis=1)  3.32 us
    ppermute x2, starting transfers between devices, on_device(): lax.ppermute(key_values[1], 'height', pairs)  2.71 us
  transfers between devices with their start and end apart: 13, of which 3 were waited for; matrix products, arithmetic and copies ran while one was open for 16% of the time, Pallas kernels for 28%

commit v1 on v0

v1 whole, which is shorter than its diff:
```python
import functools

import jax
import jax.numpy as jnp
import numpy as np
from jax import lax
from jax.experimental import pallas as pl
from jax.experimental.pallas import tpu as pltpu
from jax.sharding import PartitionSpec as P

D = 5120
HD = 128
HEADS = 24
HAD = 128
TILE = 64
HROWS = 4
WTILES = 3
PLANES = 8
WORDS = HAD // PLANES
EARLY = 2 * TILE
QKV_ORDER = "half"
OUT_ORDER = "byte"

epsilon = 1e-06
f32 = jnp.float32
bf16 = jnp.bfloat16
VMEM = pl.BlockSpec(memory_space=pltpu.VMEM)
SMEM = pl.BlockSpec(memory_space=pltpu.SMEM)
ANY = pl.BlockSpec(memory_space=pl.ANY)
HBM = pl.BlockSpec(memory_space=pltpu.HBM)


def shape_of(shape, dtype):
    return jax.ShapeDtypeStruct(tuple(shape), dtype)


def in_hbm(array):
    return pltpu.with_memory_space_constraint(array, pltpu.HBM)


def call(body, out_shape, in_specs, args, name, flops=0, out_specs=None, megabytes=16, **more):
    if out_specs is None:
        out_specs = jax.tree.map(lambda _: VMEM, out_shape)
    moved = sum(a.size * a.dtype.itemsize for a in args)
    return pl.pallas_call(
        body,
        out_shape=out_shape,
        in_specs=in_specs,
        out_specs=out_specs,
        compiler_params=pltpu.CompilerParams(vmem_limit_bytes=megabytes * 2**20),
        cost_estimate=pl.CostEstimate(
            flops=1, bytes_accessed=1, transcendentals=0
        ),
        name=name,
        **more,
    )(*args)


def lanes():
    return lax.broadcasted_iota(jnp.int32, (HAD, HAD), 1)


def hadamard(order):
    row = lax.broadcasted_iota(jnp.int32, (HAD, HAD), 0)
    column = lanes()
    word = PLANES * (column & (WORDS - 1))
    if order == "half":
        column = word + column // WORDS
    if order == "byte":
        column = word + column // (2 * WORDS) + (PLANES // 2) * ((column // WORDS) & 1)
    shared = row & column
    shared = shared ^ (shared >> 4)
    shared = shared ^ (shared >> 2)
    shared = shared ^ (shared >> 1)
    return (1 - 2 * (shared & 1)).astype(f32).astype(bf16)


def double_hadamard():
    plain = hadamard("plain")
    return jnp.concatenate([plain, plain], 0)


def plane_power(base, order):
    lane = lax.broadcasted_iota(jnp.int32, (1, HAD), 1)
    if order == "half":
        power = jnp.minimum(lane // WORDS, PLANES - 2)
    else:
        power = jnp.minimum(lane // (2 * WORDS), PLANES // 2 - 2)
    value = jnp.where(power & 1 == 1, base, 1.0)
    value = value * jnp.where(power & 2 == 2, base**2, 1.0)
    return value * jnp.where(power & 4 == 4, base**4, 1.0)


def turn_factor(order):
    return plane_power(0.25, order) * np.float32(HAD ** (-0.5))


def signed(sign_bits):
    return (2 * sign_bits - 1).astype(f32)


def pieces_of(words, order):
    if order == "half":
        packed = words.astype(jnp.int16)
        masked = [packed & jnp.int16(3 << (2 * k)) for k in range(PLANES - 1)]
        masked.append((words >> 2).astype(jnp.int16) & jnp.int16(3 << (2 * PLANES - 4)))
    else:
        pair = jnp.concatenate([words & 255, words >> 8], 0)
        packed = pair.astype(jnp.int8)
        masked = [packed & jnp.int8(3 << (2 * k)) for k in range(PLANES // 2 - 1)]
        masked.append((pair >> 2).astype(jnp.int8) & jnp.int8(3 << (PLANES - 4)))
    return [piece.astype(bf16) for piece in masked]


def decode(words, order):
    blocks = []
    for first in range(0, words.shape[0], WORDS):
        blocks += pieces_of(words[first : first + WORDS], order)
    return jnp.concatenate(blocks, 0)


def row_correction(row_list, order):
    factor_row = plane_power(4.0, order) * 1.5
    total = None
    for rows in row_list:
        for first in range(0, rows.shape[1], HAD):
            term = rows[:, first : first + HAD].astype(f32)
            total = term if total is None else total + term
    return jnp.sum(total * factor_row, axis=1, keepdims=True)


def rotate_halves(values, doubled):
    high = values.astype(bf16)
    low = (values - high.astype(f32)).astype(bf16)
    return jnp.dot(jnp.concatenate([high, low], 1), doubled, preferred_element_type=f32)


def tile_width(columns):
    for width in (256, 128):
        if columns % width == 0:
            return width


def turn_kernel(place_ref, x_hbm, sign_hbm, own_ref, send_ref, x_ref, sign_ref, sems):
    copies = [
        pltpu.make_async_copy(x_hbm, x_ref, sems.at[0]),
        pltpu.make_async_copy(sign_hbm, sign_ref, sems.at[1]),
    ]
    for copy in copies:
        copy.start()
    matrix = hadamard(QKV_ORDER)
    factor = turn_factor(QKV_ORDER)
    for copy in copies:
        copy.wait()
    blocks = x_ref.shape[1] // HAD
    first = place_ref[0] * blocks
    end = place_ref[1]
    tiles = (end, 1, 2 - end)
    for b in range(blocks):
        cols = slice(b * HAD, (b + 1) * HAD)
        sign_row = signed(sign_ref[pl.ds(first + b, 1), :])
        own = [x_ref[pl.ds(pl.multiple_of(t * TILE, TILE), TILE), cols] for t in tiles]
        flipped = (jnp.concatenate(own, 0).astype(f32) * sign_row).astype(bf16)
        turned = jnp.dot(flipped, matrix, preferred_element_type=f32)
        turned = (turned * factor).astype(bf16)
        own_ref[:, cols] = turned
        send_ref[:TILE, cols] = turned[2 * TILE :]
        send_ref[TILE:, cols] = turned[TILE : 2 * TILE]


def turn(place, own_tokens, in_sign):
    sign_rows = in_sign.reshape(-1, HAD)
    rows, inner = own_tokens.shape
    return call(
        turn_kernel,
        (shape_of((rows, inner), bf16), shape_of((EARLY, inner), bf16)),
        [SMEM, HBM, HBM],
        (place, in_hbm(own_tokens), in_hbm(sign_rows)),
        "turn",
        flops=2 * own_tokens.size * HAD,
        scratch_shapes=[
            pltpu.VMEM(own_tokens.shape, bf16),
            pltpu.VMEM(sign_rows.shape, jnp.int32),
            pltpu.SemaphoreType.DMA((2,)),
        ],
    )


def tie(array, *after):
    return call(
        lambda *refs: None,
        shape_of(array.shape, array.dtype),
        [ANY] * (1 + len(after)),
        (array, *after),
        "tie",
        out_specs=ANY,
        input_output_aliases={0: 0},
    )


def prepare_kernel(near, far, place_ref, *rest):
    shard_refs = rest[: len(near)]
    codes_hbm, sums_ref, far_ref, late_ref, near_ref, sems = rest[len(near) :]
    words, columns = near_ref.shape[2:]

    def fetch(position, kind):
        flip = (near + far)[position]
        first = pl.multiple_of((place_ref[0] ^ flip) * words, WORDS)
        there = position - len(near)
        target = near_ref.at[position, kind] if there < 0 else far_ref.at[there, kind]
        return pltpu.make_async_copy(
            codes_hbm.at[kind, pl.ds(first, words), :], target, sems.at[position, kind]
        )

    for kind in range(3):
        for position in range(len(near)):
            fetch(position, kind).start()
    for position in range(len(near), len(near + far)):
        for kind in range(3):
            fetch(position, kind).start()
    fix = row_correction([ref[...] for ref in shard_refs], QKV_ORDER)
    width = tile_width(columns)
    late_ref[...] = shard_refs[0][:TILE, :]

    def product(kind, carry):
        for position in range(len(near)):
            fetch(position, kind).wait()
        for first in range(0, columns, width):
            cols = slice(first, first + width)
            total = -fix
            for position, ref in enumerate(shard_refs):
                weights = decode(near_ref[position, kind, :, cols], QKV_ORDER)
                total = total + jnp.dot(ref[...], weights, preferred_element_type=f32)
            sums_ref[kind, :, cols] = total
        return carry

    lax.fori_loop(0, 3, product, 0)
    for position in range(len(near), len(near + far)):
        for kind in range(3):
            fetch(position, kind).wait()


def prepare(place, near, far, shards, codes):
    rows, inner = shards[0].shape
    columns = codes.shape[2]
    words = inner // PLANES
    return call(
        functools.partial(prepare_kernel, near, far),
        (
            shape_of((3, rows, columns), f32),
            shape_of((len(far), 3, words, columns), jnp.int32),
            shape_of((TILE, inner), bf16),
        ),
        [SMEM] + [VMEM] * len(near) + [HBM],
        (place, *shards, in_hbm(codes)),
        "prepare",
        flops=16 * rows * inner * 3 * columns,
        scratch_shapes=[
            pltpu.VMEM((len(near), 3, words, columns), jnp.int32),
            pltpu.SemaphoreType.DMA((len(near + far), 3)),
        ],
    )


def project_kernel(kinds, first_row, groups, positions, whole, ending, *rest):
    count = len(positions)
    shard_refs = rest[: groups * count]
    sums_ref, words_ref = rest[groups * count : groups * count + 2]
    if ending:
        scale_ref, sign_ref = rest[-3:-1]
    out_ref = rest[-1]
    columns = sums_ref.shape[2]
    width = tile_width(columns)
    shards = []
    for place in range(count):
        parts = [shard_refs[g * count + place][...] for g in range(groups)]
        shards.append(parts[0] if groups == 1 else jnp.concatenate(parts, 0))
    fix = row_correction(shards, QKV_ORDER)
    row_count = shards[0].shape[0]
    rows = slice(first_row, first_row + row_count)
    doubled = double_hadamard()
    ones = jnp.ones((HD, HD), bf16)
    for place, kind in enumerate(kinds):
        heads = []
        for first in range(0, columns, width):
            cols = slice(first, first + width)
            part = (sums_ref[kind, rows, cols] if whole else sums_ref[place, :, cols]) - fix
            for shard, position in zip(shards, positions):
                weights = decode(words_ref[position, kind, :, cols], QKV_ORDER)
                part = part + jnp.dot(shard, weights, preferred_element_type=f32)
            if not ending:
                out_ref[place, :, cols] = part
                continue
            for lane in range(0, width, HD):
                at = slice(first + lane, first + lane + HD)
                scale_row = scale_ref[kind : kind + 1, at] * np.float32(D ** (-0.5))
                heads.append(part[:, lane : lane + HD] * scale_row)
        if not ending:
            continue
        mixed = rotate_halves(jnp.concatenate(heads, 0), doubled)
        signs = []
        for head in range(len(heads)):
            sign_row = sign_ref[kind : kind + 1, head * HD : (head + 1) * HD]
            sign_row = signed(sign_row) * np.float32(HAD ** (-0.5))
            signs.append(mixed[head * row_count : (head + 1) * row_count] * sign_row)
        if kind != 2:
            square = jnp.concatenate([(part * part).astype(bf16) for part in signs], 0)
            mean = jnp.dot(square, ones, preferred_element_type=f32) * (1.0 / HD)
            factor = lax.rsqrt(mean + epsilon)
            signs = [
                part * factor[head * row_count : (head + 1) * row_count]
                for head, part in enumerate(signs)
            ]
        for head, part in enumerate(signs):
            out_ref[place, :, head * HD : (head + 1) * HD] = part.astype(bf16)


def project(kinds, first_row, groups, positions, sums, words, ending):
    inner = groups[0][0].shape[1]
    columns = sums.shape[2]
    row_count = sum(group[0].shape[0] for group in groups)
    whole = sums.shape[0] == 3
    args = [shard for group in groups for shard in group] + [sums, words]
    if ending is not None:
        args += ending
    return call(
        functools.partial(
            project_kernel, kinds, first_row, len(groups), positions, whole, ending is not None
        ),
        shape_of((len(kinds), row_count, columns), f32 if ending is None else bf16),
        [VMEM] * len(args),
        args,
        "project",
        flops=4 * row_count * inner * len(positions) * len(kinds) * columns,
    )


def near_row(row, swap_pair):
    if swap_pair is None:
        return row
    by, odd = swap_pair
    return jnp.where(lax.rem(row // by, 2) == odd, row + by, row - by)


def window_mask(place_ref, windows_ref, key_tiles, row_count):
    end = place_ref[1]
    order = (end, 1, 2 - end)
    lane = lax.broadcasted_iota(jnp.int32, (1, len(key_tiles) * TILE), 1) // TILE
    ids = None
    for index, (swap_pair, position) in enumerate(key_tiles):
        one = near_row(place_ref[2], swap_pair) * WTILES + order[position]
        ids = jnp.full(lane.shape, one, jnp.int32) if ids is None else jnp.where(lane == index, one, ids)
    masks = []
    for tile in order:
        hit = jnp.zeros(lane.shape, f32)
        for entry in range(windows_ref.shape[1]):
            hit = jnp.where(ids == windows_ref[tile, entry], 1.0, hit)
        masks.append(jnp.broadcast_to(hit, (TILE, lane.shape[1])))
    return jnp.concatenate(masks, 0)


def attend_kernel(key_tiles, blocks, has_sum, last, share_order, place_ref, windows_ref, q_ref, *rest):
    rest = list(rest)
    kv_refs = [rest.pop(0) for _ in range(blocks)]
    sum_ref = rest.pop(0) if has_sum else None
    if last:
        oin_ref, out_ref, rotated_ref = rest
    else:
        (out_ref,) = rest
    row_count, columns = q_ref.shape[1:]
    heads = [slice(head, head + HD) for head in range(0, columns, HD)]
    mask = window_mask(place_ref, windows_ref, key_tiles, row_count)
    scores = []
    for at in heads:
        keys = jnp.concatenate([ref[0, :, at] for ref in kv_refs], 0)
        scores.append(
            lax.dot_general(
                q_ref[0, :, at], keys, (((1,), (1,)), ((), ())), preferred_element_type=f32
            )
        )
    weights = [
        (jnp.exp(score * np.float32(HD ** (-0.5))) * mask).astype(bf16) for score in scores
    ]
    totals = []
    for head, at in enumerate(heads):
        values = jnp.concatenate([ref[1, :, at] for ref in kv_refs], 0)
        values = jnp.concatenate([values, jnp.ones_like(values)], 1)
        total = jnp.dot(weights[head], values, preferred_element_type=f32)
        if has_sum:
            total = total + sum_ref[head]
        totals.append(total)
    if not last:
        for head, total in enumerate(totals):
            out_ref[head] = total
        return
    matrix = hadamard(OUT_ORDER)
    factor = turn_factor(OUT_ORDER)
    end = place_ref[1]
    for head, at in enumerate(heads):
        attended = (totals[head][:, :HD] / totals[head][:, HD:]).astype(bf16)
        sign_row = signed(oin_ref[head : head + 1, :])
        flipped = (attended.astype(f32) * sign_row).astype(bf16)
        rotated = jnp.dot(flipped, matrix, preferred_element_type=f32) * factor
        for position, tile in enumerate((end, 1, 2 - end)):
            rotated_ref[pl.ds(pl.multiple_of(tile * TILE, TILE), TILE), at] = rotated[
                position * TILE : (position + 1) * TILE
            ]
    share = row_count // len(share_order)
    pieces = []
    for flip in share_order:
        owner = place_ref[0] ^ flip
        pieces.append(rotated_ref[pl.ds(pl.multiple_of(owner * share, 8), share), :])
    out_ref[...] = jnp.concatenate(pieces, 0).astype(bf16)


def attend(place, windows, queries, blocks, key_tiles, running, ending):
    row_count, columns = queries.shape[1:]
    args = [place, windows, queries, *blocks]
    if running is not None:
        args.append(running)
    scratch, share_order = [], None
    if ending is None:
        out_shape = shape_of((columns // HD, row_count, 2 * HD), f32)
    else:
        oin_sign, share_order = ending
        args.append(oin_sign.reshape(-1, HAD))
        out_shape = shape_of((row_count, columns), bf16)
        scratch = [pltpu.VMEM((row_count, columns), f32)]
    return call(
        functools.partial(
            attend_kernel,
            key_tiles,
            len(blocks),
            running is not None,
            ending is not None,
            share_order,
        ),
        out_shape,
        [SMEM] * 2 + [VMEM] * (len(args) - 2),
        args,
        "attend",
        flops=8 * row_count * columns * len(key_tiles) * TILE,
        scratch_shapes=scratch,
    )


def unpack_out_kernel(codes_ref, after_ref, weights_ref):
    for first in range(0, codes_ref.shape[0], WORDS):

        def some(step, carry):
            cols = pl.ds(pl.multiple_of(step * 512, 512), 512)
            at = first * PLANES
            for piece in pieces_of(codes_ref[first : first + WORDS, cols], OUT_ORDER):
                weights_ref[at : at + piece.shape[0], cols] = piece
                at += piece.shape[0]
            return carry

        lax.fori_loop(0, codes_ref.shape[1] // 512, some, 0)


def unpack_out(codes, after):
    words, columns = codes.shape
    return call(
        unpack_out_kernel,
        shape_of((words * PLANES, columns), bf16),
        [VMEM, ANY],
        (codes, after),
        "unpack_out",
        flops=2000 * words * columns,
    )


def out_kernel(first, rotated_ref, weights_ref, scale_ref, after_ref, send_ref, keep_ref):
    rows = rotated_ref[...]
    fix = row_correction([rows], OUT_ORDER)
    half, columns = send_ref.shape
    width = 256
    for at in range(0, columns, width):
        cols = slice(first + at, first + at + width)
        part = jnp.dot(rows, weights_ref[:, cols], preferred_element_type=f32) - fix
        for lane in range(0, width, HAD):
            place = (first + at + lane) // HAD
            scale_row = scale_ref[place : place + 1, :] * np.float32((HEADS * HD) ** (-0.5))
            done = (part[:, lane : lane + HAD] * scale_row).astype(bf16)
            send_ref[:, at + lane : at + lane + HAD] = done[:half]
            keep_ref[:, at + lane : at + lane + HAD] = done[half:]


def out_project(rotated, weights, scale_rows, after, first, columns):
    row_count, inner = rotated.shape
    result = shape_of((row_count // 2, columns), bf16)
    return call(
        functools.partial(out_kernel, first),
        (result, result),
        [VMEM] * 3 + [ANY],
        (rotated, weights, scale_rows, after),
        "out_project",
        flops=2 * row_count * inner * columns,
    )


def finish_kernel(first, has_base, sign_ref, keep_ref, more_ref, *rest):
    out_hbm, done_ref, sem = rest[1:] if has_base else rest
    columns = keep_ref.shape[1]
    doubled = double_hadamard()
    for at in range(0, columns, HAD):
        cols = slice(at, at + HAD)
        total = keep_ref[:, cols].astype(f32) + more_ref[:, cols].astype(f32)
        place = (first + at) // HAD
        sign_row = signed(sign_ref[place : place + 1, :]) * np.float32(HAD ** (-0.5))
        done_ref[:, cols] = (rotate_halves(total, doubled) * sign_row).astype(bf16)
    copy = pltpu.make_async_copy(done_ref, out_hbm.at[:, pl.ds(first, columns)], sem)
    copy.start()
    copy.wait()


def finish(base, sign_rows, keep, more, first):
    share, columns = keep.shape
    args = [sign_rows, keep, more]
    in_specs = [VMEM] * 3
    aliases = {}
    if base is not None:
        args.append(base)
        in_specs.append(ANY)
        aliases = {3: 0}
    return call(
        functools.partial(finish_kernel, first, base is not None),
        shape_of((share, D), bf16),
        in_specs,
        args,
        "finish",
        flops=4 * share * columns * HAD,
        out_specs=ANY,
        scratch_shapes=[pltpu.VMEM((share, columns), bf16), pltpu.SemaphoreType.DMA],
        input_output_aliases=aliases,
    )


def swap(shard, bit):
    peers = lax.axis_size("head")
    return lax.ppermute(shard, "head", [(i, i ^ bit) for i in range(peers)])


def row_swaps(row_tiles):
    swaps = []
    for by in (1, 3, 4, 5) if row_tiles > HROWS else (1,):
        for odd in (0, 1):
            low = [i for i in range(row_tiles - by) if (i // by) % 2 == odd]
            swaps.append((by, odd, [(i, i + by) for i in low] + [(i + by, i) for i in low]))
    return swaps


def halving_order(head_count):
    flips = [0]
    bit = head_count // 2
    while bit >= 1:
        flips = [f | bit for f in flips] + flips
        bit //= 2
    return tuple(flips)


CHUNKS = (2048, 3072)


def on_device(
    tokens,
    in_sign,
    qkv_codes,
    qkv_scale,
    qkv_sign,
    windows,
    oin_sign,
    out_codes,
    out_scale,
    out_sign,
):
    head_count = lax.axis_size("head")
    row_tiles = lax.axis_size("height")
    row_place = lax.axis_index("height")
    head_place = lax.axis_index("head").astype(jnp.int32)
    top = head_count // 2
    end = jnp.where(head_place >= top, 0, 2).astype(jnp.int32)
    place = jnp.stack([head_place, end, row_place.astype(jnp.int32)])
    low_bits = [1 << b for b in range(top.bit_length() - 1)]

    own, early = turn(place, tokens[0], in_sign)
    early = swap(early, top)
    near = {0: own}
    for bit in low_bits:
        for flip in list(near):
            near[flip ^ bit] = swap(near[flip], bit)
    codes = jnp.transpose(qkv_codes, (1, 0, 2))
    near_flips = tuple(sorted(near))
    far_flips = tuple(flip ^ top for flip in near_flips)
    sums, words, late = prepare(
        place, near_flips, far_flips, [near[flip] for flip in near_flips], codes
    )
    out_weights = unpack_out(out_codes, sums)
    late = {top: swap(late, top)}
    early = {top: tie(early, sums, out_weights)}
    for bit in low_bits:
        for flip in list(early):
            early[flip ^ bit] = swap(early[flip], bit)
    early = [early[flip] for flip in far_flips]
    swaps = row_swaps(row_tiles)
    ending = [qkv_scale, qkv_sign]
    every = tuple(range(len(far_flips)))
    partial = project((1, 2), 0, [early[:-1]], every[:-1], sums, words, None)
    key_values = [project((1, 2), 0, [early[-1:]], every[-1:], partial, words, ending)]
    early_blocks = [lax.ppermute(key_values[0], "height", pairs) for _, _, pairs in swaps]
    for bit in low_bits:
        for flip in list(late):
            late[flip ^ bit] = swap(late[flip], bit)
    late = [late[flip] for flip in far_flips]
    key_values.append(project((1, 2), EARLY, [late], every, sums, words, ending))
    late_blocks = [lax.ppermute(key_values[1], "height", pairs) for _, _, pairs in swaps]
    queries = project((0,), 0, [early, late], every, sums, words, ending)

    listed = windows[0]
    own_tiles = tuple((None, position) for position in range(WTILES))
    early_tiles = tuple(((by, odd), position) for by, odd, _ in swaps for position in (0, 1))
    late_tiles = tuple(((by, odd), 2) for by, odd, _ in swaps)
    running = attend(place, listed, queries, key_values, own_tiles, None, None)
    running = attend(place, listed, queries, early_blocks, early_tiles, running, None)
    rotated = attend(
        place,
        listed,
        queries,
        late_blocks,
        late_tiles,
        running,
        (oin_sign, halving_order(head_count)),
    )

    bits = low_bits + [top]
    scale_rows = out_scale.reshape(-1, HAD)
    sign_rows = out_sign.reshape(-1, HAD)
    result = None
    first = 0
    send = rotated
    for columns in CHUNKS:
        send, keep = out_project(rotated, out_weights, scale_rows, send, first, columns)
        part = send
        for bit in bits:
            more = swap(part, bit)
            if bit == top:
                break
            total = keep.astype(f32) + more.astype(f32)
            half = total.shape[0] // 2
            part, keep = total[:half].astype(bf16), total[half:]
        send = part
        result = finish(result, sign_rows, keep, more, first)
        first += columns
    return result[None]


def solution(mesh):
    return jax.shard_map(
        on_device,
        mesh=mesh,
        in_specs=(
            P(("clip", "height"), None, "head"),
            P(),
            P(None, None, "head"),
            P(None, "head"),
            P(None, "head"),
            P(("clip", "height"), None, None),
            P("head"),
            P("head", None),
            P(),
            P(),
        ),
        out_specs=P(("clip", "height"), "head", None),
        check_vma=False,
    )
```

time: 89.6 us -> 58.5 us (0.65)
  the two profiles are of different devices: /device:TPU:0 before, /device:TPU:16 now
where the time goes in v1:
time: 58.5 us; the launch traced here: 58.3 us
  Pallas kernels  23.1 us (39%)
  waiting for transfers between devices  21.1 us (36%)
  starting transfers between devices  13.3 us (23%)
    pallas_call x15, Pallas kernels, call(): pl.pallas_call(body, out_shape=out_shape, in_specs=in_specs, out_specs=ou...  23.1 us
    ppermute x9, waiting for transfers between devices, swap(): return lax.ppermute(shard, 'head', [(i, i ^ bit) for i in range(peers)])  18.2 us
    ppermute x9, starting transfers between devices, swap(): return lax.ppermute(shard, 'head', [(i, i ^ bit) for i in range(peers)])  5.56 us
    ppermute x2, starting transfers between devices, on_device(): lax.ppermute(key_values[1], 'height', pairs)  4.18 us
    ppermute x2, starting transfers between devices, on_device(): lax.ppermute(key_values[0], 'height', pairs)  3.56 us
    ppermute x2, waiting for transfers between devices, on_device(): lax.ppermute(key_values[1], 'height', pairs)  2.01 us
  transfers between devices with their start and end apart: 13, of which 8 were waited for; matrix products, arithmetic and copies ran while one was open for 0% of the time, Pallas kernels for 29%

profile of v1, /device:TPU:16, one launch (start us, length us, event | category | flops | bytes accessed | tf_op | source)
XLA Modules:
  0.0 58.3 jit_solution(4954938198469307951)
XLA Ops:
  0.1 1.9 %turn.1 = (bf16[192,1280]{1,0:T(8,128)(2,1)S(1)}, bf16[128,1280]{1,0:T(8,128)(2,1)S(1)}) custom-call(s32[3]{0:T(128)S(1)} %pad_add_fusion.place_ref, bf16[192,1280]{1,0:T(8,128)(2,1)} %bitcast.22, s32[40,128]{1,0:T(8,128)} %bitcast.23), custom_call_target="tpu_custom_call" | custom-call | flops 1 | bytes 1 | tf_op jit(solution)/shard_map/turn/pallas_call | solution.py:45
  2.0 1.6 %collective-permute-start = (bf16[128,1280]{1,0:T(8,128)(2,1)S(1)}, bf16[128,1280]{1,0:T(8,128)(2,1)S(1)}, u32[]{:S(2)}, u32[]{:S(2)}) collective-permute-start(bf16[128,1280]{1,0:T(8,128)(2,1)S(1)} %get-tuple-element.14), channel_id=1, source_target_pairs={{0,2},{1,3},{2,0},{3,1},{4,6},{5,7},{6,4},{7,5},{8,10},{9,11},{10,... | collective-permute-start | bytes 983048 | tf_op jit(solution)/shard_map/ppermute | solution.py:541
  3.9 5.1 %prepare.1 = (f32[3,192,768]{2,1,0:T(8,128)S(1)}, s32[2,3,160,768]{3,2,1,0:T(8,128)S(1)}, bf16[64,1280]{1,0:T(8,128)(2,1)S(1)}) custom-call(s32[3]{0:T(128)S(1)} %pad_add_fusion.place_ref, bf16[192,1280]{1,0:T(8,128)(2,1)S(1)} %get-tuple-element.15.rest_0_, bf16[192,1280]{1,0:T(8,128)(2,1)S(1)} %collective-permute-done.1.rest_1_, s32[3,640,768]{2,1,0:T(8,128)} %bitcast.21), custom_call_target="tpu_custom_call" | custom-call | flops 1 | bytes 1 | tf_op jit(solution)/shard_map/prepare/pallas_call | solution.py:45
  9.0 1.5 %unpack_out.1.refs_2_.weights_ref = bf16[768,5120]{1,0:T(8,128)(2,1)S(1)} custom-call(s32[96,5120]{1,0:T(8,128)S(1)} %copy-done, f32[3,192,768]{2,1,0:T(8,128)S(1)} %get-tuple-element.16.after_ref.refs_1_.rest_4_.rest_2_.rest_1_), custom_call_target="tpu_custom_call" | custom-call | flops 1 | bytes 1 | tf_op jit(solution)/shard_map/unpack_out/pallas_call | solution.py:45
  10.5 1.7 %collective-permute-done.refs_0_ = bf16[128,1280]{1,0:T(8,128)(2,1)S(1)} collective-permute-done((bf16[128,1280]{1,0:T(8,128)(2,1)S(1)}, bf16[128,1280]{1,0:T(8,128)(2,1)S(1)}, u32[]{:S(2)}, u32[]{:S(2)}) %collective-permute-start) | collective-permute-done | bytes 327712 | tf_op jit(solution)/shard_map/ppermute | solution.py:541
  12.2 1.5 %collective-permute-start.3 = (bf16[64,1280]{1,0:T(8,128)(2,1)S(1)}, bf16[64,1280]{1,0:T(8,128)(2,1)S(1)}, u32[]{:S(2)}, u32[]{:S(2)}) collective-permute-start(bf16[64,1280]{1,0:T(8,128)(2,1)S(1)} %get-tuple-element.17), channel_id=1, source_target_pairs={{0,2},{1,3},{2,0},{3,1},{4,6},{5,7},{6,4},{7,5},{8,10},{9,11},{10,... | collective-permute-start | bytes 491528 | tf_op jit(solution)/shard_map/ppermute | solution.py:541
  13.7 1.3 %project.6.rest_1_ = f32[2,128,768]{2,1,0:T(8,128)S(1)} custom-call(bf16[128,1280]{1,0:T(8,128)(2,1)S(1)} %tie.1.rest_0_, f32[3,192,768]{2,1,0:T(8,128)S(1)} %get-tuple-element.16.after_ref.refs_1_.rest_4_.rest_2_.rest_1_, s32[2,3,160,768]{3,2,1,0:T(8,128)S(1)} %get-tuple-element.18.rest_5_.rest_3_.rest_2_), custom_call_target="tpu_custom_call" | custom-call | flops 1 | bytes 1 | tf_op jit(solution)/shard_map/project/pallas_call | solution.py:45
  15.0 1.6 %project.7.rest_0_ = bf16[2,128,768]{2,1,0:T(8,128)(2,1)S(1)} custom-call(bf16[128,1280]{1,0:T(8,128)(2,1)S(1)} %collective-permute-done.2.rest_1_.rest_0_, f32[2,128,768]{2,1,0:T(8,128)S(1)} %project.6.rest_1_, s32[2,3,160,768]{3,2,1,0:T(8,128)S(1)} %get-tuple-element.18.rest_5_.rest_3_.rest_2_, f32[3,768]{1,0:T(4,128)S(1)} %copy-done.1, s32[3,768]{1,0:T(4,128)S(1)} %copy-done.2), custom_call_target="tpu_custom_call" | custom-call | flops 1 | bytes 1 | tf_op jit(solution)/shard_map/project/pallas_call | solution.py:45
  16.6 1.7 %collective-permute-start.7 = (bf16[2,128,768]{2,1,0:T(8,128)(2,1)S(1)}, bf16[2,128,768]{2,1,0:T(8,128)(2,1)S(1)}, u32[]{:S(2)}, u32[]{:S(2)}) collective-permute-start(bf16[2,128,768]{2,1,0:T(8,128)(2,1)S(1)} %project.7.rest_0_), channel_id=1, source_target_pairs={{0,4},{8,12},{4,0},{12,8},{1,5},{9,13},{5,1},{13,9},{2,6},{10,14},... | collective-permute-start | bytes 1179656 | tf_op jit(solution)/shard_map/ppermute | solution.py:610
  18.3 1.9 %collective-permute-start.8 = (bf16[2,128,768]{2,1,0:T(8,128)(2,1)S(1)}, bf16[2,128,768]{2,1,0:T(8,128)(2,1)S(1)}, u32[]{:S(2)}, u32[]{:S(2)}) collective-permute-start(bf16[2,128,768]{2,1,0:T(8,128)(2,1)S(1)} %project.7.rest_0_), channel_id=1, source_target_pairs={{4,8},{8,4},{5,9},{9,5},{6,10},{10,6},{7,11},{11,7},{20,24},{24,20... | collective-permute-start | bytes 1179656 | tf_op jit(solution)/shard_map/ppermute | solution.py:610
  20.3 1.4 %collective-permute-done.4.rest_3_.rest_1_ = bf16[64,1280]{1,0:T(8,128)(2,1)S(1)} collective-permute-done((bf16[64,1280]{1,0:T(8,128)(2,1)S(1)}, bf16[64,1280]{1,0:T(8,128)(2,1)S(1)}, u32[]{:S(2)}, u32[]{:S(2)}) %collective-permute-start.4) | collective-permute-done | bytes 163872 | tf_op jit(solution)/shard_map/ppermute | solution.py:541
  21.6 2.4 %project.5.rest_1_ = bf16[2,64,768]{2,1,0:T(8,128)(2,1)S(1)} custom-call(bf16[64,1280]{1,0:T(8,128)(2,1)S(1)} %collective-permute-done.3.rest_2_.rest_0_, bf16[64,1280]{1,0:T(8,128)(2,1)S(1)} %collective-permute-done.4.rest_3_.rest_1_, f32[3,192,768]{2,1,0:T(8,128)S(1)} %get-tuple-element.16.after_ref.refs_1_.rest_4_.rest_2_.rest_1_, ...), custom_call_target="tpu_custom_call" | custom-call | flops 1 | bytes 1 | tf_op jit(solution)/shard_map/project/pallas_call | solution.py:45
  24.3 4.0 %collective-permute-start.6 = (bf16[2,64,768]{2,1,0:T(8,128)(2,1)S(1)}, bf16[2,64,768]{2,1,0:T(8,128)(2,1)S(1)}, u32[]{:S(2)}, u32[]{:S(2)}) collective-permute-start(bf16[2,64,768]{2,1,0:T(8,128)(2,1)S(1)} %project.5.rest_1_), channel_id=1, source_target_pairs={{4,8},{8,4},{5,9},{9,5},{6,10},{10,6},{7,11},{11,7},{20,24},{24,20... | collective-permute-start | bytes 589832 | tf_op jit(solution)/shard_map/ppermute | solution.py:616
  28.3 1.8 %project.4.q_ref = bf16[1,192,768]{2,1,0:T(8,128)(2,1)S(1)} custom-call(bf16[128,1280]{1,0:T(8,128)(2,1)S(1)} %tie.1.rest_0_, bf16[128,1280]{1,0:T(8,128)(2,1)S(1)} %collective-permute-done.2.rest_1_.rest_0_, bf16[64,1280]{1,0:T(8,128)(2,1)S(1)} %collective-permute-done.3.rest_2_.rest_0_, bf16[64,1280]{1,0:T(8,128)(2,1)S(1)} %collective-permute-done.4.rest_3_.rest_1_, ...), custom_call_target="tpu_custom_call" | custom-call | flops 1 | bytes 1 | tf_op jit(solution)/shard_map/project/pallas_call | solution.py:45
  30.1 1.1 %attend.3.rest_2_ = f32[6,192,256]{2,1,0:T(8,128)S(1)} custom-call(s32[3]{0:T(128)S(1)} %pad_add_fusion.place_ref, s32[3,27]{1,0:T(4,128)S(1)} %bitcast.17, bf16[1,192,768]{2,1,0:T(8,128)(2,1)S(1)} %project.4.q_ref, bf16[2,128,768]{2,1,0:T(8,128)(2,1)S(1)} %project.7.rest_0_, bf16[2,64,768]{2,1,0:T(8,128)(2,1)S(1)} %project.5.rest_1_), custom_call_target="tpu_custom_call" | custom-call | flops 1 | bytes 1 | tf_op jit(solution)/shard_map/attend/pallas_call | solution.py:45
  32.1 1.1 %attend.4.rest_2_ = f32[6,192,256]{2,1,0:T(8,128)S(1)} custom-call(s32[3]{0:T(128)S(1)} %pad_add_fusion.place_ref, s32[3,27]{1,0:T(4,128)S(1)} %bitcast.18, bf16[1,192,768]{2,1,0:T(8,128)(2,1)S(1)} %project.4.q_ref, bf16[2,128,768]{2,1,0:T(8,128)(2,1)S(1)} %collective-permute-done.7.rest_0_, bf16[2,128,768]{2,1,0:T(8,128)(2,1)S(1)} %collective-permute-done.8.rest_1_, ...), custom_call_target="tpu_custom_call" | custom-call | flops 1 | bytes 1 | tf_op jit(solution)/shard_map/attend/pallas_call | solution.py:45
  33.3 2.0 %collective-permute-done.6.rest_1_ = bf16[2,64,768]{2,1,0:T(8,128)(2,1)S(1)} collective-permute-done((bf16[2,64,768]{2,1,0:T(8,128)(2,1)S(1)}, bf16[2,64,768]{2,1,0:T(8,128)(2,1)S(1)}, u32[]{:S(2)}, u32[]{:S(2)}) %collective-permute-start.6) | collective-permute-done | bytes 196640 | tf_op jit(solution)/shard_map/ppermute | solution.py:616
  35.3 1.2 %attend.5.rotated_ref.after_ref = bf16[192,768]{1,0:T(8,128)(2,1)S(1)} custom-call(s32[3]{0:T(128)S(1)} %pad_add_fusion.place_ref, s32[3,27]{1,0:T(4,128)S(1)} %bitcast.19, bf16[1,192,768]{2,1,0:T(8,128)(2,1)S(1)} %project.4.q_ref, bf16[2,64,768]{2,1,0:T(8,128)(2,1)S(1)} %collective-permute-done.5.rest_0_, ...), custom_call_target="tpu_custom_call" | custom-call | flops 1 | bytes 1 | tf_op jit(solution)/shard_map/attend/pallas_call | solution.py:45
  37.4 1.7 %collective-permute-done.9 = bf16[96,2048]{1,0:T(8,128)(2,1)S(1)} collective-permute-done((bf16[96,2048]{1,0:T(8,128)(2,1)S(1)}, bf16[96,2048]{1,0:T(8,128)(2,1)S(1)}, u32[]{:S(2)}, u32[]{:S(2)}) %collective-permute-start.9) | collective-permute-done | bytes 393248 | tf_op jit(solution)/shard_map/ppermute | solution.py:541
  39.3 1.1 %out_project.3 = (bf16[96,3072]{1,0:T(8,128)(2,1)S(1)}, bf16[96,3072]{1,0:T(8,128)(2,1)S(1)}) custom-call(bf16[192,768]{1,0:T(8,128)(2,1)S(1)} %attend.5.rotated_ref.after_ref, bf16[768,5120]{1,0:T(8,128)(2,1)S(1)} %unpack_out.1.refs_2_.weights_ref, f32[40,128]{1,0:T(8,128)S(1)} %bitcast.14, bf16[48,2048]{1,0:T(8,128)(2,1)S(1)} %slice.25.after_ref), custom_call_target="tpu_custom_call" | custom-call | flops 1 | bytes 1 | tf_op jit(solution)/shard_map/out_project/pallas_call | solution.py:45
  40.6 1.9 %collective-permute-done.10 = bf16[96,3072]{1,0:T(8,128)(2,1)S(1)} collective-permute-done((bf16[96,3072]{1,0:T(8,128)(2,1)S(1)}, bf16[96,3072]{1,0:T(8,128)(2,1)S(1)}, u32[]{:S(2)}, u32[]{:S(2)}) %collective-permute-start.10) | collective-permute-done | bytes 589856 | tf_op jit(solution)/shard_map/ppermute | solution.py:541
  43.3 1.5 %collective-permute-start.12 = (bf16[48,2048]{1,0:T(8,128)(2,1)S(1)}, bf16[48,2048]{1,0:T(8,128)(2,1)S(1)}, u32[]{:S(2)}, u32[]{:S(2)}) collective-permute-start(bf16[48,2048]{1,0:T(8,128)(2,1)S(1)} %slice.25.after_ref), channel_id=1, source_target_pairs={{0,2},{1,3},{2,0},{3,1},{4,6},{5,7},{6,4},{7,5},{8,10},{9,11},{10,... | collective-permute-start | bytes 589832 | tf_op jit(solution)/shard_map/ppermute | solution.py:541
  44.8 11.2 %collective-permute-done.12.more_ref = bf16[48,2048]{1,0:T(8,128)(2,1)S(1)} collective-permute-done((bf16[48,2048]{1,0:T(8,128)(2,1)S(1)}, bf16[48,2048]{1,0:T(8,128)(2,1)S(1)}, u32[]{:S(2)}, u32[]{:S(2)}) %collective-permute-start.12) | collective-permute-done | bytes 196640 | tf_op jit(solution)/shard_map/ppermute | solution.py:541
  57.1 1.1 %finish.3 = bf16[48,5120]{1,0:T(8,128)(2,1)} custom-call(s32[40,128]{1,0:T(8,128)S(1)} %bitcast.16, f32[48,3072]{1,0:T(8,128)S(1)} %slice.19.keep_ref, bf16[48,3072]{1,0:T(8,128)(2,1)S(1)} %collective-permute-done.11.more_ref, bf16[48,5120]{1,0:T(8,128)(2,1)} %finish.2.rest_0_), custom_call_target="tpu_custom_call", output_to_operand_aliasing={{}: (3, {})} | custom-call | flops 1 | bytes 1 | tf_op jit(solution)/shard_map/finish/pallas_call | solution.py:45
  (39 shorter events, 4.6 us)
Async XLA Ops:
  2.0 1.9 %collective-permute-start.1 = (bf16[192,1280]{1,0:T(8,128)(2,1)S(1)}, bf16[192,1280]{1,0:T(8,128)(2,1)S(1)}, u32[]{:S(2)}, u32[]{:S(2)}) collective-permute-start(bf16[192,1280]{1,0:T(8,128)(2,1)S(1)} %get-tuple-element.15.rest_0_), channel_id=1, source_target_pairs={{0,1},{1,0},{2,3},{3,2},{4,5},{5,4},{6,7},{7,6},{8,9},{9,8},{10,11... | collective-permute-start | bytes 1474568 | tf_op jit(solution)/shard_map/ppermute | solution.py:541
  2.0 10.1 %collective-permute-start = (bf16[128,1280]{1,0:T(8,128)(2,1)S(1)}, bf16[128,1280]{1,0:T(8,128)(2,1)S(1)}, u32[]{:S(2)}, u32[]{:S(2)}) collective-permute-start(bf16[128,1280]{1,0:T(8,128)(2,1)S(1)} %get-tuple-element.14), channel_id=1, source_target_pairs={{0,2},{1,3},{2,0},{3,1},{4,6},{5,7},{6,4},{7,5},{8,10},{9,11},{10,... | collective-permute-start | bytes 983048 | tf_op jit(solution)/shard_map/ppermute | solution.py:541
  3.9 5.1 %copy-start = (s32[96,5120]{1,0:T(8,128)S(1)}, s32[96,5120]{1,0:T(8,128)}, u32[]{:S(2)}) copy-start(s32[96,5120]{1,0:T(8,128)} %codes_ref.1) | copy-start | bytes 5898244
  12.2 2.8 %collective-permute-start.2 = (bf16[128,1280]{1,0:T(8,128)(2,1)S(1)}, bf16[128,1280]{1,0:T(8,128)(2,1)S(1)}, u32[]{:S(2)}, u32[]{:S(2)}) collective-permute-start(bf16[128,1280]{1,0:T(8,128)(2,1)S(1)} %tie.1.rest_0_), channel_id=1, source_target_pairs={{0,1},{1,0},{2,3},{3,2},{4,5},{5,4},{6,7},{7,6},{8,9},{9,8},{10,11... | collective-permute-start | bytes 983048 | tf_op jit(solution)/shard_map/ppermute | solution.py:541
  12.2 8.0 %collective-permute-start.3 = (bf16[64,1280]{1,0:T(8,128)(2,1)S(1)}, bf16[64,1280]{1,0:T(8,128)(2,1)S(1)}, u32[]{:S(2)}, u32[]{:S(2)}) collective-permute-start(bf16[64,1280]{1,0:T(8,128)(2,1)S(1)} %get-tuple-element.17), channel_id=1, source_target_pairs={{0,2},{1,3},{2,0},{3,1},{4,6},{5,7},{6,4},{7,5},{8,10},{9,11},{10,... | collective-permute-start | bytes 491528 | tf_op jit(solution)/shard_map/ppermute | solution.py:541
  13.7 1.3 %copy-start.1 = (f32[3,768]{1,0:T(4,128)S(1)}, f32[3,768]{1,0:T(4,128)}, u32[]{:S(2)}) copy-start(f32[3,768]{1,0:T(4,128)} %rest_3_.1) | copy-start | bytes 27652
  13.7 1.3 %copy-start.2 = (s32[3,768]{1,0:T(4,128)S(1)}, s32[3,768]{1,0:T(4,128)}, u32[]{:S(2)}) copy-start(s32[3,768]{1,0:T(4,128)} %rest_4_.3) | copy-start | bytes 27652
  16.6 11.7 %copy-start.6 = (s32[1,3,27]{2,0,1:T(1,128)S(1)}, s32[1,3,27]{2,0,1:T(1,128)}, u32[]{:S(2)}) copy-start(s32[1,3,27]{2,0,1:T(1,128)} %param.15) | copy-start | bytes 976
  16.6 14.7 %collective-permute-start.7 = (bf16[2,128,768]{2,1,0:T(8,128)(2,1)S(1)}, bf16[2,128,768]{2,1,0:T(8,128)(2,1)S(1)}, u32[]{:S(2)}, u32[]{:S(2)}) collective-permute-start(bf16[2,128,768]{2,1,0:T(8,128)(2,1)S(1)} %project.7.rest_0_), channel_id=1, source_target_pairs={{0,4},{8,12},{4,0},{12,8},{1,5},{9,13},{5,1},{13,9},{2,6},{10,14},... | collective-permute-start | bytes 1179656 | tf_op jit(solution)/shard_map/ppermute | solution.py:610
  18.3 13.9 %collective-permute-start.8 = (bf16[2,128,768]{2,1,0:T(8,128)(2,1)S(1)}, bf16[2,128,768]{2,1,0:T(8,128)(2,1)S(1)}, u32[]{:S(2)}, u32[]{:S(2)}) collective-permute-start(bf16[2,128,768]{2,1,0:T(8,128)(2,1)S(1)} %project.7.rest_0_), channel_id=1, source_target_pairs={{4,8},{8,4},{5,9},{9,5},{6,10},{10,6},{7,11},{11,7},{20,24},{24,20... | collective-permute-start | bytes 1179656 | tf_op jit(solution)/shard_map/ppermute | solution.py:610
  20.2 1.5 %collective-permute-start.4 = (bf16[64,1280]{1,0:T(8,128)(2,1)S(1)}, bf16[64,1280]{1,0:T(8,128)(2,1)S(1)}, u32[]{:S(2)}, u32[]{:S(2)}) collective-permute-start(bf16[64,1280]{1,0:T(8,128)(2,1)S(1)} %collective-permute-done.3.rest_2_.rest_0_), channel_id=1, source_target_pairs={{0,1},{1,0},{2,3},{3,2},{4,5},{5,4},{6,7},{7,6},{8,9},{9,8},{10,11... | collective-permute-start | bytes 491528 | tf_op jit(solution)/shard_map/ppermute | solution.py:541
  24.1 9.2 %collective-permute-start.5 = (bf16[2,64,768]{2,1,0:T(8,128)(2,1)S(1)}, bf16[2,64,768]{2,1,0:T(8,128)(2,1)S(1)}, u32[]{:S(2)}, u32[]{:S(2)}) collective-permute-start(bf16[2,64,768]{2,1,0:T(8,128)(2,1)S(1)} %project.5.rest_1_), channel_id=1, source_target_pairs={{0,4},{8,12},{4,0},{12,8},{1,5},{9,13},{5,1},{13,9},{2,6},{10,14},... | collective-permute-start | bytes 589832 | tf_op jit(solution)/shard_map/ppermute | solution.py:616
  24.3 11.0 %collective-permute-start.6 = (bf16[2,64,768]{2,1,0:T(8,128)(2,1)S(1)}, bf16[2,64,768]{2,1,0:T(8,128)(2,1)S(1)}, u32[]{:S(2)}, u32[]{:S(2)}) collective-permute-start(bf16[2,64,768]{2,1,0:T(8,128)(2,1)S(1)} %project.5.rest_1_), channel_id=1, source_target_pairs={{4,8},{8,4},{5,9},{9,5},{6,10},{10,6},{7,11},{11,7},{20,24},{24,20... | collective-permute-start | bytes 589832 | tf_op jit(solution)/shard_map/ppermute | solution.py:616
  31.2 4.1 %copy-start.5 = (s32[768]{0:T(1024)S(1)}, s32[768]{0:T(1024)}, u32[]{:S(2)}) copy-start(s32[768]{0:T(1024)} %param.16) | copy-start | bytes 9220
  33.3 3.2 %copy-start.3 = (f32[5120]{0:T(1024)S(1)}, f32[5120]{0:T(1024)}, u32[]{:S(2)}) copy-start(f32[5120]{0:T(1024)} %param.18) | copy-start | bytes 61444
  37.4 1.8 %collective-permute-start.9 = (bf16[96,2048]{1,0:T(8,128)(2,1)S(1)}, bf16[96,2048]{1,0:T(8,128)(2,1)S(1)}, u32[]{:S(2)}, u32[]{:S(2)}) collective-permute-start(bf16[96,2048]{1,0:T(8,128)(2,1)S(1)} %get-tuple-element.20), channel_id=1, source_target_pairs={{0,1},{1,0},{2,3},{3,2},{4,5},{5,4},{6,7},{7,6},{8,9},{9,8},{10,11... | collective-permute-start | bytes 1179656 | tf_op jit(solution)/shard_map/ppermute | solution.py:541
  40.4 2.1 %collective-permute-start.10 = (bf16[96,3072]{1,0:T(8,128)(2,1)S(1)}, bf16[96,3072]{1,0:T(8,128)(2,1)S(1)}, u32[]{:S(2)}, u32[]{:S(2)}) collective-permute-start(bf16[96,3072]{1,0:T(8,128)(2,1)S(1)} %get-tuple-element.22), channel_id=1, source_target_pairs={{0,1},{1,0},{2,3},{3,2},{4,5},{5,4},{6,7},{7,6},{8,9},{9,8},{10,11... | collective-permute-start | bytes 1769480 | tf_op jit(solution)/shard_map/ppermute | solution.py:541
  42.6 13.4 %copy-start.4 = (s32[5120]{0:T(1024)S(1)}, s32[5120]{0:T(1024)}, u32[]{:S(2)}) copy-start(s32[5120]{0:T(1024)} %param.19) | copy-start | bytes 61444
  42.7 14.4 %collective-permute-start.11 = (bf16[48,3072]{1,0:T(8,128)(2,1)S(1)}, bf16[48,3072]{1,0:T(8,128)(2,1)S(1)}, u32[]{:S(2)}, u32[]{:S(2)}) collective-permute-start(bf16[48,3072]{1,0:T(8,128)(2,1)S(1)} %slice.24), channel_id=1, source_target_pairs={{0,2},{1,3},{2,0},{3,1},{4,6},{5,7},{6,4},{7,5},{8,10},{9,11},{10,... | collective-permute-start | bytes 884744 | tf_op jit(solution)/shard_map/ppermute | solution.py:541
  43.3 12.7 %collective-permute-start.12 = (bf16[48,2048]{1,0:T(8,128)(2,1)S(1)}, bf16[48,2048]{1,0:T(8,128)(2,1)S(1)}, u32[]{:S(2)}, u32[]{:S(2)}) collective-permute-start(bf16[48,2048]{1,0:T(8,128)(2,1)S(1)} %slice.25.after_ref), channel_id=1, source_target_pairs={{0,2},{1,3},{2,0},{3,1},{4,6},{5,7},{6,4},{7,5},{8,10},{9,11},{10,... | collective-permute-start | bytes 589832 | tf_op jit(solution)/shard_map/ppermute | solution.py:541

commit v2 on v1

--- a/solution.py
+++ b/solution.py
@@ -17,7 +17,6 @@
 WTILES = 3
 PLANES = 8
 WORDS = HAD // PLANES
-EARLY = 2 * TILE
 QKV_ORDER = "half"
 OUT_ORDER = "byte"
 
@@ -38,19 +37,16 @@
     return pltpu.with_memory_space_constraint(array, pltpu.HBM)
 
 
-def call(body, out_shape, in_specs, args, name, flops=0, out_specs=None, megabytes=16, **more):
+def call(body, out_shape, in_specs, args, name, out_specs=None, megabytes=16, **more):
     if out_specs is None:
         out_specs = jax.tree.map(lambda _: VMEM, out_shape)
-    moved = sum(a.size * a.dtype.itemsize for a in args)
     return pl.pallas_call(
         body,
         out_shape=out_shape,
         in_specs=in_specs,
         out_specs=out_specs,
         compiler_params=pltpu.CompilerParams(vmem_limit_bytes=megabytes * 2**20),
-        cost_estimate=pl.CostEstimate(
-            flops=1, bytes_accessed=1, transcendentals=0
-        ),
+        cost_estimate=pl.CostEstimate(flops=1, bytes_accessed=1, transcendentals=0),
         name=name,
         **more,
     )(*args)
@@ -154,18 +150,14 @@
         copy.wait()
     blocks = x_ref.shape[1] // HAD
     first = place_ref[0] * blocks
-    end = place_ref[1]
-    tiles = (end, 1, 2 - end)
     for b in range(blocks):
         cols = slice(b * HAD, (b + 1) * HAD)
         sign_row = signed(sign_ref[pl.ds(first + b, 1), :])
-        own = [x_ref[pl.ds(pl.multiple_of(t * TILE, TILE), TILE), cols] for t in tiles]
-        flipped = (jnp.concatenate(own, 0).astype(f32) * sign_row).astype(bf16)
+        flipped = (x_ref[:, cols].astype(f32) * sign_row).astype(bf16)
         turned = jnp.dot(flipped, matrix, preferred_element_type=f32)
         turned = (turned * factor).astype(bf16)
         own_ref[:, cols] = turned
-        send_ref[:TILE, cols] = turned[2 * TILE :]
-        send_ref[TILE:, cols] = turned[TILE : 2 * TILE]
+        send_ref[:, cols] = turned[: send_ref.shape[0]]
 
 
 def turn(place, own_tokens, in_sign):
@@ -173,11 +165,10 @@
     rows, inner = own_tokens.shape
     return call(
         turn_kernel,
-        (shape_of((rows, inner), bf16), shape_of((EARLY, inner), bf16)),
+        (shape_of((rows, inner), bf16), shape_of((rows // 2, inner), bf16)),
         [SMEM, HBM, HBM],
         (place, in_hbm(own_tokens), in_hbm(sign_rows)),
         "turn",
-        flops=2 * own_tokens.size * HAD,
         scratch_shapes=[
             pltpu.VMEM(own_tokens.shape, bf16),
             pltpu.VMEM(sign_rows.shape, jnp.int32),
@@ -220,7 +211,7 @@
             fetch(position, kind).start()
     fix = row_correction([ref[...] for ref in shard_refs], QKV_ORDER)
     width = tile_width(columns)
-    late_ref[...] = shard_refs[0][:TILE, :]
+    late_ref[...] = shard_refs[0][late_ref.shape[0] :, :]
 
     def product(kind, carry):
         for position in range(len(near)):
@@ -249,12 +240,11 @@
         (
             shape_of((3, rows, columns), f32),
             shape_of((len(far), 3, words, columns), jnp.int32),
-            shape_of((TILE, inner), bf16),
+            shape_of((rows // 2, inner), bf16),
         ),
         [SMEM] + [VMEM] * len(near) + [HBM],
         (place, *shards, in_hbm(codes)),
         "prepare",
-        flops=16 * rows * inner * 3 * columns,
         scratch_shapes=[
             pltpu.VMEM((len(near), 3, words, columns), jnp.int32),
             pltpu.SemaphoreType.DMA((len(near + far), 3)),
@@ -331,7 +321,6 @@
         [VMEM] * len(args),
         args,
         "project",
-        flops=4 * row_count * inner * len(positions) * len(kinds) * columns,
     )
 
 
@@ -342,16 +331,16 @@
     return jnp.where(lax.rem(row // by, 2) == odd, row + by, row - by)
 
 
-def window_mask(place_ref, windows_ref, key_tiles, row_count):
-    end = place_ref[1]
-    order = (end, 1, 2 - end)
-    lane = lax.broadcasted_iota(jnp.int32, (1, len(key_tiles) * TILE), 1) // TILE
-    ids = None
-    for index, (swap_pair, position) in enumerate(key_tiles):
-        one = near_row(place_ref[2], swap_pair) * WTILES + order[position]
-        ids = jnp.full(lane.shape, one, jnp.int32) if ids is None else jnp.where(lane == index, one, ids)
+def window_mask(place_ref, windows_ref, segments, row_count):
+    lane = lax.broadcasted_iota(jnp.int32, (1, sum(rows for _, _, rows in segments)), 1)
+    ids, base = None, 0
+    for swap_pair, first, rows in segments:
+        tile = (lane + (first - base)) // TILE
+        ids_here = near_row(place_ref[1], swap_pair) * WTILES + tile
+        ids = ids_here if ids is None else jnp.where(lane >= base, ids_here, ids)
+        base += rows
     masks = []
-    for tile in order:
+    for tile in range(row_count // TILE):
         hit = jnp.zeros(lane.shape, f32)
         for entry in range(windows_ref.shape[1]):
             hit = jnp.where(ids == windows_ref[tile, entry], 1.0, hit)
@@ -359,7 +348,7 @@
     return jnp.concatenate(masks, 0)
 
 
-def attend_kernel(key_tiles, blocks, has_sum, last, share_order, place_ref, windows_ref, q_ref, *rest):
+def attend_kernel(segments, blocks, has_sum, last, share_order, place_ref, windows_ref, q_ref, *rest):
     rest = list(rest)
     kv_refs = [rest.pop(0) for _ in range(blocks)]
     sum_ref = rest.pop(0) if has_sum else None
@@ -369,7 +358,7 @@
         (out_ref,) = rest
     row_count, columns = q_ref.shape[1:]
     heads = [slice(head, head + HD) for head in range(0, columns, HD)]
-    mask = window_mask(place_ref, windows_ref, key_tiles, row_count)
+    mask = window_mask(place_ref, windows_ref, segments, row_count)
     scores = []
     for at in heads:
         keys = jnp.concatenate([ref[0, :, at] for ref in kv_refs], 0)
@@ -395,16 +384,11 @@
         return
     matrix = hadamard(OUT_ORDER)
     factor = turn_factor(OUT_ORDER)
-    end = place_ref[1]
     for head, at in enumerate(heads):
         attended = (totals[head][:, :HD] / totals[head][:, HD:]).astype(bf16)
         sign_row = signed(oin_ref[head : head + 1, :])
         flipped = (attended.astype(f32) * sign_row).astype(bf16)
-        rotated = jnp.dot(flipped, matrix, preferred_element_type=f32) * factor
-        for position, tile in enumerate((end, 1, 2 - end)):
-            rotated_ref[pl.ds(pl.multiple_of(tile * TILE, TILE), TILE), at] = rotated[
-                position * TILE : (position + 1) * TILE
-            ]
+        rotated_ref[:, at] = jnp.dot(flipped, matrix, preferred_element_type=f32) * factor
     share = row_count // len(share_order)
     pieces = []
     for flip in share_order:
@@ -413,7 +397,7 @@
     out_ref[...] = jnp.concatenate(pieces, 0).astype(bf16)
 
 
-def attend(place, windows, queries, blocks, key_tiles, running, ending):
+def attend(place, windows, queries, blocks, segments, running, ending):
     row_count, columns = queries.shape[1:]
     args = [place, windows, queries, *blocks]
     if running is not None:
@@ -429,7 +413,7 @@
     return call(
         functools.partial(
             attend_kernel,
-            key_tiles,
+            segments,
             len(blocks),
             running is not None,
             ending is not None,
@@ -439,7 +423,6 @@
         [SMEM] * 2 + [VMEM] * (len(args) - 2),
         args,
         "attend",
-        flops=8 * row_count * columns * len(key_tiles) * TILE,
         scratch_shapes=scratch,
     )
 
@@ -466,11 +449,10 @@
         [VMEM, ANY],
         (codes, after),
         "unpack_out",
-        flops=2000 * words * columns,
-    )
-
-
-def out_kernel(first, rotated_ref, weights_ref, scale_ref, after_ref, send_ref, keep_ref):
+    )
+
+
+def out_kernel(first, rotated_ref, weights_ref, scale_ref, send_ref, keep_ref):
     rows = rotated_ref[...]
     fix = row_correction([rows], OUT_ORDER)
     half, columns = send_ref.shape
@@ -486,16 +468,15 @@
             keep_ref[:, at + lane : at + lane + HAD] = done[half:]
 
 
-def out_project(rotated, weights, scale_rows, after, first, columns):
+def out_project(rotated, weights, scale_rows, first, columns):
     row_count, inner = rotated.shape
     result = shape_of((row_count // 2, columns), bf16)
     return call(
         functools.partial(out_kernel, first),
         (result, result),
-        [VMEM] * 3 + [ANY],
-        (rotated, weights, scale_rows, after),
+        [VMEM] * 3,
+        (rotated, weights, scale_rows),
         "out_project",
-        flops=2 * row_count * inner * columns,
     )
 
 
@@ -529,7 +510,6 @@
         in_specs,
         args,
         "finish",
-        flops=4 * share * columns * HAD,
         out_specs=ANY,
         scratch_shapes=[pltpu.VMEM((share, columns), bf16), pltpu.SemaphoreType.DMA],
         input_output_aliases=aliases,
@@ -559,7 +539,7 @@
     return tuple(flips)
 
 
-CHUNKS = (2048, 3072)
+CHUNKS = (3072, 2048)
 
 
 def on_device(
@@ -579,11 +559,11 @@
     row_place = lax.axis_index("height")
     head_place = lax.axis_index("head").astype(jnp.int32)
     top = head_count // 2
-    end = jnp.where(head_place >= top, 0, 2).astype(jnp.int32)
-    place = jnp.stack([head_place, end, row_place.astype(jnp.int32)])
+    place = jnp.stack([head_place, row_place.astype(jnp.int32)])
     low_bits = [1 << b for b in range(top.bit_length() - 1)]
 
     own, early = turn(place, tokens[0], in_sign)
+    half_rows = early.shape[0]
     early = swap(early, top)
     near = {0: own}
     for bit in low_bits:
@@ -595,39 +575,36 @@
     sums, words, late = prepare(
         place, near_flips, far_flips, [near[flip] for flip in near_flips], codes
     )
-    out_weights = unpack_out(out_codes, sums)
-    late = {top: swap(late, top)}
-    early = {top: tie(early, sums, out_weights)}
-    for bit in low_bits:
-        for flip in list(early):
-            early[flip ^ bit] = swap(early[flip], bit)
-    early = [early[flip] for flip in far_flips]
+    late = swap(late, top)
     swaps = row_swaps(row_tiles)
     ending = [qkv_scale, qkv_sign]
     every = tuple(range(len(far_flips)))
-    partial = project((1, 2), 0, [early[:-1]], every[:-1], sums, words, None)
-    key_values = [project((1, 2), 0, [early[-1:]], every[-1:], partial, words, ending)]
-    early_blocks = [lax.ppermute(key_values[0], "height", pairs) for _, _, pairs in swaps]
-    for bit in low_bits:
-        for flip in list(late):
-            late[flip ^ bit] = swap(late[flip], bit)
-    late = [late[flip] for flip in far_flips]
-    key_values.append(project((1, 2), EARLY, [late], every, sums, words, ending))
-    late_blocks = [lax.ppermute(key_values[1], "height", pairs) for _, _, pairs in swaps]
-    queries = project((0,), 0, [early, late], every, sums, words, ending)
+    halves, key_values, moved = [], [], []
+    for half, first_row in ((early, 0), (late, half_rows)):
+        shards = {top: tie(half, *key_values, sums)}
+        for bit in low_bits:
+            for flip in list(shards):
+                shards[flip ^ bit] = swap(shards[flip], bit)
+        shards = [shards[flip] for flip in far_flips]
+        halves.append(shards)
+        partial = project((1, 2), first_row, [shards[:-1]], every[:-1], sums, words, None)
+        key_values.append(project((1, 2), 0, [shards[-1:]], every[-1:], partial, words, ending))
+        moved.append([lax.ppermute(key_values[-1], "height", pairs) for _, _, pairs in swaps])
+    queries = project((0,), 0, halves, every, sums, words, ending)
+    out_weights = unpack_out(out_codes, key_values[1])
 
     listed = windows[0]
-    own_tiles = tuple((None, position) for position in range(WTILES))
-    early_tiles = tuple(((by, odd), position) for by, odd, _ in swaps for position in (0, 1))
-    late_tiles = tuple(((by, odd), 2) for by, odd, _ in swaps)
-    running = attend(place, listed, queries, key_values, own_tiles, None, None)
-    running = attend(place, listed, queries, early_blocks, early_tiles, running, None)
+    own_rows = ((None, 0, half_rows), (None, half_rows, half_rows))
+    early_rows = tuple(((by, odd), 0, half_rows) for by, odd, _ in swaps)
+    late_rows = tuple(((by, odd), half_rows, half_rows) for by, odd, _ in swaps)
+    running = attend(place, listed, queries, key_values, own_rows, None, None)
+    running = attend(place, listed, queries, moved[0], early_rows, running, None)
     rotated = attend(
         place,
         listed,
         queries,
-        late_blocks,
-        late_tiles,
+        moved[1],
+        late_rows,
         running,
         (oin_sign, halving_order(head_count)),
     )
@@ -637,10 +614,8 @@
     sign_rows = out_sign.reshape(-1, HAD)
     result = None
     first = 0
-    send = rotated
     for columns in CHUNKS:
-        send, keep = out_project(rotated, out_weights, scale_rows, send, first, columns)
-        part = send
+        part, keep = out_project(rotated, out_weights, scale_rows, first, columns)
         for bit in bits:
             more = swap(part, bit)
             if bit == top:
@@ -648,7 +623,6 @@
             total = keep.astype(f32) + more.astype(f32)
             half = total.shape[0] // 2
             part, keep = total[:half].astype(bf16), total[half:]
-        send = part
         result = finish(result, sign_rows, keep, more, first)
         first += columns
     return result[None]

time: 58.5 us -> 57.1 us (0.976)
  the two profiles are of different devices: /device:TPU:16 before, /device:TPU:0 now
where the time goes in v2:
time: 57.1 us; the launch traced here: 56 us
  Pallas kernels  23 us (40%)
  waiting for transfers between devices  16.6 us (29%)
  starting transfers between devices  15.4 us (27%)
    pallas_call x17, Pallas kernels, call(): pl.pallas_call(body, out_shape=out_shape, in_specs=in_specs, out_specs=ou...  23 us
    ppermute x9, waiting for transfers between devices, swap(): return lax.ppermute(shard, 'head', [(i, i ^ bit) for i in range(peers)])  15.9 us
    ppermute x4, starting transfers between devices, on_device(): lax.ppermute(key_values[-1], 'height', pairs)  7.8 us
    ppermute x9, starting transfers between devices, swap(): return lax.ppermute(shard, 'head', [(i, i ^ bit) for i in range(peers)])  7.62 us
  transfers between devices with their start and end apart: 13, of which 6 were waited for; matrix products, arithmetic and copies ran while one was open for 1% of the time, Pallas kernels for 32%

profile of v2, /device:TPU:0, one launch (start us, length us, event | category | flops | bytes accessed | tf_op | source)
XLA Modules:
  0.0 56.0 jit_solution(11963551541021753038)
XLA Ops:
  0.1 1.9 %turn.1 = (bf16[192,1280]{1,0:T(8,128)(2,1)S(1)}, bf16[96,1280]{1,0:T(8,128)(2,1)S(1)}) custom-call(s32[2]{0:T(128)S(1)} %pad_add_fusion.place_ref, bf16[192,1280]{1,0:T(8,128)(2,1)} %bitcast.21, s32[40,128]{1,0:T(8,128)} %bitcast.22), custom_call_target="tpu_custom_call" | custom-call | flops 1 | bytes 1 | tf_op jit(solution)/shard_map/turn/pallas_call | solution.py:43
  2.5 2.6 %collective-permute-start = (bf16[96,1280]{1,0:T(8,128)(2,1)S(1)}, bf16[96,1280]{1,0:T(8,128)(2,1)S(1)}, u32[]{:S(2)}, u32[]{:S(2)}) collective-permute-start(bf16[96,1280]{1,0:T(8,128)(2,1)S(1)} %get-tuple-element.14), channel_id=1, source_target_pairs={{0,2},{1,3},{2,0},{3,1},{4,6},{5,7},{6,4},{7,5},{8,10},{9,11},{10,... | collective-permute-start | bytes 737288 | tf_op jit(solution)/shard_map/ppermute | solution.py:521
  5.0 5.0 %prepare.1 = (f32[3,192,768]{2,1,0:T(8,128)S(1)}, s32[2,3,160,768]{3,2,1,0:T(8,128)S(1)}, bf16[96,1280]{1,0:T(8,128)(2,1)S(1)}) custom-call(s32[2]{0:T(128)S(1)} %pad_add_fusion.place_ref, bf16[192,1280]{1,0:T(8,128)(2,1)S(1)} %get-tuple-element.15.rest_0_, bf16[192,1280]{1,0:T(8,128)(2,1)S(1)} %collective-permute-done.1.rest_1_, s32[3,640,768]{2,1,0:T(8,128)} %bitcast.20), custom_call_target="tpu_custom_call" | custom-call | flops 1 | bytes 1 | tf_op jit(solution)/shard_map/prepare/pallas_call | solution.py:43
  10.1 1.5 %collective-permute-done.refs_0_ = bf16[96,1280]{1,0:T(8,128)(2,1)S(1)} collective-permute-done((bf16[96,1280]{1,0:T(8,128)(2,1)S(1)}, bf16[96,1280]{1,0:T(8,128)(2,1)S(1)}, u32[]{:S(2)}, u32[]{:S(2)}) %collective-permute-start) | collective-permute-done | bytes 245792 | tf_op jit(solution)/shard_map/ppermute | solution.py:521
  11.6 1.8 %collective-permute-start.3 = (bf16[96,1280]{1,0:T(8,128)(2,1)S(1)}, bf16[96,1280]{1,0:T(8,128)(2,1)S(1)}, u32[]{:S(2)}, u32[]{:S(2)}) collective-permute-start(bf16[96,1280]{1,0:T(8,128)(2,1)S(1)} %get-tuple-element.17), channel_id=1, source_target_pairs={{0,2},{1,3},{2,0},{3,1},{4,6},{5,7},{6,4},{7,5},{8,10},{9,11},{10,... | collective-permute-start | bytes 737288 | tf_op jit(solution)/shard_map/ppermute | solution.py:521
  13.4 1.2 %project.5.rest_1_ = f32[2,96,768]{2,1,0:T(8,128)S(1)} custom-call(bf16[96,1280]{1,0:T(8,128)(2,1)S(1)} %tie.2.rest_0_, f32[3,192,768]{2,1,0:T(8,128)S(1)} %get-tuple-element.16.refs_1_.rest_1_.refs_2_.rest_4_, s32[2,3,160,768]{3,2,1,0:T(8,128)S(1)} %get-tuple-element.18.rest_2_.rest_5_), custom_call_target="tpu_custom_call" | custom-call | flops 1 | bytes 1 | tf_op jit(solution)/shard_map/project/pallas_call | solution.py:43
  14.6 1.5 %project.6.refs_1_.rest_0_ = bf16[2,96,768]{2,1,0:T(8,128)(2,1)S(1)} custom-call(bf16[96,1280]{1,0:T(8,128)(2,1)S(1)} %collective-permute-done.2.rest_0_.rest_1_, f32[2,96,768]{2,1,0:T(8,128)S(1)} %project.5.rest_1_, s32[2,3,160,768]{3,2,1,0:T(8,128)S(1)} %get-tuple-element.18.rest_2_.rest_5_, f32[3,768]{1,0:T(4,128)S(1)} %copy-done.1, s32[3,768]{1,0:T(4,128)S(1)} %copy-done.2), custom_call_target="tpu_custom_call" | custom-call | flops 1 | bytes 1 | tf_op jit(solution)/shard_map/project/pallas_call | solution.py:43
  16.1 3.9 %collective-permute-done.3.refs_0_ = bf16[96,1280]{1,0:T(8,128)(2,1)S(1)} collective-permute-done((bf16[96,1280]{1,0:T(8,128)(2,1)S(1)}, bf16[96,1280]{1,0:T(8,128)(2,1)S(1)}, u32[]{:S(2)}, u32[]{:S(2)}) %collective-permute-start.3) | collective-permute-done | bytes 245792 | tf_op jit(solution)/shard_map/ppermute | solution.py:521
  20.0 1.8 %collective-permute-start.7 = (bf16[2,96,768]{2,1,0:T(8,128)(2,1)S(1)}, bf16[2,96,768]{2,1,0:T(8,128)(2,1)S(1)}, u32[]{:S(2)}, u32[]{:S(2)}) collective-permute-start(bf16[2,96,768]{2,1,0:T(8,128)(2,1)S(1)} %project.6.refs_1_.rest_0_), channel_id=1, source_target_pairs={{0,4},{8,12},{4,0},{12,8},{1,5},{9,13},{5,1},{13,9},{2,6},{10,14},... | collective-permute-start | bytes 884744 | tf_op jit(solution)/shard_map/ppermute | solution.py:592
  22.5 1.2 %project.8.rest_1_ = f32[2,96,768]{2,1,0:T(8,128)S(1)} custom-call(bf16[96,1280]{1,0:T(8,128)(2,1)S(1)} %tie.3.rest_2_.rest_0_, f32[3,192,768]{2,1,0:T(8,128)S(1)} %get-tuple-element.16.refs_1_.rest_1_.refs_2_.rest_4_, s32[2,3,160,768]{3,2,1,0:T(8,128)S(1)} %get-tuple-element.18.rest_2_.rest_5_), custom_call_target="tpu_custom_call" | custom-call | flops 1 | bytes 1 | tf_op jit(solution)/shard_map/project/pallas_call | solution.py:43
  23.7 1.5 %project.9.rest_1_.after_ref = bf16[2,96,768]{2,1,0:T(8,128)(2,1)S(1)} custom-call(bf16[96,1280]{1,0:T(8,128)(2,1)S(1)} %collective-permute-done.4.rest_3_.rest_0_, f32[2,96,768]{2,1,0:T(8,128)S(1)} %project.8.rest_1_, s32[2,3,160,768]{3,2,1,0:T(8,128)S(1)} %get-tuple-element.18.rest_2_.rest_5_, f32[3,768]{1,0:T(4,128)S(1)} %copy-done.1, s32[3,768]{1,0:T(4,128)S(1)} %copy-done.2), custom_call_target="tpu_custom_call" | custom-call | flops 1 | bytes 1 | tf_op jit(solution)/shard_map/project/pallas_call | solution.py:43
  25.2 4.4 %collective-permute-start.5 = (bf16[2,96,768]{2,1,0:T(8,128)(2,1)S(1)}, bf16[2,96,768]{2,1,0:T(8,128)(2,1)S(1)}, u32[]{:S(2)}, u32[]{:S(2)}) collective-permute-start(bf16[2,96,768]{2,1,0:T(8,128)(2,1)S(1)} %project.9.rest_1_.after_ref), channel_id=1, source_target_pairs={{0,4},{8,12},{4,0},{12,8},{1,5},{9,13},{5,1},{13,9},{2,6},{10,14},... | collective-permute-start | bytes 884744 | tf_op jit(solution)/shard_map/ppermute | solution.py:592
  29.6 0.8 %collective-permute-start.6 = (bf16[2,96,768]{2,1,0:T(8,128)(2,1)S(1)}, bf16[2,96,768]{2,1,0:T(8,128)(2,1)S(1)}, u32[]{:S(2)}, u32[]{:S(2)}) collective-permute-start(bf16[2,96,768]{2,1,0:T(8,128)(2,1)S(1)} %project.9.rest_1_.after_ref), channel_id=1, source_target_pairs={{4,8},{8,4},{5,9},{9,5},{6,10},{10,6},{7,11},{11,7},{20,24},{24,20... | collective-permute-start | bytes 884744 | tf_op jit(solution)/shard_map/ppermute | solution.py:592
  30.5 1.5 %unpack_out.1.weights_ref = bf16[768,5120]{1,0:T(8,128)(2,1)S(1)} custom-call(s32[96,5120]{1,0:T(8,128)S(1)} %copy-done, bf16[2,96,768]{2,1,0:T(8,128)(2,1)S(1)} %project.9.rest_1_.after_ref), custom_call_target="tpu_custom_call" | custom-call | flops 1 | bytes 1 | tf_op jit(solution)/shard_map/unpack_out/pallas_call | solution.py:43
  32.0 1.8 %project.7.q_ref = bf16[1,192,768]{2,1,0:T(8,128)(2,1)S(1)} custom-call(bf16[96,1280]{1,0:T(8,128)(2,1)S(1)} %tie.2.rest_0_, bf16[96,1280]{1,0:T(8,128)(2,1)S(1)} %collective-permute-done.2.rest_0_.rest_1_, bf16[96,1280]{1,0:T(8,128)(2,1)S(1)} %tie.3.rest_2_.rest_0_, bf16[96,1280]{1,0:T(8,128)(2,1)S(1)} %collective-permute-done.4.rest_3_.rest_0_, ...), custom_call_target="tpu_custom_call" | custom-call | flops 1 | bytes 1 | tf_op jit(solution)/shard_map/project/pallas_call | solution.py:43
  33.8 1.1 %attend.3.rest_2_ = f32[6,192,256]{2,1,0:T(8,128)S(1)} custom-call(s32[2]{0:T(128)S(1)} %pad_add_fusion.place_ref, s32[3,27]{1,0:T(4,128)S(1)} %bitcast.16, bf16[1,192,768]{2,1,0:T(8,128)(2,1)S(1)} %project.7.q_ref, bf16[2,96,768]{2,1,0:T(8,128)(2,1)S(1)} %project.6.refs_1_.rest_0_, bf16[2,96,768]{2,1,0:T(8,128)(2,1)S(1)} %project.9.rest_1_.after_ref), custom_call_target="tpu_custom_call" | custom-call | flops 1 | bytes 1 | tf_op jit(solution)/shard_map/attend/pallas_call | solution.py:43
  35.0 1.1 %attend.4.rest_2_ = f32[6,192,256]{2,1,0:T(8,128)S(1)} custom-call(s32[2]{0:T(128)S(1)} %pad_add_fusion.place_ref, s32[3,27]{1,0:T(4,128)S(1)} %bitcast.17, bf16[1,192,768]{2,1,0:T(8,128)(2,1)S(1)} %project.7.q_ref, bf16[2,96,768]{2,1,0:T(8,128)(2,1)S(1)} %collective-permute-done.7.rest_0_, bf16[2,96,768]{2,1,0:T(8,128)(2,1)S(1)} %collective-permute-done.8.rest_1_, ...), custom_call_target="tpu_custom_call" | custom-call | flops 1 | bytes 1 | tf_op jit(solution)/shard_map/attend/pallas_call | solution.py:43
  36.8 1.3 %attend.5.rotated_ref = bf16[192,768]{1,0:T(8,128)(2,1)S(1)} custom-call(s32[2]{0:T(128)S(1)} %pad_add_fusion.place_ref, s32[3,27]{1,0:T(4,128)S(1)} %bitcast.18, bf16[1,192,768]{2,1,0:T(8,128)(2,1)S(1)} %project.7.q_ref, bf16[2,96,768]{2,1,0:T(8,128)(2,1)S(1)} %collective-permute-done.5.rest_0_, bf16[2,96,768]{2,1,0:T(8,128)(2,1)S(1)} %collective-permute-done.6.rest_1_, ...), custom_call_target="tpu_custom_call" | custom-call | flops 1 | bytes 1 | tf_op jit(solution)/shard_map/attend/pallas_call | solution.py:43
  38.1 1.1 %out_project.3 = (bf16[96,3072]{1,0:T(8,128)(2,1)S(1)}, bf16[96,3072]{1,0:T(8,128)(2,1)S(1)}) custom-call(bf16[192,768]{1,0:T(8,128)(2,1)S(1)} %attend.5.rotated_ref, bf16[768,5120]{1,0:T(8,128)(2,1)S(1)} %unpack_out.1.weights_ref, f32[40,128]{1,0:T(8,128)S(1)} %bitcast.12), custom_call_target="tpu_custom_call" | custom-call | flops 1 | bytes 1 | tf_op jit(solution)/shard_map/out_project/pallas_call | solution.py:43
  41.5 1.6 %collective-permute-start.12 = (bf16[48,3072]{1,0:T(8,128)(2,1)S(1)}, bf16[48,3072]{1,0:T(8,128)(2,1)S(1)}, u32[]{:S(2)}, u32[]{:S(2)}) collective-permute-start(bf16[48,3072]{1,0:T(8,128)(2,1)S(1)} %slice.24), channel_id=1, source_target_pairs={{0,2},{1,3},{2,0},{3,1},{4,6},{5,7},{6,4},{7,5},{8,10},{9,11},{10,... | collective-permute-start | bytes 884744 | tf_op jit(solution)/shard_map/ppermute | solution.py:521
  43.9 7.5 %collective-permute-done.12.more_ref = bf16[48,3072]{1,0:T(8,128)(2,1)S(1)} collective-permute-done((bf16[48,3072]{1,0:T(8,128)(2,1)S(1)}, bf16[48,3072]{1,0:T(8,128)(2,1)S(1)}, u32[]{:S(2)}, u32[]{:S(2)}) %collective-permute-start.12) | collective-permute-done | bytes 294944 | tf_op jit(solution)/shard_map/ppermute | solution.py:521
  51.4 1.1 %finish.2.rest_0_ = bf16[48,5120]{1,0:T(8,128)(2,1)} custom-call(s32[40,128]{1,0:T(8,128)S(1)} %bitcast.14, f32[48,3072]{1,0:T(8,128)S(1)} %slice.20.keep_ref, bf16[48,3072]{1,0:T(8,128)(2,1)S(1)} %collective-permute-done.12.more_ref), custom_call_target="tpu_custom_call" | custom-call | flops 1 | bytes 1 | tf_op jit(solution)/shard_map/finish/pallas_call | solution.py:43
  52.5 2.3 %collective-permute-done.10.more_ref = bf16[48,2048]{1,0:T(8,128)(2,1)S(1)} collective-permute-done((bf16[48,2048]{1,0:T(8,128)(2,1)S(1)}, bf16[48,2048]{1,0:T(8,128)(2,1)S(1)}, u32[]{:S(2)}, u32[]{:S(2)}) %collective-permute-start.10) | collective-permute-done | bytes 196640 | tf_op jit(solution)/shard_map/ppermute | solution.py:521
  54.8 1.0 %finish.3 = bf16[48,5120]{1,0:T(8,128)(2,1)} custom-call(s32[40,128]{1,0:T(8,128)S(1)} %bitcast.15, f32[48,2048]{1,0:T(8,128)S(1)} %slice.18.keep_ref, bf16[48,2048]{1,0:T(8,128)(2,1)S(1)} %collective-permute-done.10.more_ref, bf16[48,5120]{1,0:T(8,128)(2,1)} %finish.2.rest_0_), custom_call_target="tpu_custom_call", output_to_operand_aliasing={{}: (3, {})} | custom-call | flops 1 | bytes 1 | tf_op jit(solution)/shard_map/finish/pallas_call | solution.py:43
  (41 shorter events, 5.0 us)
Async XLA Ops:
  2.0 3.1 %collective-permute-start.1 = (bf16[192,1280]{1,0:T(8,128)(2,1)S(1)}, bf16[192,1280]{1,0:T(8,128)(2,1)S(1)}, u32[]{:S(2)}, u32[]{:S(2)}) collective-permute-start(bf16[192,1280]{1,0:T(8,128)(2,1)S(1)} %get-tuple-element.15.rest_0_), channel_id=1, source_target_pairs={{0,1},{1,0},{2,3},{3,2},{4,5},{5,4},{6,7},{7,6},{8,9},{9,8},{10,11... | collective-permute-start | bytes 1474568 | tf_op jit(solution)/shard_map/ppermute | solution.py:521
  2.5 9.1 %collective-permute-start = (bf16[96,1280]{1,0:T(8,128)(2,1)S(1)}, bf16[96,1280]{1,0:T(8,128)(2,1)S(1)}, u32[]{:S(2)}, u32[]{:S(2)}) collective-permute-start(bf16[96,1280]{1,0:T(8,128)(2,1)S(1)} %get-tuple-element.14), channel_id=1, source_target_pairs={{0,2},{1,3},{2,0},{3,1},{4,6},{5,7},{6,4},{7,5},{8,10},{9,11},{10,... | collective-permute-start | bytes 737288 | tf_op jit(solution)/shard_map/ppermute | solution.py:521
  11.6 3.0 %collective-permute-start.2 = (bf16[96,1280]{1,0:T(8,128)(2,1)S(1)}, bf16[96,1280]{1,0:T(8,128)(2,1)S(1)}, u32[]{:S(2)}, u32[]{:S(2)}) collective-permute-start(bf16[96,1280]{1,0:T(8,128)(2,1)S(1)} %tie.2.rest_0_), channel_id=1, source_target_pairs={{0,1},{1,0},{2,3},{3,2},{4,5},{5,4},{6,7},{7,6},{8,9},{9,8},{10,11... | collective-permute-start | bytes 737288 | tf_op jit(solution)/shard_map/ppermute | solution.py:521
  11.6 8.4 %collective-permute-start.3 = (bf16[96,1280]{1,0:T(8,128)(2,1)S(1)}, bf16[96,1280]{1,0:T(8,128)(2,1)S(1)}, u32[]{:S(2)}, u32[]{:S(2)}) collective-permute-start(bf16[96,1280]{1,0:T(8,128)(2,1)S(1)} %get-tuple-element.17), channel_id=1, source_target_pairs={{0,2},{1,3},{2,0},{3,1},{4,6},{5,7},{6,4},{7,5},{8,10},{9,11},{10,... | collective-permute-start | bytes 737288 | tf_op jit(solution)/shard_map/ppermute | solution.py:521
  13.4 1.2 %copy-start.1 = (f32[3,768]{1,0:T(4,128)S(1)}, f32[3,768]{1,0:T(4,128)}, u32[]{:S(2)}) copy-start(f32[3,768]{1,0:T(4,128)} %rest_3_.3) | copy-start | bytes 27652
  13.4 1.2 %copy-start.2 = (s32[3,768]{1,0:T(4,128)S(1)}, s32[3,768]{1,0:T(4,128)}, u32[]{:S(2)}) copy-start(s32[3,768]{1,0:T(4,128)} %rest_4_.3) | copy-start | bytes 27652
  20.0 3.7 %collective-permute-start.4 = (bf16[96,1280]{1,0:T(8,128)(2,1)S(1)}, bf16[96,1280]{1,0:T(8,128)(2,1)S(1)}, u32[]{:S(2)}, u32[]{:S(2)}) collective-permute-start(bf16[96,1280]{1,0:T(8,128)(2,1)S(1)} %tie.3.rest_2_.rest_0_), channel_id=1, source_target_pairs={{0,1},{1,0},{2,3},{3,2},{4,5},{5,4},{6,7},{7,6},{8,9},{9,8},{10,11... | collective-permute-start | bytes 737288 | tf_op jit(solution)/shard_map/ppermute | solution.py:521
  20.0 15.0 %collective-permute-start.7 = (bf16[2,96,768]{2,1,0:T(8,128)(2,1)S(1)}, bf16[2,96,768]{2,1,0:T(8,128)(2,1)S(1)}, u32[]{:S(2)}, u32[]{:S(2)}) collective-permute-start(bf16[2,96,768]{2,1,0:T(8,128)(2,1)S(1)} %project.6.refs_1_.rest_0_), channel_id=1, source_target_pairs={{0,4},{8,12},{4,0},{12,8},{1,5},{9,13},{5,1},{13,9},{2,6},{10,14},... | collective-permute-start | bytes 884744 | tf_op jit(solution)/shard_map/ppermute | solution.py:592
  21.8 13.1 %collective-permute-start.8 = (bf16[2,96,768]{2,1,0:T(8,128)(2,1)S(1)}, bf16[2,96,768]{2,1,0:T(8,128)(2,1)S(1)}, u32[]{:S(2)}, u32[]{:S(2)}) collective-permute-start(bf16[2,96,768]{2,1,0:T(8,128)(2,1)S(1)} %project.6.refs_1_.rest_0_), channel_id=1, source_target_pairs={{4,8},{8,4},{5,9},{9,5},{6,10},{10,6},{7,11},{11,7},{20,24},{24,20... | collective-permute-start | bytes 884744 | tf_op jit(solution)/shard_map/ppermute | solution.py:592
  23.7 6.8 %copy-start.6 = (s32[1,3,27]{2,0,1:T(1,128)S(1)}, s32[1,3,27]{2,0,1:T(1,128)}, u32[]{:S(2)}) copy-start(s32[1,3,27]{2,0,1:T(1,128)} %param.15) | copy-start | bytes 976
  23.7 6.8 %copy-start = (s32[96,5120]{1,0:T(8,128)S(1)}, s32[96,5120]{1,0:T(8,128)}, u32[]{:S(2)}) copy-start(s32[96,5120]{1,0:T(8,128)} %codes_ref.1) | copy-start | bytes 5898244
  25.2 11.6 %collective-permute-start.5 = (bf16[2,96,768]{2,1,0:T(8,128)(2,1)S(1)}, bf16[2,96,768]{2,1,0:T(8,128)(2,1)S(1)}, u32[]{:S(2)}, u32[]{:S(2)}) collective-permute-start(bf16[2,96,768]{2,1,0:T(8,128)(2,1)S(1)} %project.9.rest_1_.after_ref), channel_id=1, source_target_pairs={{0,4},{8,12},{4,0},{12,8},{1,5},{9,13},{5,1},{13,9},{2,6},{10,14},... | collective-permute-start | bytes 884744 | tf_op jit(solution)/shard_map/ppermute | solution.py:592
  29.6 7.1 %collective-permute-start.6 = (bf16[2,96,768]{2,1,0:T(8,128)(2,1)S(1)}, bf16[2,96,768]{2,1,0:T(8,128)(2,1)S(1)}, u32[]{:S(2)}, u32[]{:S(2)}) collective-permute-start(bf16[2,96,768]{2,1,0:T(8,128)(2,1)S(1)} %project.9.rest_1_.after_ref), channel_id=1, source_target_pairs={{4,8},{8,4},{5,9},{9,5},{6,10},{10,6},{7,11},{11,7},{20,24},{24,20... | collective-permute-start | bytes 884744 | tf_op jit(solution)/shard_map/ppermute | solution.py:592
  34.9 1.8 %copy-start.5 = (s32[768]{0:T(1024)S(1)}, s32[768]{0:T(1024)}, u32[]{:S(2)}) copy-start(s32[768]{0:T(1024)} %param.16) | copy-start | bytes 9220
  36.8 1.3 %copy-start.3 = (f32[5120]{0:T(1024)S(1)}, f32[5120]{0:T(1024)}, u32[]{:S(2)}) copy-start(f32[5120]{0:T(1024)} %param.18) | copy-start | bytes 61444
  39.2 2.1 %collective-permute-start.11 = (bf16[96,3072]{1,0:T(8,128)(2,1)S(1)}, bf16[96,3072]{1,0:T(8,128)(2,1)S(1)}, u32[]{:S(2)}, u32[]{:S(2)}) collective-permute-start(bf16[96,3072]{1,0:T(8,128)(2,1)S(1)} %get-tuple-element.22), channel_id=1, source_target_pairs={{0,1},{1,0},{2,3},{3,2},{4,5},{5,4},{6,7},{7,6},{8,9},{9,8},{10,11... | collective-permute-start | bytes 1769480 | tf_op jit(solution)/shard_map/ppermute | solution.py:521
  40.1 2.9 %collective-permute-start.9 = (bf16[96,2048]{1,0:T(8,128)(2,1)S(1)}, bf16[96,2048]{1,0:T(8,128)(2,1)S(1)}, u32[]{:S(2)}, u32[]{:S(2)}) collective-permute-start(bf16[96,2048]{1,0:T(8,128)(2,1)S(1)} %get-tuple-element.20), channel_id=1, source_target_pairs={{0,1},{1,0},{2,3},{3,2},{4,5},{5,4},{6,7},{7,6},{8,9},{9,8},{10,11... | collective-permute-start | bytes 1179656 | tf_op jit(solution)/shard_map/ppermute | solution.py:521
  41.5 9.9 %collective-permute-start.12 = (bf16[48,3072]{1,0:T(8,128)(2,1)S(1)}, bf16[48,3072]{1,0:T(8,128)(2,1)S(1)}, u32[]{:S(2)}, u32[]{:S(2)}) collective-permute-start(bf16[48,3072]{1,0:T(8,128)(2,1)S(1)} %slice.24), channel_id=1, source_target_pairs={{0,2},{1,3},{2,0},{3,1},{4,6},{5,7},{6,4},{7,5},{8,10},{9,11},{10,... | collective-permute-start | bytes 884744 | tf_op jit(solution)/shard_map/ppermute | solution.py:521
  43.1 8.3 %copy-start.4 = (s32[5120]{0:T(1024)S(1)}, s32[5120]{0:T(1024)}, u32[]{:S(2)}) copy-start(s32[5120]{0:T(1024)} %param.19) | copy-start | bytes 61444
  43.2 11.6 %collective-permute-start.10 = (bf16[48,2048]{1,0:T(8,128)(2,1)S(1)}, bf16[48,2048]{1,0:T(8,128)(2,1)S(1)}, u32[]{:S(2)}, u32[]{:S(2)}) collective-permute-start(bf16[48,2048]{1,0:T(8,128)(2,1)S(1)} %slice.25), channel_id=1, source_target_pairs={{0,2},{1,3},{2,0},{3,1},{4,6},{5,7},{6,4},{7,5},{8,10},{9,11},{10,... | collective-permute-start | bytes 589832 | tf_op jit(solution)/shard_map/ppermute | solution.py:521

commit v3 on v2

--- a/solution.py
+++ b/solution.py
@@ -37,7 +37,7 @@
     return pltpu.with_memory_space_constraint(array, pltpu.HBM)
 
 
-def call(body, out_shape, in_specs, args, name, out_specs=None, megabytes=16, **more):
+def call(body, out_shape, in_specs, args, name, out_specs=None, megabytes=16, flops=1, **more):
     if out_specs is None:
         out_specs = jax.tree.map(lambda _: VMEM, out_shape)
     return pl.pallas_call(
@@ -46,7 +46,7 @@
         in_specs=in_specs,
         out_specs=out_specs,
         compiler_params=pltpu.CompilerParams(vmem_limit_bytes=megabytes * 2**20),
-        cost_estimate=pl.CostEstimate(flops=1, bytes_accessed=1, transcendentals=0),
+        cost_estimate=pl.CostEstimate(flops=flops, bytes_accessed=1, transcendentals=0),
         name=name,
         **more,
     )(*args)
@@ -257,7 +257,7 @@
     shard_refs = rest[: groups * count]
     sums_ref, words_ref = rest[groups * count : groups * count + 2]
     if ending:
-        scale_ref, sign_ref = rest[-3:-1]
+        scale_ref, sign_ref = rest[groups * count + 2 : groups * count + 4]
     out_ref = rest[-1]
     columns = sums_ref.shape[2]
     width = tile_width(columns)
@@ -305,12 +305,13 @@
             out_ref[place, :, head * HD : (head + 1) * HD] = part.astype(bf16)
 
 
-def project(kinds, first_row, groups, positions, sums, words, ending):
+def project(kinds, first_row, groups, positions, sums, words, ending, flops=1):
     inner = groups[0][0].shape[1]
     columns = sums.shape[2]
     row_count = sum(group[0].shape[0] for group in groups)
     whole = sums.shape[0] == 3
     args = [shard for group in groups for shard in group] + [sums, words]
+    own_args = len(args) + 2
     if ending is not None:
         args += ending
     return call(
@@ -318,9 +319,10 @@
             project_kernel, kinds, first_row, len(groups), positions, whole, ending is not None
         ),
         shape_of((len(kinds), row_count, columns), f32 if ending is None else bf16),
-        [VMEM] * len(args),
+        [VMEM] * min(len(args), own_args) + [ANY] * max(len(args) - own_args, 0),
         args,
         "project",
+        flops=flops,
     )
 
 
@@ -348,15 +350,19 @@
     return jnp.concatenate(masks, 0)
 
 
-def attend_kernel(segments, blocks, has_sum, last, share_order, place_ref, windows_ref, q_ref, *rest):
+def attend_kernel(
+    segments, halves, blocks, has_sum, last, share_order, place_ref, windows_ref, *rest
+):
     rest = list(rest)
+    q_refs = [rest.pop(0) for _ in range(halves)]
     kv_refs = [rest.pop(0) for _ in range(blocks)]
     sum_ref = rest.pop(0) if has_sum else None
     if last:
         oin_ref, out_ref, rotated_ref = rest
     else:
         (out_ref,) = rest
-    row_count, columns = q_ref.shape[1:]
+    columns = q_refs[0].shape[2]
+    row_count = sum(ref.shape[1] for ref in q_refs)
     heads = [slice(head, head + HD) for head in range(0, columns, HD)]
     mask = window_mask(place_ref, windows_ref, segments, row_count)
     scores = []
@@ -364,7 +370,10 @@
         keys = jnp.concatenate([ref[0, :, at] for ref in kv_refs], 0)
         scores.append(
             lax.dot_general(
-                q_ref[0, :, at], keys, (((1,), (1,)), ((), ())), preferred_element_type=f32
+                jnp.concatenate([ref[0, :, at] for ref in q_refs], 0),
+                keys,
+                (((1,), (1,)), ((), ())),
+                preferred_element_type=f32,
             )
         )
     weights = [
@@ -398,8 +407,9 @@
 
 
 def attend(place, windows, queries, blocks, segments, running, ending):
-    row_count, columns = queries.shape[1:]
-    args = [place, windows, queries, *blocks]
+    columns = queries[0].shape[2]
+    row_count = sum(part.shape[1] for part in queries)
+    args = [place, windows, *queries, *blocks]
     if running is not None:
         args.append(running)
     scratch, share_order = [], None
@@ -414,6 +424,7 @@
         functools.partial(
             attend_kernel,
             segments,
+            len(queries),
             len(blocks),
             running is not None,
             ending is not None,
@@ -539,7 +550,7 @@
     return tuple(flips)
 
 
-CHUNKS = (3072, 2048)
+CHUNKS = (2048, 1792, 1280)
 
 
 def on_device(
@@ -579,18 +590,20 @@
     swaps = row_swaps(row_tiles)
     ending = [qkv_scale, qkv_sign]
     every = tuple(range(len(far_flips)))
-    halves, key_values, moved = [], [], []
+    key_values, moved, queries = [], [], []
     for half, first_row in ((early, 0), (late, half_rows)):
-        shards = {top: tie(half, *key_values, sums)}
+        shards = {top: tie(half, *queries, sums)}
         for bit in low_bits:
             for flip in list(shards):
                 shards[flip ^ bit] = swap(shards[flip], bit)
         shards = [shards[flip] for flip in far_flips]
-        halves.append(shards)
-        partial = project((1, 2), first_row, [shards[:-1]], every[:-1], sums, words, None)
-        key_values.append(project((1, 2), 0, [shards[-1:]], every[-1:], partial, words, ending))
-        moved.append([lax.ppermute(key_values[-1], "height", pairs) for _, _, pairs in swaps])
-    queries = project((0,), 0, halves, every, sums, words, ending)
+        partial = project((1, 2), first_row, [shards[:-1]], every[:-1], sums, words, None, 4 * 10**9)
+        key_value = project((1, 2), 0, [shards[-1:]], every[-1:], partial, words, ending)
+        moved.append([lax.ppermute(key_value, "height", pairs) for _, _, pairs in swaps])
+        key_values.append(key_value)
+        queries.append(
+            project((0,), first_row, [shards], every, sums, words, ending + [key_value], 4 * 10**9)
+        )
     out_weights = unpack_out(out_codes, key_values[1])
 
     listed = windows[0]

time: 57.1 us -> 54.6 us (0.956)
  waiting for transfers between devices: 16.6 us -> 11.2 us
  Pallas kernels: 23 us -> 25.1 us
  local copies, waits for them, and re-layouts: 0.16 us -> 0.84 us
    ppermute x9 -> x11, waiting for transfers between devices: 15.9 us -> 9.83 us  [swap(): return lax.ppermute(shard, 'head', [(i, i ^ bit) for i in range(peers)])]
    pallas_call x17 -> x20, Pallas kernels: 23 us -> 25.1 us  [call(): pl.pallas_call(body, out_shape=out_shape, in_specs=in_specs, out_specs=ou...]
    ppermute x9 -> x11, starting transfers between devices: 7.62 us -> 8.3 us  [swap(): return lax.ppermute(shard, 'head', [(i, i ^ bit) for i in range(peers)])]
    unnamed x15 -> x13, local copies, waits for them, and re-layouts: 0.04 us -> 0.71 us
    ppermute x4, waiting for transfers between devices: 0.69 us -> 1.34 us  [on_device(): lax.ppermute(key_value, 'height', pairs)]
  transfers between devices with their start and end apart: 13 -> 15, of which waited for: 6 -> 7; matrix products, arithmetic and copies ran while one was open for 1% -> 2% of each run, Pallas kernels for 32% -> 38%
where the time goes in v3:
time: 54.6 us; the launch traced here: 53.8 us
  Pallas kernels  25.1 us (46%)
  starting transfers between devices  15.9 us (29%)
  waiting for transfers between devices  11.2 us (21%)
  local copies, waits for them, and re-layouts  0.84 us (2%)
    pallas_call x20, Pallas kernels, call(): pl.pallas_call(body, out_shape=out_shape, in_specs=in_specs, out_specs=ou...  25.1 us
    ppermute x11, waiting for transfers between devices, swap(): return lax.ppermute(shard, 'head', [(i, i ^ bit) for i in range(peers)])  9.83 us
    ppermute x11, starting transfers between devices, swap(): return lax.ppermute(shard, 'head', [(i, i ^ bit) for i in range(peers)])  8.3 us
    ppermute x4, starting transfers between devices, on_device(): lax.ppermute(key_value, 'height', pairs)  7.58 us
    ppermute x4, waiting for transfers between devices, on_device(): lax.ppermute(key_value, 'height', pairs)  1.34 us
  transfers between devices with their start and end apart: 15, of which 7 were waited for; matrix products, arithmetic and copies ran while one was open for 2% of the time, Pallas kernels for 38%

profile of v3, /device:TPU:0, one launch (start us, length us, event | category | flops | bytes accessed | tf_op | source)
XLA Modules:
  0.0 53.8 jit_solution(5839329927315476616)
XLA Ops:
  0.1 1.9 %turn.1 = (bf16[192,1280]{1,0:T(8,128)(2,1)S(1)}, bf16[96,1280]{1,0:T(8,128)(2,1)S(1)}) custom-call(s32[2]{0:T(128)S(1)} %pad_add_fusion.place_ref, bf16[192,1280]{1,0:T(8,128)(2,1)} %bitcast.23, s32[40,128]{1,0:T(8,128)} %bitcast.24), custom_call_target="tpu_custom_call" | custom-call | flops 1 | bytes 1 | tf_op jit(solution)/shard_map/turn/pallas_call | solution.py:43
  2.5 2.6 %collective-permute-start = (bf16[96,1280]{1,0:T(8,128)(2,1)S(1)}, bf16[96,1280]{1,0:T(8,128)(2,1)S(1)}, u32[]{:S(2)}, u32[]{:S(2)}) collective-permute-start(bf16[96,1280]{1,0:T(8,128)(2,1)S(1)} %get-tuple-element.16), channel_id=1, source_target_pairs={{0,2},{1,3},{2,0},{3,1},{4,6},{5,7},{6,4},{7,5},{8,10},{9,11},{10,... | collective-permute-start | bytes 737288 | tf_op jit(solution)/shard_map/ppermute | solution.py:532
  5.7 5.0 %prepare.1 = (f32[3,192,768]{2,1,0:T(8,128)S(1)}, s32[2,3,160,768]{3,2,1,0:T(8,128)S(1)}, bf16[96,1280]{1,0:T(8,128)(2,1)S(1)}) custom-call(s32[2]{0:T(128)S(1)} %pad_add_fusion.place_ref, bf16[192,1280]{1,0:T(8,128)(2,1)S(1)} %get-tuple-element.17.rest_0_, bf16[192,1280]{1,0:T(8,128)(2,1)S(1)} %collective-permute-done.1.rest_1_, s32[3,640,768]{2,1,0:T(8,128)} %bitcast.22), custom_call_target="tpu_custom_call" | custom-call | flops 1 | bytes 1 | tf_op jit(solution)/shard_map/prepare/pallas_call | solution.py:43
  11.6 1.8 %collective-permute-start.3 = (bf16[96,1280]{1,0:T(8,128)(2,1)S(1)}, bf16[96,1280]{1,0:T(8,128)(2,1)S(1)}, u32[]{:S(2)}, u32[]{:S(2)}) collective-permute-start(bf16[96,1280]{1,0:T(8,128)(2,1)S(1)} %get-tuple-element.20), channel_id=1, source_target_pairs={{0,2},{1,3},{2,0},{3,1},{4,6},{5,7},{6,4},{7,5},{8,10},{9,11},{10,... | collective-permute-start | bytes 737288 | tf_op jit(solution)/shard_map/ppermute | solution.py:532
  13.4 1.2 %project.6.rest_1_ = f32[2,96,768]{2,1,0:T(8,128)S(1)} custom-call(bf16[96,1280]{1,0:T(8,128)(2,1)S(1)} %tie.2.rest_0_, f32[3,192,768]{2,1,0:T(8,128)S(1)} %get-tuple-element.18.refs_1_.rest_1_.rest_2_.refs_2_, s32[2,3,160,768]{3,2,1,0:T(8,128)S(1)} %get-tuple-element.19.rest_2_.rest_3_), custom_call_target="tpu_custom_call" | custom-call | flops 4000000000 | bytes 1 | tf_op jit(solution)/shard_map/project/pallas_call | solution.py:43
  14.6 1.5 %project.7.rest_6_.rest_2_ = bf16[2,96,768]{2,1,0:T(8,128)(2,1)S(1)} custom-call(bf16[96,1280]{1,0:T(8,128)(2,1)S(1)} %collective-permute-done.2.rest_0_.rest_1_, f32[2,96,768]{2,1,0:T(8,128)S(1)} %project.6.rest_1_, s32[2,3,160,768]{3,2,1,0:T(8,128)S(1)} %get-tuple-element.19.rest_2_.rest_3_, f32[3,768]{1,0:T(4,128)S(1)} %copy-done.3, s32[3,768]{1,0:T(4,128)S(1)} %copy-done.4), custom_call_target="tpu_custom_call" | custom-call | flops 1 | bytes 1 | tf_op jit(solution)/shard_map/project/pallas_call | solution.py:43
  16.1 1.6 %collective-permute-start.7 = (bf16[2,96,768]{2,1,0:T(8,128)(2,1)S(1)}, bf16[2,96,768]{2,1,0:T(8,128)(2,1)S(1)}, u32[]{:S(2)}, u32[]{:S(2)}) collective-permute-start(bf16[2,96,768]{2,1,0:T(8,128)(2,1)S(1)} %project.7.rest_6_.rest_2_), channel_id=1, source_target_pairs={{0,4},{8,12},{4,0},{12,8},{1,5},{9,13},{5,1},{13,9},{2,6},{10,14},... | collective-permute-start | bytes 884744 | tf_op jit(solution)/shard_map/ppermute | solution.py:602
  18.4 1.5 %project.8.refs_1_.rest_0_ = bf16[1,96,768]{2,1,0:T(8,128)(2,1)S(1)} custom-call(bf16[96,1280]{1,0:T(8,128)(2,1)S(1)} %tie.2.rest_0_, bf16[96,1280]{1,0:T(8,128)(2,1)S(1)} %collective-permute-done.2.rest_0_.rest_1_, f32[3,192,768]{2,1,0:T(8,128)S(1)} %get-tuple-element.18.refs_1_.rest_1_.rest_2_.refs_2_, ...), custom_call_target="tpu_custom_call" | custom-call | flops 4000000000 | bytes 1 | tf_op jit(solution)/shard_map/project/pallas_call | solution.py:43
  20.0 1.2 %project.9.rest_1_ = f32[2,96,768]{2,1,0:T(8,128)S(1)} custom-call(bf16[96,1280]{1,0:T(8,128)(2,1)S(1)} %tie.3.rest_0_, f32[3,192,768]{2,1,0:T(8,128)S(1)} %get-tuple-element.18.refs_1_.rest_1_.rest_2_.refs_2_, s32[2,3,160,768]{3,2,1,0:T(8,128)S(1)} %get-tuple-element.19.rest_2_.rest_3_), custom_call_target="tpu_custom_call" | custom-call | flops 4000000000 | bytes 1 | tf_op jit(solution)/shard_map/project/pallas_call | solution.py:43
  21.5 1.5 %project.10.rest_6_.rest_3_.after_ref = bf16[2,96,768]{2,1,0:T(8,128)(2,1)S(1)} custom-call(bf16[96,1280]{1,0:T(8,128)(2,1)S(1)} %collective-permute-done.4.rest_0_.rest_1_, f32[2,96,768]{2,1,0:T(8,128)S(1)} %project.9.rest_1_, s32[2,3,160,768]{3,2,1,0:T(8,128)S(1)} %get-tuple-element.19.rest_2_.rest_3_, f32[3,768]{1,0:T(4,128)S(1)} %copy-done.3, ...), custom_call_target="tpu_custom_call" | custom-call | flops 1 | bytes 1 | tf_op jit(solution)/shard_map/project/pallas_call | solution.py:43
  23.0 4.4 %collective-permute-start.5 = (bf16[2,96,768]{2,1,0:T(8,128)(2,1)S(1)}, bf16[2,96,768]{2,1,0:T(8,128)(2,1)S(1)}, u32[]{:S(2)}, u32[]{:S(2)}) collective-permute-start(bf16[2,96,768]{2,1,0:T(8,128)(2,1)S(1)} %project.10.rest_6_.rest_3_.after_ref), channel_id=1, source_target_pairs={{0,4},{8,12},{4,0},{12,8},{1,5},{9,13},{5,1},{13,9},{2,6},{10,14},... | collective-permute-start | bytes 884744 | tf_op jit(solution)/shard_map/ppermute | solution.py:602
  27.4 0.8 %collective-permute-start.6 = (bf16[2,96,768]{2,1,0:T(8,128)(2,1)S(1)}, bf16[2,96,768]{2,1,0:T(8,128)(2,1)S(1)}, u32[]{:S(2)}, u32[]{:S(2)}) collective-permute-start(bf16[2,96,768]{2,1,0:T(8,128)(2,1)S(1)} %project.10.rest_6_.rest_3_.after_ref), channel_id=1, source_target_pairs={{4,8},{8,4},{5,9},{9,5},{6,10},{10,6},{7,11},{11,7},{20,24},{24,20... | collective-permute-start | bytes 884744 | tf_op jit(solution)/shard_map/ppermute | solution.py:602
  28.3 1.5 %unpack_out.1.weights_ref = bf16[768,5120]{1,0:T(8,128)(2,1)S(1)} custom-call(s32[96,5120]{1,0:T(8,128)S(1)} %copy-done, bf16[2,96,768]{2,1,0:T(8,128)(2,1)S(1)} %project.10.rest_6_.rest_3_.after_ref), custom_call_target="tpu_custom_call" | custom-call | flops 1 | bytes 1 | tf_op jit(solution)/shard_map/unpack_out/pallas_call | solution.py:43
  29.7 1.5 %project.11.rest_1_ = bf16[1,96,768]{2,1,0:T(8,128)(2,1)S(1)} custom-call(bf16[96,1280]{1,0:T(8,128)(2,1)S(1)} %tie.3.rest_0_, bf16[96,1280]{1,0:T(8,128)(2,1)S(1)} %collective-permute-done.4.rest_0_.rest_1_, f32[3,192,768]{2,1,0:T(8,128)S(1)} %get-tuple-element.18.refs_1_.rest_1_.rest_2_.refs_2_, s32[2,3,160,768]{3,2,1,0:T(8,128)S(1)} %get-tuple-element.19.rest_2_.rest_3_, ...), custom_call_target="tpu_custom_call" | custom-call | flops 4000000000 | bytes 1 | tf_op jit(solution)/shard_map/project/pallas_call | solution.py:43
  31.2 1.1 %attend.3.rest_4_ = f32[6,192,256]{2,1,0:T(8,128)S(1)} custom-call(s32[2]{0:T(128)S(1)} %pad_add_fusion.place_ref, s32[3,27]{1,0:T(4,128)S(1)} %bitcast.18, bf16[1,96,768]{2,1,0:T(8,128)(2,1)S(1)} %project.8.refs_1_.rest_0_, bf16[1,96,768]{2,1,0:T(8,128)(2,1)S(1)} %project.11.rest_1_, bf16[2,96,768]{2,1,0:T(8,128)(2,1)S(1)} %project.7.rest_6_.rest_2_, ...), custom_call_target="tpu_custom_call" | custom-call | flops 1 | bytes 1 | tf_op jit(solution)/shard_map/attend/pallas_call | solution.py:43
  32.3 1.1 %attend.4.rest_4_ = f32[6,192,256]{2,1,0:T(8,128)S(1)} custom-call(s32[2]{0:T(128)S(1)} %pad_add_fusion.place_ref, s32[3,27]{1,0:T(4,128)S(1)} %bitcast.19, bf16[1,96,768]{2,1,0:T(8,128)(2,1)S(1)} %project.8.refs_1_.rest_0_, bf16[1,96,768]{2,1,0:T(8,128)(2,1)S(1)} %project.11.rest_1_, bf16[2,96,768]{2,1,0:T(8,128)(2,1)S(1)} %collective-permute-done.7.rest_2_, ...), custom_call_target="tpu_custom_call" | custom-call | flops 1 | bytes 1 | tf_op jit(solution)/shard_map/attend/pallas_call | solution.py:43
  33.5 1.3 %collective-permute-done.5.rest_2_ = bf16[2,96,768]{2,1,0:T(8,128)(2,1)S(1)} collective-permute-done((bf16[2,96,768]{2,1,0:T(8,128)(2,1)S(1)}, bf16[2,96,768]{2,1,0:T(8,128)(2,1)S(1)}, u32[]{:S(2)}, u32[]{:S(2)}) %collective-permute-start.5) | collective-permute-done | bytes 294944 | tf_op jit(solution)/shard_map/ppermute | solution.py:602
  34.8 1.3 %attend.5.rotated_ref = bf16[192,768]{1,0:T(8,128)(2,1)S(1)} custom-call(s32[2]{0:T(128)S(1)} %pad_add_fusion.place_ref, s32[3,27]{1,0:T(4,128)S(1)} %bitcast.20, bf16[1,96,768]{2,1,0:T(8,128)(2,1)S(1)} %project.8.refs_1_.rest_0_, bf16[1,96,768]{2,1,0:T(8,128)(2,1)S(1)} %project.11.rest_1_, bf16[2,96,768]{2,1,0:T(8,128)(2,1)S(1)} %collective-permute-done.5.rest_2_, ...), custom_call_target="tpu_custom_call" | custom-call | flops 1 | bytes 1 | tf_op jit(solution)/shard_map/attend/pallas_call | solution.py:43
  39.7 0.9 %collective-permute-done.13 = bf16[96,2048]{1,0:T(8,128)(2,1)S(1)} collective-permute-done((bf16[96,2048]{1,0:T(8,128)(2,1)S(1)}, bf16[96,2048]{1,0:T(8,128)(2,1)S(1)}, u32[]{:S(2)}, u32[]{:S(2)}) %collective-permute-start.13) | collective-permute-done | bytes 393248 | tf_op jit(solution)/shard_map/ppermute | solution.py:532
  41.5 1.5 %collective-permute-start.10 = (bf16[48,1280]{1,0:T(8,128)(2,1)S(1)}, bf16[48,1280]{1,0:T(8,128)(2,1)S(1)}, u32[]{:S(2)}, u32[]{:S(2)}) collective-permute-start(bf16[48,1280]{1,0:T(8,128)(2,1)S(1)} %slice.38), channel_id=1, source_target_pairs={{0,2},{1,3},{2,0},{3,1},{4,6},{5,7},{6,4},{7,5},{8,10},{9,11},{10,... | collective-permute-start | bytes 368648 | tf_op jit(solution)/shard_map/ppermute | solution.py:532
  43.1 7.4 %collective-permute-done.14.more_ref = bf16[48,2048]{1,0:T(8,128)(2,1)S(1)} collective-permute-done((bf16[48,2048]{1,0:T(8,128)(2,1)S(1)}, bf16[48,2048]{1,0:T(8,128)(2,1)S(1)}, u32[]{:S(2)}, u32[]{:S(2)}) %collective-permute-start.14) | collective-permute-done | bytes 196640 | tf_op jit(solution)/shard_map/ppermute | solution.py:532
  50.5 1.0 %finish.3.rest_0_ = bf16[48,5120]{1,0:T(8,128)(2,1)} custom-call(s32[40,128]{1,0:T(8,128)S(1)} %bitcast.15, f32[48,2048]{1,0:T(8,128)S(1)} %slice.31.keep_ref, bf16[48,2048]{1,0:T(8,128)(2,1)S(1)} %collective-permute-done.14.more_ref), custom_call_target="tpu_custom_call" | custom-call | flops 1 | bytes 1 | tf_op jit(solution)/shard_map/finish/pallas_call | solution.py:43
  51.6 1.0 %finish.4.rest_0_ = bf16[48,5120]{1,0:T(8,128)(2,1)} custom-call(s32[40,128]{1,0:T(8,128)S(1)} %bitcast.16, f32[48,1792]{1,0:T(8,128)S(1)} %slice.29.keep_ref, bf16[48,1792]{1,0:T(8,128)(2,1)S(1)} %collective-permute-done.12.more_ref, bf16[48,5120]{1,0:T(8,128)(2,1)} %finish.3.rest_0_), custom_call_target="tpu_custom_call", output_to_operand_aliasing={{}: (3, {})} | custom-call | flops 1 | bytes 1 | tf_op jit(solution)/shard_map/finish/pallas_call | solution.py:43
  52.7 0.9 %finish.5 = bf16[48,5120]{1,0:T(8,128)(2,1)} custom-call(s32[40,128]{1,0:T(8,128)S(1)} %bitcast.17, f32[48,1280]{1,0:T(8,128)S(1)} %slice.27.keep_ref, bf16[48,1280]{1,0:T(8,128)(2,1)S(1)} %collective-permute-done.10.more_ref, bf16[48,5120]{1,0:T(8,128)(2,1)} %finish.4.rest_0_), custom_call_target="tpu_custom_call", output_to_operand_aliasing={{}: (3, {})} | custom-call | flops 1 | bytes 1 | tf_op jit(solution)/shard_map/finish/pallas_call | solution.py:43
  (49 shorter events, 7.8 us)
Async XLA Ops:
  2.0 3.8 %collective-permute-start.1 = (bf16[192,1280]{1,0:T(8,128)(2,1)S(1)}, bf16[192,1280]{1,0:T(8,128)(2,1)S(1)}, u32[]{:S(2)}, u32[]{:S(2)}) collective-permute-start(bf16[192,1280]{1,0:T(8,128)(2,1)S(1)} %get-tuple-element.17.rest_0_), channel_id=1, source_target_pairs={{0,1},{1,0},{2,3},{3,2},{4,5},{5,4},{6,7},{7,6},{8,9},{9,8},{10,11... | collective-permute-start | bytes 1474568 | tf_op jit(solution)/shard_map/ppermute | solution.py:532
  2.5 9.1 %collective-permute-start = (bf16[96,1280]{1,0:T(8,128)(2,1)S(1)}, bf16[96,1280]{1,0:T(8,128)(2,1)S(1)}, u32[]{:S(2)}, u32[]{:S(2)}) collective-permute-start(bf16[96,1280]{1,0:T(8,128)(2,1)S(1)} %get-tuple-element.16), channel_id=1, source_target_pairs={{0,2},{1,3},{2,0},{3,1},{4,6},{5,7},{6,4},{7,5},{8,10},{9,11},{10,... | collective-permute-start | bytes 737288 | tf_op jit(solution)/shard_map/ppermute | solution.py:532
  11.6 3.0 %collective-permute-start.2 = (bf16[96,1280]{1,0:T(8,128)(2,1)S(1)}, bf16[96,1280]{1,0:T(8,128)(2,1)S(1)}, u32[]{:S(2)}, u32[]{:S(2)}) collective-permute-start(bf16[96,1280]{1,0:T(8,128)(2,1)S(1)} %tie.2.rest_0_), channel_id=1, source_target_pairs={{0,1},{1,0},{2,3},{3,2},{4,5},{5,4},{6,7},{7,6},{8,9},{9,8},{10,11... | collective-permute-start | bytes 737288 | tf_op jit(solution)/shard_map/ppermute | solution.py:532
  11.6 8.4 %collective-permute-start.3 = (bf16[96,1280]{1,0:T(8,128)(2,1)S(1)}, bf16[96,1280]{1,0:T(8,128)(2,1)S(1)}, u32[]{:S(2)}, u32[]{:S(2)}) collective-permute-start(bf16[96,1280]{1,0:T(8,128)(2,1)S(1)} %get-tuple-element.20), channel_id=1, source_target_pairs={{0,2},{1,3},{2,0},{3,1},{4,6},{5,7},{6,4},{7,5},{8,10},{9,11},{10,... | collective-permute-start | bytes 737288 | tf_op jit(solution)/shard_map/ppermute | solution.py:532
  13.4 1.2 %copy-start.3 = (f32[3,768]{1,0:T(4,128)S(1)}, f32[3,768]{1,0:T(4,128)}, u32[]{:S(2)}) copy-start(f32[3,768]{1,0:T(4,128)} %rest_4_.7) | copy-start | bytes 27652
  13.4 1.2 %copy-start.4 = (s32[3,768]{1,0:T(4,128)S(1)}, s32[3,768]{1,0:T(4,128)}, u32[]{:S(2)}) copy-start(s32[3,768]{1,0:T(4,128)} %rest_5_.3) | copy-start | bytes 27652
  16.1 16.3 %collective-permute-start.7 = (bf16[2,96,768]{2,1,0:T(8,128)(2,1)S(1)}, bf16[2,96,768]{2,1,0:T(8,128)(2,1)S(1)}, u32[]{:S(2)}, u32[]{:S(2)}) collective-permute-start(bf16[2,96,768]{2,1,0:T(8,128)(2,1)S(1)} %project.7.rest_6_.rest_2_), channel_id=1, source_target_pairs={{0,4},{8,12},{4,0},{12,8},{1,5},{9,13},{5,1},{13,9},{2,6},{10,14},... | collective-permute-start | bytes 884744 | tf_op jit(solution)/shard_map/ppermute | solution.py:602
  17.7 14.6 %collective-permute-start.8 = (bf16[2,96,768]{2,1,0:T(8,128)(2,1)S(1)}, bf16[2,96,768]{2,1,0:T(8,128)(2,1)S(1)}, u32[]{:S(2)}, u32[]{:S(2)}) collective-permute-start(bf16[2,96,768]{2,1,0:T(8,128)(2,1)S(1)} %project.7.rest_6_.rest_2_), channel_id=1, source_target_pairs={{4,8},{8,4},{5,9},{9,5},{6,10},{10,6},{7,11},{11,7},{20,24},{24,20... | collective-permute-start | bytes 884744 | tf_op jit(solution)/shard_map/ppermute | solution.py:602
  20.0 1.5 %collective-permute-start.4 = (bf16[96,1280]{1,0:T(8,128)(2,1)S(1)}, bf16[96,1280]{1,0:T(8,128)(2,1)S(1)}, u32[]{:S(2)}, u32[]{:S(2)}) collective-permute-start(bf16[96,1280]{1,0:T(8,128)(2,1)S(1)} %tie.3.rest_0_), channel_id=1, source_target_pairs={{0,1},{1,0},{2,3},{3,2},{4,5},{5,4},{6,7},{7,6},{8,9},{9,8},{10,11... | collective-permute-start | bytes 737288 | tf_op jit(solution)/shard_map/ppermute | solution.py:532
  21.2 7.1 %copy-start = (s32[96,5120]{1,0:T(8,128)S(1)}, s32[96,5120]{1,0:T(8,128)}, u32[]{:S(2)}) copy-start(s32[96,5120]{1,0:T(8,128)} %codes_ref.1) | copy-start | bytes 5898244
  23.0 11.8 %collective-permute-start.5 = (bf16[2,96,768]{2,1,0:T(8,128)(2,1)S(1)}, bf16[2,96,768]{2,1,0:T(8,128)(2,1)S(1)}, u32[]{:S(2)}, u32[]{:S(2)}) collective-permute-start(bf16[2,96,768]{2,1,0:T(8,128)(2,1)S(1)} %project.10.rest_6_.rest_3_.after_ref), channel_id=1, source_target_pairs={{0,4},{8,12},{4,0},{12,8},{1,5},{9,13},{5,1},{13,9},{2,6},{10,14},... | collective-permute-start | bytes 884744 | tf_op jit(solution)/shard_map/ppermute | solution.py:602
  27.4 7.4 %collective-permute-start.6 = (bf16[2,96,768]{2,1,0:T(8,128)(2,1)S(1)}, bf16[2,96,768]{2,1,0:T(8,128)(2,1)S(1)}, u32[]{:S(2)}, u32[]{:S(2)}) collective-permute-start(bf16[2,96,768]{2,1,0:T(8,128)(2,1)S(1)} %project.10.rest_6_.rest_3_.after_ref), channel_id=1, source_target_pairs={{4,8},{8,4},{5,9},{9,5},{6,10},{10,6},{7,11},{11,7},{20,24},{24,20... | collective-permute-start | bytes 884744 | tf_op jit(solution)/shard_map/ppermute | solution.py:602
  32.3 2.5 %copy-start.5 = (s32[768]{0:T(1024)S(1)}, s32[768]{0:T(1024)}, u32[]{:S(2)}) copy-start(s32[768]{0:T(1024)} %param.16) | copy-start | bytes 9220
  33.4 2.7 %copy-start.1 = (f32[5120]{0:T(1024)S(1)}, f32[5120]{0:T(1024)}, u32[]{:S(2)}) copy-start(f32[5120]{0:T(1024)} %param.18) | copy-start | bytes 61444
  36.9 2.1 %collective-permute-start.11 = (bf16[96,1792]{1,0:T(8,128)(2,1)S(1)}, bf16[96,1792]{1,0:T(8,128)(2,1)S(1)}, u32[]{:S(2)}, u32[]{:S(2)}) collective-permute-start(bf16[96,1792]{1,0:T(8,128)(2,1)S(1)} %get-tuple-element.24), channel_id=1, source_target_pairs={{0,1},{1,0},{2,3},{3,2},{4,5},{5,4},{6,7},{7,6},{8,9},{9,8},{10,11... | collective-permute-start | bytes 1032200 | tf_op jit(solution)/shard_map/ppermute | solution.py:532
  38.3 3.0 %collective-permute-start.9 = (bf16[96,1280]{1,0:T(8,128)(2,1)S(1)}, bf16[96,1280]{1,0:T(8,128)(2,1)S(1)}, u32[]{:S(2)}, u32[]{:S(2)}) collective-permute-start(bf16[96,1280]{1,0:T(8,128)(2,1)S(1)} %get-tuple-element.22), channel_id=1, source_target_pairs={{0,1},{1,0},{2,3},{3,2},{4,5},{5,4},{6,7},{7,6},{8,9},{9,8},{10,11... | collective-permute-start | bytes 737288 | tf_op jit(solution)/shard_map/ppermute | solution.py:532
  38.9 1.7 %collective-permute-start.13 = (bf16[96,2048]{1,0:T(8,128)(2,1)S(1)}, bf16[96,2048]{1,0:T(8,128)(2,1)S(1)}, u32[]{:S(2)}, u32[]{:S(2)}) collective-permute-start(bf16[96,2048]{1,0:T(8,128)(2,1)S(1)} %get-tuple-element.26), channel_id=1, source_target_pairs={{0,1},{1,0},{2,3},{3,2},{4,5},{5,4},{6,7},{7,6},{8,9},{9,8},{10,11... | collective-permute-start | bytes 1179656 | tf_op jit(solution)/shard_map/ppermute | solution.py:532
  39.1 12.5 %collective-permute-start.12 = (bf16[48,1792]{1,0:T(8,128)(2,1)S(1)}, bf16[48,1792]{1,0:T(8,128)(2,1)S(1)}, u32[]{:S(2)}, u32[]{:S(2)}) collective-permute-start(bf16[48,1792]{1,0:T(8,128)(2,1)S(1)} %slice.37), channel_id=1, source_target_pairs={{0,2},{1,3},{2,0},{3,1},{4,6},{5,7},{6,4},{7,5},{8,10},{9,11},{10,... | collective-permute-start | bytes 516104 | tf_op jit(solution)/shard_map/ppermute | solution.py:532
  40.7 9.8 %copy-start.2 = (s32[5120]{0:T(1024)S(1)}, s32[5120]{0:T(1024)}, u32[]{:S(2)}) copy-start(s32[5120]{0:T(1024)} %param.19) | copy-start | bytes 61444
  40.8 9.8 %collective-permute-start.14 = (bf16[48,2048]{1,0:T(8,128)(2,1)S(1)}, bf16[48,2048]{1,0:T(8,128)(2,1)S(1)}, u32[]{:S(2)}, u32[]{:S(2)}) collective-permute-start(bf16[48,2048]{1,0:T(8,128)(2,1)S(1)} %slice.36), channel_id=1, source_target_pairs={{0,2},{1,3},{2,0},{3,1},{4,6},{5,7},{6,4},{7,5},{8,10},{9,11},{10,... | collective-permute-start | bytes 589832 | tf_op jit(solution)/shard_map/ppermute | solution.py:532
  41.5 11.2 %collective-permute-start.10 = (bf16[48,1280]{1,0:T(8,128)(2,1)S(1)}, bf16[48,1280]{1,0:T(8,128)(2,1)S(1)}, u32[]{:S(2)}, u32[]{:S(2)}) collective-permute-start(bf16[48,1280]{1,0:T(8,128)(2,1)S(1)} %slice.38), channel_id=1, source_target_pairs={{0,2},{1,3},{2,0},{3,1},{4,6},{5,7},{6,4},{7,5},{8,10},{9,11},{10,... | collective-permute-start | bytes 368648 | tf_op jit(solution)/shard_map/ppermute | solution.py:532

commit v4 on v3

--- a/solution.py
+++ b/solution.py
@@ -187,6 +187,13 @@
         out_specs=ANY,
         input_output_aliases={0: 0},
     )
+
+
+def gate(array):
+    def body(array_ref, out_ref):
+        out_ref[...] = jnp.zeros_like(out_ref)
+
+    return call(body, shape_of((8, HAD), f32), [ANY], (array,), "gate", flops=4 * 10**9)
 
 
 def prepare_kernel(near, far, place_ref, *rest):
@@ -344,8 +351,8 @@
     masks = []
     for tile in range(row_count // TILE):
         hit = jnp.zeros(lane.shape, f32)
-        for entry in range(windows_ref.shape[1]):
-            hit = jnp.where(ids == windows_ref[tile, entry], 1.0, hit)
+        for entry in range(windows_ref.shape[2]):
+            hit = jnp.where(ids == windows_ref[tile, 0, entry], 1.0, hit)
         masks.append(jnp.broadcast_to(hit, (TILE, lane.shape[1])))
     return jnp.concatenate(masks, 0)
 
@@ -491,39 +498,42 @@
     )
 
 
-def finish_kernel(first, has_base, sign_ref, keep_ref, more_ref, *rest):
-    out_hbm, done_ref, sem = rest[1:] if has_base else rest
-    columns = keep_ref.shape[1]
+def finish_kernel(chunks, sign_ref, *rest):
+    out_hbm, done_ref, sems = rest[2 * chunks :]
     doubled = double_hadamard()
-    for at in range(0, columns, HAD):
-        cols = slice(at, at + HAD)
-        total = keep_ref[:, cols].astype(f32) + more_ref[:, cols].astype(f32)
-        place = (first + at) // HAD
-        sign_row = signed(sign_ref[place : place + 1, :]) * np.float32(HAD ** (-0.5))
-        done_ref[:, cols] = (rotate_halves(total, doubled) * sign_row).astype(bf16)
-    copy = pltpu.make_async_copy(done_ref, out_hbm.at[:, pl.ds(first, columns)], sem)
-    copy.start()
-    copy.wait()
-
-
-def finish(base, sign_rows, keep, more, first):
-    share, columns = keep.shape
-    args = [sign_rows, keep, more]
-    in_specs = [VMEM] * 3
-    aliases = {}
-    if base is not None:
-        args.append(base)
-        in_specs.append(ANY)
-        aliases = {3: 0}
-    return call(
-        functools.partial(finish_kernel, first, base is not None),
+    first, copies = 0, []
+    for chunk in range(chunks):
+        keep_ref, more_ref = rest[2 * chunk : 2 * chunk + 2]
+        share, columns = keep_ref.shape
+        totals = keep_ref[...].astype(f32) + more_ref[...].astype(f32)
+        blocks = [totals[:, at : at + HAD] for at in range(0, columns, HAD)]
+        turned = rotate_halves(jnp.concatenate(blocks, 0), doubled)
+        for block in range(len(blocks)):
+            place = first // HAD + block
+            sign_row = signed(sign_ref[place : place + 1, :]) * np.float32(HAD ** (-0.5))
+            done = turned[block * share : (block + 1) * share] * sign_row
+            done_ref[:, place * HAD : (place + 1) * HAD] = done.astype(bf16)
+        cols = pl.ds(first, columns)
+        copies.append(
+            pltpu.make_async_copy(done_ref.at[:, cols], out_hbm.at[:, cols], sems.at[chunk])
+        )
+        copies[-1].start()
+        first += columns
+    for copy in copies:
+        copy.wait()
+
+
+def finish(pairs, sign_rows):
+    share = pairs[0][0].shape[0]
+    args = [sign_rows] + [array for pair in pairs for array in pair]
+    return call(
+        functools.partial(finish_kernel, len(pairs)),
         shape_of((share, D), bf16),
-        in_specs,
+        [VMEM] * len(args),
         args,
         "finish",
-        out_specs=ANY,
-        scratch_shapes=[pltpu.VMEM((share, columns), bf16), pltpu.SemaphoreType.DMA],
-        input_output_aliases=aliases,
+        out_specs=HBM,
+        scratch_shapes=[pltpu.VMEM((share, D), bf16), pltpu.SemaphoreType.DMA((len(pairs),))],
     )
 
 
@@ -550,7 +560,7 @@
     return tuple(flips)
 
 
-CHUNKS = (2048, 1792, 1280)
+CHUNKS = (2560, 2560)
 
 
 def on_device(
@@ -590,23 +600,25 @@
     swaps = row_swaps(row_tiles)
     ending = [qkv_scale, qkv_sign]
     every = tuple(range(len(far_flips)))
-    key_values, moved, queries = [], [], []
+    halves, key_values, moved, gates = [], [], [], []
     for half, first_row in ((early, 0), (late, half_rows)):
-        shards = {top: tie(half, *queries, sums)}
+        shards = {top: tie(half, *gates, sums)}
         for bit in low_bits:
             for flip in list(shards):
                 shards[flip ^ bit] = swap(shards[flip], bit)
         shards = [shards[flip] for flip in far_flips]
-        partial = project((1, 2), first_row, [shards[:-1]], every[:-1], sums, words, None, 4 * 10**9)
+        partial = project(
+            (1, 2), first_row, [shards[:-1]], every[:-1], sums, words, None, 4 * 10**9
+        )
         key_value = project((1, 2), 0, [shards[-1:]], every[-1:], partial, words, ending)
         moved.append([lax.ppermute(key_value, "height", pairs) for _, _, pairs in swaps])
+        halves.append(shards)
         key_values.append(key_value)
-        queries.append(
-            project((0,), first_row, [shards], every, sums, words, ending + [key_value], 4 * 10**9)
-        )
+        gates.append(gate(key_value))
+    queries = [project((0,), 0, halves, every, sums, words, ending, 4 * 10**9)]
     out_weights = unpack_out(out_codes, key_values[1])
 
-    listed = windows[0]
+    listed = jnp.transpose(windows, (1, 0, 2))
     own_rows = ((None, 0, half_rows), (None, half_rows, half_rows))
     early_rows = tuple(((by, odd), 0, half_rows) for by, odd, _ in swaps)
     late_rows = tuple(((by, odd), half_rows, half_rows) for by, odd, _ in swaps)
@@ -625,10 +637,12 @@
     bits = low_bits + [top]
     scale_rows = out_scale.reshape(-1, HAD)
     sign_rows = out_sign.reshape(-1, HAD)
-    result = None
+    pairs, sums_sent = [], []
     first = 0
     for columns in CHUNKS:
         part, keep = out_project(rotated, out_weights, scale_rows, first, columns)
+        if sums_sent:
+            part = tie(part, sums_sent[-1])
         for bit in bits:
             more = swap(part, bit)
             if bit == top:
@@ -636,9 +650,10 @@
             total = keep.astype(f32) + more.astype(f32)
             half = total.shape[0] // 2
             part, keep = total[:half].astype(bf16), total[half:]
-        result = finish(result, sign_rows, keep, more, first)
+            sums_sent.append(part)
+        pairs.append((keep, more))
         first += columns
-    return result[None]
+    return finish(pairs, sign_rows)[None]
 
 
 def solution(mesh):

time: 54.6 us -> 53.8 us (0.985)
  waiting for transfers between devices: 11.2 us -> 17.2 us
  starting transfers between devices: 15.9 us -> 12.5 us
  Pallas kernels: 25.1 us -> 22.2 us
  local copies, waits for them, and re-layouts: 0.84 us -> 0.16 us
    ppermute x11 -> x9, waiting for transfers between devices: 9.83 us -> 16.2 us  [swap(): return lax.ppermute(shard, 'head', [(i, i ^ bit) for i in range(peers)])]
    pallas_call x20 -> x18, Pallas kernels: 25.1 us -> 22.2 us  [call(): pl.pallas_call(body, out_shape=out_shape, in_specs=in_specs, out_specs=ou...]
    ppermute x11 -> x9, starting transfers between devices: 8.3 us -> 6.41 us  [swap(): return lax.ppermute(shard, 'head', [(i, i ^ bit) for i in range(peers)])]
    ppermute x4, starting transfers between devices: 7.58 us -> 6.11 us  [on_device(): lax.ppermute(key_value, 'height', pairs)]
    unnamed x13 -> x14, local copies, waits for them, and re-layouts: 0.71 us -> 0.04 us
  transfers between devices with their start and end apart: 15 -> 13, of which waited for: 7 -> 8; matrix products, arithmetic and copies ran while one was open for 2% -> 0% of each run, Pallas kernels for 38% -> 32%
where the time goes in v4:
time: 53.8 us; the launch traced here: 52.8 us
  Pallas kernels  22.2 us (41%)
  waiting for transfers between devices  17.2 us (32%)
  starting transfers between devices  12.5 us (23%)
    pallas_call x18, Pallas kernels, call(): pl.pallas_call(body, out_shape=out_shape, in_specs=in_specs, out_specs=ou...  22.2 us
    ppermute x9, waiting for transfers between devices, swap(): return lax.ppermute(shard, 'head', [(i, i ^ bit) for i in range(peers)])  16.2 us
    ppermute x9, starting transfers between devices, swap(): return lax.ppermute(shard, 'head', [(i, i ^ bit) for i in range(peers)])  6.41 us
    ppermute x4, starting transfers between devices, on_device(): lax.ppermute(key_value, 'height', pairs)  6.11 us
  transfers between devices with their start and end apart: 13, of which 8 were waited for; matrix products, arithmetic and copies ran while one was open for 0% of the time, Pallas kernels for 32%

profile of v4, /device:TPU:0, one launch (start us, length us, event | category | flops | bytes accessed | tf_op | source)
XLA Modules:
  0.0 52.8 jit_solution(10473765783817926435)
XLA Ops:
  0.1 1.9 %turn.1 = (bf16[192,1280]{1,0:T(8,128)(2,1)S(1)}, bf16[96,1280]{1,0:T(8,128)(2,1)S(1)}) custom-call(s32[2]{0:T(128)S(1)} %pad_add_fusion.place_ref, bf16[192,1280]{1,0:T(8,128)(2,1)} %bitcast.18, s32[40,128]{1,0:T(8,128)} %bitcast.19), custom_call_target="tpu_custom_call" | custom-call | flops 1 | bytes 1 | tf_op jit(solution)/shard_map/turn/pallas_call | solution.py:43
  2.5 2.6 %collective-permute-start = (bf16[96,1280]{1,0:T(8,128)(2,1)S(1)}, bf16[96,1280]{1,0:T(8,128)(2,1)S(1)}, u32[]{:S(2)}, u32[]{:S(2)}) collective-permute-start(bf16[96,1280]{1,0:T(8,128)(2,1)S(1)} %get-tuple-element.14), channel_id=1, source_target_pairs={{0,2},{1,3},{2,0},{3,1},{4,6},{5,7},{6,4},{7,5},{8,10},{9,11},{10,... | collective-permute-start | bytes 737288 | tf_op jit(solution)/shard_map/ppermute | solution.py:542
  5.0 5.0 %prepare.1 = (f32[3,192,768]{2,1,0:T(8,128)S(1)}, s32[2,3,160,768]{3,2,1,0:T(8,128)S(1)}, bf16[96,1280]{1,0:T(8,128)(2,1)S(1)}) custom-call(s32[2]{0:T(128)S(1)} %pad_add_fusion.place_ref, bf16[192,1280]{1,0:T(8,128)(2,1)S(1)} %get-tuple-element.15.rest_0_, bf16[192,1280]{1,0:T(8,128)(2,1)S(1)} %collective-permute-done.1.rest_1_, s32[3,640,768]{2,1,0:T(8,128)} %bitcast.17), custom_call_target="tpu_custom_call" | custom-call | flops 1 | bytes 1 | tf_op jit(solution)/shard_map/prepare/pallas_call | solution.py:43
  10.1 1.5 %collective-permute-done.refs_0_ = bf16[96,1280]{1,0:T(8,128)(2,1)S(1)} collective-permute-done((bf16[96,1280]{1,0:T(8,128)(2,1)S(1)}, bf16[96,1280]{1,0:T(8,128)(2,1)S(1)}, u32[]{:S(2)}, u32[]{:S(2)}) %collective-permute-start) | collective-permute-done | bytes 245792 | tf_op jit(solution)/shard_map/ppermute | solution.py:542
  11.6 1.8 %collective-permute-start.3 = (bf16[96,1280]{1,0:T(8,128)(2,1)S(1)}, bf16[96,1280]{1,0:T(8,128)(2,1)S(1)}, u32[]{:S(2)}, u32[]{:S(2)}) collective-permute-start(bf16[96,1280]{1,0:T(8,128)(2,1)S(1)} %get-tuple-element.17), channel_id=1, source_target_pairs={{0,2},{1,3},{2,0},{3,1},{4,6},{5,7},{6,4},{7,5},{8,10},{9,11},{10,... | collective-permute-start | bytes 737288 | tf_op jit(solution)/shard_map/ppermute | solution.py:542
  13.4 1.2 %project.5.rest_1_ = f32[2,96,768]{2,1,0:T(8,128)S(1)} custom-call(bf16[96,1280]{1,0:T(8,128)(2,1)S(1)} %tie.3.rest_0_, f32[3,192,768]{2,1,0:T(8,128)S(1)} %get-tuple-element.16.refs_1_.rest_1_.refs_2_.rest_4_, s32[2,3,160,768]{3,2,1,0:T(8,128)S(1)} %get-tuple-element.18.rest_2_.rest_5_), custom_call_target="tpu_custom_call" | custom-call | flops 4000000000 | bytes 1 | tf_op jit(solution)/shard_map/project/pallas_call | solution.py:43
  14.6 1.5 %project.6.array_ref.rest_1_ = bf16[2,96,768]{2,1,0:T(8,128)(2,1)S(1)} custom-call(bf16[96,1280]{1,0:T(8,128)(2,1)S(1)} %collective-permute-done.2.rest_0_.rest_1_, f32[2,96,768]{2,1,0:T(8,128)S(1)} %project.5.rest_1_, s32[2,3,160,768]{3,2,1,0:T(8,128)S(1)} %get-tuple-element.18.rest_2_.rest_5_, f32[3,768]{1,0:T(4,128)S(1)} %copy-done.2, s32[3,768]{1,0:T(4,128)S(1)} %copy-done.3), custom_call_target="tpu_custom_call" | custom-call | flops 1 | bytes 1 | tf_op jit(solution)/shard_map/project/pallas_call | solution.py:43
  16.1 1.6 %collective-permute-start.7 = (bf16[2,96,768]{2,1,0:T(8,128)(2,1)S(1)}, bf16[2,96,768]{2,1,0:T(8,128)(2,1)S(1)}, u32[]{:S(2)}, u32[]{:S(2)}) collective-permute-start(bf16[2,96,768]{2,1,0:T(8,128)(2,1)S(1)} %project.6.array_ref.rest_1_), channel_id=1, source_target_pairs={{0,4},{8,12},{4,0},{12,8},{1,5},{9,13},{5,1},{13,9},{2,6},{10,14},... | collective-permute-start | bytes 884744 | tf_op jit(solution)/shard_map/ppermute | solution.py:614
  18.4 1.6 %collective-permute-done.3.refs_0_ = bf16[96,1280]{1,0:T(8,128)(2,1)S(1)} collective-permute-done((bf16[96,1280]{1,0:T(8,128)(2,1)S(1)}, bf16[96,1280]{1,0:T(8,128)(2,1)S(1)}, u32[]{:S(2)}, u32[]{:S(2)}) %collective-permute-start.3) | collective-permute-done | bytes 245792 | tf_op jit(solution)/shard_map/ppermute | solution.py:542
  20.0 1.2 %project.8.rest_1_ = f32[2,96,768]{2,1,0:T(8,128)S(1)} custom-call(bf16[96,1280]{1,0:T(8,128)(2,1)S(1)} %tie.4.rest_2_.rest_0_, f32[3,192,768]{2,1,0:T(8,128)S(1)} %get-tuple-element.16.refs_1_.rest_1_.refs_2_.rest_4_, s32[2,3,160,768]{3,2,1,0:T(8,128)S(1)} %get-tuple-element.18.rest_2_.rest_5_), custom_call_target="tpu_custom_call" | custom-call | flops 4000000000 | bytes 1 | tf_op jit(solution)/shard_map/project/pallas_call | solution.py:43
  21.5 1.5 %project.9.rest_2_.after_ref = bf16[2,96,768]{2,1,0:T(8,128)(2,1)S(1)} custom-call(bf16[96,1280]{1,0:T(8,128)(2,1)S(1)} %collective-permute-done.4.rest_3_.rest_0_, f32[2,96,768]{2,1,0:T(8,128)S(1)} %project.8.rest_1_, s32[2,3,160,768]{3,2,1,0:T(8,128)S(1)} %get-tuple-element.18.rest_2_.rest_5_, f32[3,768]{1,0:T(4,128)S(1)} %copy-done.2, s32[3,768]{1,0:T(4,128)S(1)} %copy-done.3), custom_call_target="tpu_custom_call" | custom-call | flops 1 | bytes 1 | tf_op jit(solution)/shard_map/project/pallas_call | solution.py:43
  23.0 2.9 %collective-permute-start.5 = (bf16[2,96,768]{2,1,0:T(8,128)(2,1)S(1)}, bf16[2,96,768]{2,1,0:T(8,128)(2,1)S(1)}, u32[]{:S(2)}, u32[]{:S(2)}) collective-permute-start(bf16[2,96,768]{2,1,0:T(8,128)(2,1)S(1)} %project.9.rest_2_.after_ref), channel_id=1, source_target_pairs={{0,4},{8,12},{4,0},{12,8},{1,5},{9,13},{5,1},{13,9},{2,6},{10,14},... | collective-permute-start | bytes 884744 | tf_op jit(solution)/shard_map/ppermute | solution.py:614
  26.8 1.5 %unpack_out.1.weights_ref = bf16[768,5120]{1,0:T(8,128)(2,1)S(1)} custom-call(s32[96,5120]{1,0:T(8,128)S(1)} %copy-done, bf16[2,96,768]{2,1,0:T(8,128)(2,1)S(1)} %project.9.rest_2_.after_ref), custom_call_target="tpu_custom_call" | custom-call | flops 1 | bytes 1 | tf_op jit(solution)/shard_map/unpack_out/pallas_call | solution.py:43
  28.3 1.8 %project.7.rest_0_ = bf16[1,192,768]{2,1,0:T(8,128)(2,1)S(1)} custom-call(bf16[96,1280]{1,0:T(8,128)(2,1)S(1)} %tie.3.rest_0_, bf16[96,1280]{1,0:T(8,128)(2,1)S(1)} %collective-permute-done.2.rest_0_.rest_1_, bf16[96,1280]{1,0:T(8,128)(2,1)S(1)} %tie.4.rest_2_.rest_0_, bf16[96,1280]{1,0:T(8,128)(2,1)S(1)} %collective-permute-done.4.rest_3_.rest_0_, ...), custom_call_target="tpu_custom_call" | custom-call | flops 4000000000 | bytes 1 | tf_op jit(solution)/shard_map/project/pallas_call | solution.py:43
  30.1 1.1 %attend.3.rest_3_ = f32[6,192,256]{2,1,0:T(8,128)S(1)} custom-call(s32[2]{0:T(128)S(1)} %pad_add_fusion.place_ref, s32[3,1,27]{2,1,0:T(1,128)S(1)} %bitcast.13, bf16[1,192,768]{2,1,0:T(8,128)(2,1)S(1)} %project.7.rest_0_, bf16[2,96,768]{2,1,0:T(8,128)(2,1)S(1)} %project.6.array_ref.rest_1_, bf16[2,96,768]{2,1,0:T(8,128)(2,1)S(1)} %project.9.rest_2_.after_ref), custom_call_target="tpu_custom_call" | custom-call | flops 1 | bytes 1 | tf_op jit(solution)/shard_map/attend/pallas_call | solution.py:43
  31.2 1.1 %attend.4.rest_3_ = f32[6,192,256]{2,1,0:T(8,128)S(1)} custom-call(s32[2]{0:T(128)S(1)} %pad_add_fusion.place_ref, s32[3,1,27]{2,1,0:T(1,128)S(1)} %bitcast.14, bf16[1,192,768]{2,1,0:T(8,128)(2,1)S(1)} %project.7.rest_0_, bf16[2,96,768]{2,1,0:T(8,128)(2,1)S(1)} %collective-permute-done.7.rest_1_, bf16[2,96,768]{2,1,0:T(8,128)(2,1)S(1)} %collective-permute-done.8.rest_2_, ...), custom_call_target="tpu_custom_call" | custom-call | flops 1 | bytes 1 | tf_op jit(solution)/shard_map/attend/pallas_call | solution.py:43
  32.3 1.0 %collective-permute-done.5.rest_1_ = bf16[2,96,768]{2,1,0:T(8,128)(2,1)S(1)} collective-permute-done((bf16[2,96,768]{2,1,0:T(8,128)(2,1)S(1)}, bf16[2,96,768]{2,1,0:T(8,128)(2,1)S(1)}, u32[]{:S(2)}, u32[]{:S(2)}) %collective-permute-start.5) | collective-permute-done | bytes 294944 | tf_op jit(solution)/shard_map/ppermute | solution.py:614
  33.3 1.3 %attend.5.rotated_ref = bf16[192,768]{1,0:T(8,128)(2,1)S(1)} custom-call(s32[2]{0:T(128)S(1)} %pad_add_fusion.place_ref, s32[3,1,27]{2,1,0:T(1,128)S(1)} %bitcast.15, bf16[1,192,768]{2,1,0:T(8,128)(2,1)S(1)} %project.7.rest_0_, bf16[2,96,768]{2,1,0:T(8,128)(2,1)S(1)} %collective-permute-done.5.rest_1_, ...), custom_call_target="tpu_custom_call" | custom-call | flops 1 | bytes 1 | tf_op jit(solution)/shard_map/attend/pallas_call | solution.py:43
  34.6 1.0 %out_project.2 = (bf16[96,2560]{1,0:T(8,128)(2,1)S(1)}, bf16[96,2560]{1,0:T(8,128)(2,1)S(1)}) custom-call(bf16[192,768]{1,0:T(8,128)(2,1)S(1)} %attend.5.rotated_ref, bf16[768,5120]{1,0:T(8,128)(2,1)S(1)} %unpack_out.1.weights_ref, f32[40,128]{1,0:T(8,128)S(1)} %bitcast.10), custom_call_target="tpu_custom_call" | custom-call | flops 1 | bytes 1 | tf_op jit(solution)/shard_map/out_project/pallas_call | solution.py:43
  35.7 1.0 %out_project.3 = (bf16[96,2560]{1,0:T(8,128)(2,1)S(1)}, bf16[96,2560]{1,0:T(8,128)(2,1)S(1)}) custom-call(bf16[192,768]{1,0:T(8,128)(2,1)S(1)} %attend.5.rotated_ref, bf16[768,5120]{1,0:T(8,128)(2,1)S(1)} %unpack_out.1.weights_ref, f32[40,128]{1,0:T(8,128)S(1)} %bitcast.11), custom_call_target="tpu_custom_call" | custom-call | flops 1 | bytes 1 | tf_op jit(solution)/shard_map/out_project/pallas_call | solution.py:43
  38.5 1.1 %collective-permute-done.11 = bf16[96,2560]{1,0:T(8,128)(2,1)S(1)} collective-permute-done((bf16[96,2560]{1,0:T(8,128)(2,1)S(1)}, bf16[96,2560]{1,0:T(8,128)(2,1)S(1)}, u32[]{:S(2)}, u32[]{:S(2)}) %collective-permute-start.11) | collective-permute-done | bytes 491552 | tf_op jit(solution)/shard_map/ppermute | solution.py:542
  40.5 6.2 %collective-permute-done.10.rest_1_ = bf16[48,2560]{1,0:T(8,128)(2,1)S(1)} collective-permute-done((bf16[48,2560]{1,0:T(8,128)(2,1)S(1)}, bf16[48,2560]{1,0:T(8,128)(2,1)S(1)}, u32[]{:S(2)}, u32[]{:S(2)}) %collective-permute-start.10) | collective-permute-done | bytes 245792 | tf_op jit(solution)/shard_map/ppermute | solution.py:542
  46.7 4.7 %collective-permute-done.12.rest_3_ = bf16[48,2560]{1,0:T(8,128)(2,1)S(1)} collective-permute-done((bf16[48,2560]{1,0:T(8,128)(2,1)S(1)}, bf16[48,2560]{1,0:T(8,128)(2,1)S(1)}, u32[]{:S(2)}, u32[]{:S(2)}) %collective-permute-start.12) | collective-permute-done | bytes 245792 | tf_op jit(solution)/shard_map/ppermute | solution.py:542
  51.4 1.2 %finish.1 = bf16[48,5120]{1,0:T(8,128)(2,1)} custom-call(s32[40,128]{1,0:T(8,128)S(1)} %bitcast.12, f32[48,2560]{1,0:T(8,128)S(1)} %slice.18.rest_0_, bf16[48,2560]{1,0:T(8,128)(2,1)S(1)} %collective-permute-done.10.rest_1_, f32[48,2560]{1,0:T(8,128)S(1)} %slice.20.rest_2_, bf16[48,2560]{1,0:T(8,128)(2,1)S(1)} %collective-permute-done.12.rest_3_), custom_call_target="tpu_custom_call" | custom-call | flops 1 | bytes 1 | tf_op jit(solution)/shard_map/finish/pallas_call | solution.py:43
  (41 shorter events, 5.2 us)
Async XLA Ops:
  2.0 3.1 %collective-permute-start.1 = (bf16[192,1280]{1,0:T(8,128)(2,1)S(1)}, bf16[192,1280]{1,0:T(8,128)(2,1)S(1)}, u32[]{:S(2)}, u32[]{:S(2)}) collective-permute-start(bf16[192,1280]{1,0:T(8,128)(2,1)S(1)} %get-tuple-element.15.rest_0_), channel_id=1, source_target_pairs={{0,1},{1,0},{2,3},{3,2},{4,5},{5,4},{6,7},{7,6},{8,9},{9,8},{10,11... | collective-permute-start | bytes 1474568 | tf_op jit(solution)/shard_map/ppermute | solution.py:542
  2.5 9.1 %collective-permute-start = (bf16[96,1280]{1,0:T(8,128)(2,1)S(1)}, bf16[96,1280]{1,0:T(8,128)(2,1)S(1)}, u32[]{:S(2)}, u32[]{:S(2)}) collective-permute-start(bf16[96,1280]{1,0:T(8,128)(2,1)S(1)} %get-tuple-element.14), channel_id=1, source_target_pairs={{0,2},{1,3},{2,0},{3,1},{4,6},{5,7},{6,4},{7,5},{8,10},{9,11},{10,... | collective-permute-start | bytes 737288 | tf_op jit(solution)/shard_map/ppermute | solution.py:542
  11.6 3.0 %collective-permute-start.2 = (bf16[96,1280]{1,0:T(8,128)(2,1)S(1)}, bf16[96,1280]{1,0:T(8,128)(2,1)S(1)}, u32[]{:S(2)}, u32[]{:S(2)}) collective-permute-start(bf16[96,1280]{1,0:T(8,128)(2,1)S(1)} %tie.3.rest_0_), channel_id=1, source_target_pairs={{0,1},{1,0},{2,3},{3,2},{4,5},{5,4},{6,7},{7,6},{8,9},{9,8},{10,11... | collective-permute-start | bytes 737288 | tf_op jit(solution)/shard_map/ppermute | solution.py:542
  11.6 8.4 %collective-permute-start.3 = (bf16[96,1280]{1,0:T(8,128)(2,1)S(1)}, bf16[96,1280]{1,0:T(8,128)(2,1)S(1)}, u32[]{:S(2)}, u32[]{:S(2)}) collective-permute-start(bf16[96,1280]{1,0:T(8,128)(2,1)S(1)} %get-tuple-element.17), channel_id=1, source_target_pairs={{0,2},{1,3},{2,0},{3,1},{4,6},{5,7},{6,4},{7,5},{8,10},{9,11},{10,... | collective-permute-start | bytes 737288 | tf_op jit(solution)/shard_map/ppermute | solution.py:542
  13.4 1.2 %copy-start.2 = (f32[3,768]{1,0:T(4,128)S(1)}, f32[3,768]{1,0:T(4,128)}, u32[]{:S(2)}) copy-start(f32[3,768]{1,0:T(4,128)} %rest_3_.3) | copy-start | bytes 27652
  13.4 1.2 %copy-start.3 = (s32[3,768]{1,0:T(4,128)S(1)}, s32[3,768]{1,0:T(4,128)}, u32[]{:S(2)}) copy-start(s32[3,768]{1,0:T(4,128)} %rest_4_.3) | copy-start | bytes 27652
  16.1 15.2 %collective-permute-start.7 = (bf16[2,96,768]{2,1,0:T(8,128)(2,1)S(1)}, bf16[2,96,768]{2,1,0:T(8,128)(2,1)S(1)}, u32[]{:S(2)}, u32[]{:S(2)}) collective-permute-start(bf16[2,96,768]{2,1,0:T(8,128)(2,1)S(1)} %project.6.array_ref.rest_1_), channel_id=1, source_target_pairs={{0,4},{8,12},{4,0},{12,8},{1,5},{9,13},{5,1},{13,9},{2,6},{10,14},... | collective-permute-start | bytes 884744 | tf_op jit(solution)/shard_map/ppermute | solution.py:614
  17.7 13.5 %collective-permute-start.8 = (bf16[2,96,768]{2,1,0:T(8,128)(2,1)S(1)}, bf16[2,96,768]{2,1,0:T(8,128)(2,1)S(1)}, u32[]{:S(2)}, u32[]{:S(2)}) collective-permute-start(bf16[2,96,768]{2,1,0:T(8,128)(2,1)S(1)} %project.6.array_ref.rest_1_), channel_id=1, source_target_pairs={{4,8},{8,4},{5,9},{9,5},{6,10},{10,6},{7,11},{11,7},{20,24},{24,20... | collective-permute-start | bytes 884744 | tf_op jit(solution)/shard_map/ppermute | solution.py:614
  20.0 1.5 %collective-permute-start.4 = (bf16[96,1280]{1,0:T(8,128)(2,1)S(1)}, bf16[96,1280]{1,0:T(8,128)(2,1)S(1)}, u32[]{:S(2)}, u32[]{:S(2)}) collective-permute-start(bf16[96,1280]{1,0:T(8,128)(2,1)S(1)} %tie.4.rest_2_.rest_0_), channel_id=1, source_target_pairs={{0,1},{1,0},{2,3},{3,2},{4,5},{5,4},{6,7},{7,6},{8,9},{9,8},{10,11... | collective-permute-start | bytes 737288 | tf_op jit(solution)/shard_map/ppermute | solution.py:542
  21.2 5.6 %copy-start = (s32[96,5120]{1,0:T(8,128)S(1)}, s32[96,5120]{1,0:T(8,128)}, u32[]{:S(2)}) copy-start(s32[96,5120]{1,0:T(8,128)} %codes_ref.1) | copy-start | bytes 5898244
  23.0 10.4 %collective-permute-start.5 = (bf16[2,96,768]{2,1,0:T(8,128)(2,1)S(1)}, bf16[2,96,768]{2,1,0:T(8,128)(2,1)S(1)}, u32[]{:S(2)}, u32[]{:S(2)}) collective-permute-start(bf16[2,96,768]{2,1,0:T(8,128)(2,1)S(1)} %project.9.rest_2_.after_ref), channel_id=1, source_target_pairs={{0,4},{8,12},{4,0},{12,8},{1,5},{9,13},{5,1},{13,9},{2,6},{10,14},... | collective-permute-start | bytes 884744 | tf_op jit(solution)/shard_map/ppermute | solution.py:614
  25.9 7.4 %collective-permute-start.6 = (bf16[2,96,768]{2,1,0:T(8,128)(2,1)S(1)}, bf16[2,96,768]{2,1,0:T(8,128)(2,1)S(1)}, u32[]{:S(2)}, u32[]{:S(2)}) collective-permute-start(bf16[2,96,768]{2,1,0:T(8,128)(2,1)S(1)} %project.9.rest_2_.after_ref), channel_id=1, source_target_pairs={{4,8},{8,4},{5,9},{9,5},{6,10},{10,6},{7,11},{11,7},{20,24},{24,20... | collective-permute-start | bytes 884744 | tf_op jit(solution)/shard_map/ppermute | solution.py:614
  28.2 1.9 %copy-start.5 = (s32[1,3,27]{2,0,1:T(1,128)S(1)}, s32[1,3,27]{2,0,1:T(1,128)}, u32[]{:S(2)}) copy-start(s32[1,3,27]{2,0,1:T(1,128)} %param.15) | copy-start | bytes 976
  31.2 2.1 %copy-start.6 = (s32[768]{0:T(1024)S(1)}, s32[768]{0:T(1024)}, u32[]{:S(2)}) copy-start(s32[768]{0:T(1024)} %param.16) | copy-start | bytes 9220
  32.3 2.3 %copy-start.1 = (f32[5120]{0:T(1024)S(1)}, f32[5120]{0:T(1024)}, u32[]{:S(2)}) copy-start(f32[5120]{0:T(1024)} %param.18) | copy-start | bytes 61444
  35.6 1.9 %collective-permute-start.9 = (bf16[96,2560]{1,0:T(8,128)(2,1)S(1)}, bf16[96,2560]{1,0:T(8,128)(2,1)S(1)}, u32[]{:S(2)}, u32[]{:S(2)}) collective-permute-start(bf16[96,2560]{1,0:T(8,128)(2,1)S(1)} %get-tuple-element.20), channel_id=1, source_target_pairs={{0,1},{1,0},{2,3},{3,2},{4,5},{5,4},{6,7},{7,6},{8,9},{9,8},{10,11... | collective-permute-start | bytes 1474568 | tf_op jit(solution)/shard_map/ppermute | solution.py:542
  37.7 1.9 %collective-permute-start.11 = (bf16[96,2560]{1,0:T(8,128)(2,1)S(1)}, bf16[96,2560]{1,0:T(8,128)(2,1)S(1)}, u32[]{:S(2)}, u32[]{:S(2)}) collective-permute-start(bf16[96,2560]{1,0:T(8,128)(2,1)S(1)} %tie.5), channel_id=1, source_target_pairs={{0,1},{1,0},{2,3},{3,2},{4,5},{5,4},{6,7},{7,6},{8,9},{9,8},{10,11... | collective-permute-start | bytes 1474568 | tf_op jit(solution)/shard_map/ppermute | solution.py:542
  37.9 8.8 %collective-permute-start.10 = (bf16[48,2560]{1,0:T(8,128)(2,1)S(1)}, bf16[48,2560]{1,0:T(8,128)(2,1)S(1)}, u32[]{:S(2)}, u32[]{:S(2)}) collective-permute-start(bf16[48,2560]{1,0:T(8,128)(2,1)S(1)} %slice.25.refs_1_), channel_id=1, source_target_pairs={{0,2},{1,3},{2,0},{3,1},{4,6},{5,7},{6,4},{7,5},{8,10},{9,11},{10,... | collective-permute-start | bytes 737288 | tf_op jit(solution)/shard_map/ppermute | solution.py:542
  39.6 11.8 %copy-start.4 = (s32[5120]{0:T(1024)S(1)}, s32[5120]{0:T(1024)}, u32[]{:S(2)}) copy-start(s32[5120]{0:T(1024)} %param.19) | copy-start | bytes 61444
  39.8 11.6 %collective-permute-start.12 = (bf16[48,2560]{1,0:T(8,128)(2,1)S(1)}, bf16[48,2560]{1,0:T(8,128)(2,1)S(1)}, u32[]{:S(2)}, u32[]{:S(2)}) collective-permute-start(bf16[48,2560]{1,0:T(8,128)(2,1)S(1)} %slice.24), channel_id=1, source_target_pairs={{0,2},{1,3},{2,0},{3,1},{4,6},{5,7},{6,4},{7,5},{8,10},{9,11},{10,... | collective-permute-start | bytes 737288 | tf_op jit(solution)/shard_map/ppermute | solution.py:542

commit v5 on v4

--- a/solution.py
+++ b/solution.py
@@ -113,6 +113,16 @@
     for first in range(0, words.shape[0], WORDS):
         blocks += pieces_of(words[first : first + WORDS], order)
     return jnp.concatenate(blocks, 0)
+
+
+def product(rows, words_ref, at, cols, order, total):
+    words = rows.shape[1] // PLANES
+    step = 2 * WORDS if words % (2 * WORDS) == 0 else WORDS
+    for first in range(0, words, step):
+        weights = decode(words_ref[(*at, slice(first, first + step), cols)], order)
+        part = rows[:, first * PLANES : (first + step) * PLANES]
+        total = total + jnp.dot(part, weights, preferred_element_type=f32)
+    return total
 
 
 def row_correction(row_list, order):
@@ -220,19 +230,18 @@
     width = tile_width(columns)
     late_ref[...] = shard_refs[0][late_ref.shape[0] :, :]
 
-    def product(kind, carry):
+    def every_shard(kind, carry):
         for position in range(len(near)):
             fetch(position, kind).wait()
         for first in range(0, columns, width):
             cols = slice(first, first + width)
             total = -fix
             for position, ref in enumerate(shard_refs):
-                weights = decode(near_ref[position, kind, :, cols], QKV_ORDER)
-                total = total + jnp.dot(ref[...], weights, preferred_element_type=f32)
+                total = product(ref[...], near_ref, (position, kind), cols, QKV_ORDER, total)
             sums_ref[kind, :, cols] = total
         return carry
 
-    lax.fori_loop(0, 3, product, 0)
+    lax.fori_loop(0, 3, every_shard, 0)
     for position in range(len(near), len(near + far)):
         for kind in range(3):
             fetch(position, kind).wait()
@@ -283,8 +292,7 @@
             cols = slice(first, first + width)
             part = (sums_ref[kind, rows, cols] if whole else sums_ref[place, :, cols]) - fix
             for shard, position in zip(shards, positions):
-                weights = decode(words_ref[position, kind, :, cols], QKV_ORDER)
-                part = part + jnp.dot(shard, weights, preferred_element_type=f32)
+                part = product(shard, words_ref, (position, kind), cols, QKV_ORDER, part)
             if not ending:
                 out_ref[place, :, cols] = part
                 continue
@@ -498,10 +506,10 @@
     )
 
 
-def finish_kernel(chunks, sign_ref, *rest):
-    out_hbm, done_ref, sems = rest[2 * chunks :]
+def finish_kernel(chunks, first, sign_ref, *rest):
+    out_hbm, done_ref, sems = rest[-3:]
     doubled = double_hadamard()
-    first, copies = 0, []
+    copies = []
     for chunk in range(chunks):
         keep_ref, more_ref = rest[2 * chunk : 2 * chunk + 2]
         share, columns = keep_ref.shape
@@ -523,17 +531,24 @@
         copy.wait()
 
 
-def finish(pairs, sign_rows):
+def finish(pairs, sign_rows, first, base):
     share = pairs[0][0].shape[0]
     args = [sign_rows] + [array for pair in pairs for array in pair]
-    return call(
-        functools.partial(finish_kernel, len(pairs)),
+    in_specs = [VMEM] * len(args)
+    aliases = {}
+    if base is not None:
+        aliases = {len(args): 0}
+        args.append(base)
+        in_specs.append(HBM)
+    return call(
+        functools.partial(finish_kernel, len(pairs), first),
         shape_of((share, D), bf16),
-        [VMEM] * len(args),
+        in_specs,
         args,
         "finish",
         out_specs=HBM,
         scratch_shapes=[pltpu.VMEM((share, D), bf16), pltpu.SemaphoreType.DMA((len(pairs),))],
+        input_output_aliases=aliases,
     )
 
 
@@ -653,7 +668,8 @@
             sums_sent.append(part)
         pairs.append((keep, more))
         first += columns
-    return finish(pairs, sign_rows)[None]
+    base = finish(pairs[:-1], sign_rows, 0, None)
+    return finish(pairs[-1:], sign_rows, D - CHUNKS[-1], base)[None]
 
 
 def solution(mesh):

time: 53.8 us -> 55.1 us (1.024); the launches traced: 52.8 us -> 54.9 us
  starting transfers between devices: 12.5 us -> 17.7 us
  waiting for transfers between devices: 17.2 us -> 13.3 us
  Pallas kernels: 22.2 us -> 23 us
    ppermute x9, waiting for transfers between devices: 16.2 us -> 11.8 us  [swap(): return lax.ppermute(shard, 'head', [(i, i ^ bit) for i in range(peers)])]
    ppermute x4, starting transfers between devices: 6.11 us -> 9.46 us  [on_device(): lax.ppermute(key_value, 'height', pairs)]
    ppermute x9, starting transfers between devices: 6.41 us -> 8.23 us  [swap(): return lax.ppermute(shard, 'head', [(i, i ^ bit) for i in range(peers)])]
    pallas_call x18 -> x19, Pallas kernels: 22.2 us -> 23 us  [call(): pl.pallas_call(body, out_shape=out_shape, in_specs=in_specs, out_specs=ou...]
    ppermute x4, waiting for transfers between devices: 0.98 us -> 1.55 us  [on_device(): lax.ppermute(key_value, 'height', pairs)]
  transfers between devices with their start and end apart: 13 -> 13, of which waited for: 8 -> 7; matrix products, arithmetic and copies ran while one was open for 0% -> 0% of each run, Pallas kernels for 32% -> 32%
where the time goes in v5:
time: 55.1 us; the launch traced here: 54.9 us
  Pallas kernels  23 us (42%)
  starting transfers between devices  17.7 us (32%)
  waiting for transfers between devices  13.3 us (24%)
    pallas_call x19, Pallas kernels, call(): pl.pallas_call(body, out_shape=out_shape, in_specs=in_specs, out_specs=ou...  23 us
    ppermute x9, waiting for transfers between devices, swap(): return lax.ppermute(shard, 'head', [(i, i ^ bit) for i in range(peers)])  11.8 us
    ppermute x4, starting transfers between devices, on_device(): lax.ppermute(key_value, 'height', pairs)  9.46 us
    ppermute x9, starting transfers between devices, swap(): return lax.ppermute(shard, 'head', [(i, i ^ bit) for i in range(peers)])  8.23 us
    ppermute x4, waiting for transfers between devices, on_device(): lax.ppermute(key_value, 'height', pairs)  1.55 us
  transfers between devices with their start and end apart: 13, of which 7 were waited for; matrix products, arithmetic and copies ran while one was open for 0% of the time, Pallas kernels for 32%

profile of v5, /device:TPU:0, one launch (start us, length us, event | category | flops | bytes accessed | tf_op | source)
XLA Modules:
  0.0 54.9 jit_solution(4069493100679658007)
XLA Ops:
  0.1 1.9 %turn.1 = (bf16[192,1280]{1,0:T(8,128)(2,1)S(1)}, bf16[96,1280]{1,0:T(8,128)(2,1)S(1)}) custom-call(s32[2]{0:T(128)S(1)} %pad_add_fusion.place_ref, bf16[192,1280]{1,0:T(8,128)(2,1)} %bitcast.19, s32[40,128]{1,0:T(8,128)} %bitcast.20), custom_call_target="tpu_custom_call" | custom-call | flops 1 | bytes 1 | tf_op jit(solution)/shard_map/turn/pallas_call | solution.py:43
  2.5 2.6 %collective-permute-start = (bf16[96,1280]{1,0:T(8,128)(2,1)S(1)}, bf16[96,1280]{1,0:T(8,128)(2,1)S(1)}, u32[]{:S(2)}, u32[]{:S(2)}) collective-permute-start(bf16[96,1280]{1,0:T(8,128)(2,1)S(1)} %get-tuple-element.14), channel_id=1, source_target_pairs={{0,2},{1,3},{2,0},{3,1},{4,6},{5,7},{6,4},{7,5},{8,10},{9,11},{10,... | collective-permute-start | bytes 737288 | tf_op jit(solution)/shard_map/ppermute | solution.py:557
  5.0 5.0 %prepare.1 = (f32[3,192,768]{2,1,0:T(8,128)S(1)}, s32[2,3,160,768]{3,2,1,0:T(8,128)S(1)}, bf16[96,1280]{1,0:T(8,128)(2,1)S(1)}) custom-call(s32[2]{0:T(128)S(1)} %pad_add_fusion.place_ref, bf16[192,1280]{1,0:T(8,128)(2,1)S(1)} %get-tuple-element.15.rest_0_, bf16[192,1280]{1,0:T(8,128)(2,1)S(1)} %collective-permute-done.1.rest_1_, s32[3,640,768]{2,1,0:T(8,128)} %bitcast.18), custom_call_target="tpu_custom_call" | custom-call | flops 1 | bytes 1 | tf_op jit(solution)/shard_map/prepare/pallas_call | solution.py:43
  10.1 1.5 %collective-permute-done.refs_0_ = bf16[96,1280]{1,0:T(8,128)(2,1)S(1)} collective-permute-done((bf16[96,1280]{1,0:T(8,128)(2,1)S(1)}, bf16[96,1280]{1,0:T(8,128)(2,1)S(1)}, u32[]{:S(2)}, u32[]{:S(2)}) %collective-permute-start) | collective-permute-done | bytes 245792 | tf_op jit(solution)/shard_map/ppermute | solution.py:557
  11.6 1.8 %collective-permute-start.3 = (bf16[96,1280]{1,0:T(8,128)(2,1)S(1)}, bf16[96,1280]{1,0:T(8,128)(2,1)S(1)}, u32[]{:S(2)}, u32[]{:S(2)}) collective-permute-start(bf16[96,1280]{1,0:T(8,128)(2,1)S(1)} %get-tuple-element.17), channel_id=1, source_target_pairs={{0,2},{1,3},{2,0},{3,1},{4,6},{5,7},{6,4},{7,5},{8,10},{9,11},{10,... | collective-permute-start | bytes 737288 | tf_op jit(solution)/shard_map/ppermute | solution.py:557
  13.4 1.2 %project.5.rest_1_ = f32[2,96,768]{2,1,0:T(8,128)S(1)} custom-call(bf16[96,1280]{1,0:T(8,128)(2,1)S(1)} %tie.3.rest_0_, f32[3,192,768]{2,1,0:T(8,128)S(1)} %get-tuple-element.16.refs_1_.rest_1_.refs_2_.rest_4_, s32[2,3,160,768]{3,2,1,0:T(8,128)S(1)} %get-tuple-element.18.rest_2_.rest_5_), custom_call_target="tpu_custom_call" | custom-call | flops 4000000000 | bytes 1 | tf_op jit(solution)/shard_map/project/pallas_call | solution.py:43
  14.6 1.5 %project.6.array_ref.rest_1_ = bf16[2,96,768]{2,1,0:T(8,128)(2,1)S(1)} custom-call(bf16[96,1280]{1,0:T(8,128)(2,1)S(1)} %collective-permute-done.2.rest_0_.rest_1_, f32[2,96,768]{2,1,0:T(8,128)S(1)} %project.5.rest_1_, s32[2,3,160,768]{3,2,1,0:T(8,128)S(1)} %get-tuple-element.18.rest_2_.rest_5_, f32[3,768]{1,0:T(4,128)S(1)} %copy-done.3, s32[3,768]{1,0:T(4,128)S(1)} %copy-done.4), custom_call_target="tpu_custom_call" | custom-call | flops 1 | bytes 1 | tf_op jit(solution)/shard_map/project/pallas_call | solution.py:43
  16.7 4.4 %collective-permute-start.7 = (bf16[2,96,768]{2,1,0:T(8,128)(2,1)S(1)}, bf16[2,96,768]{2,1,0:T(8,128)(2,1)S(1)}, u32[]{:S(2)}, u32[]{:S(2)}) collective-permute-start(bf16[2,96,768]{2,1,0:T(8,128)(2,1)S(1)} %project.6.array_ref.rest_1_), channel_id=1, source_target_pairs={{0,4},{8,12},{4,0},{12,8},{1,5},{9,13},{5,1},{13,9},{2,6},{10,14},... | collective-permute-start | bytes 884744 | tf_op jit(solution)/shard_map/ppermute | solution.py:629
  21.2 1.2 %project.8.rest_1_ = f32[2,96,768]{2,1,0:T(8,128)S(1)} custom-call(bf16[96,1280]{1,0:T(8,128)(2,1)S(1)} %tie.4.rest_2_.rest_0_, f32[3,192,768]{2,1,0:T(8,128)S(1)} %get-tuple-element.16.refs_1_.rest_1_.refs_2_.rest_4_, s32[2,3,160,768]{3,2,1,0:T(8,128)S(1)} %get-tuple-element.18.rest_2_.rest_5_), custom_call_target="tpu_custom_call" | custom-call | flops 4000000000 | bytes 1 | tf_op jit(solution)/shard_map/project/pallas_call | solution.py:43
  22.7 1.5 %project.9.rest_2_.after_ref = bf16[2,96,768]{2,1,0:T(8,128)(2,1)S(1)} custom-call(bf16[96,1280]{1,0:T(8,128)(2,1)S(1)} %collective-permute-done.4.rest_3_.rest_0_, f32[2,96,768]{2,1,0:T(8,128)S(1)} %project.8.rest_1_, s32[2,3,160,768]{3,2,1,0:T(8,128)S(1)} %get-tuple-element.18.rest_2_.rest_5_, f32[3,768]{1,0:T(4,128)S(1)} %copy-done.3, s32[3,768]{1,0:T(4,128)S(1)} %copy-done.4), custom_call_target="tpu_custom_call" | custom-call | flops 1 | bytes 1 | tf_op jit(solution)/shard_map/project/pallas_call | solution.py:43
  25.1 3.5 %collective-permute-start.5 = (bf16[2,96,768]{2,1,0:T(8,128)(2,1)S(1)}, bf16[2,96,768]{2,1,0:T(8,128)(2,1)S(1)}, u32[]{:S(2)}, u32[]{:S(2)}) collective-permute-start(bf16[2,96,768]{2,1,0:T(8,128)(2,1)S(1)} %project.9.rest_2_.after_ref), channel_id=1, source_target_pairs={{0,4},{8,12},{4,0},{12,8},{1,5},{9,13},{5,1},{13,9},{2,6},{10,14},... | collective-permute-start | bytes 884744 | tf_op jit(solution)/shard_map/ppermute | solution.py:629
  28.5 1.4 %unpack_out.1.weights_ref = bf16[768,5120]{1,0:T(8,128)(2,1)S(1)} custom-call(s32[96,5120]{1,0:T(8,128)S(1)} %copy-done, bf16[2,96,768]{2,1,0:T(8,128)(2,1)S(1)} %project.9.rest_2_.after_ref), custom_call_target="tpu_custom_call" | custom-call | flops 1 | bytes 1 | tf_op jit(solution)/shard_map/unpack_out/pallas_call | solution.py:43
  30.0 1.8 %project.7.rest_0_ = bf16[1,192,768]{2,1,0:T(8,128)(2,1)S(1)} custom-call(bf16[96,1280]{1,0:T(8,128)(2,1)S(1)} %tie.3.rest_0_, bf16[96,1280]{1,0:T(8,128)(2,1)S(1)} %collective-permute-done.2.rest_0_.rest_1_, bf16[96,1280]{1,0:T(8,128)(2,1)S(1)} %tie.4.rest_2_.rest_0_, bf16[96,1280]{1,0:T(8,128)(2,1)S(1)} %collective-permute-done.4.rest_3_.rest_0_, ...), custom_call_target="tpu_custom_call" | custom-call | flops 4000000000 | bytes 1 | tf_op jit(solution)/shard_map/project/pallas_call | solution.py:43
  31.9 1.1 %attend.3.rest_3_ = f32[6,192,256]{2,1,0:T(8,128)S(1)} custom-call(s32[2]{0:T(128)S(1)} %pad_add_fusion.place_ref, s32[3,1,27]{2,1,0:T(1,128)S(1)} %bitcast.14, bf16[1,192,768]{2,1,0:T(8,128)(2,1)S(1)} %project.7.rest_0_, bf16[2,96,768]{2,1,0:T(8,128)(2,1)S(1)} %project.6.array_ref.rest_1_, bf16[2,96,768]{2,1,0:T(8,128)(2,1)S(1)} %project.9.rest_2_.after_ref), custom_call_target="tpu_custom_call" | custom-call | flops 1 | bytes 1 | tf_op jit(solution)/shard_map/attend/pallas_call | solution.py:43
  33.0 1.1 %attend.4.rest_3_ = f32[6,192,256]{2,1,0:T(8,128)S(1)} custom-call(s32[2]{0:T(128)S(1)} %pad_add_fusion.place_ref, s32[3,1,27]{2,1,0:T(1,128)S(1)} %bitcast.15, bf16[1,192,768]{2,1,0:T(8,128)(2,1)S(1)} %project.7.rest_0_, bf16[2,96,768]{2,1,0:T(8,128)(2,1)S(1)} %collective-permute-done.7.rest_1_, bf16[2,96,768]{2,1,0:T(8,128)(2,1)S(1)} %collective-permute-done.8.rest_2_, ...), custom_call_target="tpu_custom_call" | custom-call | flops 1 | bytes 1 | tf_op jit(solution)/shard_map/attend/pallas_call | solution.py:43
  34.1 1.5 %collective-permute-done.5.rest_1_ = bf16[2,96,768]{2,1,0:T(8,128)(2,1)S(1)} collective-permute-done((bf16[2,96,768]{2,1,0:T(8,128)(2,1)S(1)}, bf16[2,96,768]{2,1,0:T(8,128)(2,1)S(1)}, u32[]{:S(2)}, u32[]{:S(2)}) %collective-permute-start.5) | collective-permute-done | bytes 294944 | tf_op jit(solution)/shard_map/ppermute | solution.py:629
  35.6 1.3 %attend.5.rotated_ref = bf16[192,768]{1,0:T(8,128)(2,1)S(1)} custom-call(s32[2]{0:T(128)S(1)} %pad_add_fusion.place_ref, s32[3,1,27]{2,1,0:T(1,128)S(1)} %bitcast.16, bf16[1,192,768]{2,1,0:T(8,128)(2,1)S(1)} %project.7.rest_0_, bf16[2,96,768]{2,1,0:T(8,128)(2,1)S(1)} %collective-permute-done.5.rest_1_, ...), custom_call_target="tpu_custom_call" | custom-call | flops 1 | bytes 1 | tf_op jit(solution)/shard_map/attend/pallas_call | solution.py:43
  38.0 1.0 %out_project.2 = (bf16[96,2560]{1,0:T(8,128)(2,1)S(1)}, bf16[96,2560]{1,0:T(8,128)(2,1)S(1)}) custom-call(bf16[192,768]{1,0:T(8,128)(2,1)S(1)} %attend.5.rotated_ref, bf16[768,5120]{1,0:T(8,128)(2,1)S(1)} %unpack_out.1.weights_ref, f32[40,128]{1,0:T(8,128)S(1)} %bitcast.11), custom_call_target="tpu_custom_call" | custom-call | flops 1 | bytes 1 | tf_op jit(solution)/shard_map/out_project/pallas_call | solution.py:43
  40.3 1.5 %collective-permute-start.12 = (bf16[48,2560]{1,0:T(8,128)(2,1)S(1)}, bf16[48,2560]{1,0:T(8,128)(2,1)S(1)}, u32[]{:S(2)}, u32[]{:S(2)}) collective-permute-start(bf16[48,2560]{1,0:T(8,128)(2,1)S(1)} %slice.25.refs_1_), channel_id=1, source_target_pairs={{0,2},{1,3},{2,0},{3,1},{4,6},{5,7},{6,4},{7,5},{8,10},{9,11},{10,... | collective-permute-start | bytes 737288 | tf_op jit(solution)/shard_map/ppermute | solution.py:557
  42.1 1.6 %collective-permute-start.11 = (bf16[48,2560]{1,0:T(8,128)(2,1)S(1)}, bf16[48,2560]{1,0:T(8,128)(2,1)S(1)}, u32[]{:S(2)}, u32[]{:S(2)}) collective-permute-start(bf16[48,2560]{1,0:T(8,128)(2,1)S(1)} %slice.24), channel_id=1, source_target_pairs={{0,2},{1,3},{2,0},{3,1},{4,6},{5,7},{6,4},{7,5},{8,10},{9,11},{10,... | collective-permute-start | bytes 737288 | tf_op jit(solution)/shard_map/ppermute | solution.py:557
  43.8 5.3 %collective-permute-done.12.rest_1_ = bf16[48,2560]{1,0:T(8,128)(2,1)S(1)} collective-permute-done((bf16[48,2560]{1,0:T(8,128)(2,1)S(1)}, bf16[48,2560]{1,0:T(8,128)(2,1)S(1)}, u32[]{:S(2)}, u32[]{:S(2)}) %collective-permute-start.12) | collective-permute-done | bytes 245792 | tf_op jit(solution)/shard_map/ppermute | solution.py:557
  49.0 1.0 %finish.2.rest_2_ = bf16[48,5120]{1,0:T(8,128)(2,1)} custom-call(s32[40,128]{1,0:T(8,128)S(1)} %bitcast.12, f32[48,2560]{1,0:T(8,128)S(1)} %slice.21.rest_0_, bf16[48,2560]{1,0:T(8,128)(2,1)S(1)} %collective-permute-done.12.rest_1_), custom_call_target="tpu_custom_call" | custom-call | flops 1 | bytes 1 | tf_op jit(solution)/shard_map/finish/pallas_call | solution.py:43
  50.1 3.6 %collective-permute-done.11.rest_1_ = bf16[48,2560]{1,0:T(8,128)(2,1)S(1)} collective-permute-done((bf16[48,2560]{1,0:T(8,128)(2,1)S(1)}, bf16[48,2560]{1,0:T(8,128)(2,1)S(1)}, u32[]{:S(2)}, u32[]{:S(2)}) %collective-permute-start.11) | collective-permute-done | bytes 245792 | tf_op jit(solution)/shard_map/ppermute | solution.py:557
  53.8 1.0 %finish.3 = bf16[48,5120]{1,0:T(8,128)(2,1)} custom-call(s32[40,128]{1,0:T(8,128)S(1)} %bitcast.13, f32[48,2560]{1,0:T(8,128)S(1)} %slice.19.rest_0_, bf16[48,2560]{1,0:T(8,128)(2,1)S(1)} %collective-permute-done.11.rest_1_, bf16[48,5120]{1,0:T(8,128)(2,1)} %finish.2.rest_2_), custom_call_target="tpu_custom_call", output_to_operand_aliasing={{}: (3, {})} | custom-call | flops 1 | bytes 1 | tf_op jit(solution)/shard_map/finish/pallas_call | solution.py:43
  (42 shorter events, 5.1 us)
Async XLA Ops:
  2.0 3.1 %collective-permute-start.1 = (bf16[192,1280]{1,0:T(8,128)(2,1)S(1)}, bf16[192,1280]{1,0:T(8,128)(2,1)S(1)}, u32[]{:S(2)}, u32[]{:S(2)}) collective-permute-start(bf16[192,1280]{1,0:T(8,128)(2,1)S(1)} %get-tuple-element.15.rest_0_), channel_id=1, source_target_pairs={{0,1},{1,0},{2,3},{3,2},{4,5},{5,4},{6,7},{7,6},{8,9},{9,8},{10,11... | collective-permute-start | bytes 1474568 | tf_op jit(solution)/shard_map/ppermute | solution.py:557
  2.5 9.1 %collective-permute-start = (bf16[96,1280]{1,0:T(8,128)(2,1)S(1)}, bf16[96,1280]{1,0:T(8,128)(2,1)S(1)}, u32[]{:S(2)}, u32[]{:S(2)}) collective-permute-start(bf16[96,1280]{1,0:T(8,128)(2,1)S(1)} %get-tuple-element.14), channel_id=1, source_target_pairs={{0,2},{1,3},{2,0},{3,1},{4,6},{5,7},{6,4},{7,5},{8,10},{9,11},{10,... | collective-permute-start | bytes 737288 | tf_op jit(solution)/shard_map/ppermute | solution.py:557
  11.6 3.0 %collective-permute-start.2 = (bf16[96,1280]{1,0:T(8,128)(2,1)S(1)}, bf16[96,1280]{1,0:T(8,128)(2,1)S(1)}, u32[]{:S(2)}, u32[]{:S(2)}) collective-permute-start(bf16[96,1280]{1,0:T(8,128)(2,1)S(1)} %tie.3.rest_0_), channel_id=1, source_target_pairs={{0,1},{1,0},{2,3},{3,2},{4,5},{5,4},{6,7},{7,6},{8,9},{9,8},{10,11... | collective-permute-start | bytes 737288 | tf_op jit(solution)/shard_map/ppermute | solution.py:557
  11.6 9.6 %collective-permute-start.3 = (bf16[96,1280]{1,0:T(8,128)(2,1)S(1)}, bf16[96,1280]{1,0:T(8,128)(2,1)S(1)}, u32[]{:S(2)}, u32[]{:S(2)}) collective-permute-start(bf16[96,1280]{1,0:T(8,128)(2,1)S(1)} %get-tuple-element.17), channel_id=1, source_target_pairs={{0,2},{1,3},{2,0},{3,1},{4,6},{5,7},{6,4},{7,5},{8,10},{9,11},{10,... | collective-permute-start | bytes 737288 | tf_op jit(solution)/shard_map/ppermute | solution.py:557
  13.4 1.2 %copy-start.3 = (f32[3,768]{1,0:T(4,128)S(1)}, f32[3,768]{1,0:T(4,128)}, u32[]{:S(2)}) copy-start(f32[3,768]{1,0:T(4,128)} %rest_3_.3) | copy-start | bytes 27652
  13.4 1.2 %copy-start.4 = (s32[3,768]{1,0:T(4,128)S(1)}, s32[3,768]{1,0:T(4,128)}, u32[]{:S(2)}) copy-start(s32[3,768]{1,0:T(4,128)} %rest_4_.3) | copy-start | bytes 27652
  16.1 16.9 %collective-permute-start.8 = (bf16[2,96,768]{2,1,0:T(8,128)(2,1)S(1)}, bf16[2,96,768]{2,1,0:T(8,128)(2,1)S(1)}, u32[]{:S(2)}, u32[]{:S(2)}) collective-permute-start(bf16[2,96,768]{2,1,0:T(8,128)(2,1)S(1)} %project.6.array_ref.rest_1_), channel_id=1, source_target_pairs={{4,8},{8,4},{5,9},{9,5},{6,10},{10,6},{7,11},{11,7},{20,24},{24,20... | collective-permute-start | bytes 884744 | tf_op jit(solution)/shard_map/ppermute | solution.py:629
  16.7 16.2 %collective-permute-start.7 = (bf16[2,96,768]{2,1,0:T(8,128)(2,1)S(1)}, bf16[2,96,768]{2,1,0:T(8,128)(2,1)S(1)}, u32[]{:S(2)}, u32[]{:S(2)}) collective-permute-start(bf16[2,96,768]{2,1,0:T(8,128)(2,1)S(1)} %project.6.array_ref.rest_1_), channel_id=1, source_target_pairs={{0,4},{8,12},{4,0},{12,8},{1,5},{9,13},{5,1},{13,9},{2,6},{10,14},... | collective-permute-start | bytes 884744 | tf_op jit(solution)/shard_map/ppermute | solution.py:629
  21.2 1.5 %collective-permute-start.4 = (bf16[96,1280]{1,0:T(8,128)(2,1)S(1)}, bf16[96,1280]{1,0:T(8,128)(2,1)S(1)}, u32[]{:S(2)}, u32[]{:S(2)}) collective-permute-start(bf16[96,1280]{1,0:T(8,128)(2,1)S(1)} %tie.4.rest_2_.rest_0_), channel_id=1, source_target_pairs={{0,1},{1,0},{2,3},{3,2},{4,5},{5,4},{6,7},{7,6},{8,9},{9,8},{10,11... | collective-permute-start | bytes 737288 | tf_op jit(solution)/shard_map/ppermute | solution.py:557
  22.4 6.1 %copy-start = (s32[96,5120]{1,0:T(8,128)S(1)}, s32[96,5120]{1,0:T(8,128)}, u32[]{:S(2)}) copy-start(s32[96,5120]{1,0:T(8,128)} %codes_ref.1) | copy-start | bytes 5898244
  24.2 9.9 %collective-permute-start.6 = (bf16[2,96,768]{2,1,0:T(8,128)(2,1)S(1)}, bf16[2,96,768]{2,1,0:T(8,128)(2,1)S(1)}, u32[]{:S(2)}, u32[]{:S(2)}) collective-permute-start(bf16[2,96,768]{2,1,0:T(8,128)(2,1)S(1)} %project.9.rest_2_.after_ref), channel_id=1, source_target_pairs={{4,8},{8,4},{5,9},{9,5},{6,10},{10,6},{7,11},{11,7},{20,24},{24,20... | collective-permute-start | bytes 884744 | tf_op jit(solution)/shard_map/ppermute | solution.py:629
  25.1 10.6 %collective-permute-start.5 = (bf16[2,96,768]{2,1,0:T(8,128)(2,1)S(1)}, bf16[2,96,768]{2,1,0:T(8,128)(2,1)S(1)}, u32[]{:S(2)}, u32[]{:S(2)}) collective-permute-start(bf16[2,96,768]{2,1,0:T(8,128)(2,1)S(1)} %project.9.rest_2_.after_ref), channel_id=1, source_target_pairs={{0,4},{8,12},{4,0},{12,8},{1,5},{9,13},{5,1},{13,9},{2,6},{10,14},... | collective-permute-start | bytes 884744 | tf_op jit(solution)/shard_map/ppermute | solution.py:629
  30.0 1.9 %copy-start.5 = (s32[1,3,27]{2,0,1:T(1,128)S(1)}, s32[1,3,27]{2,0,1:T(1,128)}, u32[]{:S(2)}) copy-start(s32[1,3,27]{2,0,1:T(1,128)} %param.15) | copy-start | bytes 976
  32.9 2.7 %copy-start.6 = (s32[768]{0:T(1024)S(1)}, s32[768]{0:T(1024)}, u32[]{:S(2)}) copy-start(s32[768]{0:T(1024)} %param.16) | copy-start | bytes 9220
  34.1 2.9 %copy-start.1 = (f32[5120]{0:T(1024)S(1)}, f32[5120]{0:T(1024)}, u32[]{:S(2)}) copy-start(f32[5120]{0:T(1024)} %param.18) | copy-start | bytes 61444
  37.9 1.9 %collective-permute-start.9 = (bf16[96,2560]{1,0:T(8,128)(2,1)S(1)}, bf16[96,2560]{1,0:T(8,128)(2,1)S(1)}, u32[]{:S(2)}, u32[]{:S(2)}) collective-permute-start(bf16[96,2560]{1,0:T(8,128)(2,1)S(1)} %get-tuple-element.22), channel_id=1, source_target_pairs={{0,1},{1,0},{2,3},{3,2},{4,5},{5,4},{6,7},{7,6},{8,9},{9,8},{10,11... | collective-permute-start | bytes 1474568 | tf_op jit(solution)/shard_map/ppermute | solution.py:557
  40.0 9.0 %copy-start.2 = (s32[5120]{0:T(1024)S(1)}, s32[5120]{0:T(1024)}, u32[]{:S(2)}) copy-start(s32[5120]{0:T(1024)} %param.19) | copy-start | bytes 61444
  40.1 1.9 %collective-permute-start.10 = (bf16[96,2560]{1,0:T(8,128)(2,1)S(1)}, bf16[96,2560]{1,0:T(8,128)(2,1)S(1)}, u32[]{:S(2)}, u32[]{:S(2)}) collective-permute-start(bf16[96,2560]{1,0:T(8,128)(2,1)S(1)} %tie.5), channel_id=1, source_target_pairs={{0,1},{1,0},{2,3},{3,2},{4,5},{5,4},{6,7},{7,6},{8,9},{9,8},{10,11... | collective-permute-start | bytes 1474568 | tf_op jit(solution)/shard_map/ppermute | solution.py:557
  40.3 8.8 %collective-permute-start.12 = (bf16[48,2560]{1,0:T(8,128)(2,1)S(1)}, bf16[48,2560]{1,0:T(8,128)(2,1)S(1)}, u32[]{:S(2)}, u32[]{:S(2)}) collective-permute-start(bf16[48,2560]{1,0:T(8,128)(2,1)S(1)} %slice.25.refs_1_), channel_id=1, source_target_pairs={{0,2},{1,3},{2,0},{3,1},{4,6},{5,7},{6,4},{7,5},{8,10},{9,11},{10,... | collective-permute-start | bytes 737288 | tf_op jit(solution)/shard_map/ppermute | solution.py:557
  42.1 11.6 %collective-permute-start.11 = (bf16[48,2560]{1,0:T(8,128)(2,1)S(1)}, bf16[48,2560]{1,0:T(8,128)(2,1)S(1)}, u32[]{:S(2)}, u32[]{:S(2)}) collective-permute-start(bf16[48,2560]{1,0:T(8,128)(2,1)S(1)} %slice.24), channel_id=1, source_target_pairs={{0,2},{1,3},{2,0},{3,1},{4,6},{5,7},{6,4},{7,5},{8,10},{9,11},{10,... | collective-permute-start | bytes 737288 | tf_op jit(solution)/shard_map/ppermute | solution.py:557

commit v6 on v5

--- a/solution.py
+++ b/solution.py
@@ -115,16 +115,6 @@
     return jnp.concatenate(blocks, 0)
 
 
-def product(rows, words_ref, at, cols, order, total):
-    words = rows.shape[1] // PLANES
-    step = 2 * WORDS if words % (2 * WORDS) == 0 else WORDS
-    for first in range(0, words, step):
-        weights = decode(words_ref[(*at, slice(first, first + step), cols)], order)
-        part = rows[:, first * PLANES : (first + step) * PLANES]
-        total = total + jnp.dot(part, weights, preferred_element_type=f32)
-    return total
-
-
 def row_correction(row_list, order):
     factor_row = plane_power(4.0, order) * 1.5
     total = None
@@ -145,6 +135,10 @@
     for width in (256, 128):
         if columns % width == 0:
             return width
+
+
+def early_rows(rows):
+    return rows * 7 // 12 // WORDS * WORDS
 
 
 def turn_kernel(place_ref, x_hbm, sign_hbm, own_ref, send_ref, x_ref, sign_ref, sems):
@@ -175,7 +169,7 @@
     rows, inner = own_tokens.shape
     return call(
         turn_kernel,
-        (shape_of((rows, inner), bf16), shape_of((rows // 2, inner), bf16)),
+        (shape_of((rows, inner), bf16), shape_of((early_rows(rows), inner), bf16)),
         [SMEM, HBM, HBM],
         (place, in_hbm(own_tokens), in_hbm(sign_rows)),
         "turn",
@@ -228,7 +222,7 @@
             fetch(position, kind).start()
     fix = row_correction([ref[...] for ref in shard_refs], QKV_ORDER)
     width = tile_width(columns)
-    late_ref[...] = shard_refs[0][late_ref.shape[0] :, :]
+    late_ref[...] = shard_refs[0][shard_refs[0].shape[0] - late_ref.shape[0] :, :]
 
     def every_shard(kind, carry):
         for position in range(len(near)):
@@ -237,7 +231,8 @@
             cols = slice(first, first + width)
             total = -fix
             for position, ref in enumerate(shard_refs):
-                total = product(ref[...], near_ref, (position, kind), cols, QKV_ORDER, total)
+                weights = decode(near_ref[position, kind, :, cols], QKV_ORDER)
+                total = total + jnp.dot(ref[...], weights, preferred_element_type=f32)
             sums_ref[kind, :, cols] = total
         return carry
 
@@ -256,7 +251,7 @@
         (
             shape_of((3, rows, columns), f32),
             shape_of((len(far), 3, words, columns), jnp.int32),
-            shape_of((rows // 2, inner), bf16),
+            shape_of((rows - early_rows(rows), inner), bf16),
         ),
         [SMEM] + [VMEM] * len(near) + [HBM],
         (place, *shards, in_hbm(codes)),
@@ -292,7 +287,8 @@
             cols = slice(first, first + width)
             part = (sums_ref[kind, rows, cols] if whole else sums_ref[place, :, cols]) - fix
             for shard, position in zip(shards, positions):
-                part = product(shard, words_ref, (position, kind), cols, QKV_ORDER, part)
+                weights = decode(words_ref[position, kind, :, cols], QKV_ORDER)
+                part = part + jnp.dot(shard, weights, preferred_element_type=f32)
             if not ending:
                 out_ref[place, :, cols] = part
                 continue
@@ -560,7 +556,7 @@
 def row_swaps(row_tiles):
     swaps = []
     for by in (1, 3, 4, 5) if row_tiles > HROWS else (1,):
-        for odd in (0, 1):
+        for odd in (1, 0):
             low = [i for i in range(row_tiles - by) if (i // by) % 2 == odd]
             swaps.append((by, odd, [(i, i + by) for i in low] + [(i + by, i) for i in low]))
     return swaps
@@ -634,17 +630,18 @@
     out_weights = unpack_out(out_codes, key_values[1])
 
     listed = jnp.transpose(windows, (1, 0, 2))
-    own_rows = ((None, 0, half_rows), (None, half_rows, half_rows))
-    early_rows = tuple(((by, odd), 0, half_rows) for by, odd, _ in swaps)
-    late_rows = tuple(((by, odd), half_rows, half_rows) for by, odd, _ in swaps)
-    running = attend(place, listed, queries, key_values, own_rows, None, None)
-    running = attend(place, listed, queries, moved[0], early_rows, running, None)
+    late_rows = own.shape[0] - half_rows
+    own_keys = ((None, 0, half_rows), (None, half_rows, late_rows))
+    early_keys = tuple(((by, odd), 0, half_rows) for by, odd, _ in swaps)
+    late_keys = tuple(((by, odd), half_rows, late_rows) for by, odd, _ in swaps)
+    running = attend(place, listed, queries, key_values, own_keys, None, None)
+    running = attend(place, listed, queries, moved[0], early_keys, running, None)
     rotated = attend(
         place,
         listed,
         queries,
         moved[1],
-        late_rows,
+        late_keys,
         running,
         (oin_sign, halving_order(head_count)),
     )

time: 55.1 us -> 52.6 us (0.955)
  the two profiles are of different devices: /device:TPU:0 before, /device:TPU:16 now
where the time goes in v6:
time: 52.6 us; the launch traced here: 52.4 us
  Pallas kernels  23.1 us (44%)
  starting transfers between devices  14.3 us (27%)
  waiting for transfers between devices  14 us (27%)
    pallas_call x19, Pallas kernels, call(): pl.pallas_call(body, out_shape=out_shape, in_specs=in_specs, out_specs=ou...  23.1 us
    ppermute x9, waiting for transfers between devices, swap(): return lax.ppermute(shard, 'head', [(i, i ^ bit) for i in range(peers)])  11.7 us
    ppermute x4, starting transfers between devices, on_device(): lax.ppermute(key_value, 'height', pairs)  7.73 us
    ppermute x9, starting transfers between devices, swap(): return lax.ppermute(shard, 'head', [(i, i ^ bit) for i in range(peers)])  6.57 us
    ppermute x4, waiting for transfers between devices, on_device(): lax.ppermute(key_value, 'height', pairs)  2.36 us
  transfers between devices with their start and end apart: 13, of which 9 were waited for; matrix products, arithmetic and copies ran while one was open for 0% of the time, Pallas kernels for 34%

profile of v6, /device:TPU:16, one launch (start us, length us, event | category | flops | bytes accessed | tf_op | source)
XLA Modules:
  0.0 52.4 jit_solution(334192840926071)
XLA Ops:
  0.1 1.9 %turn.1 = (bf16[192,1280]{1,0:T(8,128)(2,1)S(1)}, bf16[112,1280]{1,0:T(8,128)(2,1)S(1)}) custom-call(s32[2]{0:T(128)S(1)} %pad_add_fusion.place_ref, bf16[192,1280]{1,0:T(8,128)(2,1)} %bitcast.19, s32[40,128]{1,0:T(8,128)} %bitcast.20), custom_call_target="tpu_custom_call" | custom-call | flops 1 | bytes 1 | tf_op jit(solution)/shard_map/turn/pallas_call | solution.py:43
  2.0 1.6 %collective-permute-start = (bf16[112,1280]{1,0:T(8,128)(2,1)S(1)}, bf16[112,1280]{1,0:T(8,128)(2,1)S(1)}, u32[]{:S(2)}, u32[]{:S(2)}) collective-permute-start(bf16[112,1280]{1,0:T(8,128)(2,1)S(1)} %get-tuple-element.14), channel_id=1, source_target_pairs={{0,2},{1,3},{2,0},{3,1},{4,6},{5,7},{6,4},{7,5},{8,10},{9,11},{10,... | collective-permute-start | bytes 860168 | tf_op jit(solution)/shard_map/ppermute | solution.py:553
  3.9 5.0 %prepare.1 = (f32[3,192,768]{2,1,0:T(8,128)S(1)}, s32[2,3,160,768]{3,2,1,0:T(8,128)S(1)}, bf16[80,1280]{1,0:T(8,128)(2,1)S(1)}) custom-call(s32[2]{0:T(128)S(1)} %pad_add_fusion.place_ref, bf16[192,1280]{1,0:T(8,128)(2,1)S(1)} %get-tuple-element.15.rest_0_, bf16[192,1280]{1,0:T(8,128)(2,1)S(1)} %collective-permute-done.1.rest_1_, s32[3,640,768]{2,1,0:T(8,128)} %bitcast.18), custom_call_target="tpu_custom_call" | custom-call | flops 1 | bytes 1 | tf_op jit(solution)/shard_map/prepare/pallas_call | solution.py:43
  8.9 1.6 %collective-permute-start.3 = (bf16[80,1280]{1,0:T(8,128)(2,1)S(1)}, bf16[80,1280]{1,0:T(8,128)(2,1)S(1)}, u32[]{:S(2)}, u32[]{:S(2)}) collective-permute-start(bf16[80,1280]{1,0:T(8,128)(2,1)S(1)} %get-tuple-element.17), channel_id=1, source_target_pairs={{0,2},{1,3},{2,0},{3,1},{4,6},{5,7},{6,4},{7,5},{8,10},{9,11},{10,... | collective-permute-start | bytes 614408 | tf_op jit(solution)/shard_map/ppermute | solution.py:553
  11.3 1.3 %project.5.rest_1_ = f32[2,112,768]{2,1,0:T(8,128)S(1)} custom-call(bf16[112,1280]{1,0:T(8,128)(2,1)S(1)} %tie.3.rest_0_, f32[3,192,768]{2,1,0:T(8,128)S(1)} %get-tuple-element.16.refs_1_.rest_1_.refs_2_.rest_4_, s32[2,3,160,768]{3,2,1,0:T(8,128)S(1)} %get-tuple-element.18.rest_2_.rest_5_), custom_call_target="tpu_custom_call" | custom-call | flops 4000000000 | bytes 1 | tf_op jit(solution)/shard_map/project/pallas_call | solution.py:43
  12.9 1.5 %project.6.array_ref.rest_1_ = bf16[2,112,768]{2,1,0:T(8,128)(2,1)S(1)} custom-call(bf16[112,1280]{1,0:T(8,128)(2,1)S(1)} %collective-permute-done.2.rest_0_.rest_1_, f32[2,112,768]{2,1,0:T(8,128)S(1)} %project.5.rest_1_, s32[2,3,160,768]{3,2,1,0:T(8,128)S(1)} %get-tuple-element.18.rest_2_.rest_5_, f32[3,768]{1,0:T(4,128)S(1)} %copy-done.3, ...), custom_call_target="tpu_custom_call" | custom-call | flops 1 | bytes 1 | tf_op jit(solution)/shard_map/project/pallas_call | solution.py:43
  14.4 1.6 %collective-permute-start.8 = (bf16[2,112,768]{2,1,0:T(8,128)(2,1)S(1)}, bf16[2,112,768]{2,1,0:T(8,128)(2,1)S(1)}, u32[]{:S(2)}, u32[]{:S(2)}) collective-permute-start(bf16[2,112,768]{2,1,0:T(8,128)(2,1)S(1)} %project.6.array_ref.rest_1_), channel_id=1, source_target_pairs={{0,4},{8,12},{4,0},{12,8},{1,5},{9,13},{5,1},{13,9},{2,6},{10,14},... | collective-permute-start | bytes 1032200 | tf_op jit(solution)/shard_map/ppermute | solution.py:625
  16.0 1.9 %collective-permute-start.7 = (bf16[2,112,768]{2,1,0:T(8,128)(2,1)S(1)}, bf16[2,112,768]{2,1,0:T(8,128)(2,1)S(1)}, u32[]{:S(2)}, u32[]{:S(2)}) collective-permute-start(bf16[2,112,768]{2,1,0:T(8,128)(2,1)S(1)} %project.6.array_ref.rest_1_), channel_id=1, source_target_pairs={{4,8},{8,4},{5,9},{9,5},{6,10},{10,6},{7,11},{11,7},{20,24},{24,20... | collective-permute-start | bytes 1032200 | tf_op jit(solution)/shard_map/ppermute | solution.py:625
  18.1 1.2 %project.8.rest_1_ = f32[2,80,768]{2,1,0:T(8,128)S(1)} custom-call(bf16[80,1280]{1,0:T(8,128)(2,1)S(1)} %tie.4.rest_2_.rest_0_, f32[3,192,768]{2,1,0:T(8,128)S(1)} %get-tuple-element.16.refs_1_.rest_1_.refs_2_.rest_4_, s32[2,3,160,768]{3,2,1,0:T(8,128)S(1)} %get-tuple-element.18.rest_2_.rest_5_), custom_call_target="tpu_custom_call" | custom-call | flops 4000000000 | bytes 1 | tf_op jit(solution)/shard_map/project/pallas_call | solution.py:43
  19.5 1.4 %project.9.rest_2_.after_ref = bf16[2,80,768]{2,1,0:T(8,128)(2,1)S(1)} custom-call(bf16[80,1280]{1,0:T(8,128)(2,1)S(1)} %collective-permute-done.4.rest_3_.rest_0_, f32[2,80,768]{2,1,0:T(8,128)S(1)} %project.8.rest_1_, s32[2,3,160,768]{3,2,1,0:T(8,128)S(1)} %get-tuple-element.18.rest_2_.rest_5_, f32[3,768]{1,0:T(4,128)S(1)} %copy-done.3, s32[3,768]{1,0:T(4,128)S(1)} %copy-done.4), custom_call_target="tpu_custom_call" | custom-call | flops 1 | bytes 1 | tf_op jit(solution)/shard_map/project/pallas_call | solution.py:43
  21.0 4.1 %collective-permute-start.5 = (bf16[2,80,768]{2,1,0:T(8,128)(2,1)S(1)}, bf16[2,80,768]{2,1,0:T(8,128)(2,1)S(1)}, u32[]{:S(2)}, u32[]{:S(2)}) collective-permute-start(bf16[2,80,768]{2,1,0:T(8,128)(2,1)S(1)} %project.9.rest_2_.after_ref), channel_id=1, source_target_pairs={{4,8},{8,4},{5,9},{9,5},{6,10},{10,6},{7,11},{11,7},{20,24},{24,20... | collective-permute-start | bytes 737288 | tf_op jit(solution)/shard_map/ppermute | solution.py:625
  25.2 1.5 %unpack_out.1.weights_ref = bf16[768,5120]{1,0:T(8,128)(2,1)S(1)} custom-call(s32[96,5120]{1,0:T(8,128)S(1)} %copy-done, bf16[2,80,768]{2,1,0:T(8,128)(2,1)S(1)} %project.9.rest_2_.after_ref), custom_call_target="tpu_custom_call" | custom-call | flops 1 | bytes 1 | tf_op jit(solution)/shard_map/unpack_out/pallas_call | solution.py:43
  26.6 1.8 %project.7.rest_0_ = bf16[1,192,768]{2,1,0:T(8,128)(2,1)S(1)} custom-call(bf16[112,1280]{1,0:T(8,128)(2,1)S(1)} %tie.3.rest_0_, bf16[112,1280]{1,0:T(8,128)(2,1)S(1)} %collective-permute-done.2.rest_0_.rest_1_, bf16[80,1280]{1,0:T(8,128)(2,1)S(1)} %tie.4.rest_2_.rest_0_, bf16[80,1280]{1,0:T(8,128)(2,1)S(1)} %collective-permute-done.4.rest_3_.rest_0_, ...), custom_call_target="tpu_custom_call" | custom-call | flops 4000000000 | bytes 1 | tf_op jit(solution)/shard_map/project/pallas_call | solution.py:43
  28.5 1.1 %attend.3.rest_3_ = f32[6,192,256]{2,1,0:T(8,128)S(1)} custom-call(s32[2]{0:T(128)S(1)} %pad_add_fusion.place_ref, s32[3,1,27]{2,1,0:T(1,128)S(1)} %bitcast.14, bf16[1,192,768]{2,1,0:T(8,128)(2,1)S(1)} %project.7.rest_0_, bf16[2,112,768]{2,1,0:T(8,128)(2,1)S(1)} %project.6.array_ref.rest_1_, bf16[2,80,768]{2,1,0:T(8,128)(2,1)S(1)} %project.9.rest_2_.after_ref), custom_call_target="tpu_custom_call" | custom-call | flops 1 | bytes 1 | tf_op jit(solution)/shard_map/attend/pallas_call | solution.py:43
  29.6 1.1 %attend.4.rest_3_ = f32[6,192,256]{2,1,0:T(8,128)S(1)} custom-call(s32[2]{0:T(128)S(1)} %pad_add_fusion.place_ref, s32[3,1,27]{2,1,0:T(1,128)S(1)} %bitcast.15, bf16[1,192,768]{2,1,0:T(8,128)(2,1)S(1)} %project.7.rest_0_, bf16[2,112,768]{2,1,0:T(8,128)(2,1)S(1)} %collective-permute-done.7.rest_1_, bf16[2,112,768]{2,1,0:T(8,128)(2,1)S(1)} %collective-permute-done.8.rest_2_, ...), custom_call_target="tpu_custom_call" | custom-call | flops 1 | bytes 1 | tf_op jit(solution)/shard_map/attend/pallas_call | solution.py:43
  30.8 2.4 %collective-permute-done.5.rest_1_ = bf16[2,80,768]{2,1,0:T(8,128)(2,1)S(1)} collective-permute-done((bf16[2,80,768]{2,1,0:T(8,128)(2,1)S(1)}, bf16[2,80,768]{2,1,0:T(8,128)(2,1)S(1)}, u32[]{:S(2)}, u32[]{:S(2)}) %collective-permute-start.5) | collective-permute-done | bytes 245792 | tf_op jit(solution)/shard_map/ppermute | solution.py:625
  33.1 1.3 %attend.5.rotated_ref = bf16[192,768]{1,0:T(8,128)(2,1)S(1)} custom-call(s32[2]{0:T(128)S(1)} %pad_add_fusion.place_ref, s32[3,1,27]{2,1,0:T(1,128)S(1)} %bitcast.16, bf16[1,192,768]{2,1,0:T(8,128)(2,1)S(1)} %project.7.rest_0_, bf16[2,80,768]{2,1,0:T(8,128)(2,1)S(1)} %collective-permute-done.5.rest_1_, ...), custom_call_target="tpu_custom_call" | custom-call | flops 1 | bytes 1 | tf_op jit(solution)/shard_map/attend/pallas_call | solution.py:43
  34.4 1.0 %out_project.3 = (bf16[96,2560]{1,0:T(8,128)(2,1)S(1)}, bf16[96,2560]{1,0:T(8,128)(2,1)S(1)}) custom-call(bf16[192,768]{1,0:T(8,128)(2,1)S(1)} %attend.5.rotated_ref, bf16[768,5120]{1,0:T(8,128)(2,1)S(1)} %unpack_out.1.weights_ref, f32[40,128]{1,0:T(8,128)S(1)} %bitcast.10), custom_call_target="tpu_custom_call" | custom-call | flops 1 | bytes 1 | tf_op jit(solution)/shard_map/out_project/pallas_call | solution.py:43
  37.7 1.5 %collective-permute-start.12 = (bf16[48,2560]{1,0:T(8,128)(2,1)S(1)}, bf16[48,2560]{1,0:T(8,128)(2,1)S(1)}, u32[]{:S(2)}, u32[]{:S(2)}) collective-permute-start(bf16[48,2560]{1,0:T(8,128)(2,1)S(1)} %slice.25.refs_1_), channel_id=1, source_target_pairs={{0,2},{1,3},{2,0},{3,1},{4,6},{5,7},{6,4},{7,5},{8,10},{9,11},{10,... | collective-permute-start | bytes 737288 | tf_op jit(solution)/shard_map/ppermute | solution.py:553
  39.6 1.5 %collective-permute-start.11 = (bf16[48,2560]{1,0:T(8,128)(2,1)S(1)}, bf16[48,2560]{1,0:T(8,128)(2,1)S(1)}, u32[]{:S(2)}, u32[]{:S(2)}) collective-permute-start(bf16[48,2560]{1,0:T(8,128)(2,1)S(1)} %slice.24), channel_id=1, source_target_pairs={{0,2},{1,3},{2,0},{3,1},{4,6},{5,7},{6,4},{7,5},{8,10},{9,11},{10,... | collective-permute-start | bytes 737288 | tf_op jit(solution)/shard_map/ppermute | solution.py:553
  41.2 5.3 %collective-permute-done.12.rest_1_ = bf16[48,2560]{1,0:T(8,128)(2,1)S(1)} collective-permute-done((bf16[48,2560]{1,0:T(8,128)(2,1)S(1)}, bf16[48,2560]{1,0:T(8,128)(2,1)S(1)}, u32[]{:S(2)}, u32[]{:S(2)}) %collective-permute-start.12) | collective-permute-done | bytes 245792 | tf_op jit(solution)/shard_map/ppermute | solution.py:553
  46.5 1.0 %finish.2.rest_2_ = bf16[48,5120]{1,0:T(8,128)(2,1)} custom-call(s32[40,128]{1,0:T(8,128)S(1)} %bitcast.12, f32[48,2560]{1,0:T(8,128)S(1)} %slice.21.rest_0_, bf16[48,2560]{1,0:T(8,128)(2,1)S(1)} %collective-permute-done.12.rest_1_), custom_call_target="tpu_custom_call" | custom-call | flops 1 | bytes 1 | tf_op jit(solution)/shard_map/finish/pallas_call | solution.py:43
  47.6 3.6 %collective-permute-done.11.rest_1_ = bf16[48,2560]{1,0:T(8,128)(2,1)S(1)} collective-permute-done((bf16[48,2560]{1,0:T(8,128)(2,1)S(1)}, bf16[48,2560]{1,0:T(8,128)(2,1)S(1)}, u32[]{:S(2)}, u32[]{:S(2)}) %collective-permute-start.11) | collective-permute-done | bytes 245792 | tf_op jit(solution)/shard_map/ppermute | solution.py:553
  51.2 1.0 %finish.3 = bf16[48,5120]{1,0:T(8,128)(2,1)} custom-call(s32[40,128]{1,0:T(8,128)S(1)} %bitcast.13, f32[48,2560]{1,0:T(8,128)S(1)} %slice.19.rest_0_, bf16[48,2560]{1,0:T(8,128)(2,1)S(1)} %collective-permute-done.11.rest_1_, bf16[48,5120]{1,0:T(8,128)(2,1)} %finish.2.rest_2_), custom_call_target="tpu_custom_call", output_to_operand_aliasing={{}: (3, {})} | custom-call | flops 1 | bytes 1 | tf_op jit(solution)/shard_map/finish/pallas_call | solution.py:43
  (42 shorter events, 4.7 us)
Async XLA Ops:
  2.0 1.9 %collective-permute-start.1 = (bf16[192,1280]{1,0:T(8,128)(2,1)S(1)}, bf16[192,1280]{1,0:T(8,128)(2,1)S(1)}, u32[]{:S(2)}, u32[]{:S(2)}) collective-permute-start(bf16[192,1280]{1,0:T(8,128)(2,1)S(1)} %get-tuple-element.15.rest_0_), channel_id=1, source_target_pairs={{0,1},{1,0},{2,3},{3,2},{4,5},{5,4},{6,7},{7,6},{8,9},{9,8},{10,11... | collective-permute-start | bytes 1474568 | tf_op jit(solution)/shard_map/ppermute | solution.py:553
  2.0 9.2 %collective-permute-start = (bf16[112,1280]{1,0:T(8,128)(2,1)S(1)}, bf16[112,1280]{1,0:T(8,128)(2,1)S(1)}, u32[]{:S(2)}, u32[]{:S(2)}) collective-permute-start(bf16[112,1280]{1,0:T(8,128)(2,1)S(1)} %get-tuple-element.14), channel_id=1, source_target_pairs={{0,2},{1,3},{2,0},{3,1},{4,6},{5,7},{6,4},{7,5},{8,10},{9,11},{10,... | collective-permute-start | bytes 860168 | tf_op jit(solution)/shard_map/ppermute | solution.py:553
  8.9 9.0 %collective-permute-start.3 = (bf16[80,1280]{1,0:T(8,128)(2,1)S(1)}, bf16[80,1280]{1,0:T(8,128)(2,1)S(1)}, u32[]{:S(2)}, u32[]{:S(2)}) collective-permute-start(bf16[80,1280]{1,0:T(8,128)(2,1)S(1)} %get-tuple-element.17), channel_id=1, source_target_pairs={{0,2},{1,3},{2,0},{3,1},{4,6},{5,7},{6,4},{7,5},{8,10},{9,11},{10,... | collective-permute-start | bytes 614408 | tf_op jit(solution)/shard_map/ppermute | solution.py:553
  11.3 1.6 %collective-permute-start.2 = (bf16[112,1280]{1,0:T(8,128)(2,1)S(1)}, bf16[112,1280]{1,0:T(8,128)(2,1)S(1)}, u32[]{:S(2)}, u32[]{:S(2)}) collective-permute-start(bf16[112,1280]{1,0:T(8,128)(2,1)S(1)} %tie.3.rest_0_), channel_id=1, source_target_pairs={{0,1},{1,0},{2,3},{3,2},{4,5},{5,4},{6,7},{7,6},{8,9},{9,8},{10,11... | collective-permute-start | bytes 860168 | tf_op jit(solution)/shard_map/ppermute | solution.py:553
  11.3 1.6 %copy-start.3 = (f32[3,768]{1,0:T(4,128)S(1)}, f32[3,768]{1,0:T(4,128)}, u32[]{:S(2)}) copy-start(f32[3,768]{1,0:T(4,128)} %rest_3_.3) | copy-start | bytes 27652
  11.3 1.6 %copy-start.4 = (s32[3,768]{1,0:T(4,128)S(1)}, s32[3,768]{1,0:T(4,128)}, u32[]{:S(2)}) copy-start(s32[3,768]{1,0:T(4,128)} %rest_4_.3) | copy-start | bytes 27652
  14.4 15.2 %collective-permute-start.8 = (bf16[2,112,768]{2,1,0:T(8,128)(2,1)S(1)}, bf16[2,112,768]{2,1,0:T(8,128)(2,1)S(1)}, u32[]{:S(2)}, u32[]{:S(2)}) collective-permute-start(bf16[2,112,768]{2,1,0:T(8,128)(2,1)S(1)} %project.6.array_ref.rest_1_), channel_id=1, source_target_pairs={{0,4},{8,12},{4,0},{12,8},{1,5},{9,13},{5,1},{13,9},{2,6},{10,14},... | collective-permute-start | bytes 1032200 | tf_op jit(solution)/shard_map/ppermute | solution.py:625
  16.0 13.6 %collective-permute-start.7 = (bf16[2,112,768]{2,1,0:T(8,128)(2,1)S(1)}, bf16[2,112,768]{2,1,0:T(8,128)(2,1)S(1)}, u32[]{:S(2)}, u32[]{:S(2)}) collective-permute-start(bf16[2,112,768]{2,1,0:T(8,128)(2,1)S(1)} %project.6.array_ref.rest_1_), channel_id=1, source_target_pairs={{4,8},{8,4},{5,9},{9,5},{6,10},{10,6},{7,11},{11,7},{20,24},{24,20... | collective-permute-start | bytes 1032200 | tf_op jit(solution)/shard_map/ppermute | solution.py:625
  18.0 1.5 %collective-permute-start.4 = (bf16[80,1280]{1,0:T(8,128)(2,1)S(1)}, bf16[80,1280]{1,0:T(8,128)(2,1)S(1)}, u32[]{:S(2)}, u32[]{:S(2)}) collective-permute-start(bf16[80,1280]{1,0:T(8,128)(2,1)S(1)} %tie.4.rest_2_.rest_0_), channel_id=1, source_target_pairs={{0,1},{1,0},{2,3},{3,2},{4,5},{5,4},{6,7},{7,6},{8,9},{9,8},{10,11... | collective-permute-start | bytes 614408 | tf_op jit(solution)/shard_map/ppermute | solution.py:553
  19.2 5.9 %copy-start = (s32[96,5120]{1,0:T(8,128)S(1)}, s32[96,5120]{1,0:T(8,128)}, u32[]{:S(2)}) copy-start(s32[96,5120]{1,0:T(8,128)} %codes_ref.1) | copy-start | bytes 5898244
  21.0 9.8 %collective-permute-start.6 = (bf16[2,80,768]{2,1,0:T(8,128)(2,1)S(1)}, bf16[2,80,768]{2,1,0:T(8,128)(2,1)S(1)}, u32[]{:S(2)}, u32[]{:S(2)}) collective-permute-start(bf16[2,80,768]{2,1,0:T(8,128)(2,1)S(1)} %project.9.rest_2_.after_ref), channel_id=1, source_target_pairs={{0,4},{8,12},{4,0},{12,8},{1,5},{9,13},{5,1},{13,9},{2,6},{10,14},... | collective-permute-start | bytes 737288 | tf_op jit(solution)/shard_map/ppermute | solution.py:625
  21.0 12.1 %collective-permute-start.5 = (bf16[2,80,768]{2,1,0:T(8,128)(2,1)S(1)}, bf16[2,80,768]{2,1,0:T(8,128)(2,1)S(1)}, u32[]{:S(2)}, u32[]{:S(2)}) collective-permute-start(bf16[2,80,768]{2,1,0:T(8,128)(2,1)S(1)} %project.9.rest_2_.after_ref), channel_id=1, source_target_pairs={{4,8},{8,4},{5,9},{9,5},{6,10},{10,6},{7,11},{11,7},{20,24},{24,20... | collective-permute-start | bytes 737288 | tf_op jit(solution)/shard_map/ppermute | solution.py:625
  26.6 1.9 %copy-start.5 = (s32[1,3,27]{2,0,1:T(1,128)S(1)}, s32[1,3,27]{2,0,1:T(1,128)}, u32[]{:S(2)}) copy-start(s32[1,3,27]{2,0,1:T(1,128)} %param.15) | copy-start | bytes 976
  29.6 3.5 %copy-start.6 = (s32[768]{0:T(1024)S(1)}, s32[768]{0:T(1024)}, u32[]{:S(2)}) copy-start(s32[768]{0:T(1024)} %param.16) | copy-start | bytes 9220
  30.7 3.7 %copy-start.1 = (f32[5120]{0:T(1024)S(1)}, f32[5120]{0:T(1024)}, u32[]{:S(2)}) copy-start(f32[5120]{0:T(1024)} %param.18) | copy-start | bytes 61444
  35.4 1.9 %collective-permute-start.9 = (bf16[96,2560]{1,0:T(8,128)(2,1)S(1)}, bf16[96,2560]{1,0:T(8,128)(2,1)S(1)}, u32[]{:S(2)}, u32[]{:S(2)}) collective-permute-start(bf16[96,2560]{1,0:T(8,128)(2,1)S(1)} %get-tuple-element.22), channel_id=1, source_target_pairs={{0,1},{1,0},{2,3},{3,2},{4,5},{5,4},{6,7},{7,6},{8,9},{9,8},{10,11... | collective-permute-start | bytes 1474568 | tf_op jit(solution)/shard_map/ppermute | solution.py:553
  37.5 9.0 %copy-start.2 = (s32[5120]{0:T(1024)S(1)}, s32[5120]{0:T(1024)}, u32[]{:S(2)}) copy-start(s32[5120]{0:T(1024)} %param.19) | copy-start | bytes 61444
  37.5 1.9 %collective-permute-start.10 = (bf16[96,2560]{1,0:T(8,128)(2,1)S(1)}, bf16[96,2560]{1,0:T(8,128)(2,1)S(1)}, u32[]{:S(2)}, u32[]{:S(2)}) collective-permute-start(bf16[96,2560]{1,0:T(8,128)(2,1)S(1)} %tie.5), channel_id=1, source_target_pairs={{0,1},{1,0},{2,3},{3,2},{4,5},{5,4},{6,7},{7,6},{8,9},{9,8},{10,11... | collective-permute-start | bytes 1474568 | tf_op jit(solution)/shard_map/ppermute | solution.py:553
  37.7 8.8 %collective-permute-start.12 = (bf16[48,2560]{1,0:T(8,128)(2,1)S(1)}, bf16[48,2560]{1,0:T(8,128)(2,1)S(1)}, u32[]{:S(2)}, u32[]{:S(2)}) collective-permute-start(bf16[48,2560]{1,0:T(8,128)(2,1)S(1)} %slice.25.refs_1_), channel_id=1, source_target_pairs={{0,2},{1,3},{2,0},{3,1},{4,6},{5,7},{6,4},{7,5},{8,10},{9,11},{10,... | collective-permute-start | bytes 737288 | tf_op jit(solution)/shard_map/ppermute | solution.py:553
  39.6 11.6 %collective-permute-start.11 = (bf16[48,2560]{1,0:T(8,128)(2,1)S(1)}, bf16[48,2560]{1,0:T(8,128)(2,1)S(1)}, u32[]{:S(2)}, u32[]{:S(2)}) collective-permute-start(bf16[48,2560]{1,0:T(8,128)(2,1)S(1)} %slice.24), channel_id=1, source_target_pairs={{0,2},{1,3},{2,0},{3,1},{4,6},{5,7},{6,4},{7,5},{8,10},{9,11},{10,... | collective-permute-start | bytes 737288 | tf_op jit(solution)/shard_map/ppermute | solution.py:553

commit v7 on v6

--- a/solution.py
+++ b/solution.py
@@ -132,9 +132,7 @@
 
 
 def tile_width(columns):
-    for width in (256, 128):
-        if columns % width == 0:
-            return width
+    return columns
 
 
 def early_rows(rows):
@@ -478,7 +476,7 @@
     rows = rotated_ref[...]
     fix = row_correction([rows], OUT_ORDER)
     half, columns = send_ref.shape
-    width = 256
+    width = 512
     for at in range(0, columns, width):
         cols = slice(first + at, first + at + width)
         part = jnp.dot(rows, weights_ref[:, cols], preferred_element_type=f32) - fix
@@ -636,12 +634,13 @@
     late_keys = tuple(((by, odd), half_rows, late_rows) for by, odd, _ in swaps)
     running = attend(place, listed, queries, key_values, own_keys, None, None)
     running = attend(place, listed, queries, moved[0], early_keys, running, None)
+    running = attend(place, listed, queries, moved[1][1:], late_keys[1:], running, None)
     rotated = attend(
         place,
         listed,
         queries,
-        moved[1],
-        late_keys,
+        moved[1][:1],
+        late_keys[:1],
         running,
         (oin_sign, halving_order(head_count)),
     )

time: 52.6 us -> 52.5 us (level)
  the two profiles are of different devices: /device:TPU:16 before, /device:TPU:0 now
where the time goes in v7:
time: 52.5 us; the launch traced here: 52.3 us
  Pallas kernels  24 us (46%)
  starting transfers between devices  16.2 us (31%)
  waiting for transfers between devices  11.2 us (21%)
    pallas_call x20, Pallas kernels, call(): pl.pallas_call(body, out_shape=out_shape, in_specs=in_specs, out_specs=ou...  24 us
    ppermute x9, waiting for transfers between devices, swap(): return lax.ppermute(shard, 'head', [(i, i ^ bit) for i in range(peers)])  11.1 us
    ppermute x9, starting transfers between devices, swap(): return lax.ppermute(shard, 'head', [(i, i ^ bit) for i in range(peers)])  8.32 us
    ppermute x4, starting transfers between devices, on_device(): lax.ppermute(key_value, 'height', pairs)  7.87 us
  transfers between devices with their start and end apart: 13, of which 7 were waited for; matrix products, arithmetic and copies ran while one was open for 0% of the time, Pallas kernels for 36%

profile of v7, /device:TPU:0, one launch (start us, length us, event | category | flops | bytes accessed | tf_op | source)
XLA Modules:
  0.0 52.3 jit_solution(14693650250937479470)
XLA Ops:
  0.1 1.9 %turn.1 = (bf16[192,1280]{1,0:T(8,128)(2,1)S(1)}, bf16[112,1280]{1,0:T(8,128)(2,1)S(1)}) custom-call(s32[2]{0:T(128)S(1)} %pad_add_fusion.place_ref, bf16[192,1280]{1,0:T(8,128)(2,1)} %bitcast.20, s32[40,128]{1,0:T(8,128)} %bitcast.21), custom_call_target="tpu_custom_call" | custom-call | flops 1 | bytes 1 | tf_op jit(solution)/shard_map/turn/pallas_call | solution.py:43
  2.5 2.6 %collective-permute-start = (bf16[112,1280]{1,0:T(8,128)(2,1)S(1)}, bf16[112,1280]{1,0:T(8,128)(2,1)S(1)}, u32[]{:S(2)}, u32[]{:S(2)}) collective-permute-start(bf16[112,1280]{1,0:T(8,128)(2,1)S(1)} %get-tuple-element.14), channel_id=1, source_target_pairs={{0,2},{1,3},{2,0},{3,1},{4,6},{5,7},{6,4},{7,5},{8,10},{9,11},{10,... | collective-permute-start | bytes 860168 | tf_op jit(solution)/shard_map/ppermute | solution.py:551
  5.0 5.0 %prepare.1 = (f32[3,192,768]{2,1,0:T(8,128)S(1)}, s32[2,3,160,768]{3,2,1,0:T(8,128)S(1)}, bf16[80,1280]{1,0:T(8,128)(2,1)S(1)}) custom-call(s32[2]{0:T(128)S(1)} %pad_add_fusion.place_ref, bf16[192,1280]{1,0:T(8,128)(2,1)S(1)} %get-tuple-element.15.rest_0_, bf16[192,1280]{1,0:T(8,128)(2,1)S(1)} %collective-permute-done.1.rest_1_, s32[3,640,768]{2,1,0:T(8,128)} %bitcast.19), custom_call_target="tpu_custom_call" | custom-call | flops 1 | bytes 1 | tf_op jit(solution)/shard_map/prepare/pallas_call | solution.py:43
  10.1 1.8 %collective-permute-start.3 = (bf16[80,1280]{1,0:T(8,128)(2,1)S(1)}, bf16[80,1280]{1,0:T(8,128)(2,1)S(1)}, u32[]{:S(2)}, u32[]{:S(2)}) collective-permute-start(bf16[80,1280]{1,0:T(8,128)(2,1)S(1)} %get-tuple-element.17), channel_id=1, source_target_pairs={{0,2},{1,3},{2,0},{3,1},{4,6},{5,7},{6,4},{7,5},{8,10},{9,11},{10,... | collective-permute-start | bytes 614408 | tf_op jit(solution)/shard_map/ppermute | solution.py:551
  12.5 1.3 %project.5.rest_1_ = f32[2,112,768]{2,1,0:T(8,128)S(1)} custom-call(bf16[112,1280]{1,0:T(8,128)(2,1)S(1)} %tie.3.rest_0_, f32[3,192,768]{2,1,0:T(8,128)S(1)} %get-tuple-element.16.refs_1_.rest_1_.refs_2_.rest_4_, s32[2,3,160,768]{3,2,1,0:T(8,128)S(1)} %get-tuple-element.18.rest_2_.rest_5_), custom_call_target="tpu_custom_call" | custom-call | flops 4000000000 | bytes 1 | tf_op jit(solution)/shard_map/project/pallas_call | solution.py:43
  14.0 1.5 %project.6.array_ref.rest_1_ = bf16[2,112,768]{2,1,0:T(8,128)(2,1)S(1)} custom-call(bf16[112,1280]{1,0:T(8,128)(2,1)S(1)} %collective-permute-done.2.rest_0_.rest_1_, f32[2,112,768]{2,1,0:T(8,128)S(1)} %project.5.rest_1_, s32[2,3,160,768]{3,2,1,0:T(8,128)S(1)} %get-tuple-element.18.rest_2_.rest_5_, f32[3,768]{1,0:T(4,128)S(1)} %copy-done.3, ...), custom_call_target="tpu_custom_call" | custom-call | flops 1 | bytes 1 | tf_op jit(solution)/shard_map/project/pallas_call | solution.py:43
  15.6 1.9 %collective-permute-start.8 = (bf16[2,112,768]{2,1,0:T(8,128)(2,1)S(1)}, bf16[2,112,768]{2,1,0:T(8,128)(2,1)S(1)}, u32[]{:S(2)}, u32[]{:S(2)}) collective-permute-start(bf16[2,112,768]{2,1,0:T(8,128)(2,1)S(1)} %project.6.array_ref.rest_1_), channel_id=1, source_target_pairs={{0,4},{8,12},{4,0},{12,8},{1,5},{9,13},{5,1},{13,9},{2,6},{10,14},... | collective-permute-start | bytes 1032200 | tf_op jit(solution)/shard_map/ppermute | solution.py:623
  18.3 1.2 %project.8.rest_1_ = f32[2,80,768]{2,1,0:T(8,128)S(1)} custom-call(bf16[80,1280]{1,0:T(8,128)(2,1)S(1)} %tie.4.rest_2_.rest_0_, f32[3,192,768]{2,1,0:T(8,128)S(1)} %get-tuple-element.16.refs_1_.rest_1_.refs_2_.rest_4_, s32[2,3,160,768]{3,2,1,0:T(8,128)S(1)} %get-tuple-element.18.rest_2_.rest_5_), custom_call_target="tpu_custom_call" | custom-call | flops 4000000000 | bytes 1 | tf_op jit(solution)/shard_map/project/pallas_call | solution.py:43
  19.7 1.5 %project.9.rest_2_.after_ref = bf16[2,80,768]{2,1,0:T(8,128)(2,1)S(1)} custom-call(bf16[80,1280]{1,0:T(8,128)(2,1)S(1)} %collective-permute-done.4.rest_3_.rest_0_, f32[2,80,768]{2,1,0:T(8,128)S(1)} %project.8.rest_1_, s32[2,3,160,768]{3,2,1,0:T(8,128)S(1)} %get-tuple-element.18.rest_2_.rest_5_, f32[3,768]{1,0:T(4,128)S(1)} %copy-done.3, s32[3,768]{1,0:T(4,128)S(1)} %copy-done.4), custom_call_target="tpu_custom_call" | custom-call | flops 1 | bytes 1 | tf_op jit(solution)/shard_map/project/pallas_call | solution.py:43
  21.2 4.4 %collective-permute-start.6 = (bf16[2,80,768]{2,1,0:T(8,128)(2,1)S(1)}, bf16[2,80,768]{2,1,0:T(8,128)(2,1)S(1)}, u32[]{:S(2)}, u32[]{:S(2)}) collective-permute-start(bf16[2,80,768]{2,1,0:T(8,128)(2,1)S(1)} %project.9.rest_2_.after_ref), channel_id=1, source_target_pairs={{0,4},{8,12},{4,0},{12,8},{1,5},{9,13},{5,1},{13,9},{2,6},{10,14},... | collective-permute-start | bytes 737288 | tf_op jit(solution)/shard_map/ppermute | solution.py:623
  26.5 1.5 %unpack_out.1.weights_ref = bf16[768,5120]{1,0:T(8,128)(2,1)S(1)} custom-call(s32[96,5120]{1,0:T(8,128)S(1)} %copy-done, bf16[2,80,768]{2,1,0:T(8,128)(2,1)S(1)} %project.9.rest_2_.after_ref), custom_call_target="tpu_custom_call" | custom-call | flops 1 | bytes 1 | tf_op jit(solution)/shard_map/unpack_out/pallas_call | solution.py:43
  28.0 1.8 %project.7.rest_0_ = bf16[1,192,768]{2,1,0:T(8,128)(2,1)S(1)} custom-call(bf16[112,1280]{1,0:T(8,128)(2,1)S(1)} %tie.3.rest_0_, bf16[112,1280]{1,0:T(8,128)(2,1)S(1)} %collective-permute-done.2.rest_0_.rest_1_, bf16[80,1280]{1,0:T(8,128)(2,1)S(1)} %tie.4.rest_2_.rest_0_, bf16[80,1280]{1,0:T(8,128)(2,1)S(1)} %collective-permute-done.4.rest_3_.rest_0_, ...), custom_call_target="tpu_custom_call" | custom-call | flops 4000000000 | bytes 1 | tf_op jit(solution)/shard_map/project/pallas_call | solution.py:43
  29.8 1.1 %attend.4.rest_3_ = f32[6,192,256]{2,1,0:T(8,128)S(1)} custom-call(s32[2]{0:T(128)S(1)} %pad_add_fusion.place_ref, s32[3,1,27]{2,1,0:T(1,128)S(1)} %bitcast.14, bf16[1,192,768]{2,1,0:T(8,128)(2,1)S(1)} %project.7.rest_0_, bf16[2,112,768]{2,1,0:T(8,128)(2,1)S(1)} %project.6.array_ref.rest_1_, bf16[2,80,768]{2,1,0:T(8,128)(2,1)S(1)} %project.9.rest_2_.after_ref), custom_call_target="tpu_custom_call" | custom-call | flops 1 | bytes 1 | tf_op jit(solution)/shard_map/attend/pallas_call | solution.py:43
  30.9 1.1 %attend.5.rest_2_ = f32[6,192,256]{2,1,0:T(8,128)S(1)} custom-call(s32[2]{0:T(128)S(1)} %pad_add_fusion.place_ref, s32[3,1,27]{2,1,0:T(1,128)S(1)} %bitcast.15, bf16[1,192,768]{2,1,0:T(8,128)(2,1)S(1)} %project.7.rest_0_, bf16[2,112,768]{2,1,0:T(8,128)(2,1)S(1)} %collective-permute-done.7.rest_1_, bf16[2,112,768]{2,1,0:T(8,128)(2,1)S(1)} %collective-permute-done.8.rest_2_, ...), custom_call_target="tpu_custom_call" | custom-call | flops 1 | bytes 1 | tf_op jit(solution)/shard_map/attend/pallas_call | solution.py:43
  32.1 1.0 %attend.6.rest_2_ = f32[6,192,256]{2,1,0:T(8,128)S(1)} custom-call(s32[2]{0:T(128)S(1)} %pad_add_fusion.place_ref, s32[3,1,27]{2,1,0:T(1,128)S(1)} %bitcast.16, bf16[1,192,768]{2,1,0:T(8,128)(2,1)S(1)} %project.7.rest_0_, bf16[2,80,768]{2,1,0:T(8,128)(2,1)S(1)} %collective-permute-done.6.rest_1_, f32[6,192,256]{2,1,0:T(8,128)S(1)} %attend.5.rest_2_), custom_call_target="tpu_custom_call" | custom-call | flops 1 | bytes 1 | tf_op jit(solution)/shard_map/attend/pallas_call | solution.py:43
  33.1 1.2 %attend.7.rotated_ref = bf16[192,768]{1,0:T(8,128)(2,1)S(1)} custom-call(s32[2]{0:T(128)S(1)} %pad_add_fusion.place_ref, s32[3,1,27]{2,1,0:T(1,128)S(1)} %bitcast.17, bf16[1,192,768]{2,1,0:T(8,128)(2,1)S(1)} %project.7.rest_0_, bf16[2,80,768]{2,1,0:T(8,128)(2,1)S(1)} %collective-permute-done.5.rest_1_, f32[6,192,256]{2,1,0:T(8,128)S(1)} %attend.6.rest_2_, ...), custom_call_target="tpu_custom_call" | custom-call | flops 1 | bytes 1 | tf_op jit(solution)/shard_map/attend/pallas_call | solution.py:43
  34.3 1.0 %out_project.3 = (bf16[96,2560]{1,0:T(8,128)(2,1)S(1)}, bf16[96,2560]{1,0:T(8,128)(2,1)S(1)}) custom-call(bf16[192,768]{1,0:T(8,128)(2,1)S(1)} %attend.7.rotated_ref, bf16[768,5120]{1,0:T(8,128)(2,1)S(1)} %unpack_out.1.weights_ref, f32[40,128]{1,0:T(8,128)S(1)} %bitcast.10), custom_call_target="tpu_custom_call" | custom-call | flops 1 | bytes 1 | tf_op jit(solution)/shard_map/out_project/pallas_call | solution.py:43
  35.3 1.0 %out_project.2 = (bf16[96,2560]{1,0:T(8,128)(2,1)S(1)}, bf16[96,2560]{1,0:T(8,128)(2,1)S(1)}) custom-call(bf16[192,768]{1,0:T(8,128)(2,1)S(1)} %attend.7.rotated_ref, bf16[768,5120]{1,0:T(8,128)(2,1)S(1)} %unpack_out.1.weights_ref, f32[40,128]{1,0:T(8,128)S(1)} %bitcast.11), custom_call_target="tpu_custom_call" | custom-call | flops 1 | bytes 1 | tf_op jit(solution)/shard_map/out_project/pallas_call | solution.py:43
  37.6 1.5 %collective-permute-start.12 = (bf16[48,2560]{1,0:T(8,128)(2,1)S(1)}, bf16[48,2560]{1,0:T(8,128)(2,1)S(1)}, u32[]{:S(2)}, u32[]{:S(2)}) collective-permute-start(bf16[48,2560]{1,0:T(8,128)(2,1)S(1)} %slice.25.refs_1_), channel_id=1, source_target_pairs={{0,2},{1,3},{2,0},{3,1},{4,6},{5,7},{6,4},{7,5},{8,10},{9,11},{10,... | collective-permute-start | bytes 737288 | tf_op jit(solution)/shard_map/ppermute | solution.py:551
  39.5 1.5 %collective-permute-start.11 = (bf16[48,2560]{1,0:T(8,128)(2,1)S(1)}, bf16[48,2560]{1,0:T(8,128)(2,1)S(1)}, u32[]{:S(2)}, u32[]{:S(2)}) collective-permute-start(bf16[48,2560]{1,0:T(8,128)(2,1)S(1)} %slice.24), channel_id=1, source_target_pairs={{0,2},{1,3},{2,0},{3,1},{4,6},{5,7},{6,4},{7,5},{8,10},{9,11},{10,... | collective-permute-start | bytes 737288 | tf_op jit(solution)/shard_map/ppermute | solution.py:551
  41.1 5.3 %collective-permute-done.12.rest_1_ = bf16[48,2560]{1,0:T(8,128)(2,1)S(1)} collective-permute-done((bf16[48,2560]{1,0:T(8,128)(2,1)S(1)}, bf16[48,2560]{1,0:T(8,128)(2,1)S(1)}, u32[]{:S(2)}, u32[]{:S(2)}) %collective-permute-start.12) | collective-permute-done | bytes 245792 | tf_op jit(solution)/shard_map/ppermute | solution.py:551
  46.4 1.0 %finish.2.rest_2_ = bf16[48,5120]{1,0:T(8,128)(2,1)} custom-call(s32[40,128]{1,0:T(8,128)S(1)} %bitcast.12, f32[48,2560]{1,0:T(8,128)S(1)} %slice.21.rest_0_, bf16[48,2560]{1,0:T(8,128)(2,1)S(1)} %collective-permute-done.12.rest_1_), custom_call_target="tpu_custom_call" | custom-call | flops 1 | bytes 1 | tf_op jit(solution)/shard_map/finish/pallas_call | solution.py:43
  47.5 3.6 %collective-permute-done.11.rest_1_ = bf16[48,2560]{1,0:T(8,128)(2,1)S(1)} collective-permute-done((bf16[48,2560]{1,0:T(8,128)(2,1)S(1)}, bf16[48,2560]{1,0:T(8,128)(2,1)S(1)}, u32[]{:S(2)}, u32[]{:S(2)}) %collective-permute-start.11) | collective-permute-done | bytes 245792 | tf_op jit(solution)/shard_map/ppermute | solution.py:551
  51.1 1.0 %finish.3 = bf16[48,5120]{1,0:T(8,128)(2,1)} custom-call(s32[40,128]{1,0:T(8,128)S(1)} %bitcast.13, f32[48,2560]{1,0:T(8,128)S(1)} %slice.19.rest_0_, bf16[48,2560]{1,0:T(8,128)(2,1)S(1)} %collective-permute-done.11.rest_1_, bf16[48,5120]{1,0:T(8,128)(2,1)} %finish.2.rest_2_), custom_call_target="tpu_custom_call", output_to_operand_aliasing={{}: (3, {})} | custom-call | flops 1 | bytes 1 | tf_op jit(solution)/shard_map/finish/pallas_call | solution.py:43
  (43 shorter events, 5.1 us)
Async XLA Ops:
  2.0 3.1 %collective-permute-start.1 = (bf16[192,1280]{1,0:T(8,128)(2,1)S(1)}, bf16[192,1280]{1,0:T(8,128)(2,1)S(1)}, u32[]{:S(2)}, u32[]{:S(2)}) collective-permute-start(bf16[192,1280]{1,0:T(8,128)(2,1)S(1)} %get-tuple-element.15.rest_0_), channel_id=1, source_target_pairs={{0,1},{1,0},{2,3},{3,2},{4,5},{5,4},{6,7},{7,6},{8,9},{9,8},{10,11... | collective-permute-start | bytes 1474568 | tf_op jit(solution)/shard_map/ppermute | solution.py:551
  2.5 10.0 %collective-permute-start = (bf16[112,1280]{1,0:T(8,128)(2,1)S(1)}, bf16[112,1280]{1,0:T(8,128)(2,1)S(1)}, u32[]{:S(2)}, u32[]{:S(2)}) collective-permute-start(bf16[112,1280]{1,0:T(8,128)(2,1)S(1)} %get-tuple-element.14), channel_id=1, source_target_pairs={{0,2},{1,3},{2,0},{3,1},{4,6},{5,7},{6,4},{7,5},{8,10},{9,11},{10,... | collective-permute-start | bytes 860168 | tf_op jit(solution)/shard_map/ppermute | solution.py:551
  10.1 8.1 %collective-permute-start.3 = (bf16[80,1280]{1,0:T(8,128)(2,1)S(1)}, bf16[80,1280]{1,0:T(8,128)(2,1)S(1)}, u32[]{:S(2)}, u32[]{:S(2)}) collective-permute-start(bf16[80,1280]{1,0:T(8,128)(2,1)S(1)} %get-tuple-element.17), channel_id=1, source_target_pairs={{0,2},{1,3},{2,0},{3,1},{4,6},{5,7},{6,4},{7,5},{8,10},{9,11},{10,... | collective-permute-start | bytes 614408 | tf_op jit(solution)/shard_map/ppermute | solution.py:551
  12.5 1.6 %collective-permute-start.2 = (bf16[112,1280]{1,0:T(8,128)(2,1)S(1)}, bf16[112,1280]{1,0:T(8,128)(2,1)S(1)}, u32[]{:S(2)}, u32[]{:S(2)}) collective-permute-start(bf16[112,1280]{1,0:T(8,128)(2,1)S(1)} %tie.3.rest_0_), channel_id=1, source_target_pairs={{0,1},{1,0},{2,3},{3,2},{4,5},{5,4},{6,7},{7,6},{8,9},{9,8},{10,11... | collective-permute-start | bytes 860168 | tf_op jit(solution)/shard_map/ppermute | solution.py:551
  12.5 1.6 %copy-start.3 = (f32[3,768]{1,0:T(4,128)S(1)}, f32[3,768]{1,0:T(4,128)}, u32[]{:S(2)}) copy-start(f32[3,768]{1,0:T(4,128)} %rest_3_.3) | copy-start | bytes 27652
  12.5 1.6 %copy-start.4 = (s32[3,768]{1,0:T(4,128)S(1)}, s32[3,768]{1,0:T(4,128)}, u32[]{:S(2)}) copy-start(s32[3,768]{1,0:T(4,128)} %rest_4_.3) | copy-start | bytes 27652
  15.6 15.3 %collective-permute-start.8 = (bf16[2,112,768]{2,1,0:T(8,128)(2,1)S(1)}, bf16[2,112,768]{2,1,0:T(8,128)(2,1)S(1)}, u32[]{:S(2)}, u32[]{:S(2)}) collective-permute-start(bf16[2,112,768]{2,1,0:T(8,128)(2,1)S(1)} %project.6.array_ref.rest_1_), channel_id=1, source_target_pairs={{0,4},{8,12},{4,0},{12,8},{1,5},{9,13},{5,1},{13,9},{2,6},{10,14},... | collective-permute-start | bytes 1032200 | tf_op jit(solution)/shard_map/ppermute | solution.py:623
  17.5 13.4 %collective-permute-start.7 = (bf16[2,112,768]{2,1,0:T(8,128)(2,1)S(1)}, bf16[2,112,768]{2,1,0:T(8,128)(2,1)S(1)}, u32[]{:S(2)}, u32[]{:S(2)}) collective-permute-start(bf16[2,112,768]{2,1,0:T(8,128)(2,1)S(1)} %project.6.array_ref.rest_1_), channel_id=1, source_target_pairs={{4,8},{8,4},{5,9},{9,5},{6,10},{10,6},{7,11},{11,7},{20,24},{24,20... | collective-permute-start | bytes 1032200 | tf_op jit(solution)/shard_map/ppermute | solution.py:623
  18.2 1.5 %collective-permute-start.4 = (bf16[80,1280]{1,0:T(8,128)(2,1)S(1)}, bf16[80,1280]{1,0:T(8,128)(2,1)S(1)}, u32[]{:S(2)}, u32[]{:S(2)}) collective-permute-start(bf16[80,1280]{1,0:T(8,128)(2,1)S(1)} %tie.4.rest_2_.rest_0_), channel_id=1, source_target_pairs={{0,1},{1,0},{2,3},{3,2},{4,5},{5,4},{6,7},{7,6},{8,9},{9,8},{10,11... | collective-permute-start | bytes 614408 | tf_op jit(solution)/shard_map/ppermute | solution.py:551
  19.4 7.0 %copy-start = (s32[96,5120]{1,0:T(8,128)S(1)}, s32[96,5120]{1,0:T(8,128)}, u32[]{:S(2)}) copy-start(s32[96,5120]{1,0:T(8,128)} %codes_ref.1) | copy-start | bytes 5898244
  21.2 10.9 %collective-permute-start.6 = (bf16[2,80,768]{2,1,0:T(8,128)(2,1)S(1)}, bf16[2,80,768]{2,1,0:T(8,128)(2,1)S(1)}, u32[]{:S(2)}, u32[]{:S(2)}) collective-permute-start(bf16[2,80,768]{2,1,0:T(8,128)(2,1)S(1)} %project.9.rest_2_.after_ref), channel_id=1, source_target_pairs={{0,4},{8,12},{4,0},{12,8},{1,5},{9,13},{5,1},{13,9},{2,6},{10,14},... | collective-permute-start | bytes 737288 | tf_op jit(solution)/shard_map/ppermute | solution.py:623
  25.6 7.4 %collective-permute-start.5 = (bf16[2,80,768]{2,1,0:T(8,128)(2,1)S(1)}, bf16[2,80,768]{2,1,0:T(8,128)(2,1)S(1)}, u32[]{:S(2)}, u32[]{:S(2)}) collective-permute-start(bf16[2,80,768]{2,1,0:T(8,128)(2,1)S(1)} %project.9.rest_2_.after_ref), channel_id=1, source_target_pairs={{4,8},{8,4},{5,9},{9,5},{6,10},{10,6},{7,11},{11,7},{20,24},{24,20... | collective-permute-start | bytes 737288 | tf_op jit(solution)/shard_map/ppermute | solution.py:623
  27.9 1.8 %copy-start.5 = (s32[1,3,27]{2,0,1:T(1,128)S(1)}, s32[1,3,27]{2,0,1:T(1,128)}, u32[]{:S(2)}) copy-start(s32[1,3,27]{2,0,1:T(1,128)} %param.15) | copy-start | bytes 976
  32.0 1.1 %copy-start.6 = (s32[768]{0:T(1024)S(1)}, s32[768]{0:T(1024)}, u32[]{:S(2)}) copy-start(s32[768]{0:T(1024)} %param.16) | copy-start | bytes 9220
  32.0 2.2 %copy-start.1 = (f32[5120]{0:T(1024)S(1)}, f32[5120]{0:T(1024)}, u32[]{:S(2)}) copy-start(f32[5120]{0:T(1024)} %param.18) | copy-start | bytes 61444
  35.3 1.9 %collective-permute-start.9 = (bf16[96,2560]{1,0:T(8,128)(2,1)S(1)}, bf16[96,2560]{1,0:T(8,128)(2,1)S(1)}, u32[]{:S(2)}, u32[]{:S(2)}) collective-permute-start(bf16[96,2560]{1,0:T(8,128)(2,1)S(1)} %get-tuple-element.22), channel_id=1, source_target_pairs={{0,1},{1,0},{2,3},{3,2},{4,5},{5,4},{6,7},{7,6},{8,9},{9,8},{10,11... | collective-permute-start | bytes 1474568 | tf_op jit(solution)/shard_map/ppermute | solution.py:551
  37.4 9.0 %copy-start.2 = (s32[5120]{0:T(1024)S(1)}, s32[5120]{0:T(1024)}, u32[]{:S(2)}) copy-start(s32[5120]{0:T(1024)} %param.19) | copy-start | bytes 61444
  37.4 1.9 %collective-permute-start.10 = (bf16[96,2560]{1,0:T(8,128)(2,1)S(1)}, bf16[96,2560]{1,0:T(8,128)(2,1)S(1)}, u32[]{:S(2)}, u32[]{:S(2)}) collective-permute-start(bf16[96,2560]{1,0:T(8,128)(2,1)S(1)} %tie.5), channel_id=1, source_target_pairs={{0,1},{1,0},{2,3},{3,2},{4,5},{5,4},{6,7},{7,6},{8,9},{9,8},{10,11... | collective-permute-start | bytes 1474568 | tf_op jit(solution)/shard_map/ppermute | solution.py:551
  37.6 8.8 %collective-permute-start.12 = (bf16[48,2560]{1,0:T(8,128)(2,1)S(1)}, bf16[48,2560]{1,0:T(8,128)(2,1)S(1)}, u32[]{:S(2)}, u32[]{:S(2)}) collective-permute-start(bf16[48,2560]{1,0:T(8,128)(2,1)S(1)} %slice.25.refs_1_), channel_id=1, source_target_pairs={{0,2},{1,3},{2,0},{3,1},{4,6},{5,7},{6,4},{7,5},{8,10},{9,11},{10,... | collective-permute-start | bytes 737288 | tf_op jit(solution)/shard_map/ppermute | solution.py:551
  39.5 11.6 %collective-permute-start.11 = (bf16[48,2560]{1,0:T(8,128)(2,1)S(1)}, bf16[48,2560]{1,0:T(8,128)(2,1)S(1)}, u32[]{:S(2)}, u32[]{:S(2)}) collective-permute-start(bf16[48,2560]{1,0:T(8,128)(2,1)S(1)} %slice.24), channel_id=1, source_target_pairs={{0,2},{1,3},{2,0},{3,1},{4,6},{5,7},{6,4},{7,5},{8,10},{9,11},{10,... | collective-permute-start | bytes 737288 | tf_op jit(solution)/shard_map/ppermute | solution.py:551

commit v8 on v7

--- a/solution.py
+++ b/solution.py
@@ -131,15 +131,11 @@
     return jnp.dot(jnp.concatenate([high, low], 1), doubled, preferred_element_type=f32)
 
 
-def tile_width(columns):
-    return columns
-
-
 def early_rows(rows):
     return rows * 7 // 12 // WORDS * WORDS
 
 
-def turn_kernel(place_ref, x_hbm, sign_hbm, own_ref, send_ref, x_ref, sign_ref, sems):
+def turn_kernel(x_hbm, sign_hbm, own_ref, send_ref, x_ref, sign_ref, sems):
     copies = [
         pltpu.make_async_copy(x_hbm, x_ref, sems.at[0]),
         pltpu.make_async_copy(sign_hbm, sign_ref, sems.at[1]),
@@ -151,7 +147,7 @@
     for copy in copies:
         copy.wait()
     blocks = x_ref.shape[1] // HAD
-    first = place_ref[0] * blocks
+    first = lax.axis_index("head") * blocks
     for b in range(blocks):
         cols = slice(b * HAD, (b + 1) * HAD)
         sign_row = signed(sign_ref[pl.ds(first + b, 1), :])
@@ -162,14 +158,14 @@
         send_ref[:, cols] = turned[: send_ref.shape[0]]
 
 
-def turn(place, own_tokens, in_sign):
+def turn(own_tokens, in_sign):
     sign_rows = in_sign.reshape(-1, HAD)
     rows, inner = own_tokens.shape
     return call(
         turn_kernel,
         (shape_of((rows, inner), bf16), shape_of((early_rows(rows), inner), bf16)),
-        [SMEM, HBM, HBM],
-        (place, in_hbm(own_tokens), in_hbm(sign_rows)),
+        [HBM, HBM],
+        (in_hbm(own_tokens), in_hbm(sign_rows)),
         "turn",
         scratch_shapes=[
             pltpu.VMEM(own_tokens.shape, bf16),
@@ -198,14 +194,14 @@
     return call(body, shape_of((8, HAD), f32), [ANY], (array,), "gate", flops=4 * 10**9)
 
 
-def prepare_kernel(near, far, place_ref, *rest):
+def prepare_kernel(near, far, *rest):
     shard_refs = rest[: len(near)]
     codes_hbm, sums_ref, far_ref, late_ref, near_ref, sems = rest[len(near) :]
     words, columns = near_ref.shape[2:]
 
     def fetch(position, kind):
         flip = (near + far)[position]
-        first = pl.multiple_of((place_ref[0] ^ flip) * words, WORDS)
+        first = pl.multiple_of((lax.axis_index("head") ^ flip) * words, WORDS)
         there = position - len(near)
         target = near_ref.at[position, kind] if there < 0 else far_ref.at[there, kind]
         return pltpu.make_async_copy(
@@ -219,19 +215,16 @@
         for kind in range(3):
             fetch(position, kind).start()
     fix = row_correction([ref[...] for ref in shard_refs], QKV_ORDER)
-    width = tile_width(columns)
     late_ref[...] = shard_refs[0][shard_refs[0].shape[0] - late_ref.shape[0] :, :]
 
     def every_shard(kind, carry):
         for position in range(len(near)):
             fetch(position, kind).wait()
-        for first in range(0, columns, width):
-            cols = slice(first, first + width)
-            total = -fix
-            for position, ref in enumerate(shard_refs):
-                weights = decode(near_ref[position, kind, :, cols], QKV_ORDER)
-                total = total + jnp.dot(ref[...], weights, preferred_element_type=f32)
-            sums_ref[kind, :, cols] = total
+        total = -fix
+        for position, ref in enumerate(shard_refs):
+            weights = decode(near_ref[position, kind], QKV_ORDER)
+            total = total + jnp.dot(ref[...], weights, preferred_element_type=f32)
+        sums_ref[kind] = total
         return carry
 
     lax.fori_loop(0, 3, every_shard, 0)
@@ -240,7 +233,7 @@
             fetch(position, kind).wait()
 
 
-def prepare(place, near, far, shards, codes):
+def prepare(near, far, shards, codes):
     rows, inner = shards[0].shape
     columns = codes.shape[2]
     words = inner // PLANES
@@ -251,8 +244,8 @@
             shape_of((len(far), 3, words, columns), jnp.int32),
             shape_of((rows - early_rows(rows), inner), bf16),
         ),
-        [SMEM] + [VMEM] * len(near) + [HBM],
-        (place, *shards, in_hbm(codes)),
+        [VMEM] * len(near) + [HBM],
+        (*shards, in_hbm(codes)),
         "prepare",
         scratch_shapes=[
             pltpu.VMEM((len(near), 3, words, columns), jnp.int32),
@@ -269,7 +262,6 @@
         scale_ref, sign_ref = rest[groups * count + 2 : groups * count + 4]
     out_ref = rest[-1]
     columns = sums_ref.shape[2]
-    width = tile_width(columns)
     shards = []
     for place in range(count):
         parts = [shard_refs[g * count + place][...] for g in range(groups)]
@@ -280,22 +272,18 @@
     doubled = double_hadamard()
     ones = jnp.ones((HD, HD), bf16)
     for place, kind in enumerate(kinds):
+        part = (sums_ref[kind, rows, :] if whole else sums_ref[place]) - fix
+        for shard, position in zip(shards, positions):
+            weights = decode(words_ref[position, kind], QKV_ORDER)
+            part = part + jnp.dot(shard, weights, preferred_element_type=f32)
+        if not ending:
+            out_ref[place] = part
+            continue
         heads = []
-        for first in range(0, columns, width):
-            cols = slice(first, first + width)
-            part = (sums_ref[kind, rows, cols] if whole else sums_ref[place, :, cols]) - fix
-            for shard, position in zip(shards, positions):
-                weights = decode(words_ref[position, kind, :, cols], QKV_ORDER)
-                part = part + jnp.dot(shard, weights, preferred_element_type=f32)
-            if not ending:
-                out_ref[place, :, cols] = part
-                continue
-            for lane in range(0, width, HD):
-                at = slice(first + lane, first + lane + HD)
-                scale_row = scale_ref[kind : kind + 1, at] * np.float32(D ** (-0.5))
-                heads.append(part[:, lane : lane + HD] * scale_row)
-        if not ending:
-            continue
+        for first in range(0, columns, HD):
+            at = slice(first, first + HD)
+            scale_row = scale_ref[kind : kind + 1, at] * np.float32(D ** (-0.5))
+            heads.append(part[:, at] * scale_row)
         mixed = rotate_halves(jnp.concatenate(heads, 0), doubled)
         signs = []
         for head in range(len(heads)):
@@ -342,29 +330,38 @@
     return jnp.where(lax.rem(row // by, 2) == odd, row + by, row - by)
 
 
-def window_mask(place_ref, windows_ref, segments, row_count):
-    lane = lax.broadcasted_iota(jnp.int32, (1, sum(rows for _, _, rows in segments)), 1)
-    ids, base = None, 0
-    for swap_pair, first, rows in segments:
-        tile = (lane + (first - base)) // TILE
-        ids_here = near_row(place_ref[1], swap_pair) * WTILES + tile
-        ids = ids_here if ids is None else jnp.where(lane >= base, ids_here, ids)
-        base += rows
-    masks = []
-    for tile in range(row_count // TILE):
-        hit = jnp.zeros(lane.shape, f32)
-        for entry in range(windows_ref.shape[2]):
-            hit = jnp.where(ids == windows_ref[tile, 0, entry], 1.0, hit)
-        masks.append(jnp.broadcast_to(hit, (TILE, lane.shape[1])))
-    return jnp.concatenate(masks, 0)
-
-
-def attend_kernel(
-    segments, halves, blocks, has_sum, last, share_order, place_ref, windows_ref, *rest
-):
+def masks_kernel(steps, windows_ref, after_ref, *mask_refs):
+    row = lax.axis_index("height")
+    for segments, mask_ref in zip(steps, mask_refs):
+        lane = lax.broadcasted_iota(jnp.int32, (1, mask_ref.shape[1]), 1)
+        ids, base = None, 0
+        for swap_pair, first, rows in segments:
+            tile = (lane + (first - base)) // TILE
+            ids_here = near_row(row, swap_pair) * WTILES + tile
+            ids = ids_here if ids is None else jnp.where(lane >= base, ids_here, ids)
+            base += rows
+        for tile in range(mask_ref.shape[0]):
+            hit = jnp.zeros(lane.shape, f32)
+            for entry in range(windows_ref.shape[2]):
+                hit = jnp.where(ids == windows_ref[tile, 0, entry], 1.0, hit)
+            mask_ref[tile : tile + 1, :] = hit
+
+
+def make_masks(windows, after, steps):
+    listed = jnp.transpose(windows, (1, 0, 2))
+    shapes = [
+        shape_of((listed.shape[0], sum(rows for _, _, rows in segments)), f32) for segments in steps
+    ]
+    return call(
+        functools.partial(masks_kernel, steps), shapes, [SMEM, ANY], (listed, after), "window_masks"
+    )
+
+
+def attend_kernel(halves, blocks, has_sum, last, share_order, *rest):
     rest = list(rest)
     q_refs = [rest.pop(0) for _ in range(halves)]
     kv_refs = [rest.pop(0) for _ in range(blocks)]
+    mask_ref = rest.pop(0)
     sum_ref = rest.pop(0) if has_sum else None
     if last:
         oin_ref, out_ref, rotated_ref = rest
@@ -373,7 +370,13 @@
     columns = q_refs[0].shape[2]
     row_count = sum(ref.shape[1] for ref in q_refs)
     heads = [slice(head, head + HD) for head in range(0, columns, HD)]
-    mask = window_mask(place_ref, windows_ref, segments, row_count)
+    mask = jnp.concatenate(
+        [
+            jnp.broadcast_to(mask_ref[t : t + 1, :], (TILE, mask_ref.shape[1]))
+            for t in range(row_count // TILE)
+        ],
+        0,
+    )
     scores = []
     for at in heads:
         keys = jnp.concatenate([ref[0, :, at] for ref in kv_refs], 0)
@@ -410,15 +413,15 @@
     share = row_count // len(share_order)
     pieces = []
     for flip in share_order:
-        owner = place_ref[0] ^ flip
+        owner = lax.axis_index("head") ^ flip
         pieces.append(rotated_ref[pl.ds(pl.multiple_of(owner * share, 8), share), :])
     out_ref[...] = jnp.concatenate(pieces, 0).astype(bf16)
 
 
-def attend(place, windows, queries, blocks, segments, running, ending):
+def attend(queries, blocks, mask, running, ending):
     columns = queries[0].shape[2]
     row_count = sum(part.shape[1] for part in queries)
-    args = [place, windows, *queries, *blocks]
+    args = [*queries, *blocks, mask]
     if running is not None:
         args.append(running)
     scratch, share_order = [], None
@@ -432,7 +435,6 @@
     return call(
         functools.partial(
             attend_kernel,
-            segments,
             len(queries),
             len(blocks),
             running is not None,
@@ -440,7 +442,7 @@
             share_order,
         ),
         out_shape,
-        [SMEM] * 2 + [VMEM] * (len(args) - 2),
+        [VMEM] * len(args),
         args,
         "attend",
         scratch_shapes=scratch,
@@ -586,13 +588,10 @@
 ):
     head_count = lax.axis_size("head")
     row_tiles = lax.axis_size("height")
-    row_place = lax.axis_index("height")
-    head_place = lax.axis_index("head").astype(jnp.int32)
     top = head_count // 2
-    place = jnp.stack([head_place, row_place.astype(jnp.int32)])
     low_bits = [1 << b for b in range(top.bit_length() - 1)]
 
-    own, early = turn(place, tokens[0], in_sign)
+    own, early = turn(tokens[0], in_sign)
     half_rows = early.shape[0]
     early = swap(early, top)
     near = {0: own}
@@ -603,7 +602,7 @@
     near_flips = tuple(sorted(near))
     far_flips = tuple(flip ^ top for flip in near_flips)
     sums, words, late = prepare(
-        place, near_flips, far_flips, [near[flip] for flip in near_flips], codes
+        near_flips, far_flips, [near[flip] for flip in near_flips], codes
     )
     late = swap(late, top)
     swaps = row_swaps(row_tiles)
@@ -627,22 +626,17 @@
     queries = [project((0,), 0, halves, every, sums, words, ending, 4 * 10**9)]
     out_weights = unpack_out(out_codes, key_values[1])
 
-    listed = jnp.transpose(windows, (1, 0, 2))
     late_rows = own.shape[0] - half_rows
     own_keys = ((None, 0, half_rows), (None, half_rows, late_rows))
     early_keys = tuple(((by, odd), 0, half_rows) for by, odd, _ in swaps)
     late_keys = tuple(((by, odd), half_rows, late_rows) for by, odd, _ in swaps)
-    running = attend(place, listed, queries, key_values, own_keys, None, None)
-    running = attend(place, listed, queries, moved[0], early_keys, running, None)
-    running = attend(place, listed, queries, moved[1][1:], late_keys[1:], running, None)
+    steps = (own_keys, early_keys, late_keys[1:], late_keys[:1])
+    masks = make_masks(windows, key_values[1], steps)
+    running = attend(queries, key_values, masks[0], None, None)
+    running = attend(queries, moved[0], masks[1], running, None)
+    running = attend(queries, moved[1][1:], masks[2], running, None)
     rotated = attend(
-        place,
-        listed,
-        queries,
-        moved[1][:1],
-        late_keys[:1],
-        running,
-        (oin_sign, halving_order(head_count)),
+        queries, moved[1][:1], masks[3], running, (oin_sign, halving_order(head_count))
     )
 
     bits = low_bits + [top]

time: 52.5 us -> 51.3 us (0.977); the launches traced: 52.3 us -> 50.5 us
  Pallas kernels: 24 us -> 21.4 us
  waiting for transfers between devices: 11.2 us -> 12 us
    pallas_call x20 -> x21, Pallas kernels: 24 us -> 21.4 us  [call(): pl.pallas_call(body, out_shape=out_shape, in_specs=in_specs, out_specs=ou...]
    ppermute x9, waiting for transfers between devices: 11.1 us -> 11.7 us  [swap(): return lax.ppermute(shard, 'head', [(i, i ^ bit) for i in range(peers)])]
  transfers between devices with their start and end apart: 13 -> 13, of which waited for: 7 -> 8; matrix products, arithmetic and copies ran while one was open for 0% -> 0% of each run, Pallas kernels for 36% -> 34%
where the time goes in v8:
time: 51.3 us; the launch traced here: 50.5 us
  Pallas kernels  21.4 us (42%)
  starting transfers between devices  16.2 us (32%)
  waiting for transfers between devices  12 us (23%)
    pallas_call x21, Pallas kernels, call(): pl.pallas_call(body, out_shape=out_shape, in_specs=in_specs, out_specs=ou...  21.4 us
    ppermute x9, waiting for transfers between devices, swap(): return lax.ppermute(shard, 'head', [(i, i ^ bit) for i in range(peers)])  11.7 us
    ppermute x9, starting transfers between devices, swap(): return lax.ppermute(shard, 'head', [(i, i ^ bit) for i in range(peers)])  8.36 us
    ppermute x4, starting transfers between devices, on_device(): lax.ppermute(key_value, 'height', pairs)  7.89 us
  transfers between devices with their start and end apart: 13, of which 8 were waited for; matrix products, arithmetic and copies ran while one was open for 0% of the time, Pallas kernels for 34%

profile of v8, /device:TPU:0, one launch (start us, length us, event | category | flops | bytes accessed | tf_op | source)
XLA Modules:
  0.0 50.5 jit_solution(15858362367895799685)
XLA Ops:
  0.0 1.3 %turn.1 = (bf16[192,1280]{1,0:T(8,128)(2,1)S(1)}, bf16[112,1280]{1,0:T(8,128)(2,1)S(1)}) custom-call(bf16[192,1280]{1,0:T(8,128)(2,1)} %bitcast.15, s32[40,128]{1,0:T(8,128)} %bitcast.16), custom_call_target="tpu_custom_call" | custom-call | flops 1 | bytes 1 | tf_op jit(solution)/shard_map/turn/pallas_call | solution.py:43
  1.9 2.6 %collective-permute-start = (bf16[112,1280]{1,0:T(8,128)(2,1)S(1)}, bf16[112,1280]{1,0:T(8,128)(2,1)S(1)}, u32[]{:S(2)}, u32[]{:S(2)}) collective-permute-start(bf16[112,1280]{1,0:T(8,128)(2,1)S(1)} %get-tuple-element.18), channel_id=1, source_target_pairs={{0,2},{1,3},{2,0},{3,1},{4,6},{5,7},{6,4},{7,5},{8,10},{9,11},{10,... | collective-permute-start | bytes 860168 | tf_op jit(solution)/shard_map/ppermute | solution.py:553
  4.4 4.5 %prepare.1 = (f32[3,192,768]{2,1,0:T(8,128)S(1)}, s32[2,3,160,768]{3,2,1,0:T(8,128)S(1)}, bf16[80,1280]{1,0:T(8,128)(2,1)S(1)}) custom-call(bf16[192,1280]{1,0:T(8,128)(2,1)S(1)} %get-tuple-element.19.rest_0_, bf16[192,1280]{1,0:T(8,128)(2,1)S(1)} %collective-permute-done.1.rest_1_, s32[3,640,768]{2,1,0:T(8,128)} %bitcast.14), custom_call_target="tpu_custom_call" | custom-call | flops 1 | bytes 1 | tf_op jit(solution)/shard_map/prepare/pallas_call | solution.py:43
  8.9 1.8 %collective-permute-start.3 = (bf16[80,1280]{1,0:T(8,128)(2,1)S(1)}, bf16[80,1280]{1,0:T(8,128)(2,1)S(1)}, u32[]{:S(2)}, u32[]{:S(2)}) collective-permute-start(bf16[80,1280]{1,0:T(8,128)(2,1)S(1)} %get-tuple-element.21), channel_id=1, source_target_pairs={{0,2},{1,3},{2,0},{3,1},{4,6},{5,7},{6,4},{7,5},{8,10},{9,11},{10,... | collective-permute-start | bytes 614408 | tf_op jit(solution)/shard_map/ppermute | solution.py:553
  10.8 1.1 %collective-permute-done.refs_0_ = bf16[112,1280]{1,0:T(8,128)(2,1)S(1)} collective-permute-done((bf16[112,1280]{1,0:T(8,128)(2,1)S(1)}, bf16[112,1280]{1,0:T(8,128)(2,1)S(1)}, u32[]{:S(2)}, u32[]{:S(2)}) %collective-permute-start) | collective-permute-done | bytes 286752 | tf_op jit(solution)/shard_map/ppermute | solution.py:553
  11.9 1.3 %project.5.rest_1_ = f32[2,112,768]{2,1,0:T(8,128)S(1)} custom-call(bf16[112,1280]{1,0:T(8,128)(2,1)S(1)} %tie.3.rest_0_, f32[3,192,768]{2,1,0:T(8,128)S(1)} %get-tuple-element.20.refs_1_.rest_1_.refs_2_.rest_4_, s32[2,3,160,768]{3,2,1,0:T(8,128)S(1)} %get-tuple-element.22.rest_2_.rest_5_), custom_call_target="tpu_custom_call" | custom-call | flops 4000000000 | bytes 1 | tf_op jit(solution)/shard_map/project/pallas_call | solution.py:43
  13.5 1.5 %project.6.array_ref.rest_1_ = bf16[2,112,768]{2,1,0:T(8,128)(2,1)S(1)} custom-call(bf16[112,1280]{1,0:T(8,128)(2,1)S(1)} %collective-permute-done.2.rest_0_.rest_1_, f32[2,112,768]{2,1,0:T(8,128)S(1)} %project.5.rest_1_, s32[2,3,160,768]{3,2,1,0:T(8,128)S(1)} %get-tuple-element.22.rest_2_.rest_5_, f32[3,768]{1,0:T(4,128)S(1)} %copy-done.3, ...), custom_call_target="tpu_custom_call" | custom-call | flops 1 | bytes 1 | tf_op jit(solution)/shard_map/project/pallas_call | solution.py:43
  15.0 1.9 %collective-permute-start.8 = (bf16[2,112,768]{2,1,0:T(8,128)(2,1)S(1)}, bf16[2,112,768]{2,1,0:T(8,128)(2,1)S(1)}, u32[]{:S(2)}, u32[]{:S(2)}) collective-permute-start(bf16[2,112,768]{2,1,0:T(8,128)(2,1)S(1)} %project.6.array_ref.rest_1_), channel_id=1, source_target_pairs={{0,4},{8,12},{4,0},{12,8},{1,5},{9,13},{5,1},{13,9},{2,6},{10,14},... | collective-permute-start | bytes 1032200 | tf_op jit(solution)/shard_map/ppermute | solution.py:622
  17.7 1.2 %project.8.rest_1_ = f32[2,80,768]{2,1,0:T(8,128)S(1)} custom-call(bf16[80,1280]{1,0:T(8,128)(2,1)S(1)} %tie.4.rest_2_.rest_0_, f32[3,192,768]{2,1,0:T(8,128)S(1)} %get-tuple-element.20.refs_1_.rest_1_.refs_2_.rest_4_, s32[2,3,160,768]{3,2,1,0:T(8,128)S(1)} %get-tuple-element.22.rest_2_.rest_5_), custom_call_target="tpu_custom_call" | custom-call | flops 4000000000 | bytes 1 | tf_op jit(solution)/shard_map/project/pallas_call | solution.py:43
  19.2 1.4 %project.9.after_ref.rest_2_ = bf16[2,80,768]{2,1,0:T(8,128)(2,1)S(1)} custom-call(bf16[80,1280]{1,0:T(8,128)(2,1)S(1)} %collective-permute-done.4.rest_3_.rest_0_, f32[2,80,768]{2,1,0:T(8,128)S(1)} %project.8.rest_1_, s32[2,3,160,768]{3,2,1,0:T(8,128)S(1)} %get-tuple-element.22.rest_2_.rest_5_, f32[3,768]{1,0:T(4,128)S(1)} %copy-done.3, s32[3,768]{1,0:T(4,128)S(1)} %copy-done.4), custom_call_target="tpu_custom_call" | custom-call | flops 1 | bytes 1 | tf_op jit(solution)/shard_map/project/pallas_call | solution.py:43
  20.6 4.4 %collective-permute-start.6 = (bf16[2,80,768]{2,1,0:T(8,128)(2,1)S(1)}, bf16[2,80,768]{2,1,0:T(8,128)(2,1)S(1)}, u32[]{:S(2)}, u32[]{:S(2)}) collective-permute-start(bf16[2,80,768]{2,1,0:T(8,128)(2,1)S(1)} %project.9.after_ref.rest_2_), channel_id=1, source_target_pairs={{0,4},{8,12},{4,0},{12,8},{1,5},{9,13},{5,1},{13,9},{2,6},{10,14},... | collective-permute-start | bytes 737288 | tf_op jit(solution)/shard_map/ppermute | solution.py:622
  25.1 0.8 %collective-permute-start.5 = (bf16[2,80,768]{2,1,0:T(8,128)(2,1)S(1)}, bf16[2,80,768]{2,1,0:T(8,128)(2,1)S(1)}, u32[]{:S(2)}, u32[]{:S(2)}) collective-permute-start(bf16[2,80,768]{2,1,0:T(8,128)(2,1)S(1)} %project.9.after_ref.rest_2_), channel_id=1, source_target_pairs={{4,8},{8,4},{5,9},{9,5},{6,10},{10,6},{7,11},{11,7},{20,24},{24,20... | collective-permute-start | bytes 737288 | tf_op jit(solution)/shard_map/ppermute | solution.py:622
  25.9 0.7 %window_masks.1 = (f32[3,192]{1,0:T(4,128)S(1)}, f32[3,224]{1,0:T(4,128)S(1)}, f32[3,80]{1,0:T(4,128)S(1)}, f32[3,80]{1,0:T(4,128)S(1)}) custom-call(s32[3,1,27]{2,1,0:T(1,128)S(1)} %bitcast.13, bf16[2,80,768]{2,1,0:T(8,128)(2,1)S(1)} %project.9.after_ref.rest_2_), custom_call_target="tpu_custom_call" | custom-call | flops 1 | bytes 1 | tf_op jit(solution)/shard_map/window_masks/pallas_call | solution.py:43
  26.7 1.5 %unpack_out.1.weights_ref = bf16[768,5120]{1,0:T(8,128)(2,1)S(1)} custom-call(s32[96,5120]{1,0:T(8,128)S(1)} %copy-done, bf16[2,80,768]{2,1,0:T(8,128)(2,1)S(1)} %project.9.after_ref.rest_2_), custom_call_target="tpu_custom_call" | custom-call | flops 1 | bytes 1 | tf_op jit(solution)/shard_map/unpack_out/pallas_call | solution.py:43
  28.1 1.8 %project.7.rest_0_ = bf16[1,192,768]{2,1,0:T(8,128)(2,1)S(1)} custom-call(bf16[112,1280]{1,0:T(8,128)(2,1)S(1)} %tie.3.rest_0_, bf16[112,1280]{1,0:T(8,128)(2,1)S(1)} %collective-permute-done.2.rest_0_.rest_1_, bf16[80,1280]{1,0:T(8,128)(2,1)S(1)} %tie.4.rest_2_.rest_0_, bf16[80,1280]{1,0:T(8,128)(2,1)S(1)} %collective-permute-done.4.rest_3_.rest_0_, ...), custom_call_target="tpu_custom_call" | custom-call | flops 4000000000 | bytes 1 | tf_op jit(solution)/shard_map/project/pallas_call | solution.py:43
  32.5 1.0 %out_project.3 = (bf16[96,2560]{1,0:T(8,128)(2,1)S(1)}, bf16[96,2560]{1,0:T(8,128)(2,1)S(1)}) custom-call(bf16[192,768]{1,0:T(8,128)(2,1)S(1)} %attend.7.rotated_ref, bf16[768,5120]{1,0:T(8,128)(2,1)S(1)} %unpack_out.1.weights_ref, f32[40,128]{1,0:T(8,128)S(1)} %bitcast.8), custom_call_target="tpu_custom_call" | custom-call | flops 1 | bytes 1 | tf_op jit(solution)/shard_map/out_project/pallas_call | solution.py:43
  33.6 1.0 %out_project.2 = (bf16[96,2560]{1,0:T(8,128)(2,1)S(1)}, bf16[96,2560]{1,0:T(8,128)(2,1)S(1)}) custom-call(bf16[192,768]{1,0:T(8,128)(2,1)S(1)} %attend.7.rotated_ref, bf16[768,5120]{1,0:T(8,128)(2,1)S(1)} %unpack_out.1.weights_ref, f32[40,128]{1,0:T(8,128)S(1)} %bitcast.9), custom_call_target="tpu_custom_call" | custom-call | flops 1 | bytes 1 | tf_op jit(solution)/shard_map/out_project/pallas_call | solution.py:43
  34.6 0.9 %collective-permute-done.9 = bf16[96,2560]{1,0:T(8,128)(2,1)S(1)} collective-permute-done((bf16[96,2560]{1,0:T(8,128)(2,1)S(1)}, bf16[96,2560]{1,0:T(8,128)(2,1)S(1)}, u32[]{:S(2)}, u32[]{:S(2)}) %collective-permute-start.9) | collective-permute-done | bytes 491552 | tf_op jit(solution)/shard_map/ppermute | solution.py:553
  35.8 1.5 %collective-permute-start.12 = (bf16[48,2560]{1,0:T(8,128)(2,1)S(1)}, bf16[48,2560]{1,0:T(8,128)(2,1)S(1)}, u32[]{:S(2)}, u32[]{:S(2)}) collective-permute-start(bf16[48,2560]{1,0:T(8,128)(2,1)S(1)} %slice.25.refs_1_), channel_id=1, source_target_pairs={{0,2},{1,3},{2,0},{3,1},{4,6},{5,7},{6,4},{7,5},{8,10},{9,11},{10,... | collective-permute-start | bytes 737288 | tf_op jit(solution)/shard_map/ppermute | solution.py:553
  37.7 1.6 %collective-permute-start.11 = (bf16[48,2560]{1,0:T(8,128)(2,1)S(1)}, bf16[48,2560]{1,0:T(8,128)(2,1)S(1)}, u32[]{:S(2)}, u32[]{:S(2)}) collective-permute-start(bf16[48,2560]{1,0:T(8,128)(2,1)S(1)} %slice.24), channel_id=1, source_target_pairs={{0,2},{1,3},{2,0},{3,1},{4,6},{5,7},{6,4},{7,5},{8,10},{9,11},{10,... | collective-permute-start | bytes 737288 | tf_op jit(solution)/shard_map/ppermute | solution.py:553
  39.3 5.3 %collective-permute-done.12.rest_1_ = bf16[48,2560]{1,0:T(8,128)(2,1)S(1)} collective-permute-done((bf16[48,2560]{1,0:T(8,128)(2,1)S(1)}, bf16[48,2560]{1,0:T(8,128)(2,1)S(1)}, u32[]{:S(2)}, u32[]{:S(2)}) %collective-permute-start.12) | collective-permute-done | bytes 245792 | tf_op jit(solution)/shard_map/ppermute | solution.py:553
  44.6 1.0 %finish.2.rest_2_ = bf16[48,5120]{1,0:T(8,128)(2,1)} custom-call(s32[40,128]{1,0:T(8,128)S(1)} %bitcast.10, f32[48,2560]{1,0:T(8,128)S(1)} %slice.21.rest_0_, bf16[48,2560]{1,0:T(8,128)(2,1)S(1)} %collective-permute-done.12.rest_1_), custom_call_target="tpu_custom_call" | custom-call | flops 1 | bytes 1 | tf_op jit(solution)/shard_map/finish/pallas_call | solution.py:43
  45.7 3.6 %collective-permute-done.11.rest_1_ = bf16[48,2560]{1,0:T(8,128)(2,1)S(1)} collective-permute-done((bf16[48,2560]{1,0:T(8,128)(2,1)S(1)}, bf16[48,2560]{1,0:T(8,128)(2,1)S(1)}, u32[]{:S(2)}, u32[]{:S(2)}) %collective-permute-start.11) | collective-permute-done | bytes 245792 | tf_op jit(solution)/shard_map/ppermute | solution.py:553
  49.3 1.0 %finish.3 = bf16[48,5120]{1,0:T(8,128)(2,1)} custom-call(s32[40,128]{1,0:T(8,128)S(1)} %bitcast.11, f32[48,2560]{1,0:T(8,128)S(1)} %slice.19.rest_0_, bf16[48,2560]{1,0:T(8,128)(2,1)S(1)} %collective-permute-done.11.rest_1_, bf16[48,5120]{1,0:T(8,128)(2,1)} %finish.2.rest_2_), custom_call_target="tpu_custom_call", output_to_operand_aliasing={{}: (3, {})} | custom-call | flops 1 | bytes 1 | tf_op jit(solution)/shard_map/finish/pallas_call | solution.py:43
  (43 shorter events, 5.1 us)
Async XLA Ops:
  1.3 3.1 %collective-permute-start.1 = (bf16[192,1280]{1,0:T(8,128)(2,1)S(1)}, bf16[192,1280]{1,0:T(8,128)(2,1)S(1)}, u32[]{:S(2)}, u32[]{:S(2)}) collective-permute-start(bf16[192,1280]{1,0:T(8,128)(2,1)S(1)} %get-tuple-element.19.rest_0_), channel_id=1, source_target_pairs={{0,1},{1,0},{2,3},{3,2},{4,5},{5,4},{6,7},{7,6},{8,9},{9,8},{10,11... | collective-permute-start | bytes 1474568 | tf_op jit(solution)/shard_map/ppermute | solution.py:553
  1.9 10.0 %collective-permute-start = (bf16[112,1280]{1,0:T(8,128)(2,1)S(1)}, bf16[112,1280]{1,0:T(8,128)(2,1)S(1)}, u32[]{:S(2)}, u32[]{:S(2)}) collective-permute-start(bf16[112,1280]{1,0:T(8,128)(2,1)S(1)} %get-tuple-element.18), channel_id=1, source_target_pairs={{0,2},{1,3},{2,0},{3,1},{4,6},{5,7},{6,4},{7,5},{8,10},{9,11},{10,... | collective-permute-start | bytes 860168 | tf_op jit(solution)/shard_map/ppermute | solution.py:553
  8.9 8.7 %collective-permute-start.3 = (bf16[80,1280]{1,0:T(8,128)(2,1)S(1)}, bf16[80,1280]{1,0:T(8,128)(2,1)S(1)}, u32[]{:S(2)}, u32[]{:S(2)}) collective-permute-start(bf16[80,1280]{1,0:T(8,128)(2,1)S(1)} %get-tuple-element.21), channel_id=1, source_target_pairs={{0,2},{1,3},{2,0},{3,1},{4,6},{5,7},{6,4},{7,5},{8,10},{9,11},{10,... | collective-permute-start | bytes 614408 | tf_op jit(solution)/shard_map/ppermute | solution.py:553
  11.9 1.6 %collective-permute-start.2 = (bf16[112,1280]{1,0:T(8,128)(2,1)S(1)}, bf16[112,1280]{1,0:T(8,128)(2,1)S(1)}, u32[]{:S(2)}, u32[]{:S(2)}) collective-permute-start(bf16[112,1280]{1,0:T(8,128)(2,1)S(1)} %tie.3.rest_0_), channel_id=1, source_target_pairs={{0,1},{1,0},{2,3},{3,2},{4,5},{5,4},{6,7},{7,6},{8,9},{9,8},{10,11... | collective-permute-start | bytes 860168 | tf_op jit(solution)/shard_map/ppermute | solution.py:553
  11.9 1.6 %copy-start.3 = (f32[3,768]{1,0:T(4,128)S(1)}, f32[3,768]{1,0:T(4,128)}, u32[]{:S(2)}) copy-start(f32[3,768]{1,0:T(4,128)} %rest_3_.3) | copy-start | bytes 27652
  11.9 1.6 %copy-start.4 = (s32[3,768]{1,0:T(4,128)S(1)}, s32[3,768]{1,0:T(4,128)}, u32[]{:S(2)}) copy-start(s32[3,768]{1,0:T(4,128)} %rest_4_.3) | copy-start | bytes 27652
  15.0 15.5 %collective-permute-start.8 = (bf16[2,112,768]{2,1,0:T(8,128)(2,1)S(1)}, bf16[2,112,768]{2,1,0:T(8,128)(2,1)S(1)}, u32[]{:S(2)}, u32[]{:S(2)}) collective-permute-start(bf16[2,112,768]{2,1,0:T(8,128)(2,1)S(1)} %project.6.array_ref.rest_1_), channel_id=1, source_target_pairs={{0,4},{8,12},{4,0},{12,8},{1,5},{9,13},{5,1},{13,9},{2,6},{10,14},... | collective-permute-start | bytes 1032200 | tf_op jit(solution)/shard_map/ppermute | solution.py:622
  16.9 13.6 %collective-permute-start.7 = (bf16[2,112,768]{2,1,0:T(8,128)(2,1)S(1)}, bf16[2,112,768]{2,1,0:T(8,128)(2,1)S(1)}, u32[]{:S(2)}, u32[]{:S(2)}) collective-permute-start(bf16[2,112,768]{2,1,0:T(8,128)(2,1)S(1)} %project.6.array_ref.rest_1_), channel_id=1, source_target_pairs={{4,8},{8,4},{5,9},{9,5},{6,10},{10,6},{7,11},{11,7},{20,24},{24,20... | collective-permute-start | bytes 1032200 | tf_op jit(solution)/shard_map/ppermute | solution.py:622
  17.6 1.5 %collective-permute-start.4 = (bf16[80,1280]{1,0:T(8,128)(2,1)S(1)}, bf16[80,1280]{1,0:T(8,128)(2,1)S(1)}, u32[]{:S(2)}, u32[]{:S(2)}) collective-permute-start(bf16[80,1280]{1,0:T(8,128)(2,1)S(1)} %tie.4.rest_2_.rest_0_), channel_id=1, source_target_pairs={{0,1},{1,0},{2,3},{3,2},{4,5},{5,4},{6,7},{7,6},{8,9},{9,8},{10,11... | collective-permute-start | bytes 614408 | tf_op jit(solution)/shard_map/ppermute | solution.py:553
  18.9 7.0 %copy-start.6 = (s32[1,3,27]{2,0,1:T(1,128)S(1)}, s32[1,3,27]{2,0,1:T(1,128)}, u32[]{:S(2)}) copy-start(s32[1,3,27]{2,0,1:T(1,128)} %param.15) | copy-start | bytes 976
  18.9 7.8 %copy-start = (s32[96,5120]{1,0:T(8,128)S(1)}, s32[96,5120]{1,0:T(8,128)}, u32[]{:S(2)}) copy-start(s32[96,5120]{1,0:T(8,128)} %codes_ref.1) | copy-start | bytes 5898244
  20.6 10.8 %collective-permute-start.6 = (bf16[2,80,768]{2,1,0:T(8,128)(2,1)S(1)}, bf16[2,80,768]{2,1,0:T(8,128)(2,1)S(1)}, u32[]{:S(2)}, u32[]{:S(2)}) collective-permute-start(bf16[2,80,768]{2,1,0:T(8,128)(2,1)S(1)} %project.9.after_ref.rest_2_), channel_id=1, source_target_pairs={{0,4},{8,12},{4,0},{12,8},{1,5},{9,13},{5,1},{13,9},{2,6},{10,14},... | collective-permute-start | bytes 737288 | tf_op jit(solution)/shard_map/ppermute | solution.py:622
  25.1 6.8 %collective-permute-start.5 = (bf16[2,80,768]{2,1,0:T(8,128)(2,1)S(1)}, bf16[2,80,768]{2,1,0:T(8,128)(2,1)S(1)}, u32[]{:S(2)}, u32[]{:S(2)}) collective-permute-start(bf16[2,80,768]{2,1,0:T(8,128)(2,1)S(1)} %project.9.after_ref.rest_2_), channel_id=1, source_target_pairs={{4,8},{8,4},{5,9},{9,5},{6,10},{10,6},{7,11},{11,7},{20,24},{24,20... | collective-permute-start | bytes 737288 | tf_op jit(solution)/shard_map/ppermute | solution.py:622
  31.1 0.8 %copy-start.5 = (s32[768]{0:T(1024)S(1)}, s32[768]{0:T(1024)}, u32[]{:S(2)}) copy-start(s32[768]{0:T(1024)} %param.16) | copy-start | bytes 9220
  31.4 1.1 %copy-start.1 = (f32[5120]{0:T(1024)S(1)}, f32[5120]{0:T(1024)}, u32[]{:S(2)}) copy-start(f32[5120]{0:T(1024)} %param.18) | copy-start | bytes 61444
  33.5 1.9 %collective-permute-start.9 = (bf16[96,2560]{1,0:T(8,128)(2,1)S(1)}, bf16[96,2560]{1,0:T(8,128)(2,1)S(1)}, u32[]{:S(2)}, u32[]{:S(2)}) collective-permute-start(bf16[96,2560]{1,0:T(8,128)(2,1)S(1)} %get-tuple-element.30), channel_id=1, source_target_pairs={{0,1},{1,0},{2,3},{3,2},{4,5},{5,4},{6,7},{7,6},{8,9},{9,8},{10,11... | collective-permute-start | bytes 1474568 | tf_op jit(solution)/shard_map/ppermute | solution.py:553
  35.6 9.0 %copy-start.2 = (s32[5120]{0:T(1024)S(1)}, s32[5120]{0:T(1024)}, u32[]{:S(2)}) copy-start(s32[5120]{0:T(1024)} %param.19) | copy-start | bytes 61444
  35.6 1.9 %collective-permute-start.10 = (bf16[96,2560]{1,0:T(8,128)(2,1)S(1)}, bf16[96,2560]{1,0:T(8,128)(2,1)S(1)}, u32[]{:S(2)}, u32[]{:S(2)}) collective-permute-start(bf16[96,2560]{1,0:T(8,128)(2,1)S(1)} %tie.5), channel_id=1, source_target_pairs={{0,1},{1,0},{2,3},{3,2},{4,5},{5,4},{6,7},{7,6},{8,9},{9,8},{10,11... | collective-permute-start | bytes 1474568 | tf_op jit(solution)/shard_map/ppermute | solution.py:553
  35.8 8.8 %collective-permute-start.12 = (bf16[48,2560]{1,0:T(8,128)(2,1)S(1)}, bf16[48,2560]{1,0:T(8,128)(2,1)S(1)}, u32[]{:S(2)}, u32[]{:S(2)}) collective-permute-start(bf16[48,2560]{1,0:T(8,128)(2,1)S(1)} %slice.25.refs_1_), channel_id=1, source_target_pairs={{0,2},{1,3},{2,0},{3,1},{4,6},{5,7},{6,4},{7,5},{8,10},{9,11},{10,... | collective-permute-start | bytes 737288 | tf_op jit(solution)/shard_map/ppermute | solution.py:553
  37.7 11.6 %collective-permute-start.11 = (bf16[48,2560]{1,0:T(8,128)(2,1)S(1)}, bf16[48,2560]{1,0:T(8,128)(2,1)S(1)}, u32[]{:S(2)}, u32[]{:S(2)}) collective-permute-start(bf16[48,2560]{1,0:T(8,128)(2,1)S(1)} %slice.24), channel_id=1, source_target_pairs={{0,2},{1,3},{2,0},{3,1},{4,6},{5,7},{6,4},{7,5},{8,10},{9,11},{10,... | collective-permute-start | bytes 737288 | tf_op jit(solution)/shard_map/ppermute | solution.py:553

commit v9 on v8

--- a/solution.py
+++ b/solution.py
@@ -19,6 +19,7 @@
 WORDS = HAD // PLANES
 QKV_ORDER = "half"
 OUT_ORDER = "byte"
+FINISH_BLOCK = 5 * HAD
 
 epsilon = 1e-06
 f32 = jnp.float32
@@ -132,7 +133,7 @@
 
 
 def early_rows(rows):
-    return rows * 7 // 12 // WORDS * WORDS
+    return rows * 5 // 12 // WORDS * WORDS
 
 
 def turn_kernel(x_hbm, sign_hbm, own_ref, send_ref, x_ref, sign_ref, sems):
@@ -509,20 +510,24 @@
     for chunk in range(chunks):
         keep_ref, more_ref = rest[2 * chunk : 2 * chunk + 2]
         share, columns = keep_ref.shape
-        totals = keep_ref[...].astype(f32) + more_ref[...].astype(f32)
-        blocks = [totals[:, at : at + HAD] for at in range(0, columns, HAD)]
-        turned = rotate_halves(jnp.concatenate(blocks, 0), doubled)
-        for block in range(len(blocks)):
-            place = first // HAD + block
-            sign_row = signed(sign_ref[place : place + 1, :]) * np.float32(HAD ** (-0.5))
-            done = turned[block * share : (block + 1) * share] * sign_row
-            done_ref[:, place * HAD : (place + 1) * HAD] = done.astype(bf16)
-        cols = pl.ds(first, columns)
-        copies.append(
-            pltpu.make_async_copy(done_ref.at[:, cols], out_hbm.at[:, cols], sems.at[chunk])
-        )
-        copies[-1].start()
-        first += columns
+        for part in range(0, columns, FINISH_BLOCK):
+            cols = slice(part, part + FINISH_BLOCK)
+            totals = keep_ref[:, cols].astype(f32) + more_ref[:, cols].astype(f32)
+            blocks = [totals[:, at : at + HAD] for at in range(0, FINISH_BLOCK, HAD)]
+            turned = rotate_halves(jnp.concatenate(blocks, 0), doubled)
+            for block in range(len(blocks)):
+                place = first // HAD + block
+                sign_row = signed(sign_ref[place : place + 1, :]) * np.float32(HAD ** (-0.5))
+                done = turned[block * share : (block + 1) * share] * sign_row
+                done_ref[:, place * HAD : (place + 1) * HAD] = done.astype(bf16)
+            where = pl.ds(first, FINISH_BLOCK)
+            copies.append(
+                pltpu.make_async_copy(
+                    done_ref.at[:, where], out_hbm.at[:, where], sems.at[len(copies)]
+                )
+            )
+            copies[-1].start()
+            first += FINISH_BLOCK
     for copy in copies:
         copy.wait()
 
@@ -543,7 +548,10 @@
         args,
         "finish",
         out_specs=HBM,
-        scratch_shapes=[pltpu.VMEM((share, D), bf16), pltpu.SemaphoreType.DMA((len(pairs),))],
+        scratch_shapes=[
+            pltpu.VMEM((share, D), bf16),
+            pltpu.SemaphoreType.DMA((D // FINISH_BLOCK,)),
+        ],
         input_output_aliases=aliases,
     )
 

time: 51.3 us -> 53.5 us (1.043)
  the two profiles are of different devices: /device:TPU:0 before, /device:TPU:20 now
where the time goes in v9:
time: 53.5 us; the launch traced here: 53.3 us
  Pallas kernels  21.3 us (40%)
  waiting for transfers between devices  17.5 us (33%)
  starting transfers between devices  13.7 us (26%)
    pallas_call x21, Pallas kernels, call(): pl.pallas_call(body, out_shape=out_shape, in_specs=in_specs, out_specs=ou...  21.3 us
    ppermute x9, waiting for transfers between devices, swap(): return lax.ppermute(shard, 'head', [(i, i ^ bit) for i in range(peers)])  13.3 us
    ppermute x4, starting transfers between devices, on_device(): lax.ppermute(key_value, 'height', pairs)  7.28 us
    ppermute x9, starting transfers between devices, swap(): return lax.ppermute(shard, 'head', [(i, i ^ bit) for i in range(peers)])  6.42 us
    ppermute x4, waiting for transfers between devices, on_device(): lax.ppermute(key_value, 'height', pairs)  4.13 us
  transfers between devices with their start and end apart: 13, of which 10 were waited for; matrix products, arithmetic and copies ran while one was open for 0% of the time, Pallas kernels for 33%

profile of v9, /device:TPU:20, one launch (start us, length us, event | category | flops | bytes accessed | tf_op | source)
XLA Modules:
  0.0 53.3 jit_solution(9145874480123934299)
XLA Ops:
  0.0 1.3 %turn.1 = (bf16[192,1280]{1,0:T(8,128)(2,1)S(1)}, bf16[80,1280]{1,0:T(8,128)(2,1)S(1)}) custom-call(bf16[192,1280]{1,0:T(8,128)(2,1)} %bitcast.15, s32[40,128]{1,0:T(8,128)} %bitcast.16), custom_call_target="tpu_custom_call" | custom-call | flops 1 | bytes 1 | tf_op jit(solution)/shard_map/turn/pallas_call | solution.py:44
  1.4 1.5 %collective-permute-start = (bf16[80,1280]{1,0:T(8,128)(2,1)S(1)}, bf16[80,1280]{1,0:T(8,128)(2,1)S(1)}, u32[]{:S(2)}, u32[]{:S(2)}) collective-permute-start(bf16[80,1280]{1,0:T(8,128)(2,1)S(1)} %get-tuple-element.18), channel_id=1, source_target_pairs={{0,2},{1,3},{2,0},{3,1},{4,6},{5,7},{6,4},{7,5},{8,10},{9,11},{10,... | collective-permute-start | bytes 614408 | tf_op jit(solution)/shard_map/ppermute | solution.py:561
  3.3 4.5 %prepare.1 = (f32[3,192,768]{2,1,0:T(8,128)S(1)}, s32[2,3,160,768]{3,2,1,0:T(8,128)S(1)}, bf16[112,1280]{1,0:T(8,128)(2,1)S(1)}) custom-call(bf16[192,1280]{1,0:T(8,128)(2,1)S(1)} %get-tuple-element.19.rest_0_, bf16[192,1280]{1,0:T(8,128)(2,1)S(1)} %collective-permute-done.1.rest_1_, s32[3,640,768]{2,1,0:T(8,128)} %bitcast.14), custom_call_target="tpu_custom_call" | custom-call | flops 1 | bytes 1 | tf_op jit(solution)/shard_map/prepare/pallas_call | solution.py:44
  7.8 1.2 %collective-permute-done.refs_0_ = bf16[80,1280]{1,0:T(8,128)(2,1)S(1)} collective-permute-done((bf16[80,1280]{1,0:T(8,128)(2,1)S(1)}, bf16[80,1280]{1,0:T(8,128)(2,1)S(1)}, u32[]{:S(2)}, u32[]{:S(2)}) %collective-permute-start) | collective-permute-done | bytes 204832 | tf_op jit(solution)/shard_map/ppermute | solution.py:561
  8.9 1.5 %collective-permute-start.3 = (bf16[112,1280]{1,0:T(8,128)(2,1)S(1)}, bf16[112,1280]{1,0:T(8,128)(2,1)S(1)}, u32[]{:S(2)}, u32[]{:S(2)}) collective-permute-start(bf16[112,1280]{1,0:T(8,128)(2,1)S(1)} %get-tuple-element.21), channel_id=1, source_target_pairs={{0,2},{1,3},{2,0},{3,1},{4,6},{5,7},{6,4},{7,5},{8,10},{9,11},{10,... | collective-permute-start | bytes 860168 | tf_op jit(solution)/shard_map/ppermute | solution.py:561
  10.4 1.2 %project.5.rest_1_ = f32[2,80,768]{2,1,0:T(8,128)S(1)} custom-call(bf16[80,1280]{1,0:T(8,128)(2,1)S(1)} %tie.3.rest_0_, f32[3,192,768]{2,1,0:T(8,128)S(1)} %get-tuple-element.20.refs_1_.rest_1_.refs_2_.rest_4_, s32[2,3,160,768]{3,2,1,0:T(8,128)S(1)} %get-tuple-element.22.rest_2_.rest_5_), custom_call_target="tpu_custom_call" | custom-call | flops 4000000000 | bytes 1 | tf_op jit(solution)/shard_map/project/pallas_call | solution.py:44
  11.6 1.4 %project.6.array_ref.rest_1_ = bf16[2,80,768]{2,1,0:T(8,128)(2,1)S(1)} custom-call(bf16[80,1280]{1,0:T(8,128)(2,1)S(1)} %collective-permute-done.2.rest_0_.rest_1_, f32[2,80,768]{2,1,0:T(8,128)S(1)} %project.5.rest_1_, s32[2,3,160,768]{3,2,1,0:T(8,128)S(1)} %get-tuple-element.22.rest_2_.rest_5_, f32[3,768]{1,0:T(4,128)S(1)} %copy-done.3, s32[3,768]{1,0:T(4,128)S(1)} %copy-done.4), custom_call_target="tpu_custom_call" | custom-call | flops 1 | bytes 1 | tf_op jit(solution)/shard_map/project/pallas_call | solution.py:44
  13.1 1.6 %collective-permute-start.8 = (bf16[2,80,768]{2,1,0:T(8,128)(2,1)S(1)}, bf16[2,80,768]{2,1,0:T(8,128)(2,1)S(1)}, u32[]{:S(2)}, u32[]{:S(2)}) collective-permute-start(bf16[2,80,768]{2,1,0:T(8,128)(2,1)S(1)} %project.6.array_ref.rest_1_), channel_id=1, source_target_pairs={{0,4},{8,12},{4,0},{12,8},{1,5},{9,13},{5,1},{13,9},{2,6},{10,14},... | collective-permute-start | bytes 737288 | tf_op jit(solution)/shard_map/ppermute | solution.py:630
  14.7 1.9 %collective-permute-start.7 = (bf16[2,80,768]{2,1,0:T(8,128)(2,1)S(1)}, bf16[2,80,768]{2,1,0:T(8,128)(2,1)S(1)}, u32[]{:S(2)}, u32[]{:S(2)}) collective-permute-start(bf16[2,80,768]{2,1,0:T(8,128)(2,1)S(1)} %project.6.array_ref.rest_1_), channel_id=1, source_target_pairs={{4,8},{8,4},{5,9},{9,5},{6,10},{10,6},{7,11},{11,7},{20,24},{24,20... | collective-permute-start | bytes 737288 | tf_op jit(solution)/shard_map/ppermute | solution.py:630
  16.6 1.5 %collective-permute-done.3.refs_0_ = bf16[112,1280]{1,0:T(8,128)(2,1)S(1)} collective-permute-done((bf16[112,1280]{1,0:T(8,128)(2,1)S(1)}, bf16[112,1280]{1,0:T(8,128)(2,1)S(1)}, u32[]{:S(2)}, u32[]{:S(2)}) %collective-permute-start.3) | collective-permute-done | bytes 286752 | tf_op jit(solution)/shard_map/ppermute | solution.py:561
  18.2 1.3 %project.8.rest_1_ = f32[2,112,768]{2,1,0:T(8,128)S(1)} custom-call(bf16[112,1280]{1,0:T(8,128)(2,1)S(1)} %tie.4.rest_2_.rest_0_, f32[3,192,768]{2,1,0:T(8,128)S(1)} %get-tuple-element.20.refs_1_.rest_1_.refs_2_.rest_4_, s32[2,3,160,768]{3,2,1,0:T(8,128)S(1)} %get-tuple-element.22.rest_2_.rest_5_), custom_call_target="tpu_custom_call" | custom-call | flops 4000000000 | bytes 1 | tf_op jit(solution)/shard_map/project/pallas_call | solution.py:44
  19.7 1.5 %project.9.after_ref.rest_2_ = bf16[2,112,768]{2,1,0:T(8,128)(2,1)S(1)} custom-call(bf16[112,1280]{1,0:T(8,128)(2,1)S(1)} %collective-permute-done.4.rest_3_.rest_0_, f32[2,112,768]{2,1,0:T(8,128)S(1)} %project.8.rest_1_, s32[2,3,160,768]{3,2,1,0:T(8,128)S(1)} %get-tuple-element.22.rest_2_.rest_5_, f32[3,768]{1,0:T(4,128)S(1)} %copy-done.3, ...), custom_call_target="tpu_custom_call" | custom-call | flops 1 | bytes 1 | tf_op jit(solution)/shard_map/project/pallas_call | solution.py:44
  21.3 1.6 %collective-permute-start.6 = (bf16[2,112,768]{2,1,0:T(8,128)(2,1)S(1)}, bf16[2,112,768]{2,1,0:T(8,128)(2,1)S(1)}, u32[]{:S(2)}, u32[]{:S(2)}) collective-permute-start(bf16[2,112,768]{2,1,0:T(8,128)(2,1)S(1)} %project.9.after_ref.rest_2_), channel_id=1, source_target_pairs={{0,4},{8,12},{4,0},{12,8},{1,5},{9,13},{5,1},{13,9},{2,6},{10,14},... | collective-permute-start | bytes 1032200 | tf_op jit(solution)/shard_map/ppermute | solution.py:630
  22.9 2.1 %collective-permute-start.5 = (bf16[2,112,768]{2,1,0:T(8,128)(2,1)S(1)}, bf16[2,112,768]{2,1,0:T(8,128)(2,1)S(1)}, u32[]{:S(2)}, u32[]{:S(2)}) collective-permute-start(bf16[2,112,768]{2,1,0:T(8,128)(2,1)S(1)} %project.9.after_ref.rest_2_), channel_id=1, source_target_pairs={{4,8},{8,4},{5,9},{9,5},{6,10},{10,6},{7,11},{11,7},{20,24},{24,20... | collective-permute-start | bytes 1032200 | tf_op jit(solution)/shard_map/ppermute | solution.py:630
  25.8 1.5 %unpack_out.1.weights_ref = bf16[768,5120]{1,0:T(8,128)(2,1)S(1)} custom-call(s32[96,5120]{1,0:T(8,128)S(1)} %copy-done, bf16[2,112,768]{2,1,0:T(8,128)(2,1)S(1)} %project.9.after_ref.rest_2_), custom_call_target="tpu_custom_call" | custom-call | flops 1 | bytes 1 | tf_op jit(solution)/shard_map/unpack_out/pallas_call | solution.py:44
  27.2 1.8 %project.7.rest_0_ = bf16[1,192,768]{2,1,0:T(8,128)(2,1)S(1)} custom-call(bf16[80,1280]{1,0:T(8,128)(2,1)S(1)} %tie.3.rest_0_, bf16[80,1280]{1,0:T(8,128)(2,1)S(1)} %collective-permute-done.2.rest_0_.rest_1_, bf16[112,1280]{1,0:T(8,128)(2,1)S(1)} %tie.4.rest_2_.rest_0_, bf16[112,1280]{1,0:T(8,128)(2,1)S(1)} %collective-permute-done.4.rest_3_.rest_0_, ...), custom_call_target="tpu_custom_call" | custom-call | flops 4000000000 | bytes 1 | tf_op jit(solution)/shard_map/project/pallas_call | solution.py:44
  30.1 1.4 %collective-permute-done.6.rest_1_ = bf16[2,112,768]{2,1,0:T(8,128)(2,1)S(1)} collective-permute-done((bf16[2,112,768]{2,1,0:T(8,128)(2,1)S(1)}, bf16[2,112,768]{2,1,0:T(8,128)(2,1)S(1)}, u32[]{:S(2)}, u32[]{:S(2)}) %collective-permute-start.6) | collective-permute-done | bytes 344096 | tf_op jit(solution)/shard_map/ppermute | solution.py:630
  32.0 2.7 %collective-permute-done.5.rest_1_ = bf16[2,112,768]{2,1,0:T(8,128)(2,1)S(1)} collective-permute-done((bf16[2,112,768]{2,1,0:T(8,128)(2,1)S(1)}, bf16[2,112,768]{2,1,0:T(8,128)(2,1)S(1)}, u32[]{:S(2)}, u32[]{:S(2)}) %collective-permute-start.5) | collective-permute-done | bytes 344096 | tf_op jit(solution)/shard_map/ppermute | solution.py:630
  38.7 1.5 %collective-permute-start.12 = (bf16[48,2560]{1,0:T(8,128)(2,1)S(1)}, bf16[48,2560]{1,0:T(8,128)(2,1)S(1)}, u32[]{:S(2)}, u32[]{:S(2)}) collective-permute-start(bf16[48,2560]{1,0:T(8,128)(2,1)S(1)} %slice.25.refs_1_), channel_id=1, source_target_pairs={{0,2},{1,3},{2,0},{3,1},{4,6},{5,7},{6,4},{7,5},{8,10},{9,11},{10,... | collective-permute-start | bytes 737288 | tf_op jit(solution)/shard_map/ppermute | solution.py:561
  40.5 1.5 %collective-permute-start.11 = (bf16[48,2560]{1,0:T(8,128)(2,1)S(1)}, bf16[48,2560]{1,0:T(8,128)(2,1)S(1)}, u32[]{:S(2)}, u32[]{:S(2)}) collective-permute-start(bf16[48,2560]{1,0:T(8,128)(2,1)S(1)} %slice.24), channel_id=1, source_target_pairs={{0,2},{1,3},{2,0},{3,1},{4,6},{5,7},{6,4},{7,5},{8,10},{9,11},{10,... | collective-permute-start | bytes 737288 | tf_op jit(solution)/shard_map/ppermute | solution.py:561
  42.1 5.3 %collective-permute-done.12.rest_1_ = bf16[48,2560]{1,0:T(8,128)(2,1)S(1)} collective-permute-done((bf16[48,2560]{1,0:T(8,128)(2,1)S(1)}, bf16[48,2560]{1,0:T(8,128)(2,1)S(1)}, u32[]{:S(2)}, u32[]{:S(2)}) %collective-permute-start.12) | collective-permute-done | bytes 245792 | tf_op jit(solution)/shard_map/ppermute | solution.py:561
  47.4 1.0 %finish.2.rest_2_ = bf16[48,5120]{1,0:T(8,128)(2,1)} custom-call(s32[40,128]{1,0:T(8,128)S(1)} %bitcast.10, f32[48,2560]{1,0:T(8,128)S(1)} %slice.21.rest_0_, bf16[48,2560]{1,0:T(8,128)(2,1)S(1)} %collective-permute-done.12.rest_1_), custom_call_target="tpu_custom_call" | custom-call | flops 1 | bytes 1 | tf_op jit(solution)/shard_map/finish/pallas_call | solution.py:44
  48.5 3.6 %collective-permute-done.11.rest_1_ = bf16[48,2560]{1,0:T(8,128)(2,1)S(1)} collective-permute-done((bf16[48,2560]{1,0:T(8,128)(2,1)S(1)}, bf16[48,2560]{1,0:T(8,128)(2,1)S(1)}, u32[]{:S(2)}, u32[]{:S(2)}) %collective-permute-start.11) | collective-permute-done | bytes 245792 | tf_op jit(solution)/shard_map/ppermute | solution.py:561
  52.2 1.0 %finish.3 = bf16[48,5120]{1,0:T(8,128)(2,1)} custom-call(s32[40,128]{1,0:T(8,128)S(1)} %bitcast.11, f32[48,2560]{1,0:T(8,128)S(1)} %slice.19.rest_0_, bf16[48,2560]{1,0:T(8,128)(2,1)S(1)} %collective-permute-done.11.rest_1_, bf16[48,5120]{1,0:T(8,128)(2,1)} %finish.2.rest_2_), custom_call_target="tpu_custom_call", output_to_operand_aliasing={{}: (3, {})} | custom-call | flops 1 | bytes 1 | tf_op jit(solution)/shard_map/finish/pallas_call | solution.py:44
  (43 shorter events, 7.2 us)
Async XLA Ops:
  1.4 1.9 %collective-permute-start.1 = (bf16[192,1280]{1,0:T(8,128)(2,1)S(1)}, bf16[192,1280]{1,0:T(8,128)(2,1)S(1)}, u32[]{:S(2)}, u32[]{:S(2)}) collective-permute-start(bf16[192,1280]{1,0:T(8,128)(2,1)S(1)} %get-tuple-element.19.rest_0_), channel_id=1, source_target_pairs={{0,1},{1,0},{2,3},{3,2},{4,5},{5,4},{6,7},{7,6},{8,9},{9,8},{10,11... | collective-permute-start | bytes 1474568 | tf_op jit(solution)/shard_map/ppermute | solution.py:561
  1.4 7.5 %collective-permute-start = (bf16[80,1280]{1,0:T(8,128)(2,1)S(1)}, bf16[80,1280]{1,0:T(8,128)(2,1)S(1)}, u32[]{:S(2)}, u32[]{:S(2)}) collective-permute-start(bf16[80,1280]{1,0:T(8,128)(2,1)S(1)} %get-tuple-element.18), channel_id=1, source_target_pairs={{0,2},{1,3},{2,0},{3,1},{4,6},{5,7},{6,4},{7,5},{8,10},{9,11},{10,... | collective-permute-start | bytes 614408 | tf_op jit(solution)/shard_map/ppermute | solution.py:561
  8.9 2.7 %collective-permute-start.2 = (bf16[80,1280]{1,0:T(8,128)(2,1)S(1)}, bf16[80,1280]{1,0:T(8,128)(2,1)S(1)}, u32[]{:S(2)}, u32[]{:S(2)}) collective-permute-start(bf16[80,1280]{1,0:T(8,128)(2,1)S(1)} %tie.3.rest_0_), channel_id=1, source_target_pairs={{0,1},{1,0},{2,3},{3,2},{4,5},{5,4},{6,7},{7,6},{8,9},{9,8},{10,11... | collective-permute-start | bytes 614408 | tf_op jit(solution)/shard_map/ppermute | solution.py:561
  8.9 9.2 %collective-permute-start.3 = (bf16[112,1280]{1,0:T(8,128)(2,1)S(1)}, bf16[112,1280]{1,0:T(8,128)(2,1)S(1)}, u32[]{:S(2)}, u32[]{:S(2)}) collective-permute-start(bf16[112,1280]{1,0:T(8,128)(2,1)S(1)} %get-tuple-element.21), channel_id=1, source_target_pairs={{0,2},{1,3},{2,0},{3,1},{4,6},{5,7},{6,4},{7,5},{8,10},{9,11},{10,... | collective-permute-start | bytes 860168 | tf_op jit(solution)/shard_map/ppermute | solution.py:561
  10.4 1.2 %copy-start.3 = (f32[3,768]{1,0:T(4,128)S(1)}, f32[3,768]{1,0:T(4,128)}, u32[]{:S(2)}) copy-start(f32[3,768]{1,0:T(4,128)} %rest_3_.3) | copy-start | bytes 27652
  10.4 1.2 %copy-start.4 = (s32[3,768]{1,0:T(4,128)S(1)}, s32[3,768]{1,0:T(4,128)}, u32[]{:S(2)}) copy-start(s32[3,768]{1,0:T(4,128)} %rest_4_.3) | copy-start | bytes 27652
  13.1 16.5 %collective-permute-start.8 = (bf16[2,80,768]{2,1,0:T(8,128)(2,1)S(1)}, bf16[2,80,768]{2,1,0:T(8,128)(2,1)S(1)}, u32[]{:S(2)}, u32[]{:S(2)}) collective-permute-start(bf16[2,80,768]{2,1,0:T(8,128)(2,1)S(1)} %project.6.array_ref.rest_1_), channel_id=1, source_target_pairs={{0,4},{8,12},{4,0},{12,8},{1,5},{9,13},{5,1},{13,9},{2,6},{10,14},... | collective-permute-start | bytes 737288 | tf_op jit(solution)/shard_map/ppermute | solution.py:630
  14.7 14.9 %collective-permute-start.7 = (bf16[2,80,768]{2,1,0:T(8,128)(2,1)S(1)}, bf16[2,80,768]{2,1,0:T(8,128)(2,1)S(1)}, u32[]{:S(2)}, u32[]{:S(2)}) collective-permute-start(bf16[2,80,768]{2,1,0:T(8,128)(2,1)S(1)} %project.6.array_ref.rest_1_), channel_id=1, source_target_pairs={{4,8},{8,4},{5,9},{9,5},{6,10},{10,6},{7,11},{11,7},{20,24},{24,20... | collective-permute-start | bytes 737288 | tf_op jit(solution)/shard_map/ppermute | solution.py:630
  18.2 1.6 %collective-permute-start.4 = (bf16[112,1280]{1,0:T(8,128)(2,1)S(1)}, bf16[112,1280]{1,0:T(8,128)(2,1)S(1)}, u32[]{:S(2)}, u32[]{:S(2)}) collective-permute-start(bf16[112,1280]{1,0:T(8,128)(2,1)S(1)} %tie.4.rest_2_.rest_0_), channel_id=1, source_target_pairs={{0,1},{1,0},{2,3},{3,2},{4,5},{5,4},{6,7},{7,6},{8,9},{9,8},{10,11... | collective-permute-start | bytes 860168 | tf_op jit(solution)/shard_map/ppermute | solution.py:561
  19.4 5.6 %copy-start.6 = (s32[1,3,27]{2,0,1:T(1,128)S(1)}, s32[1,3,27]{2,0,1:T(1,128)}, u32[]{:S(2)}) copy-start(s32[1,3,27]{2,0,1:T(1,128)} %param.15) | copy-start | bytes 976
  19.5 6.3 %copy-start = (s32[96,5120]{1,0:T(8,128)S(1)}, s32[96,5120]{1,0:T(8,128)}, u32[]{:S(2)}) copy-start(s32[96,5120]{1,0:T(8,128)} %codes_ref.1) | copy-start | bytes 5898244
  21.3 10.3 %collective-permute-start.6 = (bf16[2,112,768]{2,1,0:T(8,128)(2,1)S(1)}, bf16[2,112,768]{2,1,0:T(8,128)(2,1)S(1)}, u32[]{:S(2)}, u32[]{:S(2)}) collective-permute-start(bf16[2,112,768]{2,1,0:T(8,128)(2,1)S(1)} %project.9.after_ref.rest_2_), channel_id=1, source_target_pairs={{0,4},{8,12},{4,0},{12,8},{1,5},{9,13},{5,1},{13,9},{2,6},{10,14},... | collective-permute-start | bytes 1032200 | tf_op jit(solution)/shard_map/ppermute | solution.py:630
  22.9 11.8 %collective-permute-start.5 = (bf16[2,112,768]{2,1,0:T(8,128)(2,1)S(1)}, bf16[2,112,768]{2,1,0:T(8,128)(2,1)S(1)}, u32[]{:S(2)}, u32[]{:S(2)}) collective-permute-start(bf16[2,112,768]{2,1,0:T(8,128)(2,1)S(1)} %project.9.after_ref.rest_2_), channel_id=1, source_target_pairs={{4,8},{8,4},{5,9},{9,5},{6,10},{10,6},{7,11},{11,7},{20,24},{24,20... | collective-permute-start | bytes 1032200 | tf_op jit(solution)/shard_map/ppermute | solution.py:630
  30.1 4.6 %copy-start.5 = (s32[768]{0:T(1024)S(1)}, s32[768]{0:T(1024)}, u32[]{:S(2)}) copy-start(s32[768]{0:T(1024)} %param.16) | copy-start | bytes 9220
  31.6 3.8 %copy-start.1 = (f32[5120]{0:T(1024)S(1)}, f32[5120]{0:T(1024)}, u32[]{:S(2)}) copy-start(f32[5120]{0:T(1024)} %param.18) | copy-start | bytes 61444
  36.3 1.9 %collective-permute-start.9 = (bf16[96,2560]{1,0:T(8,128)(2,1)S(1)}, bf16[96,2560]{1,0:T(8,128)(2,1)S(1)}, u32[]{:S(2)}, u32[]{:S(2)}) collective-permute-start(bf16[96,2560]{1,0:T(8,128)(2,1)S(1)} %get-tuple-element.30), channel_id=1, source_target_pairs={{0,1},{1,0},{2,3},{3,2},{4,5},{5,4},{6,7},{7,6},{8,9},{9,8},{10,11... | collective-permute-start | bytes 1474568 | tf_op jit(solution)/shard_map/ppermute | solution.py:561
  38.4 9.0 %copy-start.2 = (s32[5120]{0:T(1024)S(1)}, s32[5120]{0:T(1024)}, u32[]{:S(2)}) copy-start(s32[5120]{0:T(1024)} %param.19) | copy-start | bytes 61444
  38.4 1.9 %collective-permute-start.10 = (bf16[96,2560]{1,0:T(8,128)(2,1)S(1)}, bf16[96,2560]{1,0:T(8,128)(2,1)S(1)}, u32[]{:S(2)}, u32[]{:S(2)}) collective-permute-start(bf16[96,2560]{1,0:T(8,128)(2,1)S(1)} %tie.5), channel_id=1, source_target_pairs={{0,1},{1,0},{2,3},{3,2},{4,5},{5,4},{6,7},{7,6},{8,9},{9,8},{10,11... | collective-permute-start | bytes 1474568 | tf_op jit(solution)/shard_map/ppermute | solution.py:561
  38.7 8.8 %collective-permute-start.12 = (bf16[48,2560]{1,0:T(8,128)(2,1)S(1)}, bf16[48,2560]{1,0:T(8,128)(2,1)S(1)}, u32[]{:S(2)}, u32[]{:S(2)}) collective-permute-start(bf16[48,2560]{1,0:T(8,128)(2,1)S(1)} %slice.25.refs_1_), channel_id=1, source_target_pairs={{0,2},{1,3},{2,0},{3,1},{4,6},{5,7},{6,4},{7,5},{8,10},{9,11},{10,... | collective-permute-start | bytes 737288 | tf_op jit(solution)/shard_map/ppermute | solution.py:561
  40.5 11.6 %collective-permute-start.11 = (bf16[48,2560]{1,0:T(8,128)(2,1)S(1)}, bf16[48,2560]{1,0:T(8,128)(2,1)S(1)}, u32[]{:S(2)}, u32[]{:S(2)}) collective-permute-start(bf16[48,2560]{1,0:T(8,128)(2,1)S(1)} %slice.24), channel_id=1, source_target_pairs={{0,2},{1,3},{2,0},{3,1},{4,6},{5,7},{6,4},{7,5},{8,10},{9,11},{10,... | collective-permute-start | bytes 737288 | tf_op jit(solution)/shard_map/ppermute | solution.py:561

commit v10 on v8

--- a/solution.py
+++ b/solution.py
@@ -132,7 +132,7 @@
 
 
 def early_rows(rows):
-    return rows * 7 // 12 // WORDS * WORDS
+    return rows // 2 // WORDS * WORDS
 
 
 def turn_kernel(x_hbm, sign_hbm, own_ref, send_ref, x_ref, sign_ref, sems):

time: 51.3 us -> 52.3 us (1.019)
  waiting for transfers between devices: 12 us -> 17.2 us
  starting transfers between devices: 16.2 us -> 12.4 us
    ppermute x9, waiting for transfers between devices: 11.7 us -> 15.8 us  [swap(): return lax.ppermute(shard, 'head', [(i, i ^ bit) for i in range(peers)])]
    ppermute x9, starting transfers between devices: 8.36 us -> 6.34 us  [swap(): return lax.ppermute(shard, 'head', [(i, i ^ bit) for i in range(peers)])]
    ppermute x4, starting transfers between devices: 7.89 us -> 6.1 us  [on_device(): lax.ppermute(key_value, 'height', pairs)]
    ppermute x4, waiting for transfers between devices: 0.36 us -> 1.41 us  [on_device(): lax.ppermute(key_value, 'height', pairs)]
  transfers between devices with their start and end apart: 13 -> 13, of which waited for: 8 -> 8; matrix products, arithmetic and copies ran while one was open for 0% -> 0% of each run, Pallas kernels for 34% -> 33%
where the time goes in v10:
time: 52.3 us; the launch traced here: 51.8 us
  Pallas kernels  21.3 us (41%)
  waiting for transfers between devices  17.2 us (33%)
  starting transfers between devices  12.4 us (24%)
    pallas_call x21, Pallas kernels, call(): pl.pallas_call(body, out_shape=out_shape, in_specs=in_specs, out_specs=ou...  21.3 us
    ppermute x9, waiting for transfers between devices, swap(): return lax.ppermute(shard, 'head', [(i, i ^ bit) for i in range(peers)])  15.8 us
    ppermute x9, starting transfers between devices, swap(): return lax.ppermute(shard, 'head', [(i, i ^ bit) for i in range(peers)])  6.34 us
    ppermute x4, starting transfers between devices, on_device(): lax.ppermute(key_value, 'height', pairs)  6.1 us
    ppermute x4, waiting for transfers between devices, on_device(): lax.ppermute(key_value, 'height', pairs)  1.41 us
  transfers between devices with their start and end apart: 13, of which 8 were waited for; matrix products, arithmetic and copies ran while one was open for 0% of the time, Pallas kernels for 33%

profile of v10, /device:TPU:0, one launch (start us, length us, event | category | flops | bytes accessed | tf_op | source)
XLA Modules:
  0.0 51.8 jit_solution(5435148601935208298)
XLA Ops:
  0.0 1.3 %turn.1 = (bf16[192,1280]{1,0:T(8,128)(2,1)S(1)}, bf16[96,1280]{1,0:T(8,128)(2,1)S(1)}) custom-call(bf16[192,1280]{1,0:T(8,128)(2,1)} %bitcast.15, s32[40,128]{1,0:T(8,128)} %bitcast.16), custom_call_target="tpu_custom_call" | custom-call | flops 1 | bytes 1 | tf_op jit(solution)/shard_map/turn/pallas_call | solution.py:43
  1.9 2.6 %collective-permute-start = (bf16[96,1280]{1,0:T(8,128)(2,1)S(1)}, bf16[96,1280]{1,0:T(8,128)(2,1)S(1)}, u32[]{:S(2)}, u32[]{:S(2)}) collective-permute-start(bf16[96,1280]{1,0:T(8,128)(2,1)S(1)} %get-tuple-element.18), channel_id=1, source_target_pairs={{0,2},{1,3},{2,0},{3,1},{4,6},{5,7},{6,4},{7,5},{8,10},{9,11},{10,... | collective-permute-start | bytes 737288 | tf_op jit(solution)/shard_map/ppermute | solution.py:553
  4.4 4.5 %prepare.1 = (f32[3,192,768]{2,1,0:T(8,128)S(1)}, s32[2,3,160,768]{3,2,1,0:T(8,128)S(1)}, bf16[96,1280]{1,0:T(8,128)(2,1)S(1)}) custom-call(bf16[192,1280]{1,0:T(8,128)(2,1)S(1)} %get-tuple-element.19.rest_0_, bf16[192,1280]{1,0:T(8,128)(2,1)S(1)} %collective-permute-done.1.rest_1_, s32[3,640,768]{2,1,0:T(8,128)} %bitcast.14), custom_call_target="tpu_custom_call" | custom-call | flops 1 | bytes 1 | tf_op jit(solution)/shard_map/prepare/pallas_call | solution.py:43
  8.9 2.1 %collective-permute-done.refs_0_ = bf16[96,1280]{1,0:T(8,128)(2,1)S(1)} collective-permute-done((bf16[96,1280]{1,0:T(8,128)(2,1)S(1)}, bf16[96,1280]{1,0:T(8,128)(2,1)S(1)}, u32[]{:S(2)}, u32[]{:S(2)}) %collective-permute-start) | collective-permute-done | bytes 245792 | tf_op jit(solution)/shard_map/ppermute | solution.py:553
  11.0 1.8 %collective-permute-start.3 = (bf16[96,1280]{1,0:T(8,128)(2,1)S(1)}, bf16[96,1280]{1,0:T(8,128)(2,1)S(1)}, u32[]{:S(2)}, u32[]{:S(2)}) collective-permute-start(bf16[96,1280]{1,0:T(8,128)(2,1)S(1)} %get-tuple-element.21), channel_id=1, source_target_pairs={{0,2},{1,3},{2,0},{3,1},{4,6},{5,7},{6,4},{7,5},{8,10},{9,11},{10,... | collective-permute-start | bytes 737288 | tf_op jit(solution)/shard_map/ppermute | solution.py:553
  12.7 1.2 %project.5.rest_1_ = f32[2,96,768]{2,1,0:T(8,128)S(1)} custom-call(bf16[96,1280]{1,0:T(8,128)(2,1)S(1)} %tie.3.rest_0_, f32[3,192,768]{2,1,0:T(8,128)S(1)} %get-tuple-element.20.refs_1_.rest_1_.refs_2_.rest_4_, s32[2,3,160,768]{3,2,1,0:T(8,128)S(1)} %get-tuple-element.22.rest_2_.rest_5_), custom_call_target="tpu_custom_call" | custom-call | flops 4000000000 | bytes 1 | tf_op jit(solution)/shard_map/project/pallas_call | solution.py:43
  14.0 1.5 %project.6.array_ref.rest_1_ = bf16[2,96,768]{2,1,0:T(8,128)(2,1)S(1)} custom-call(bf16[96,1280]{1,0:T(8,128)(2,1)S(1)} %collective-permute-done.2.rest_0_.rest_1_, f32[2,96,768]{2,1,0:T(8,128)S(1)} %project.5.rest_1_, s32[2,3,160,768]{3,2,1,0:T(8,128)S(1)} %get-tuple-element.22.rest_2_.rest_5_, f32[3,768]{1,0:T(4,128)S(1)} %copy-done.3, s32[3,768]{1,0:T(4,128)S(1)} %copy-done.4), custom_call_target="tpu_custom_call" | custom-call | flops 1 | bytes 1 | tf_op jit(solution)/shard_map/project/pallas_call | solution.py:43
  15.4 1.6 %collective-permute-start.8 = (bf16[2,96,768]{2,1,0:T(8,128)(2,1)S(1)}, bf16[2,96,768]{2,1,0:T(8,128)(2,1)S(1)}, u32[]{:S(2)}, u32[]{:S(2)}) collective-permute-start(bf16[2,96,768]{2,1,0:T(8,128)(2,1)S(1)} %project.6.array_ref.rest_1_), channel_id=1, source_target_pairs={{0,4},{8,12},{4,0},{12,8},{1,5},{9,13},{5,1},{13,9},{2,6},{10,14},... | collective-permute-start | bytes 884744 | tf_op jit(solution)/shard_map/ppermute | solution.py:622
  17.8 1.6 %collective-permute-done.3.refs_0_ = bf16[96,1280]{1,0:T(8,128)(2,1)S(1)} collective-permute-done((bf16[96,1280]{1,0:T(8,128)(2,1)S(1)}, bf16[96,1280]{1,0:T(8,128)(2,1)S(1)}, u32[]{:S(2)}, u32[]{:S(2)}) %collective-permute-start.3) | collective-permute-done | bytes 245792 | tf_op jit(solution)/shard_map/ppermute | solution.py:553
  19.4 1.2 %project.8.rest_1_ = f32[2,96,768]{2,1,0:T(8,128)S(1)} custom-call(bf16[96,1280]{1,0:T(8,128)(2,1)S(1)} %tie.4.rest_2_.rest_0_, f32[3,192,768]{2,1,0:T(8,128)S(1)} %get-tuple-element.20.refs_1_.rest_1_.refs_2_.rest_4_, s32[2,3,160,768]{3,2,1,0:T(8,128)S(1)} %get-tuple-element.22.rest_2_.rest_5_), custom_call_target="tpu_custom_call" | custom-call | flops 4000000000 | bytes 1 | tf_op jit(solution)/shard_map/project/pallas_call | solution.py:43
  20.9 1.5 %project.9.after_ref.rest_2_ = bf16[2,96,768]{2,1,0:T(8,128)(2,1)S(1)} custom-call(bf16[96,1280]{1,0:T(8,128)(2,1)S(1)} %collective-permute-done.4.rest_3_.rest_0_, f32[2,96,768]{2,1,0:T(8,128)S(1)} %project.8.rest_1_, s32[2,3,160,768]{3,2,1,0:T(8,128)S(1)} %get-tuple-element.22.rest_2_.rest_5_, f32[3,768]{1,0:T(4,128)S(1)} %copy-done.3, s32[3,768]{1,0:T(4,128)S(1)} %copy-done.4), custom_call_target="tpu_custom_call" | custom-call | flops 1 | bytes 1 | tf_op jit(solution)/shard_map/project/pallas_call | solution.py:43
  22.3 2.9 %collective-permute-start.6 = (bf16[2,96,768]{2,1,0:T(8,128)(2,1)S(1)}, bf16[2,96,768]{2,1,0:T(8,128)(2,1)S(1)}, u32[]{:S(2)}, u32[]{:S(2)}) collective-permute-start(bf16[2,96,768]{2,1,0:T(8,128)(2,1)S(1)} %project.9.after_ref.rest_2_), channel_id=1, source_target_pairs={{0,4},{8,12},{4,0},{12,8},{1,5},{9,13},{5,1},{13,9},{2,6},{10,14},... | collective-permute-start | bytes 884744 | tf_op jit(solution)/shard_map/ppermute | solution.py:622
  25.3 0.8 %collective-permute-start.5 = (bf16[2,96,768]{2,1,0:T(8,128)(2,1)S(1)}, bf16[2,96,768]{2,1,0:T(8,128)(2,1)S(1)}, u32[]{:S(2)}, u32[]{:S(2)}) collective-permute-start(bf16[2,96,768]{2,1,0:T(8,128)(2,1)S(1)} %project.9.after_ref.rest_2_), channel_id=1, source_target_pairs={{4,8},{8,4},{5,9},{9,5},{6,10},{10,6},{7,11},{11,7},{20,24},{24,20... | collective-permute-start | bytes 884744 | tf_op jit(solution)/shard_map/ppermute | solution.py:622
  26.9 1.5 %unpack_out.1.weights_ref = bf16[768,5120]{1,0:T(8,128)(2,1)S(1)} custom-call(s32[96,5120]{1,0:T(8,128)S(1)} %copy-done, bf16[2,96,768]{2,1,0:T(8,128)(2,1)S(1)} %project.9.after_ref.rest_2_), custom_call_target="tpu_custom_call" | custom-call | flops 1 | bytes 1 | tf_op jit(solution)/shard_map/unpack_out/pallas_call | solution.py:43
  28.4 1.8 %project.7.rest_0_ = bf16[1,192,768]{2,1,0:T(8,128)(2,1)S(1)} custom-call(bf16[96,1280]{1,0:T(8,128)(2,1)S(1)} %tie.3.rest_0_, bf16[96,1280]{1,0:T(8,128)(2,1)S(1)} %collective-permute-done.2.rest_0_.rest_1_, bf16[96,1280]{1,0:T(8,128)(2,1)S(1)} %tie.4.rest_2_.rest_0_, bf16[96,1280]{1,0:T(8,128)(2,1)S(1)} %collective-permute-done.4.rest_3_.rest_0_, ...), custom_call_target="tpu_custom_call" | custom-call | flops 4000000000 | bytes 1 | tf_op jit(solution)/shard_map/project/pallas_call | solution.py:43
  31.3 1.4 %collective-permute-done.6.rest_1_ = bf16[2,96,768]{2,1,0:T(8,128)(2,1)S(1)} collective-permute-done((bf16[2,96,768]{2,1,0:T(8,128)(2,1)S(1)}, bf16[2,96,768]{2,1,0:T(8,128)(2,1)S(1)}, u32[]{:S(2)}, u32[]{:S(2)}) %collective-permute-start.6) | collective-permute-done | bytes 294944 | tf_op jit(solution)/shard_map/ppermute | solution.py:622
  33.8 1.0 %out_project.3 = (bf16[96,2560]{1,0:T(8,128)(2,1)S(1)}, bf16[96,2560]{1,0:T(8,128)(2,1)S(1)}) custom-call(bf16[192,768]{1,0:T(8,128)(2,1)S(1)} %attend.7.rotated_ref, bf16[768,5120]{1,0:T(8,128)(2,1)S(1)} %unpack_out.1.weights_ref, f32[40,128]{1,0:T(8,128)S(1)} %bitcast.8), custom_call_target="tpu_custom_call" | custom-call | flops 1 | bytes 1 | tf_op jit(solution)/shard_map/out_project/pallas_call | solution.py:43
  34.9 1.0 %out_project.2 = (bf16[96,2560]{1,0:T(8,128)(2,1)S(1)}, bf16[96,2560]{1,0:T(8,128)(2,1)S(1)}) custom-call(bf16[192,768]{1,0:T(8,128)(2,1)S(1)} %attend.7.rotated_ref, bf16[768,5120]{1,0:T(8,128)(2,1)S(1)} %unpack_out.1.weights_ref, f32[40,128]{1,0:T(8,128)S(1)} %bitcast.9), custom_call_target="tpu_custom_call" | custom-call | flops 1 | bytes 1 | tf_op jit(solution)/shard_map/out_project/pallas_call | solution.py:43
  35.9 0.9 %collective-permute-done.9 = bf16[96,2560]{1,0:T(8,128)(2,1)S(1)} collective-permute-done((bf16[96,2560]{1,0:T(8,128)(2,1)S(1)}, bf16[96,2560]{1,0:T(8,128)(2,1)S(1)}, u32[]{:S(2)}, u32[]{:S(2)}) %collective-permute-start.9) | collective-permute-done | bytes 491552 | tf_op jit(solution)/shard_map/ppermute | solution.py:553
  37.7 1.1 %collective-permute-done.10 = bf16[96,2560]{1,0:T(8,128)(2,1)S(1)} collective-permute-done((bf16[96,2560]{1,0:T(8,128)(2,1)S(1)}, bf16[96,2560]{1,0:T(8,128)(2,1)S(1)}, u32[]{:S(2)}, u32[]{:S(2)}) %collective-permute-start.10) | collective-permute-done | bytes 491552 | tf_op jit(solution)/shard_map/ppermute | solution.py:553
  39.7 6.2 %collective-permute-done.12.rest_1_ = bf16[48,2560]{1,0:T(8,128)(2,1)S(1)} collective-permute-done((bf16[48,2560]{1,0:T(8,128)(2,1)S(1)}, bf16[48,2560]{1,0:T(8,128)(2,1)S(1)}, u32[]{:S(2)}, u32[]{:S(2)}) %collective-permute-start.12) | collective-permute-done | bytes 245792 | tf_op jit(solution)/shard_map/ppermute | solution.py:553
  45.9 1.0 %finish.2.rest_2_ = bf16[48,5120]{1,0:T(8,128)(2,1)} custom-call(s32[40,128]{1,0:T(8,128)S(1)} %bitcast.10, f32[48,2560]{1,0:T(8,128)S(1)} %slice.21.rest_0_, bf16[48,2560]{1,0:T(8,128)(2,1)S(1)} %collective-permute-done.12.rest_1_), custom_call_target="tpu_custom_call" | custom-call | flops 1 | bytes 1 | tf_op jit(solution)/shard_map/finish/pallas_call | solution.py:43
  47.0 3.6 %collective-permute-done.11.rest_1_ = bf16[48,2560]{1,0:T(8,128)(2,1)S(1)} collective-permute-done((bf16[48,2560]{1,0:T(8,128)(2,1)S(1)}, bf16[48,2560]{1,0:T(8,128)(2,1)S(1)}, u32[]{:S(2)}, u32[]{:S(2)}) %collective-permute-start.11) | collective-permute-done | bytes 245792 | tf_op jit(solution)/shard_map/ppermute | solution.py:553
  50.6 1.0 %finish.3 = bf16[48,5120]{1,0:T(8,128)(2,1)} custom-call(s32[40,128]{1,0:T(8,128)S(1)} %bitcast.11, f32[48,2560]{1,0:T(8,128)S(1)} %slice.19.rest_0_, bf16[48,2560]{1,0:T(8,128)(2,1)S(1)} %collective-permute-done.11.rest_1_, bf16[48,5120]{1,0:T(8,128)(2,1)} %finish.2.rest_2_), custom_call_target="tpu_custom_call", output_to_operand_aliasing={{}: (3, {})} | custom-call | flops 1 | bytes 1 | tf_op jit(solution)/shard_map/finish/pallas_call | solution.py:43
  (43 shorter events, 6.2 us)
Async XLA Ops:
  1.3 3.1 %collective-permute-start.1 = (bf16[192,1280]{1,0:T(8,128)(2,1)S(1)}, bf16[192,1280]{1,0:T(8,128)(2,1)S(1)}, u32[]{:S(2)}, u32[]{:S(2)}) collective-permute-start(bf16[192,1280]{1,0:T(8,128)(2,1)S(1)} %get-tuple-element.19.rest_0_), channel_id=1, source_target_pairs={{0,1},{1,0},{2,3},{3,2},{4,5},{5,4},{6,7},{7,6},{8,9},{9,8},{10,11... | collective-permute-start | bytes 1474568 | tf_op jit(solution)/shard_map/ppermute | solution.py:553
  1.9 9.1 %collective-permute-start = (bf16[96,1280]{1,0:T(8,128)(2,1)S(1)}, bf16[96,1280]{1,0:T(8,128)(2,1)S(1)}, u32[]{:S(2)}, u32[]{:S(2)}) collective-permute-start(bf16[96,1280]{1,0:T(8,128)(2,1)S(1)} %get-tuple-element.18), channel_id=1, source_target_pairs={{0,2},{1,3},{2,0},{3,1},{4,6},{5,7},{6,4},{7,5},{8,10},{9,11},{10,... | collective-permute-start | bytes 737288 | tf_op jit(solution)/shard_map/ppermute | solution.py:553
  11.0 3.0 %collective-permute-start.2 = (bf16[96,1280]{1,0:T(8,128)(2,1)S(1)}, bf16[96,1280]{1,0:T(8,128)(2,1)S(1)}, u32[]{:S(2)}, u32[]{:S(2)}) collective-permute-start(bf16[96,1280]{1,0:T(8,128)(2,1)S(1)} %tie.3.rest_0_), channel_id=1, source_target_pairs={{0,1},{1,0},{2,3},{3,2},{4,5},{5,4},{6,7},{7,6},{8,9},{9,8},{10,11... | collective-permute-start | bytes 737288 | tf_op jit(solution)/shard_map/ppermute | solution.py:553
  11.0 8.4 %collective-permute-start.3 = (bf16[96,1280]{1,0:T(8,128)(2,1)S(1)}, bf16[96,1280]{1,0:T(8,128)(2,1)S(1)}, u32[]{:S(2)}, u32[]{:S(2)}) collective-permute-start(bf16[96,1280]{1,0:T(8,128)(2,1)S(1)} %get-tuple-element.21), channel_id=1, source_target_pairs={{0,2},{1,3},{2,0},{3,1},{4,6},{5,7},{6,4},{7,5},{8,10},{9,11},{10,... | collective-permute-start | bytes 737288 | tf_op jit(solution)/shard_map/ppermute | solution.py:553
  12.7 1.2 %copy-start.3 = (f32[3,768]{1,0:T(4,128)S(1)}, f32[3,768]{1,0:T(4,128)}, u32[]{:S(2)}) copy-start(f32[3,768]{1,0:T(4,128)} %rest_3_.3) | copy-start | bytes 27652
  12.7 1.2 %copy-start.4 = (s32[3,768]{1,0:T(4,128)S(1)}, s32[3,768]{1,0:T(4,128)}, u32[]{:S(2)}) copy-start(s32[3,768]{1,0:T(4,128)} %rest_4_.3) | copy-start | bytes 27652
  15.4 15.3 %collective-permute-start.8 = (bf16[2,96,768]{2,1,0:T(8,128)(2,1)S(1)}, bf16[2,96,768]{2,1,0:T(8,128)(2,1)S(1)}, u32[]{:S(2)}, u32[]{:S(2)}) collective-permute-start(bf16[2,96,768]{2,1,0:T(8,128)(2,1)S(1)} %project.6.array_ref.rest_1_), channel_id=1, source_target_pairs={{0,4},{8,12},{4,0},{12,8},{1,5},{9,13},{5,1},{13,9},{2,6},{10,14},... | collective-permute-start | bytes 884744 | tf_op jit(solution)/shard_map/ppermute | solution.py:622
  17.1 13.7 %collective-permute-start.7 = (bf16[2,96,768]{2,1,0:T(8,128)(2,1)S(1)}, bf16[2,96,768]{2,1,0:T(8,128)(2,1)S(1)}, u32[]{:S(2)}, u32[]{:S(2)}) collective-permute-start(bf16[2,96,768]{2,1,0:T(8,128)(2,1)S(1)} %project.6.array_ref.rest_1_), channel_id=1, source_target_pairs={{4,8},{8,4},{5,9},{9,5},{6,10},{10,6},{7,11},{11,7},{20,24},{24,20... | collective-permute-start | bytes 884744 | tf_op jit(solution)/shard_map/ppermute | solution.py:622
  19.4 1.5 %collective-permute-start.4 = (bf16[96,1280]{1,0:T(8,128)(2,1)S(1)}, bf16[96,1280]{1,0:T(8,128)(2,1)S(1)}, u32[]{:S(2)}, u32[]{:S(2)}) collective-permute-start(bf16[96,1280]{1,0:T(8,128)(2,1)S(1)} %tie.4.rest_2_.rest_0_), channel_id=1, source_target_pairs={{0,1},{1,0},{2,3},{3,2},{4,5},{5,4},{6,7},{7,6},{8,9},{9,8},{10,11... | collective-permute-start | bytes 737288 | tf_op jit(solution)/shard_map/ppermute | solution.py:553
  20.6 5.6 %copy-start.6 = (s32[1,3,27]{2,0,1:T(1,128)S(1)}, s32[1,3,27]{2,0,1:T(1,128)}, u32[]{:S(2)}) copy-start(s32[1,3,27]{2,0,1:T(1,128)} %param.15) | copy-start | bytes 976
  20.6 6.3 %copy-start = (s32[96,5120]{1,0:T(8,128)S(1)}, s32[96,5120]{1,0:T(8,128)}, u32[]{:S(2)}) copy-start(s32[96,5120]{1,0:T(8,128)} %codes_ref.1) | copy-start | bytes 5898244
  22.3 10.4 %collective-permute-start.6 = (bf16[2,96,768]{2,1,0:T(8,128)(2,1)S(1)}, bf16[2,96,768]{2,1,0:T(8,128)(2,1)S(1)}, u32[]{:S(2)}, u32[]{:S(2)}) collective-permute-start(bf16[2,96,768]{2,1,0:T(8,128)(2,1)S(1)} %project.9.after_ref.rest_2_), channel_id=1, source_target_pairs={{0,4},{8,12},{4,0},{12,8},{1,5},{9,13},{5,1},{13,9},{2,6},{10,14},... | collective-permute-start | bytes 884744 | tf_op jit(solution)/shard_map/ppermute | solution.py:622
  25.3 7.9 %collective-permute-start.5 = (bf16[2,96,768]{2,1,0:T(8,128)(2,1)S(1)}, bf16[2,96,768]{2,1,0:T(8,128)(2,1)S(1)}, u32[]{:S(2)}, u32[]{:S(2)}) collective-permute-start(bf16[2,96,768]{2,1,0:T(8,128)(2,1)S(1)} %project.9.after_ref.rest_2_), channel_id=1, source_target_pairs={{4,8},{8,4},{5,9},{9,5},{6,10},{10,6},{7,11},{11,7},{20,24},{24,20... | collective-permute-start | bytes 884744 | tf_op jit(solution)/shard_map/ppermute | solution.py:622
  31.3 1.9 %copy-start.5 = (s32[768]{0:T(1024)S(1)}, s32[768]{0:T(1024)}, u32[]{:S(2)}) copy-start(s32[768]{0:T(1024)} %param.16) | copy-start | bytes 9220
  32.7 1.1 %copy-start.1 = (f32[5120]{0:T(1024)S(1)}, f32[5120]{0:T(1024)}, u32[]{:S(2)}) copy-start(f32[5120]{0:T(1024)} %param.18) | copy-start | bytes 61444
  34.8 1.9 %collective-permute-start.9 = (bf16[96,2560]{1,0:T(8,128)(2,1)S(1)}, bf16[96,2560]{1,0:T(8,128)(2,1)S(1)}, u32[]{:S(2)}, u32[]{:S(2)}) collective-permute-start(bf16[96,2560]{1,0:T(8,128)(2,1)S(1)} %get-tuple-element.30), channel_id=1, source_target_pairs={{0,1},{1,0},{2,3},{3,2},{4,5},{5,4},{6,7},{7,6},{8,9},{9,8},{10,11... | collective-permute-start | bytes 1474568 | tf_op jit(solution)/shard_map/ppermute | solution.py:553
  36.9 9.0 %copy-start.2 = (s32[5120]{0:T(1024)S(1)}, s32[5120]{0:T(1024)}, u32[]{:S(2)}) copy-start(s32[5120]{0:T(1024)} %param.19) | copy-start | bytes 61444
  36.9 1.9 %collective-permute-start.10 = (bf16[96,2560]{1,0:T(8,128)(2,1)S(1)}, bf16[96,2560]{1,0:T(8,128)(2,1)S(1)}, u32[]{:S(2)}, u32[]{:S(2)}) collective-permute-start(bf16[96,2560]{1,0:T(8,128)(2,1)S(1)} %tie.5), channel_id=1, source_target_pairs={{0,1},{1,0},{2,3},{3,2},{4,5},{5,4},{6,7},{7,6},{8,9},{9,8},{10,11... | collective-permute-start | bytes 1474568 | tf_op jit(solution)/shard_map/ppermute | solution.py:553
  37.1 8.8 %collective-permute-start.12 = (bf16[48,2560]{1,0:T(8,128)(2,1)S(1)}, bf16[48,2560]{1,0:T(8,128)(2,1)S(1)}, u32[]{:S(2)}, u32[]{:S(2)}) collective-permute-start(bf16[48,2560]{1,0:T(8,128)(2,1)S(1)} %slice.25.refs_1_), channel_id=1, source_target_pairs={{0,2},{1,3},{2,0},{3,1},{4,6},{5,7},{6,4},{7,5},{8,10},{9,11},{10,... | collective-permute-start | bytes 737288 | tf_op jit(solution)/shard_map/ppermute | solution.py:553
  39.0 11.6 %collective-permute-start.11 = (bf16[48,2560]{1,0:T(8,128)(2,1)S(1)}, bf16[48,2560]{1,0:T(8,128)(2,1)S(1)}, u32[]{:S(2)}, u32[]{:S(2)}) collective-permute-start(bf16[48,2560]{1,0:T(8,128)(2,1)S(1)} %slice.24), channel_id=1, source_target_pairs={{0,2},{1,3},{2,0},{3,1},{4,6},{5,7},{6,4},{7,5},{8,10},{9,11},{10,... | collective-permute-start | bytes 737288 | tf_op jit(solution)/shard_map/ppermute | solution.py:553

commit v11 on v8

--- a/solution.py
+++ b/solution.py
@@ -19,6 +19,7 @@
 WORDS = HAD // PLANES
 QKV_ORDER = "half"
 OUT_ORDER = "byte"
+TURN_PIECES = 5
 
 epsilon = 1e-06
 f32 = jnp.float32
@@ -136,19 +137,24 @@
 
 
 def turn_kernel(x_hbm, sign_hbm, own_ref, send_ref, x_ref, sign_ref, sems):
-    copies = [
-        pltpu.make_async_copy(x_hbm, x_ref, sems.at[0]),
-        pltpu.make_async_copy(sign_hbm, sign_ref, sems.at[1]),
-    ]
-    for copy in copies:
+    blocks = x_ref.shape[1] // HAD
+    per_piece = blocks // TURN_PIECES
+    signs = pltpu.make_async_copy(sign_hbm, sign_ref, sems.at[TURN_PIECES])
+    copies = []
+    for piece in range(TURN_PIECES):
+        where = pl.ds(piece * per_piece * HAD, per_piece * HAD)
+        copies.append(
+            pltpu.make_async_copy(x_hbm.at[:, where], x_ref.at[:, where], sems.at[piece])
+        )
+    for copy in [signs] + copies:
         copy.start()
     matrix = hadamard(QKV_ORDER)
     factor = turn_factor(QKV_ORDER)
-    for copy in copies:
-        copy.wait()
-    blocks = x_ref.shape[1] // HAD
+    signs.wait()
     first = lax.axis_index("head") * blocks
     for b in range(blocks):
+        if b % per_piece == 0:
+            copies[b // per_piece].wait()
         cols = slice(b * HAD, (b + 1) * HAD)
         sign_row = signed(sign_ref[pl.ds(first + b, 1), :])
         flipped = (x_ref[:, cols].astype(f32) * sign_row).astype(bf16)
@@ -170,7 +176,7 @@
         scratch_shapes=[
             pltpu.VMEM(own_tokens.shape, bf16),
             pltpu.VMEM(sign_rows.shape, jnp.int32),
-            pltpu.SemaphoreType.DMA((2,)),
+            pltpu.SemaphoreType.DMA((TURN_PIECES + 1,)),
         ],
     )
 

time: 51.3 us -> 51.8 us (level)
  no operation moved by 1% of the time
where the time goes in v11:
time: 51.8 us; the launch traced here: 51 us
  Pallas kernels  21.8 us (42%)
  starting transfers between devices  16.2 us (31%)
  waiting for transfers between devices  12.1 us (23%)
    pallas_call x21, Pallas kernels, call(): pl.pallas_call(body, out_shape=out_shape, in_specs=in_specs, out_specs=ou...  21.8 us
    ppermute x9, waiting for transfers between devices, swap(): return lax.ppermute(shard, 'head', [(i, i ^ bit) for i in range(peers)])  11.7 us
    ppermute x9, starting transfers between devices, swap(): return lax.ppermute(shard, 'head', [(i, i ^ bit) for i in range(peers)])  8.35 us
    ppermute x4, starting transfers between devices, on_device(): lax.ppermute(key_value, 'height', pairs)  7.89 us
  transfers between devices with their start and end apart: 13, of which 8 were waited for; matrix products, arithmetic and copies ran while one was open for 0% of the time, Pallas kernels for 34%

profile of v11, /device:TPU:0, one launch (start us, length us, event | category | flops | bytes accessed | tf_op | source)
XLA Modules:
  0.0 51.0 jit_solution(10105881816107664836)
XLA Ops:
  0.0 1.8 %turn.1 = (bf16[192,1280]{1,0:T(8,128)(2,1)S(1)}, bf16[112,1280]{1,0:T(8,128)(2,1)S(1)}) custom-call(bf16[192,1280]{1,0:T(8,128)(2,1)} %bitcast.15, s32[40,128]{1,0:T(8,128)} %bitcast.16), custom_call_target="tpu_custom_call" | custom-call | flops 1 | bytes 1 | tf_op jit(solution)/shard_map/turn/pallas_call | solution.py:44
  2.3 2.6 %collective-permute-start = (bf16[112,1280]{1,0:T(8,128)(2,1)S(1)}, bf16[112,1280]{1,0:T(8,128)(2,1)S(1)}, u32[]{:S(2)}, u32[]{:S(2)}) collective-permute-start(bf16[112,1280]{1,0:T(8,128)(2,1)S(1)} %get-tuple-element.18), channel_id=1, source_target_pairs={{0,2},{1,3},{2,0},{3,1},{4,6},{5,7},{6,4},{7,5},{8,10},{9,11},{10,... | collective-permute-start | bytes 860168 | tf_op jit(solution)/shard_map/ppermute | solution.py:559
  4.9 4.5 %prepare.1 = (f32[3,192,768]{2,1,0:T(8,128)S(1)}, s32[2,3,160,768]{3,2,1,0:T(8,128)S(1)}, bf16[80,1280]{1,0:T(8,128)(2,1)S(1)}) custom-call(bf16[192,1280]{1,0:T(8,128)(2,1)S(1)} %get-tuple-element.19.rest_0_, bf16[192,1280]{1,0:T(8,128)(2,1)S(1)} %collective-permute-done.1.rest_1_, s32[3,640,768]{2,1,0:T(8,128)} %bitcast.14), custom_call_target="tpu_custom_call" | custom-call | flops 1 | bytes 1 | tf_op jit(solution)/shard_map/prepare/pallas_call | solution.py:44
  9.4 1.8 %collective-permute-start.3 = (bf16[80,1280]{1,0:T(8,128)(2,1)S(1)}, bf16[80,1280]{1,0:T(8,128)(2,1)S(1)}, u32[]{:S(2)}, u32[]{:S(2)}) collective-permute-start(bf16[80,1280]{1,0:T(8,128)(2,1)S(1)} %get-tuple-element.21), channel_id=1, source_target_pairs={{0,2},{1,3},{2,0},{3,1},{4,6},{5,7},{6,4},{7,5},{8,10},{9,11},{10,... | collective-permute-start | bytes 614408 | tf_op jit(solution)/shard_map/ppermute | solution.py:559
  11.2 1.1 %collective-permute-done.refs_0_ = bf16[112,1280]{1,0:T(8,128)(2,1)S(1)} collective-permute-done((bf16[112,1280]{1,0:T(8,128)(2,1)S(1)}, bf16[112,1280]{1,0:T(8,128)(2,1)S(1)}, u32[]{:S(2)}, u32[]{:S(2)}) %collective-permute-start) | collective-permute-done | bytes 286752 | tf_op jit(solution)/shard_map/ppermute | solution.py:559
  12.4 1.3 %project.5.rest_1_ = f32[2,112,768]{2,1,0:T(8,128)S(1)} custom-call(bf16[112,1280]{1,0:T(8,128)(2,1)S(1)} %tie.3.rest_0_, f32[3,192,768]{2,1,0:T(8,128)S(1)} %get-tuple-element.20.refs_1_.rest_1_.refs_2_.rest_4_, s32[2,3,160,768]{3,2,1,0:T(8,128)S(1)} %get-tuple-element.22.rest_2_.rest_5_), custom_call_target="tpu_custom_call" | custom-call | flops 4000000000 | bytes 1 | tf_op jit(solution)/shard_map/project/pallas_call | solution.py:44
  13.9 1.5 %project.6.array_ref.rest_1_ = bf16[2,112,768]{2,1,0:T(8,128)(2,1)S(1)} custom-call(bf16[112,1280]{1,0:T(8,128)(2,1)S(1)} %collective-permute-done.2.rest_0_.rest_1_, f32[2,112,768]{2,1,0:T(8,128)S(1)} %project.5.rest_1_, s32[2,3,160,768]{3,2,1,0:T(8,128)S(1)} %get-tuple-element.22.rest_2_.rest_5_, f32[3,768]{1,0:T(4,128)S(1)} %copy-done.3, ...), custom_call_target="tpu_custom_call" | custom-call | flops 1 | bytes 1 | tf_op jit(solution)/shard_map/project/pallas_call | solution.py:44
  15.5 1.9 %collective-permute-start.8 = (bf16[2,112,768]{2,1,0:T(8,128)(2,1)S(1)}, bf16[2,112,768]{2,1,0:T(8,128)(2,1)S(1)}, u32[]{:S(2)}, u32[]{:S(2)}) collective-permute-start(bf16[2,112,768]{2,1,0:T(8,128)(2,1)S(1)} %project.6.array_ref.rest_1_), channel_id=1, source_target_pairs={{0,4},{8,12},{4,0},{12,8},{1,5},{9,13},{5,1},{13,9},{2,6},{10,14},... | collective-permute-start | bytes 1032200 | tf_op jit(solution)/shard_map/ppermute | solution.py:628
  18.2 1.2 %project.8.rest_1_ = f32[2,80,768]{2,1,0:T(8,128)S(1)} custom-call(bf16[80,1280]{1,0:T(8,128)(2,1)S(1)} %tie.4.rest_2_.rest_0_, f32[3,192,768]{2,1,0:T(8,128)S(1)} %get-tuple-element.20.refs_1_.rest_1_.refs_2_.rest_4_, s32[2,3,160,768]{3,2,1,0:T(8,128)S(1)} %get-tuple-element.22.rest_2_.rest_5_), custom_call_target="tpu_custom_call" | custom-call | flops 4000000000 | bytes 1 | tf_op jit(solution)/shard_map/project/pallas_call | solution.py:44
  19.6 1.4 %project.9.after_ref.rest_2_ = bf16[2,80,768]{2,1,0:T(8,128)(2,1)S(1)} custom-call(bf16[80,1280]{1,0:T(8,128)(2,1)S(1)} %collective-permute-done.4.rest_3_.rest_0_, f32[2,80,768]{2,1,0:T(8,128)S(1)} %project.8.rest_1_, s32[2,3,160,768]{3,2,1,0:T(8,128)S(1)} %get-tuple-element.22.rest_2_.rest_5_, f32[3,768]{1,0:T(4,128)S(1)} %copy-done.3, s32[3,768]{1,0:T(4,128)S(1)} %copy-done.4), custom_call_target="tpu_custom_call" | custom-call | flops 1 | bytes 1 | tf_op jit(solution)/shard_map/project/pallas_call | solution.py:44
  21.1 4.4 %collective-permute-start.6 = (bf16[2,80,768]{2,1,0:T(8,128)(2,1)S(1)}, bf16[2,80,768]{2,1,0:T(8,128)(2,1)S(1)}, u32[]{:S(2)}, u32[]{:S(2)}) collective-permute-start(bf16[2,80,768]{2,1,0:T(8,128)(2,1)S(1)} %project.9.after_ref.rest_2_), channel_id=1, source_target_pairs={{0,4},{8,12},{4,0},{12,8},{1,5},{9,13},{5,1},{13,9},{2,6},{10,14},... | collective-permute-start | bytes 737288 | tf_op jit(solution)/shard_map/ppermute | solution.py:628
  25.5 0.8 %collective-permute-start.5 = (bf16[2,80,768]{2,1,0:T(8,128)(2,1)S(1)}, bf16[2,80,768]{2,1,0:T(8,128)(2,1)S(1)}, u32[]{:S(2)}, u32[]{:S(2)}) collective-permute-start(bf16[2,80,768]{2,1,0:T(8,128)(2,1)S(1)} %project.9.after_ref.rest_2_), channel_id=1, source_target_pairs={{4,8},{8,4},{5,9},{9,5},{6,10},{10,6},{7,11},{11,7},{20,24},{24,20... | collective-permute-start | bytes 737288 | tf_op jit(solution)/shard_map/ppermute | solution.py:628
  26.4 0.7 %window_masks.1 = (f32[3,192]{1,0:T(4,128)S(1)}, f32[3,224]{1,0:T(4,128)S(1)}, f32[3,80]{1,0:T(4,128)S(1)}, f32[3,80]{1,0:T(4,128)S(1)}) custom-call(s32[3,1,27]{2,1,0:T(1,128)S(1)} %bitcast.13, bf16[2,80,768]{2,1,0:T(8,128)(2,1)S(1)} %project.9.after_ref.rest_2_), custom_call_target="tpu_custom_call" | custom-call | flops 1 | bytes 1 | tf_op jit(solution)/shard_map/window_masks/pallas_call | solution.py:44
  27.1 1.5 %unpack_out.1.weights_ref = bf16[768,5120]{1,0:T(8,128)(2,1)S(1)} custom-call(s32[96,5120]{1,0:T(8,128)S(1)} %copy-done, bf16[2,80,768]{2,1,0:T(8,128)(2,1)S(1)} %project.9.after_ref.rest_2_), custom_call_target="tpu_custom_call" | custom-call | flops 1 | bytes 1 | tf_op jit(solution)/shard_map/unpack_out/pallas_call | solution.py:44
  28.6 1.8 %project.7.rest_0_ = bf16[1,192,768]{2,1,0:T(8,128)(2,1)S(1)} custom-call(bf16[112,1280]{1,0:T(8,128)(2,1)S(1)} %tie.3.rest_0_, bf16[112,1280]{1,0:T(8,128)(2,1)S(1)} %collective-permute-done.2.rest_0_.rest_1_, bf16[80,1280]{1,0:T(8,128)(2,1)S(1)} %tie.4.rest_2_.rest_0_, bf16[80,1280]{1,0:T(8,128)(2,1)S(1)} %collective-permute-done.4.rest_3_.rest_0_, ...), custom_call_target="tpu_custom_call" | custom-call | flops 4000000000 | bytes 1 | tf_op jit(solution)/shard_map/project/pallas_call | solution.py:44
  33.0 1.0 %out_project.3 = (bf16[96,2560]{1,0:T(8,128)(2,1)S(1)}, bf16[96,2560]{1,0:T(8,128)(2,1)S(1)}) custom-call(bf16[192,768]{1,0:T(8,128)(2,1)S(1)} %attend.7.rotated_ref, bf16[768,5120]{1,0:T(8,128)(2,1)S(1)} %unpack_out.1.weights_ref, f32[40,128]{1,0:T(8,128)S(1)} %bitcast.8), custom_call_target="tpu_custom_call" | custom-call | flops 1 | bytes 1 | tf_op jit(solution)/shard_map/out_project/pallas_call | solution.py:44
  34.1 1.0 %out_project.2 = (bf16[96,2560]{1,0:T(8,128)(2,1)S(1)}, bf16[96,2560]{1,0:T(8,128)(2,1)S(1)}) custom-call(bf16[192,768]{1,0:T(8,128)(2,1)S(1)} %attend.7.rotated_ref, bf16[768,5120]{1,0:T(8,128)(2,1)S(1)} %unpack_out.1.weights_ref, f32[40,128]{1,0:T(8,128)S(1)} %bitcast.9), custom_call_target="tpu_custom_call" | custom-call | flops 1 | bytes 1 | tf_op jit(solution)/shard_map/out_project/pallas_call | solution.py:44
  35.1 0.9 %collective-permute-done.9 = bf16[96,2560]{1,0:T(8,128)(2,1)S(1)} collective-permute-done((bf16[96,2560]{1,0:T(8,128)(2,1)S(1)}, bf16[96,2560]{1,0:T(8,128)(2,1)S(1)}, u32[]{:S(2)}, u32[]{:S(2)}) %collective-permute-start.9) | collective-permute-done | bytes 491552 | tf_op jit(solution)/shard_map/ppermute | solution.py:559
  36.3 1.5 %collective-permute-start.12 = (bf16[48,2560]{1,0:T(8,128)(2,1)S(1)}, bf16[48,2560]{1,0:T(8,128)(2,1)S(1)}, u32[]{:S(2)}, u32[]{:S(2)}) collective-permute-start(bf16[48,2560]{1,0:T(8,128)(2,1)S(1)} %slice.25.refs_1_), channel_id=1, source_target_pairs={{0,2},{1,3},{2,0},{3,1},{4,6},{5,7},{6,4},{7,5},{8,10},{9,11},{10,... | collective-permute-start | bytes 737288 | tf_op jit(solution)/shard_map/ppermute | solution.py:559
  38.2 1.6 %collective-permute-start.11 = (bf16[48,2560]{1,0:T(8,128)(2,1)S(1)}, bf16[48,2560]{1,0:T(8,128)(2,1)S(1)}, u32[]{:S(2)}, u32[]{:S(2)}) collective-permute-start(bf16[48,2560]{1,0:T(8,128)(2,1)S(1)} %slice.24), channel_id=1, source_target_pairs={{0,2},{1,3},{2,0},{3,1},{4,6},{5,7},{6,4},{7,5},{8,10},{9,11},{10,... | collective-permute-start | bytes 737288 | tf_op jit(solution)/shard_map/ppermute | solution.py:559
  39.8 5.3 %collective-permute-done.12.rest_1_ = bf16[48,2560]{1,0:T(8,128)(2,1)S(1)} collective-permute-done((bf16[48,2560]{1,0:T(8,128)(2,1)S(1)}, bf16[48,2560]{1,0:T(8,128)(2,1)S(1)}, u32[]{:S(2)}, u32[]{:S(2)}) %collective-permute-start.12) | collective-permute-done | bytes 245792 | tf_op jit(solution)/shard_map/ppermute | solution.py:559
  45.1 1.0 %finish.2.rest_2_ = bf16[48,5120]{1,0:T(8,128)(2,1)} custom-call(s32[40,128]{1,0:T(8,128)S(1)} %bitcast.10, f32[48,2560]{1,0:T(8,128)S(1)} %slice.21.rest_0_, bf16[48,2560]{1,0:T(8,128)(2,1)S(1)} %collective-permute-done.12.rest_1_), custom_call_target="tpu_custom_call" | custom-call | flops 1 | bytes 1 | tf_op jit(solution)/shard_map/finish/pallas_call | solution.py:44
  46.2 3.6 %collective-permute-done.11.rest_1_ = bf16[48,2560]{1,0:T(8,128)(2,1)S(1)} collective-permute-done((bf16[48,2560]{1,0:T(8,128)(2,1)S(1)}, bf16[48,2560]{1,0:T(8,128)(2,1)S(1)}, u32[]{:S(2)}, u32[]{:S(2)}) %collective-permute-start.11) | collective-permute-done | bytes 245792 | tf_op jit(solution)/shard_map/ppermute | solution.py:559
  49.8 1.0 %finish.3 = bf16[48,5120]{1,0:T(8,128)(2,1)} custom-call(s32[40,128]{1,0:T(8,128)S(1)} %bitcast.11, f32[48,2560]{1,0:T(8,128)S(1)} %slice.19.rest_0_, bf16[48,2560]{1,0:T(8,128)(2,1)S(1)} %collective-permute-done.11.rest_1_, bf16[48,5120]{1,0:T(8,128)(2,1)} %finish.2.rest_2_), custom_call_target="tpu_custom_call", output_to_operand_aliasing={{}: (3, {})} | custom-call | flops 1 | bytes 1 | tf_op jit(solution)/shard_map/finish/pallas_call | solution.py:44
  (43 shorter events, 5.2 us)
Async XLA Ops:
  1.8 3.1 %collective-permute-start.1 = (bf16[192,1280]{1,0:T(8,128)(2,1)S(1)}, bf16[192,1280]{1,0:T(8,128)(2,1)S(1)}, u32[]{:S(2)}, u32[]{:S(2)}) collective-permute-start(bf16[192,1280]{1,0:T(8,128)(2,1)S(1)} %get-tuple-element.19.rest_0_), channel_id=1, source_target_pairs={{0,1},{1,0},{2,3},{3,2},{4,5},{5,4},{6,7},{7,6},{8,9},{9,8},{10,11... | collective-permute-start | bytes 1474568 | tf_op jit(solution)/shard_map/ppermute | solution.py:559
  2.3 10.0 %collective-permute-start = (bf16[112,1280]{1,0:T(8,128)(2,1)S(1)}, bf16[112,1280]{1,0:T(8,128)(2,1)S(1)}, u32[]{:S(2)}, u32[]{:S(2)}) collective-permute-start(bf16[112,1280]{1,0:T(8,128)(2,1)S(1)} %get-tuple-element.18), channel_id=1, source_target_pairs={{0,2},{1,3},{2,0},{3,1},{4,6},{5,7},{6,4},{7,5},{8,10},{9,11},{10,... | collective-permute-start | bytes 860168 | tf_op jit(solution)/shard_map/ppermute | solution.py:559
  9.4 8.7 %collective-permute-start.3 = (bf16[80,1280]{1,0:T(8,128)(2,1)S(1)}, bf16[80,1280]{1,0:T(8,128)(2,1)S(1)}, u32[]{:S(2)}, u32[]{:S(2)}) collective-permute-start(bf16[80,1280]{1,0:T(8,128)(2,1)S(1)} %get-tuple-element.21), channel_id=1, source_target_pairs={{0,2},{1,3},{2,0},{3,1},{4,6},{5,7},{6,4},{7,5},{8,10},{9,11},{10,... | collective-permute-start | bytes 614408 | tf_op jit(solution)/shard_map/ppermute | solution.py:559
  12.4 1.6 %collective-permute-start.2 = (bf16[112,1280]{1,0:T(8,128)(2,1)S(1)}, bf16[112,1280]{1,0:T(8,128)(2,1)S(1)}, u32[]{:S(2)}, u32[]{:S(2)}) collective-permute-start(bf16[112,1280]{1,0:T(8,128)(2,1)S(1)} %tie.3.rest_0_), channel_id=1, source_target_pairs={{0,1},{1,0},{2,3},{3,2},{4,5},{5,4},{6,7},{7,6},{8,9},{9,8},{10,11... | collective-permute-start | bytes 860168 | tf_op jit(solution)/shard_map/ppermute | solution.py:559
  12.4 1.6 %copy-start.3 = (f32[3,768]{1,0:T(4,128)S(1)}, f32[3,768]{1,0:T(4,128)}, u32[]{:S(2)}) copy-start(f32[3,768]{1,0:T(4,128)} %rest_3_.3) | copy-start | bytes 27652
  12.4 1.6 %copy-start.4 = (s32[3,768]{1,0:T(4,128)S(1)}, s32[3,768]{1,0:T(4,128)}, u32[]{:S(2)}) copy-start(s32[3,768]{1,0:T(4,128)} %rest_4_.3) | copy-start | bytes 27652
  15.5 15.5 %collective-permute-start.8 = (bf16[2,112,768]{2,1,0:T(8,128)(2,1)S(1)}, bf16[2,112,768]{2,1,0:T(8,128)(2,1)S(1)}, u32[]{:S(2)}, u32[]{:S(2)}) collective-permute-start(bf16[2,112,768]{2,1,0:T(8,128)(2,1)S(1)} %project.6.array_ref.rest_1_), channel_id=1, source_target_pairs={{0,4},{8,12},{4,0},{12,8},{1,5},{9,13},{5,1},{13,9},{2,6},{10,14},... | collective-permute-start | bytes 1032200 | tf_op jit(solution)/shard_map/ppermute | solution.py:628
  17.4 13.6 %collective-permute-start.7 = (bf16[2,112,768]{2,1,0:T(8,128)(2,1)S(1)}, bf16[2,112,768]{2,1,0:T(8,128)(2,1)S(1)}, u32[]{:S(2)}, u32[]{:S(2)}) collective-permute-start(bf16[2,112,768]{2,1,0:T(8,128)(2,1)S(1)} %project.6.array_ref.rest_1_), channel_id=1, source_target_pairs={{4,8},{8,4},{5,9},{9,5},{6,10},{10,6},{7,11},{11,7},{20,24},{24,20... | collective-permute-start | bytes 1032200 | tf_op jit(solution)/shard_map/ppermute | solution.py:628
  18.1 1.5 %collective-permute-start.4 = (bf16[80,1280]{1,0:T(8,128)(2,1)S(1)}, bf16[80,1280]{1,0:T(8,128)(2,1)S(1)}, u32[]{:S(2)}, u32[]{:S(2)}) collective-permute-start(bf16[80,1280]{1,0:T(8,128)(2,1)S(1)} %tie.4.rest_2_.rest_0_), channel_id=1, source_target_pairs={{0,1},{1,0},{2,3},{3,2},{4,5},{5,4},{6,7},{7,6},{8,9},{9,8},{10,11... | collective-permute-start | bytes 614408 | tf_op jit(solution)/shard_map/ppermute | solution.py:559
  19.3 7.0 %copy-start.6 = (s32[1,3,27]{2,0,1:T(1,128)S(1)}, s32[1,3,27]{2,0,1:T(1,128)}, u32[]{:S(2)}) copy-start(s32[1,3,27]{2,0,1:T(1,128)} %param.15) | copy-start | bytes 976
  19.3 7.8 %copy-start = (s32[96,5120]{1,0:T(8,128)S(1)}, s32[96,5120]{1,0:T(8,128)}, u32[]{:S(2)}) copy-start(s32[96,5120]{1,0:T(8,128)} %codes_ref.1) | copy-start | bytes 5898244
  21.1 10.8 %collective-permute-start.6 = (bf16[2,80,768]{2,1,0:T(8,128)(2,1)S(1)}, bf16[2,80,768]{2,1,0:T(8,128)(2,1)S(1)}, u32[]{:S(2)}, u32[]{:S(2)}) collective-permute-start(bf16[2,80,768]{2,1,0:T(8,128)(2,1)S(1)} %project.9.after_ref.rest_2_), channel_id=1, source_target_pairs={{0,4},{8,12},{4,0},{12,8},{1,5},{9,13},{5,1},{13,9},{2,6},{10,14},... | collective-permute-start | bytes 737288 | tf_op jit(solution)/shard_map/ppermute | solution.py:628
  25.5 6.8 %collective-permute-start.5 = (bf16[2,80,768]{2,1,0:T(8,128)(2,1)S(1)}, bf16[2,80,768]{2,1,0:T(8,128)(2,1)S(1)}, u32[]{:S(2)}, u32[]{:S(2)}) collective-permute-start(bf16[2,80,768]{2,1,0:T(8,128)(2,1)S(1)} %project.9.after_ref.rest_2_), channel_id=1, source_target_pairs={{4,8},{8,4},{5,9},{9,5},{6,10},{10,6},{7,11},{11,7},{20,24},{24,20... | collective-permute-start | bytes 737288 | tf_op jit(solution)/shard_map/ppermute | solution.py:628
  31.5 0.8 %copy-start.5 = (s32[768]{0:T(1024)S(1)}, s32[768]{0:T(1024)}, u32[]{:S(2)}) copy-start(s32[768]{0:T(1024)} %param.16) | copy-start | bytes 9220
  31.9 1.1 %copy-start.1 = (f32[5120]{0:T(1024)S(1)}, f32[5120]{0:T(1024)}, u32[]{:S(2)}) copy-start(f32[5120]{0:T(1024)} %param.18) | copy-start | bytes 61444
  34.0 1.9 %collective-permute-start.9 = (bf16[96,2560]{1,0:T(8,128)(2,1)S(1)}, bf16[96,2560]{1,0:T(8,128)(2,1)S(1)}, u32[]{:S(2)}, u32[]{:S(2)}) collective-permute-start(bf16[96,2560]{1,0:T(8,128)(2,1)S(1)} %get-tuple-element.30), channel_id=1, source_target_pairs={{0,1},{1,0},{2,3},{3,2},{4,5},{5,4},{6,7},{7,6},{8,9},{9,8},{10,11... | collective-permute-start | bytes 1474568 | tf_op jit(solution)/shard_map/ppermute | solution.py:559
  36.1 9.0 %copy-start.2 = (s32[5120]{0:T(1024)S(1)}, s32[5120]{0:T(1024)}, u32[]{:S(2)}) copy-start(s32[5120]{0:T(1024)} %param.19) | copy-start | bytes 61444
  36.1 1.9 %collective-permute-start.10 = (bf16[96,2560]{1,0:T(8,128)(2,1)S(1)}, bf16[96,2560]{1,0:T(8,128)(2,1)S(1)}, u32[]{:S(2)}, u32[]{:S(2)}) collective-permute-start(bf16[96,2560]{1,0:T(8,128)(2,1)S(1)} %tie.5), channel_id=1, source_target_pairs={{0,1},{1,0},{2,3},{3,2},{4,5},{5,4},{6,7},{7,6},{8,9},{9,8},{10,11... | collective-permute-start | bytes 1474568 | tf_op jit(solution)/shard_map/ppermute | solution.py:559
  36.3 8.8 %collective-permute-start.12 = (bf16[48,2560]{1,0:T(8,128)(2,1)S(1)}, bf16[48,2560]{1,0:T(8,128)(2,1)S(1)}, u32[]{:S(2)}, u32[]{:S(2)}) collective-permute-start(bf16[48,2560]{1,0:T(8,128)(2,1)S(1)} %slice.25.refs_1_), channel_id=1, source_target_pairs={{0,2},{1,3},{2,0},{3,1},{4,6},{5,7},{6,4},{7,5},{8,10},{9,11},{10,... | collective-permute-start | bytes 737288 | tf_op jit(solution)/shard_map/ppermute | solution.py:559
  38.2 11.6 %collective-permute-start.11 = (bf16[48,2560]{1,0:T(8,128)(2,1)S(1)}, bf16[48,2560]{1,0:T(8,128)(2,1)S(1)}, u32[]{:S(2)}, u32[]{:S(2)}) collective-permute-start(bf16[48,2560]{1,0:T(8,128)(2,1)S(1)} %slice.24), channel_id=1, source_target_pairs={{0,2},{1,3},{2,0},{3,1},{4,6},{5,7},{6,4},{7,5},{8,10},{9,11},{10,... | collective-permute-start | bytes 737288 | tf_op jit(solution)/shard_map/ppermute | solution.py:559
